TPU v7x, 32 devices: a whole 2x2x4 slice. The times are simulated.
32 devices in a mesh: groups: 2 (over y), item: 4 (over z), dp: 2 (over core), tensor: 2 (over x).
Axes of the slice: x: 2, y: 2, z: 4, core: 2. Of those that a mesh axis runs over, the one named last changes fastest.
Arguments:
- events: bfloat16 [12288, 1024], P(('groups', 'item', 'dp')), parts along dimension 0, may hold values from -6 to 6
- lengths: int32 [16], P('groups'), parts along dimension 0, may hold values from 192 to 768, as said below
- packing: int32 [16], P('groups'), parts along dimension 0, may hold values from 0 to 7, each once
- positions: int32 [16, 64], P('groups'), parts along dimension 0, may hold values from 0 to 767, as said below
- logged: int32 [16, 64], P('groups'), parts along dimension 0, may hold values from 0 to 16383
- w_uvqk: bfloat16 [1024, 1024], P(None, 'tensor'), may hold values from -0.1875 to 0.1875
- w_out: bfloat16 [256, 1024], P('tensor'), may hold values from -0.375 to 0.375
- catalogue: bfloat16 [16384, 1024], P(('item', 'dp', 'tensor')), may hold values from -0.46875 to 0.46875
Outputs:
- scoring_state: bfloat16 [1024, 1024], P(('groups', 'item', 'dp'), 'tensor'), parts along dimension 0
- log_propensity: float32 [1024], P(('groups', 'item', 'dp')), parts along dimension 0
There are 2 independent parts, one for each index of `groups`. A program takes and returns all parts, laid end to end along the dimension named above; an argument that names none is the same for every part. Nothing has to cross between parts.
Inputs may be any that keep to these rules, and one draw needn't show every extreme that they name: `lengths`: one history has exactly 768 valid events and one exactly 192. positions[h, k] < lengths[h]. `packing`: each history id appears once.
All inputs are finite; a program needn't handle non-finite values.
Results may differ from a plain program's by a relative error of at most 0.0048.
Values may be sent and summed in bfloat16 or wider, within the bound.
No kernel may reach another device: no remote copies, remote signals or barrier semaphores. Data moves between devices by JAX's collectives and lax.ppermute only.
A program may use at most 64 MiB of HBM per device.

v0:
```python
import math

import jax
import jax.numpy as jnp
from jax import lax
from jax.sharding import PartitionSpec as P

DH = 128


def pick_target(logits, item_ids, item_base):
    local_ids = item_ids - item_base
    matches = jnp.arange(logits.shape[1], dtype=jnp.int32)[None, :] == local_ids[:, None]
    return jnp.sum(jnp.where(matches, logits, 0.0), axis=1)


def local(events, lengths, packing, positions, logged, w_uvqk, w_out, catalogue):
    slot_rows, model_width = events.shape
    hist_count = packing.shape[0]
    imp_count = positions.shape[1]
    local_heads = w_out.shape[0] // DH
    item_count = catalogue.shape[0]
    slot_index = lax.axis_index(("item", "dp"))
    hist_ids = jnp.arange(hist_count, dtype=jnp.int32)
    slot_pick = (packing[:, None] == hist_ids[None, :]).astype(jnp.int32)
    owned = (hist_ids == slot_index).astype(jnp.int32)
    hist_row = jnp.sum(slot_pick * owned[:, None], axis=0)
    hist_length = jnp.sum(hist_row * lengths)
    event_spots = jnp.sum(hist_row[:, None] * positions, axis=0)
    slot_items = jnp.sum(slot_pick[:, :, None] * logged[None, :, :], axis=1).reshape(
        hist_count * imp_count
    )
    item_base = lax.axis_index(("item", "dp", "tensor")) * item_count
    split_weights = w_uvqk.reshape(model_width, local_heads, 4, DH)
    w_values_keys = split_weights[:, :, 1::2].reshape(model_width, local_heads * 2 * DH)
    w_gate_query = split_weights[:, :, 0::2].reshape(model_width, local_heads * 2 * DH)
    values_keys = jnp.dot(events, w_values_keys, preferred_element_type=jnp.float32)
    values_keys = (
        jax.nn.silu(values_keys).astype(jnp.bfloat16).reshape(slot_rows, local_heads, 2, DH)
    )
    chosen = jnp.take(events, event_spots, axis=0)
    gate_query = jnp.dot(chosen, w_gate_query, preferred_element_type=jnp.float32)
    gate_query = jax.nn.silu(gate_query).astype(jnp.bfloat16).reshape(imp_count, local_heads, 2, DH)
    scores = jnp.einsum(
        "ied,med->iem",
        gate_query[:, :, 1],
        values_keys[:, :, 1],
        preferred_element_type=jnp.float32,
    ) / math.sqrt(DH)
    slot_range = jnp.arange(slot_rows, dtype=jnp.int32)
    is_valid = (slot_range[None, :] <= event_spots[:, None]) & (slot_range[None, :] < hist_length)
    weights = jnp.where(is_valid[:, None, :], jax.nn.silu(scores), 0.0).astype(jnp.bfloat16)
    attended = jnp.einsum(
        "iem,med->ied", weights, values_keys[:, :, 0], preferred_element_type=jnp.float32
    )
    inverse = lax.rsqrt(jnp.mean(attended * attended, axis=-1, keepdims=True) + 1e-06)
    gated_rows = (attended * inverse * gate_query[:, :, 0].astype(jnp.float32)).astype(jnp.bfloat16)
    gated_rows = gated_rows.reshape(imp_count, local_heads * DH)
    partial_out = jnp.dot(gated_rows, w_out, preferred_element_type=jnp.float32)
    residual = chosen.astype(jnp.float32)
    col_share = model_width // lax.axis_size("tensor")
    col_start = lax.axis_index("tensor") * col_share
    summed = lax.psum(partial_out, "tensor")
    hidden_state = (summed + residual).astype(jnp.bfloat16)
    state_out = lax.dynamic_slice_in_dim(hidden_state, col_start, col_share, 1)
    logits = lax.dot_general(
        lax.all_gather(hidden_state, ("item", "dp"), axis=0, tiled=True),
        catalogue,
        (((1,), (1,)), ((), ())),
        preferred_element_type=jnp.float32,
    )
    new_totals = jnp.sum(jnp.exp(logits), axis=1)
    new_target = pick_target(logits, slot_items, item_base)
    whole_totals, whole_target = lax.psum((new_totals, new_target), ("item", "dp", "tensor"))
    mine_totals = lax.dynamic_slice_in_dim(whole_totals, slot_index * imp_count, imp_count, 0)
    mine_target = lax.dynamic_slice_in_dim(whole_target, slot_index * imp_count, imp_count, 0)
    return (state_out, mine_target - jnp.log(mine_totals))


def solution(mesh):
    placed = (
        P(("groups", "item", "dp"), None),
        P("groups"),
        P("groups"),
        P("groups", None),
        P("groups", None),
        P(None, "tensor"),
        P("tensor", None),
        P(("item", "dp", "tensor"), None),
    )
    return jax.shard_map(
        local,
        mesh=mesh,
        in_specs=placed,
        out_specs=(P(("groups", "item", "dp"), "tensor"), P(("groups", "item", "dp"))),
        check_vma=False,
    )
```

profile of v0, /device:TPU:0, one launch (start us, length us, event | category | flops | bytes accessed | tf_op | source)
XLA Modules:
  0.0 136.1 jit_solution(11309855949234600494)
XLA Ops:
  7.2 0.0 copy-start
  7.2 0.0 all-reduce.3.cloned.1.call-start
  7.2 0.9 select_reduce_fusion.1
  8.1 0.8 multiply_reduce_fusion.2
  8.9 1.3 reshape.175
  10.3 0.0 copy-start.5
  10.3 12.4 %slice.21 = bf16[1024,1,2,128]{3,2,0,1:T(2,128)(2,1)} slice(bf16[1024,1,4,128]{3,2,0,1:T(4,128)(2,1)S(1)} %reshape.175), slice={[0:1024:1], [0:1:1], [0:4:2], [0:128:1]} | slice | bytes 1048576 | tf_op jit(solution)/shard_map/slice | solution.py:36
  22.6 12.4 %slice.18 = bf16[1024,1,2,128]{3,2,0,1:T(2,128)(2,1)} slice(bf16[1024,1,4,128]{3,2,0,1:T(4,128)(2,1)S(1)} %reshape.175), slice={[0:1024:1], [0:1:1], [1:4:2], [0:128:1]} | slice | bytes 1048576 | tf_op jit(solution)/shard_map/slice | solution.py:35
  35.0 0.0 copy-start.1
  35.0 2.5 %gather_fusion = bf16[64,1024]{1,0:T(8,128)(2,1)S(1)} fusion(bf16[768,1024]{1,0:T(8,128)(2,1)} %param.8, s32[1024]{0:T(1024)S(1)} %pad_clamp_fusion), kind=kCustom, calls=%fused_computation | custom fusion | bytes 262400 | tf_op jit(solution)/shard_map/jit(_take)/gather | solution.py:41
  37.5 1.3 multiply_convert_fusion.1
  38.8 0.1 fusion.30
  38.9 0.0 copy-done.5
  38.9 0.6 multiply_reduce_fusion.3
  39.5 0.6 iota_compare_fusion.2
  40.2 0.0 copy-done.1
  40.2 0.0 copy-start.2
  40.2 2.1 %multiply_convert_fusion = bf16[768,256]{0,1:T(8,128)(2,1)S(1)} fusion(bf16[768,1024]{1,0:T(8,128)(2,1)} %param.8, bf16[128,8,2,128]{3,2,1,0:T(2,128)(2,1)S(1)} %bitcast.81), kind=kOutput, calls=%fused_computation.7 | convolution fusion | flops 403636224 | bytes 2490368 | tf_op jit(solution)/shard_map/dot_general | solution.py:37
  42.4 0.0 copy-start.4
  42.4 0.0 copy-start.3
  42.4 0.4 multiply_reduce_fusion.1
  42.8 0.0 copy-done.2
  42.8 0.9 fusion.21
  43.8 0.0 all-reduce.3.cloned.1.call-update
  43.8 0.0 all-gather.2.cloned.1.call-start
  43.9 26.0 %all-reduce.3.cloned.1.call-done = f32[64,1024]{1,0:T(8,128)} async-done(((f32[64,1024]{1,0:T(8,128)}), f32[64,1024]{1,0:T(8,128)}) %all-reduce.3.cloned.1.call-update) | async-done | bytes 262160 | tf_op jit(solution)/shard_map/psum | solution.py:63
  69.8 1.7 %add_convert_fusion = bf16[64,1024]{1,0:T(8,128)(2,1)} fusion(f32[64,1024]{1,0:T(8,128)} %all-reduce.3.cloned.1.call-done, bf16[64,1024]{1,0:T(8,128)(2,1)S(1)} %gather_fusion, pred[64]{0:T(512)(128)(4,1)S(1)} %compare_and_fusion), kind=kLoop, calls=%fused_computation.14 | loop fusion | flops 262144 | bytes 524352 | tf_op jit(solution)/shard_map/convert_element_type | solution.py:64
  71.5 0.0 all-gather.2.cloned.1.call-update
  71.6 0.0 copy-done.4
  71.6 0.1 fusion.24
  71.6 0.0 copy-done.3
  71.7 0.1 multiply_reduce_fusion
  71.8 0.1 sub.18
  71.8 1.5 %constant_dynamic-slice_fusion = bf16[64,512]{1,0:T(8,128)(2,1)} fusion(bf16[64,1024]{1,0:T(8,128)(2,1)} %add_convert_fusion, s32[]{:T(128)S(6)} %select_n.39), kind=kLoop, calls=%fused_computation.52 | loop fusion | bytes 131076 | tf_op jit(solution)/shard_map/dynamic_slice | solution.py:65
  73.3 20.5 %all-gather.2.cloned.1.call-done = bf16[512,1024]{1,0:T(8,128)(2,1)} async-done(((bf16[64,1024]{1,0:T(8,128)(2,1)}), bf16[512,1024]{1,0:T(8,128)(2,1)}) %all-gather.2.cloned.1.call-update) | async-done | bytes 1048592 | tf_op jit(solution)/shard_map/all_gather | solution.py:67
  93.8 0.0 copy-done
  93.8 2.8 %select_reduce_fusion = (f32[512]{0:T(512)S(1)}, f32[512]{0:T(512)S(1)}) fusion(s32[512]{0:T(512)S(1)} %sub.18, bf16[512,1024]{1,0:T(8,128)(2,1)} %all-gather.2.cloned.1.call-done, bf16[1024,1024]{1,0:T(8,128)(2,1)S(1)} %copy-done), kind=kOutput, calls=%fused_computation.2 | convolution fusion | flops 1075837952 | bytes 3151872 | tf_op jit(solution)/shard_map/dot_general | solution.py:66
  96.6 32.1 %all-reduce = (f32[512]{0:T(512)S(1)}, f32[512]{0:T(512)S(1)}) all-reduce(f32[512]{0:T(512)S(1)} %get-tuple-element.3, f32[512]{0:T(512)S(1)} %get-tuple-element.2), channel_id=1, replica_groups=mesh['groups'=2,'item'=4,'dp'=2,'tensor'=2] {'item','dp','tensor'}, use_global_device_ids=true, to_apply=%region_9.10 | all-reduce | flops 1024 | bytes 8192 | tf_op jit(solution)/shard_map/psum | solution.py:74
  128.7 0.6 log_subtract_fusion
  (7 shorter events, 0.1 us)
Async XLA Ops:
  7.2 86.7 %copy-start = (bf16[1024,1024]{1,0:T(8,128)(2,1)S(1)}, bf16[1024,1024]{1,0:T(8,128)(2,1)}, u32[]{:S(2)}) copy-start(bf16[1024,1024]{1,0:T(8,128)(2,1)} %param.15) | copy-start | bytes 6291460
  7.2 62.7 %all-reduce.3.cloned.1.call-start = ((), (), s32[]{:S(2)}) async-start(), calls=%async_computation | async-start | bytes 524288 | tf_op jit(solution)/shard_map/psum | solution.py:63
  10.3 28.6 %copy-start.5 = (s32[8]{0:T(128)S(1)}, s32[8]{0:T(128)}, u32[]{:S(2)}) copy-start(s32[8]{0:T(128)} %param.9) | copy-start | bytes 100
  35.0 5.2 %copy-start.1 = (bf16[1024,1,2,128]{3,2,0,1:T(2,128)(2,1)S(1)}, bf16[1024,1,2,128]{3,2,0,1:T(2,128)(2,1)}, u32[]{:S(2)}) copy-start(bf16[1024,1,2,128]{3,2,0,1:T(2,128)(2,1)} %slice.18) | copy-start | bytes 1572868
  40.2 2.6 %copy-start.2 = (bf16[128,1024]{1,0:T(8,128)(2,1)S(1)}, bf16[128,1024]{1,0:T(8,128)(2,1)}, u32[]{:S(2)}) copy-start(bf16[128,1024]{1,0:T(8,128)(2,1)} %param.14) | copy-start | bytes 786436
  42.4 29.2 %copy-start.4 = (s32[8]{0:T(128)S(1)}, s32[8]{0:T(128)}, u32[]{:S(2)}) copy-start(s32[8]{0:T(128)} %param.10) | copy-start | bytes 100
  42.4 29.3 %copy-start.3 = (s32[8,64]{1,0:T(8,128)S(1)}, s32[8,64]{1,0:T(8,128)}, u32[]{:S(2)}) copy-start(s32[8,64]{1,0:T(8,128)} %param.12) | copy-start | bytes 6148
  43.8 50.0 %all-gather.2.cloned.1.call-start = ((), (), s32[]{:S(2)}) async-start(), calls=%async_computation.1 | async-start | bytes 1179648 | tf_op jit(solution)/shard_map/all_gather | solution.py:67
Sparse Core Ops, SparseCore 0:
  43.9 25.8 all-reduce.2
  71.7 22.0 all-gather.1
where the time goes:
time: 137 us; the launch traced here: 136 us
  waiting for transfers between devices  46.5 us (34%)
  blocking collectives  32.1 us (23%)
  local copies, waits for them, and re-layouts  30.2 us (22%)
  between operations  14.2 us (10%)
  matrix products  7.63 us (6%)
  other arithmetic  5.41 us (4%)
    psum x1, blocking collectives, local(): lax.psum((new_totals, new_target), ('item', 'dp', 'tensor'))  32.1 us
    psum x1, waiting for transfers between devices, local(): summed = lax.psum(partial_out, 'tensor')  26 us
    all_gather x1, waiting for transfers between devices, local(): lax.all_gather(hidden_state, ('item', 'dp'), axis=0, tiled=True)  20.5 us
    slice x1, local copies, waits for them, and re-layouts, local(): split_weights[:, :, 1::2].reshape(model_width, local_heads * 2 * DH)  12.4 us
    slice x1, local copies, waits for them, and re-layouts, local(): split_weights[:, :, 0::2].reshape(model_width, local_heads * 2 * DH)  12.4 us
    dot_general x1, matrix products, local(): lax.dot_general(lax.all_gather(hidden_state, ('item', 'dp'), axis=0, tile...  2.82 us
  transfers between devices with their start and end apart: 2, of which 2 were waited for; matrix products, arithmetic and copies ran while one was open for 1% of the time, Pallas kernels for 0%

commit v1 on v0

v1 whole, which is shorter than its diff:
```python
import functools
import math

import jax
import jax.numpy as jnp
from jax import lax
from jax.experimental import pallas as pl
from jax.experimental.pallas import tpu as pltpu
from jax.sharding import PartitionSpec as P

DH = 128
SLOTS = ("item", "dp")
EVERY = ("item", "dp", "tensor")
NT = (((1,), (1,)), ((), ()))
VMEM_LIMIT = 32 * 1024 * 1024


def whole_spec(space=pltpu.VMEM):
    return pl.BlockSpec(memory_space=space)


def position_column(packing, positions, slot):
    row = positions[pl.ds(packing[slot], 1), :].astype(jnp.float32)
    count = row.shape[1]
    diagonal = lax.broadcasted_iota(jnp.int32, (count, count), 0) == lax.broadcasted_iota(
        jnp.int32, (count, count), 1
    )
    return jnp.sum(jnp.where(diagonal, row, 0.0), axis=1, keepdims=True).astype(jnp.int32)


def pick_kernel(place, packing, positions, events, chosen):
    rows = events.shape[0]
    spots = position_column(packing, positions, place[0])
    lanes = lax.broadcasted_iota(jnp.int32, (spots.shape[0], rows), 1)
    one_hot = jnp.where(lanes == spots, 1.0, 0.0).astype(jnp.bfloat16)
    chosen[...] = jnp.dot(one_hot, events[...], preferred_element_type=jnp.float32).astype(
        jnp.bfloat16
    )


def attend_kernel(place, packing, lengths, positions, events, chosen, w_uvqk, gated):
    rows = events.shape[0]
    slot = place[0]
    length = lengths[packing[slot]]
    spots = position_column(packing, positions, slot)
    lanes = lax.broadcasted_iota(jnp.int32, (spots.shape[0], rows), 1)
    valid = (lanes <= spots) & (lanes < length)
    for head in range(gated.shape[1] // DH):
        first = head * 4 * DH
        w_part = [w_uvqk[:, first + k * DH : first + (k + 1) * DH] for k in range(4)]
        w_gate_query = jnp.concatenate([w_part[0], w_part[2]], axis=1)
        w_value_key = jnp.concatenate([w_part[1], w_part[3]], axis=1)
        gate_query = jnp.dot(chosen[...], w_gate_query, preferred_element_type=jnp.float32)
        gate_query = jax.nn.silu(gate_query).astype(jnp.bfloat16)
        value_key = jnp.dot(events[...], w_value_key, preferred_element_type=jnp.float32)
        value_key = jax.nn.silu(value_key).astype(jnp.bfloat16)
        scores = lax.dot_general(
            gate_query[:, DH:], value_key[:, DH:], NT, preferred_element_type=jnp.float32
        ) / math.sqrt(DH)
        weights = jnp.where(valid, jax.nn.silu(scores), 0.0).astype(jnp.bfloat16)
        attended = jnp.dot(weights, value_key[:, :DH], preferred_element_type=jnp.float32)
        inverse = lax.rsqrt(jnp.mean(attended * attended, axis=-1, keepdims=True) + 1e-06)
        gated[:, head * DH : (head + 1) * DH] = (
            attended * inverse * gate_query[:, :DH].astype(jnp.float32)
        ).astype(jnp.bfloat16)


def score_kernel(slots, tensors, place, packing, logged, *refs):
    chosen, refs = refs[:slots], refs[slots:]
    gated, refs = refs[:slots], refs[slots:]
    w_out, refs = refs[:tensors], refs[tensors:]
    catalogue, state, sums, hidden, wanted = refs
    slot, tensor = place[0], place[1]
    imps = chosen[0].shape[0]
    items = catalogue.shape[0]
    local_width = w_out[0].shape[0]
    for r in range(slots):
        total = chosen[r][...].astype(jnp.float32)
        for t in range(tensors):
            total += jnp.dot(
                gated[r][:, t * local_width : (t + 1) * local_width],
                w_out[t][...],
                preferred_element_type=jnp.float32,
            )
        hidden[r * imps : (r + 1) * imps, :] = total.astype(jnp.bfloat16)
        wanted[0:1, r * imps : (r + 1) * imps] = logged[pl.ds(packing[slot ^ r], 1), :]
    share = state.shape[1]
    state[...] = hidden[0:imps, pl.ds(pl.multiple_of(tensor * share, share), share)]
    item_base = (slot * tensors + tensor) * items
    step_rows = min(256, slots * imps)
    step_items = min(256, items)
    for row in range(0, slots * imps, step_rows):
        ids = wanted[0:1, row : row + step_rows] - item_base
        total = jnp.zeros((8, step_rows), jnp.float32)
        target = jnp.zeros((8, step_rows), jnp.float32)
        for item in range(0, items, step_items):
            logits = lax.dot_general(
                catalogue[item : item + step_items, :],
                hidden[row : row + step_rows, :],
                NT,
                preferred_element_type=jnp.float32,
            )
            item_ids = item + lax.broadcasted_iota(jnp.int32, logits.shape, 0)
            found = jnp.where(item_ids == ids, logits, 0.0)
            total += jnp.sum(jnp.exp(logits).reshape(-1, 8, step_rows), axis=0)
            target += jnp.sum(found.reshape(-1, 8, step_rows), axis=0)
        total = jnp.sum(total, axis=0, keepdims=True)
        target = jnp.sum(target, axis=0, keepdims=True)
        for part in range(step_rows // imps):
            owner = slot ^ (row // imps + part)
            both = jnp.concatenate(
                [v[:, part * imps : (part + 1) * imps] for v in (total, target)], axis=1
            )
            for t in range(tensors):
                sums[owner * tensors + t] = both


def from_others(x, axes, count):
    return [x] + [
        lax.ppermute(x, axes, [(i, i ^ r) for i in range(count)]) for r in range(1, count)
    ]


def local(events, lengths, packing, positions, logged, w_uvqk, w_out, catalogue):
    rows, width = events.shape
    imps = positions.shape[1]
    items = catalogue.shape[0]
    local_width = w_out.shape[0]
    tensors = lax.axis_size("tensor")
    slots = lax.axis_size(SLOTS)
    params = pltpu.CompilerParams(vmem_limit_bytes=VMEM_LIMIT)
    place = jnp.stack([lax.axis_index(SLOTS), lax.axis_index("tensor")]).astype(jnp.int32)
    smem, vmem = whole_spec(pltpu.SMEM), whole_spec()

    chosen = pl.pallas_call(
        pick_kernel,
        out_shape=jax.ShapeDtypeStruct((imps, width), jnp.bfloat16),
        in_specs=[smem, smem, vmem, vmem],
        out_specs=vmem,
        compiler_params=params,
        cost_estimate=pl.CostEstimate(
            flops=2 * imps * rows * width, bytes_accessed=2 * rows * width, transcendentals=0
        ),
        name="pick",
    )(place, packing, positions, events)
    all_chosen = from_others(chosen, SLOTS, slots)
    all_w_out = from_others(w_out, "tensor", tensors)

    gated = pl.pallas_call(
        attend_kernel,
        out_shape=jax.ShapeDtypeStruct((imps, local_width), jnp.bfloat16),
        in_specs=[smem, smem, smem, vmem, vmem, vmem, vmem],
        out_specs=vmem,
        compiler_params=params,
        cost_estimate=pl.CostEstimate(
            flops=4 * rows * width * local_width,
            bytes_accessed=2 * rows * width + 8 * width * local_width,
            transcendentals=2 * rows * local_width,
        ),
        name="attend",
    )(place, packing, lengths, positions, events, chosen, w_uvqk)
    gated = jnp.concatenate(from_others(gated, "tensor", tensors), axis=1)
    all_gated = from_others(gated, SLOTS, slots)

    state, sums = pl.pallas_call(
        functools.partial(score_kernel, slots, tensors),
        out_shape=(
            jax.ShapeDtypeStruct((imps, width // tensors), jnp.bfloat16),
            jax.ShapeDtypeStruct((slots * tensors, 1, 2 * imps), jnp.float32),
        ),
        in_specs=[smem, smem, vmem] + [vmem] * (2 * slots + tensors + 1),
        out_specs=(vmem, vmem),
        scratch_shapes=[
            pltpu.VMEM((slots * imps, width), jnp.bfloat16),
            pltpu.VMEM((1, slots * imps), jnp.int32),
        ],
        compiler_params=params,
        cost_estimate=pl.CostEstimate(
            flops=2 * slots * imps * width * (items + local_width * tensors),
            bytes_accessed=2 * items * width,
            transcendentals=slots * imps * items,
        ),
        name="score",
    )(place, packing, logged, *all_chosen, *all_gated, *all_w_out, catalogue)
    sums = lax.all_to_all(sums, EVERY, split_axis=0, concat_axis=0, tiled=True)
    sums = jnp.sum(sums, axis=(0, 1))
    return (state, sums[imps:] - jnp.log(sums[:imps]))


def solution(mesh):
    placed = (
        P(("groups", "item", "dp"), None),
        P("groups"),
        P("groups"),
        P("groups", None),
        P("groups", None),
        P(None, "tensor"),
        P("tensor", None),
        P(("item", "dp", "tensor"), None),
    )
    return jax.shard_map(
        local,
        mesh=mesh,
        in_specs=placed,
        out_specs=(P(("groups", "item", "dp"), "tensor"), P(("groups", "item", "dp"))),
        check_vma=False,
    )
```

time: 137 us -> 63 us (0.46)
  waiting for transfers between devices: 46.5 us -> 17.1 us
  local copies, waits for them, and re-layouts: 30.2 us -> 3.64 us
  starting transfers between devices: 0.08 us -> 24.3 us
  blocking collectives: 32.1 us -> 10.5 us
  between operations: 14.2 us -> 0.7 us
  matrix products: 7.63 us -> 0 us
  Pallas kernels: 0 us -> 5.77 us
  other arithmetic: 5.41 us -> 0.7 us
    psum x1 -> x0, blocking collectives: 32.1 us -> none  [local(): lax.psum((new_totals, new_target), ('item', 'dp', 'tensor'))]
    psum x1 -> x0, waiting for transfers between devices: 26 us -> none  [local(): summed = lax.psum(partial_out, 'tensor')]
    slice x3 -> x0, local copies, waits for them, and re-layouts: 24.8 us -> none  [the longest x1 12.4 us: local(): split_weights[:, :, 1::2].reshape(model_width, local_heads * 2 * DH)]
    ppermute x0 -> x16, starting transfers between devices: none -> 24.3 us  [from_others(): lax.ppermute(x, axes, [(i, i ^ r) for i in range(count)])]
    all_gather x1 -> x0, waiting for transfers between devices: 20.5 us -> none  [local(): lax.all_gather(hidden_state, ('item', 'dp'), axis=0, tiled=True)]
    ppermute x0 -> x16, waiting for transfers between devices: none -> 17.1 us  [from_others(): lax.ppermute(x, axes, [(i, i ^ r) for i in range(count)])]
    all_to_all x0 -> x1, blocking collectives: none -> 10.5 us  [local(): sums = lax.all_to_all(sums, EVERY, split_axis=0, concat_axis=0, tiled=True)]
    dot_general x5 -> x0, matrix products: 7.63 us -> none  [the longest x1 2.82 us: local(): lax.dot_general(lax.all_gather(hidden_state, ('item', 'dp'), axis=0, tile...]
  transfers between devices with their start and end apart: 2 -> 16, of which waited for: 2 -> 6; matrix products, arithmetic and copies ran while one was open for 1% -> 0% of each run, Pallas kernels for 0% -> 0%
where the time goes in v1:
time: 63 us; the launch traced here: 62.7 us
  starting transfers between devices  24.3 us (39%)
  waiting for transfers between devices  17.1 us (27%)
  blocking collectives  10.5 us (17%)
  Pallas kernels  5.77 us (9%)
  local copies, waits for them, and re-layouts  3.64 us (6%)
  other arithmetic  0.7 us (1%)
  between operations  0.7 us (1%)
    ppermute x16, starting transfers between devices, from_others(): lax.ppermute(x, axes, [(i, i ^ r) for i in range(count)])  24.3 us
    ppermute x16, waiting for transfers between devices, from_others(): lax.ppermute(x, axes, [(i, i ^ r) for i in range(count)])  17.1 us
    all_to_all x1, blocking collectives, local(): sums = lax.all_to_all(sums, EVERY, split_axis=0, concat_axis=0, tiled=True)  10.5 us
    unnamed x16, local copies, waits for them, and re-layouts  3.64 us
    pallas_call x1, Pallas kernels, local(): pl.pallas_call(functools.partial(score_kernel, slots, tensors), out_shape...  3.13 us
    pallas_call x1, Pallas kernels, local(): pl.pallas_call(attend_kernel, out_shape=jax.ShapeDtypeStruct((imps, local...  1.64 us
  transfers between devices with their start and end apart: 16, of which 6 were waited for; matrix products, arithmetic and copies ran while one was open for 0% of the time, Pallas kernels for 0%

profile of v1, /device:TPU:0, one launch (start us, length us, event | category | flops | bytes accessed | tf_op | source)
XLA Modules:
  0.0 62.7 jit_solution(11545619968633812797)
XLA Ops:
  0.6 0.1 pad_add_fusion.place
  0.7 0.0 copy-start
  0.7 1.4 %copy-done = bf16[768,1024]{1,0:T(8,128)(2,1)S(1)} copy-done((bf16[768,1024]{1,0:T(8,128)(2,1)S(1)}, bf16[768,1024]{1,0:T(8,128)(2,1)}, u32[]{:S(2)}) %copy-start) | copy-done | bytes 1572888
  2.1 0.0 copy-start.2
  2.1 0.7 %copy-done.2 = s32[8,64]{1,0:T(8,128)S(1)} copy-done((s32[8,64]{1,0:T(8,128)S(1)}, s32[8,64]{1,0:T(8,128)}, u32[]{:S(2)}) %copy-start.2) | copy-done | bytes 2072
  2.8 0.7 %copy-done.3 = s32[8]{0:T(128)S(1)} copy-done((s32[8]{0:T(128)S(1)}, s32[8]{0:T(128)}, u32[]{:S(2)}) %copy-start.3) | copy-done | bytes 56
  3.5 1.0 %pick.1.chosen.refs_0_ = bf16[64,1024]{1,0:T(8,128)(2,1)S(1)} custom-call(s32[2]{0:T(128)S(1)} %pad_add_fusion.place, s32[8]{0:T(128)S(1)} %copy-done.3, s32[8,64]{1,0:T(8,128)S(1)} %copy-done.2, bf16[768,1024]{1,0:T(8,128)(2,1)S(1)} %copy-done), custom_call_target="tpu_custom_call" | custom-call | flops 100663296 | bytes 1572864 | tf_op jit(solution)/shard_map/pick/pallas_call | solution.py:135
  4.5 0.2 copy-done.1
  4.7 0.7 %copy-done.4 = s32[8]{0:T(128)S(1)} copy-done((s32[8]{0:T(128)S(1)}, s32[8]{0:T(128)}, u32[]{:S(2)}) %copy-start.4) | copy-done | bytes 56
  5.3 1.6 %attend.1 = bf16[64,128]{1,0:T(8,128)(2,1)S(1)} custom-call(s32[2]{0:T(128)S(1)} %pad_add_fusion.place, s32[8]{0:T(128)S(1)} %copy-done.3, s32[8]{0:T(128)S(1)} %copy-done.4, s32[8,64]{1,0:T(8,128)S(1)} %copy-done.2, bf16[768,1024]{1,0:T(8,128)(2,1)S(1)} %copy-done, bf16[64,1024]{1,0:T(8,128)(2,1)S(1)} %pick.1.chosen.refs_0_, bf16[1024,512]{1,0:T(8,128)(2,1)S(1)} %copy-done.1), custom_call_target="tpu_custom_call" | custom-call | flops 402653184 | bytes 2621440 | tf_op jit(solution)/shard_map/attend/pallas_call | solution.py:149
  7.0 3.0 %collective-permute-start.7 = (bf16[64,128]{1,0:T(8,128)(2,1)S(1)}, bf16[64,128]{1,0:T(8,128)(2,1)S(1)}, u32[]{:S(2)}, u32[]{:S(2)}) collective-permute-start(bf16[64,128]{1,0:T(8,128)(2,1)S(1)} %attend.1), channel_id=1, source_target_pairs={{0,1},{1,0},{2,3},{3,2},{4,5},{5,4},{6,7},{7,6},{8,9},{9,8},{10,11... | collective-permute-start | bytes 49160 | tf_op jit(solution)/shard_map/ppermute | solution.py:120
  10.0 1.7 %collective-permute-done.7 = bf16[64,128]{1,0:T(8,128)(2,1)S(1)} collective-permute-done((bf16[64,128]{1,0:T(8,128)(2,1)S(1)}, bf16[64,128]{1,0:T(8,128)(2,1)S(1)}, u32[]{:S(2)}, u32[]{:S(2)}) %collective-permute-start.7) | collective-permute-done | bytes 16416 | tf_op jit(solution)/shard_map/ppermute | solution.py:120
  11.7 2.4 %collective-permute-start.14 = (bf16[64,256]{1,0:T(8,128)(2,1)S(1)}, bf16[64,256]{1,0:T(8,128)(2,1)S(1)}, u32[]{:S(2)}, u32[]{:S(2)}) collective-permute-start(bf16[64,256]{1,0:T(8,128)(2,1)S(1)} %pad_maximum_fusion.refs_8_), channel_id=1, source_target_pairs={{0,14},{2,12},{4,10},{6,8},{8,6},{10,4},{12,2},{14,0},{1,15},{3,13... | collective-permute-start | bytes 98312 | tf_op jit(solution)/shard_map/ppermute | solution.py:120
  14.1 1.8 %collective-permute-start.13 = (bf16[64,256]{1,0:T(8,128)(2,1)S(1)}, bf16[64,256]{1,0:T(8,128)(2,1)S(1)}, u32[]{:S(2)}, u32[]{:S(2)}) collective-permute-start(bf16[64,256]{1,0:T(8,128)(2,1)S(1)} %pad_maximum_fusion.refs_8_), channel_id=1, source_target_pairs={{0,12},{2,14},{4,8},{6,10},{8,4},{10,6},{12,0},{14,2},{1,13},{3,15... | collective-permute-start | bytes 98312 | tf_op jit(solution)/shard_map/ppermute | solution.py:120
  15.9 0.4 collective-permute-start.12
  16.3 2.2 %collective-permute-start.11 = (bf16[64,256]{1,0:T(8,128)(2,1)S(1)}, bf16[64,256]{1,0:T(8,128)(2,1)S(1)}, u32[]{:S(2)}, u32[]{:S(2)}) collective-permute-start(bf16[64,256]{1,0:T(8,128)(2,1)S(1)} %pad_maximum_fusion.refs_8_), channel_id=1, source_target_pairs={{0,8},{2,10},{4,12},{6,14},{8,0},{10,2},{12,4},{14,6},{1,9},{3,11}... | collective-permute-start | bytes 98312 | tf_op jit(solution)/shard_map/ppermute | solution.py:120
  18.5 1.8 %collective-permute-start.6 = (bf16[64,1024]{1,0:T(8,128)(2,1)S(1)}, bf16[64,1024]{1,0:T(8,128)(2,1)S(1)}, u32[]{:S(2)}, u32[]{:S(2)}) collective-permute-start(bf16[64,1024]{1,0:T(8,128)(2,1)S(1)} %pick.1.chosen.refs_0_), channel_id=1, source_target_pairs={{0,14},{2,12},{4,10},{6,8},{8,6},{10,4},{12,2},{14,0},{1,15},{3,13... | collective-permute-start | bytes 393224 | tf_op jit(solution)/shard_map/ppermute | solution.py:120
  20.3 0.0 collective-permute-done.14.refs_15_
  20.3 1.8 %collective-permute-start.5 = (bf16[64,1024]{1,0:T(8,128)(2,1)S(1)}, bf16[64,1024]{1,0:T(8,128)(2,1)S(1)}, u32[]{:S(2)}, u32[]{:S(2)}) collective-permute-start(bf16[64,1024]{1,0:T(8,128)(2,1)S(1)} %pick.1.chosen.refs_0_), channel_id=1, source_target_pairs={{0,12},{2,14},{4,8},{6,10},{8,4},{10,6},{12,0},{14,2},{1,13},{3,15... | collective-permute-start | bytes 393224 | tf_op jit(solution)/shard_map/ppermute | solution.py:120
  22.1 0.0 collective-permute-done.13.refs_14_
  22.1 0.0 collective-permute-start.4
  22.1 0.0 collective-permute-done.12.refs_13_
  22.1 0.0 copy-done.6
  22.1 1.6 %collective-permute-start.15 = (bf16[128,1024]{1,0:T(8,128)(2,1)S(1)}, bf16[128,1024]{1,0:T(8,128)(2,1)S(1)}, u32[]{:S(2)}, u32[]{:S(2)}) collective-permute-start(bf16[128,1024]{1,0:T(8,128)(2,1)S(1)} %copy-done.6), channel_id=1, source_target_pairs={{0,1},{1,0},{2,3},{3,2},{4,5},{5,4},{6,7},{7,6},{8,9},{9,8},{10,11... | collective-permute-start | bytes 786440 | tf_op jit(solution)/shard_map/ppermute | solution.py:120
  23.7 0.0 collective-permute-done.11.refs_12_
  23.7 2.0 %collective-permute-start.10 = (bf16[64,256]{1,0:T(8,128)(2,1)S(1)}, bf16[64,256]{1,0:T(8,128)(2,1)S(1)}, u32[]{:S(2)}, u32[]{:S(2)}) collective-permute-start(bf16[64,256]{1,0:T(8,128)(2,1)S(1)} %pad_maximum_fusion.refs_8_), channel_id=1, source_target_pairs={{0,6},{2,4},{4,2},{6,0},{8,14},{10,12},{12,10},{14,8},{1,7},{3,5},... | collective-permute-start | bytes 98312 | tf_op jit(solution)/shard_map/ppermute | solution.py:120
  25.7 4.3 %collective-permute-done.10.refs_11_ = bf16[64,256]{1,0:T(8,128)(2,1)S(1)} collective-permute-done((bf16[64,256]{1,0:T(8,128)(2,1)S(1)}, bf16[64,256]{1,0:T(8,128)(2,1)S(1)}, u32[]{:S(2)}, u32[]{:S(2)}) %collective-permute-start.10) | collective-permute-done | bytes 32800 | tf_op jit(solution)/shard_map/ppermute | solution.py:120
  30.0 3.1 %collective-permute-start.9 = (bf16[64,256]{1,0:T(8,128)(2,1)S(1)}, bf16[64,256]{1,0:T(8,128)(2,1)S(1)}, u32[]{:S(2)}, u32[]{:S(2)}) collective-permute-start(bf16[64,256]{1,0:T(8,128)(2,1)S(1)} %pad_maximum_fusion.refs_8_), channel_id=1, source_target_pairs={{0,4},{2,6},{4,0},{6,2},{8,12},{10,14},{12,8},{14,10},{1,5},{3,7},... | collective-permute-start | bytes 98312 | tf_op jit(solution)/shard_map/ppermute | solution.py:120
  33.1 1.9 %collective-permute-done.9.refs_10_ = bf16[64,256]{1,0:T(8,128)(2,1)S(1)} collective-permute-done((bf16[64,256]{1,0:T(8,128)(2,1)S(1)}, bf16[64,256]{1,0:T(8,128)(2,1)S(1)}, u32[]{:S(2)}, u32[]{:S(2)}) %collective-permute-start.9) | collective-permute-done | bytes 32800 | tf_op jit(solution)/shard_map/ppermute | solution.py:120
  35.0 0.0 collective-permute-start.8
  35.0 1.2 %collective-permute-done.8.refs_9_ = bf16[64,256]{1,0:T(8,128)(2,1)S(1)} collective-permute-done((bf16[64,256]{1,0:T(8,128)(2,1)S(1)}, bf16[64,256]{1,0:T(8,128)(2,1)S(1)}, u32[]{:S(2)}, u32[]{:S(2)}) %collective-permute-start.8) | collective-permute-done | bytes 32800 | tf_op jit(solution)/shard_map/ppermute | solution.py:120
  36.2 2.4 %collective-permute-start.3 = (bf16[64,1024]{1,0:T(8,128)(2,1)S(1)}, bf16[64,1024]{1,0:T(8,128)(2,1)S(1)}, u32[]{:S(2)}, u32[]{:S(2)}) collective-permute-start(bf16[64,1024]{1,0:T(8,128)(2,1)S(1)} %pick.1.chosen.refs_0_), channel_id=1, source_target_pairs={{0,8},{2,10},{4,12},{6,14},{8,0},{10,2},{12,4},{14,6},{1,9},{3,11}... | collective-permute-start | bytes 393224 | tf_op jit(solution)/shard_map/ppermute | solution.py:120
  38.6 0.0 collective-permute-done.6.refs_7_
  38.6 0.0 collective-permute-start.2
  38.6 0.0 collective-permute-done.5.refs_6_
  38.6 1.5 %collective-permute-start.1 = (bf16[64,1024]{1,0:T(8,128)(2,1)S(1)}, bf16[64,1024]{1,0:T(8,128)(2,1)S(1)}, u32[]{:S(2)}, u32[]{:S(2)}) collective-permute-start(bf16[64,1024]{1,0:T(8,128)(2,1)S(1)} %pick.1.chosen.refs_0_), channel_id=1, source_target_pairs={{0,4},{2,6},{4,0},{6,2},{8,12},{10,14},{12,8},{14,10},{1,5},{3,7},... | collective-permute-start | bytes 393224 | tf_op jit(solution)/shard_map/ppermute | solution.py:120
  40.1 0.0 collective-permute-done.4.refs_5_
  40.1 0.3 collective-permute-start
  40.4 5.2 %collective-permute-done.3.refs_4_ = bf16[64,1024]{1,0:T(8,128)(2,1)S(1)} collective-permute-done((bf16[64,1024]{1,0:T(8,128)(2,1)S(1)}, bf16[64,1024]{1,0:T(8,128)(2,1)S(1)}, u32[]{:S(2)}, u32[]{:S(2)}) %collective-permute-start.3) | collective-permute-done | bytes 131104 | tf_op jit(solution)/shard_map/ppermute | solution.py:120
  45.6 0.0 collective-permute-done.2.refs_3_
  45.6 2.8 %collective-permute-done.1.refs_2_ = bf16[64,1024]{1,0:T(8,128)(2,1)S(1)} collective-permute-done((bf16[64,1024]{1,0:T(8,128)(2,1)S(1)}, bf16[64,1024]{1,0:T(8,128)(2,1)S(1)}, u32[]{:S(2)}, u32[]{:S(2)}) %collective-permute-start.1) | collective-permute-done | bytes 131104 | tf_op jit(solution)/shard_map/ppermute | solution.py:120
  48.4 0.0 collective-permute-done.refs_1_
  48.4 0.0 collective-permute-done.15.refs_17_
  48.4 0.0 copy-done.7
  48.4 0.0 copy-done.5
  48.5 3.1 %score.1 = (bf16[64,512]{1,0:T(8,128)(2,1)}, f32[16,1,128]{2,1,0:T(1,128)S(1)}) custom-call(s32[2]{0:T(128)S(1)} %pad_add_fusion.place, s32[8]{0:T(128)S(1)} %copy-done.3, s32[8,64]{1,0:T(8,128)S(1)} %copy-done.7, bf16[64,1024]{1,0:T(8,128)(2,1)S(1)} %pick.1.chosen.refs_0_, bf16[64,1024]{1,0:T(8,128)(2,1)S(1)} %collective-permute-done.refs_1_, ...), custom_call_target="tpu_custom_call" | custom-call | flops 1342177280 | bytes 2097152 | tf_op jit(solution)/shard_map/score/pallas_call | solution.py:165
  51.6 10.5 %all_to_all.5 = f32[16,1,128]{2,1,0:T(1,128)S(1)} all-to-all(f32[16,1,128]{2,1,0:T(1,128)S(1)} %get-tuple-element.5), channel_id=1, replica_groups=mesh['groups'=2,'item'=4,'dp'=2,'tensor'=2] {'item','dp','tensor'}, dimensions={0} | all-to-all | bytes 16384 | tf_op jit(solution)/shard_map/all_to_all | solution.py:185
  62.1 0.6 log_subtract_fusion
  (8 shorter events, 0.0 us)
Async XLA Ops:
  0.7 1.4 %copy-start = (bf16[768,1024]{1,0:T(8,128)(2,1)S(1)}, bf16[768,1024]{1,0:T(8,128)(2,1)}, u32[]{:S(2)}) copy-start(bf16[768,1024]{1,0:T(8,128)(2,1)} %events.3) | copy-start | bytes 4718596
  2.1 0.7 %copy-start.2 = (s32[8,64]{1,0:T(8,128)S(1)}, s32[8,64]{1,0:T(8,128)}, u32[]{:S(2)}) copy-start(s32[8,64]{1,0:T(8,128)} %positions.3) | copy-start | bytes 6148
  2.8 0.7 %copy-start.3 = (s32[8]{0:T(128)S(1)}, s32[8]{0:T(128)}, u32[]{:S(2)}) copy-start(s32[8]{0:T(128)} %packing.5) | copy-start | bytes 100
  3.5 1.2 %copy-start.1 = (bf16[1024,512]{1,0:T(8,128)(2,1)S(1)}, bf16[1024,512]{1,0:T(8,128)(2,1)}, u32[]{:S(2)}) copy-start(bf16[1024,512]{1,0:T(8,128)(2,1)} %w_uvqk.1) | copy-start | bytes 3145732
  3.5 18.7 %copy-start.6 = (bf16[128,1024]{1,0:T(8,128)(2,1)S(1)}, bf16[128,1024]{1,0:T(8,128)(2,1)}, u32[]{:S(2)}) copy-start(bf16[128,1024]{1,0:T(8,128)(2,1)} %refs_16_.1) | copy-start | bytes 786436
  3.5 45.0 %copy-start.7 = (s32[8,64]{1,0:T(8,128)S(1)}, s32[8,64]{1,0:T(8,128)}, u32[]{:S(2)}) copy-start(s32[8,64]{1,0:T(8,128)} %logged.1) | copy-start | bytes 6148
  4.7 0.7 %copy-start.4 = (s32[8]{0:T(128)S(1)}, s32[8]{0:T(128)}, u32[]{:S(2)}) copy-start(s32[8]{0:T(128)} %lengths.1) | copy-start | bytes 100
  5.3 43.1 %copy-start.5 = (bf16[1024,1024]{1,0:T(8,128)(2,1)S(1)}, bf16[1024,1024]{1,0:T(8,128)(2,1)}, u32[]{:S(2)}) copy-start(bf16[1024,1024]{1,0:T(8,128)(2,1)} %refs_18_.1) | copy-start | bytes 6291460
  7.0 4.7 %collective-permute-start.7 = (bf16[64,128]{1,0:T(8,128)(2,1)S(1)}, bf16[64,128]{1,0:T(8,128)(2,1)S(1)}, u32[]{:S(2)}, u32[]{:S(2)}) collective-permute-start(bf16[64,128]{1,0:T(8,128)(2,1)S(1)} %attend.1), channel_id=1, source_target_pairs={{0,1},{1,0},{2,3},{3,2},{4,5},{5,4},{6,7},{7,6},{8,9},{9,8},{10,11... | collective-permute-start | bytes 49160 | tf_op jit(solution)/shard_map/ppermute | solution.py:120
  11.7 8.6 %collective-permute-start.14 = (bf16[64,256]{1,0:T(8,128)(2,1)S(1)}, bf16[64,256]{1,0:T(8,128)(2,1)S(1)}, u32[]{:S(2)}, u32[]{:S(2)}) collective-permute-start(bf16[64,256]{1,0:T(8,128)(2,1)S(1)} %pad_maximum_fusion.refs_8_), channel_id=1, source_target_pairs={{0,14},{2,12},{4,10},{6,8},{8,6},{10,4},{12,2},{14,0},{1,15},{3,13... | collective-permute-start | bytes 98312 | tf_op jit(solution)/shard_map/ppermute | solution.py:120
  14.1 8.0 %collective-permute-start.13 = (bf16[64,256]{1,0:T(8,128)(2,1)S(1)}, bf16[64,256]{1,0:T(8,128)(2,1)S(1)}, u32[]{:S(2)}, u32[]{:S(2)}) collective-permute-start(bf16[64,256]{1,0:T(8,128)(2,1)S(1)} %pad_maximum_fusion.refs_8_), channel_id=1, source_target_pairs={{0,12},{2,14},{4,8},{6,10},{8,4},{10,6},{12,0},{14,2},{1,13},{3,15... | collective-permute-start | bytes 98312 | tf_op jit(solution)/shard_map/ppermute | solution.py:120
  15.9 6.2 %collective-permute-start.12 = (bf16[64,256]{1,0:T(8,128)(2,1)S(1)}, bf16[64,256]{1,0:T(8,128)(2,1)S(1)}, u32[]{:S(2)}, u32[]{:S(2)}) collective-permute-start(bf16[64,256]{1,0:T(8,128)(2,1)S(1)} %pad_maximum_fusion.refs_8_), channel_id=1, source_target_pairs={{0,10},{2,8},{4,14},{6,12},{8,2},{10,0},{12,6},{14,4},{1,11},{3,9}... | collective-permute-start | bytes 98312 | tf_op jit(solution)/shard_map/ppermute | solution.py:120
  16.3 7.4 %collective-permute-start.11 = (bf16[64,256]{1,0:T(8,128)(2,1)S(1)}, bf16[64,256]{1,0:T(8,128)(2,1)S(1)}, u32[]{:S(2)}, u32[]{:S(2)}) collective-permute-start(bf16[64,256]{1,0:T(8,128)(2,1)S(1)} %pad_maximum_fusion.refs_8_), channel_id=1, source_target_pairs={{0,8},{2,10},{4,12},{6,14},{8,0},{10,2},{12,4},{14,6},{1,9},{3,11}... | collective-permute-start | bytes 98312 | tf_op jit(solution)/shard_map/ppermute | solution.py:120
  18.5 20.0 %collective-permute-start.6 = (bf16[64,1024]{1,0:T(8,128)(2,1)S(1)}, bf16[64,1024]{1,0:T(8,128)(2,1)S(1)}, u32[]{:S(2)}, u32[]{:S(2)}) collective-permute-start(bf16[64,1024]{1,0:T(8,128)(2,1)S(1)} %pick.1.chosen.refs_0_), channel_id=1, source_target_pairs={{0,14},{2,12},{4,10},{6,8},{8,6},{10,4},{12,2},{14,0},{1,15},{3,13... | collective-permute-start | bytes 393224 | tf_op jit(solution)/shard_map/ppermute | solution.py:120
  20.3 18.2 %collective-permute-start.5 = (bf16[64,1024]{1,0:T(8,128)(2,1)S(1)}, bf16[64,1024]{1,0:T(8,128)(2,1)S(1)}, u32[]{:S(2)}, u32[]{:S(2)}) collective-permute-start(bf16[64,1024]{1,0:T(8,128)(2,1)S(1)} %pick.1.chosen.refs_0_), channel_id=1, source_target_pairs={{0,12},{2,14},{4,8},{6,10},{8,4},{10,6},{12,0},{14,2},{1,13},{3,15... | collective-permute-start | bytes 393224 | tf_op jit(solution)/shard_map/ppermute | solution.py:120
  22.1 17.9 %collective-permute-start.4 = (bf16[64,1024]{1,0:T(8,128)(2,1)S(1)}, bf16[64,1024]{1,0:T(8,128)(2,1)S(1)}, u32[]{:S(2)}, u32[]{:S(2)}) collective-permute-start(bf16[64,1024]{1,0:T(8,128)(2,1)S(1)} %pick.1.chosen.refs_0_), channel_id=1, source_target_pairs={{0,10},{2,8},{4,14},{6,12},{8,2},{10,0},{12,6},{14,4},{1,11},{3,9}... | collective-permute-start | bytes 393224 | tf_op jit(solution)/shard_map/ppermute | solution.py:120
  22.1 26.3 %collective-permute-start.15 = (bf16[128,1024]{1,0:T(8,128)(2,1)S(1)}, bf16[128,1024]{1,0:T(8,128)(2,1)S(1)}, u32[]{:S(2)}, u32[]{:S(2)}) collective-permute-start(bf16[128,1024]{1,0:T(8,128)(2,1)S(1)} %copy-done.6), channel_id=1, source_target_pairs={{0,1},{1,0},{2,3},{3,2},{4,5},{5,4},{6,7},{7,6},{8,9},{9,8},{10,11... | collective-permute-start | bytes 786440 | tf_op jit(solution)/shard_map/ppermute | solution.py:120
  23.7 6.3 %collective-permute-start.10 = (bf16[64,256]{1,0:T(8,128)(2,1)S(1)}, bf16[64,256]{1,0:T(8,128)(2,1)S(1)}, u32[]{:S(2)}, u32[]{:S(2)}) collective-permute-start(bf16[64,256]{1,0:T(8,128)(2,1)S(1)} %pad_maximum_fusion.refs_8_), channel_id=1, source_target_pairs={{0,6},{2,4},{4,2},{6,0},{8,14},{10,12},{12,10},{14,8},{1,7},{3,5},... | collective-permute-start | bytes 98312 | tf_op jit(solution)/shard_map/ppermute | solution.py:120
  30.0 5.0 %collective-permute-start.9 = (bf16[64,256]{1,0:T(8,128)(2,1)S(1)}, bf16[64,256]{1,0:T(8,128)(2,1)S(1)}, u32[]{:S(2)}, u32[]{:S(2)}) collective-permute-start(bf16[64,256]{1,0:T(8,128)(2,1)S(1)} %pad_maximum_fusion.refs_8_), channel_id=1, source_target_pairs={{0,4},{2,6},{4,0},{6,2},{8,12},{10,14},{12,8},{14,10},{1,5},{3,7},... | collective-permute-start | bytes 98312 | tf_op jit(solution)/shard_map/ppermute | solution.py:120
  35.0 1.2 %collective-permute-start.8 = (bf16[64,256]{1,0:T(8,128)(2,1)S(1)}, bf16[64,256]{1,0:T(8,128)(2,1)S(1)}, u32[]{:S(2)}, u32[]{:S(2)}) collective-permute-start(bf16[64,256]{1,0:T(8,128)(2,1)S(1)} %pad_maximum_fusion.refs_8_), channel_id=1, source_target_pairs={{0,2},{2,0},{4,6},{6,4},{8,10},{10,8},{12,14},{14,12},{1,3},{3,1},... | collective-permute-start | bytes 98312 | tf_op jit(solution)/shard_map/ppermute | solution.py:120
  36.2 9.4 %collective-permute-start.3 = (bf16[64,1024]{1,0:T(8,128)(2,1)S(1)}, bf16[64,1024]{1,0:T(8,128)(2,1)S(1)}, u32[]{:S(2)}, u32[]{:S(2)}) collective-permute-start(bf16[64,1024]{1,0:T(8,128)(2,1)S(1)} %pick.1.chosen.refs_0_), channel_id=1, source_target_pairs={{0,8},{2,10},{4,12},{6,14},{8,0},{10,2},{12,4},{14,6},{1,9},{3,11}... | collective-permute-start | bytes 393224 | tf_op jit(solution)/shard_map/ppermute | solution.py:120
  38.6 7.0 %collective-permute-start.2 = (bf16[64,1024]{1,0:T(8,128)(2,1)S(1)}, bf16[64,1024]{1,0:T(8,128)(2,1)S(1)}, u32[]{:S(2)}, u32[]{:S(2)}) collective-permute-start(bf16[64,1024]{1,0:T(8,128)(2,1)S(1)} %pick.1.chosen.refs_0_), channel_id=1, source_target_pairs={{0,6},{2,4},{4,2},{6,0},{8,14},{10,12},{12,10},{14,8},{1,7},{3,5},... | collective-permute-start | bytes 393224 | tf_op jit(solution)/shard_map/ppermute | solution.py:120
  38.6 9.9 %collective-permute-start.1 = (bf16[64,1024]{1,0:T(8,128)(2,1)S(1)}, bf16[64,1024]{1,0:T(8,128)(2,1)S(1)}, u32[]{:S(2)}, u32[]{:S(2)}) collective-permute-start(bf16[64,1024]{1,0:T(8,128)(2,1)S(1)} %pick.1.chosen.refs_0_), channel_id=1, source_target_pairs={{0,4},{2,6},{4,0},{6,2},{8,12},{10,14},{12,8},{14,10},{1,5},{3,7},... | collective-permute-start | bytes 393224 | tf_op jit(solution)/shard_map/ppermute | solution.py:120
  40.1 8.4 %collective-permute-start = (bf16[64,1024]{1,0:T(8,128)(2,1)S(1)}, bf16[64,1024]{1,0:T(8,128)(2,1)S(1)}, u32[]{:S(2)}, u32[]{:S(2)}) collective-permute-start(bf16[64,1024]{1,0:T(8,128)(2,1)S(1)} %pick.1.chosen.refs_0_), channel_id=1, source_target_pairs={{0,2},{2,0},{4,6},{6,4},{8,10},{10,8},{12,14},{14,12},{1,3},{3,1},... | collective-permute-start | bytes 393224 | tf_op jit(solution)/shard_map/ppermute | solution.py:120

commit v2 on v1

v2 whole, which is shorter than its diff:
```python
import functools
import math

import jax
import jax.numpy as jnp
from jax import lax
from jax.experimental import pallas as pl
from jax.experimental.pallas import tpu as pltpu
from jax.sharding import PartitionSpec as P

DH = 128
SLOTS = ("item", "dp")
COLUMN = ("item", "tensor")
NT = (((1,), (1,)), ((), ()))
VMEM_LIMIT = 32 * 1024 * 1024
EVENT_PARTS = 4


def spec(space):
    return pl.BlockSpec(memory_space=space)


def pick_kernel(
    shards,
    place,
    packing,
    lengths,
    positions,
    logged,
    events,
    chosen,
    limits,
    wanted,
    packing_s,
    lengths_s,
    positions_v,
    logged_v,
    events_v,
    sems,
):
    rows = events.shape[0]
    items_axis, dps = shards
    imps = positions.shape[1]
    part_rows = rows // EVENT_PARTS
    copies = [
        pltpu.make_async_copy(source, target, sems.at[k])
        for k, (source, target) in enumerate(
            [
                (packing, packing_s),
                (lengths, lengths_s),
                (positions, positions_v),
                (logged, logged_v),
            ]
            + [
                (events.at[pl.ds(k * part_rows, part_rows)], events_v.at[pl.ds(k * part_rows, part_rows)])
                for k in range(EVENT_PARTS)
            ]
        )
    ]
    for copy in copies:
        copy.start()
    for copy in copies[:4]:
        copy.wait()
    item, dp = place[0], place[1]
    history = packing_s[item * dps + dp]
    row = positions_v[pl.ds(history, 1), :].astype(jnp.float32)
    diagonal = lax.broadcasted_iota(jnp.int32, (imps, imps), 0) == lax.broadcasted_iota(
        jnp.int32, (imps, imps), 1
    )
    spots = jnp.sum(jnp.where(diagonal, row, 0.0), axis=1, keepdims=True).astype(jnp.int32)
    limits[...] = jnp.broadcast_to(jnp.minimum(spots, lengths_s[history] - 1), limits.shape)
    for k in range(items_axis):
        wanted[0:1, k * imps : (k + 1) * imps] = logged_v[pl.ds(packing_s[k * dps + dp], 1), :]
    total = jnp.zeros((imps, events.shape[1]), jnp.float32)
    for k in range(EVENT_PARTS):
        copies[4 + k].wait()
        lanes = k * part_rows + lax.broadcasted_iota(jnp.int32, (imps, part_rows), 1)
        one_hot = jnp.where(lanes == spots, 1.0, 0.0).astype(jnp.bfloat16)
        total += jnp.dot(
            one_hot,
            events_v[k * part_rows : (k + 1) * part_rows, :],
            preferred_element_type=jnp.float32,
        )
    total = total.astype(jnp.bfloat16)
    for k in range(items_axis):
        chosen[k] = total


def attend_kernel(place, limits, events, chosen, w_uvqk, gated):
    rows = events.shape[0]
    own = chosen[place[0]]
    lanes = lax.broadcasted_iota(jnp.int32, (own.shape[0], rows), 1)
    valid = lanes <= limits[:, 0:1]
    for head in range(gated.shape[2] // DH):
        first = head * 4 * DH
        w_part = [w_uvqk[:, first + k * DH : first + (k + 1) * DH] for k in range(4)]
        w_gate_query = jnp.concatenate([w_part[0], w_part[2]], axis=1)
        w_value_key = jnp.concatenate([w_part[1], w_part[3]], axis=1)
        gate_query = jnp.dot(own, w_gate_query, preferred_element_type=jnp.float32)
        gate_query = jax.nn.silu(gate_query).astype(jnp.bfloat16)
        value_key = jnp.dot(events[...], w_value_key, preferred_element_type=jnp.float32)
        value_key = jax.nn.silu(value_key).astype(jnp.bfloat16)
        scores = lax.dot_general(
            gate_query[:, DH:], value_key[:, DH:], NT, preferred_element_type=jnp.float32
        ) / math.sqrt(DH)
        weights = jnp.where(valid, jax.nn.silu(scores), 0.0).astype(jnp.bfloat16)
        attended = jnp.dot(weights, value_key[:, :DH], preferred_element_type=jnp.float32)
        inverse = lax.rsqrt(jnp.mean(attended * attended, axis=-1, keepdims=True) + 1e-06)
        gated_rows = (attended * inverse * gate_query[:, :DH].astype(jnp.float32)).astype(
            jnp.bfloat16
        )
        for k in range(gated.shape[0]):
            gated[k, :, head * DH : (head + 1) * DH] = gated_rows


def score_kernel(sizes, place, wanted, chosen, gated, *refs):
    items_axis, dps, tensors = sizes
    w_out, refs = refs[:tensors], refs[tensors:]
    catalogue, refs = refs[:dps], refs[dps:]
    state, sums, hidden = refs
    item, dp, tensor = place[0], place[1], place[2]
    imps = chosen.shape[1]
    items = catalogue[0].shape[0]
    for k in range(items_axis):
        total = chosen[k].astype(jnp.float32)
        for t in range(tensors):
            total += jnp.dot(
                gated[k * tensors + (tensor ^ t)], w_out[t][...], preferred_element_type=jnp.float32
            )
        hidden[k * imps : (k + 1) * imps, :] = total.astype(jnp.bfloat16)
    share = state.shape[1]
    state[...] = hidden[
        pl.ds(pl.multiple_of(item * imps, imps), imps),
        pl.ds(pl.multiple_of(tensor * share, share), share),
    ]
    step_rows = min(256, items_axis * imps)
    step_items = min(256, items)
    for row in range(0, items_axis * imps, step_rows):
        total = jnp.zeros((8, step_rows), jnp.float32)
        target = jnp.zeros((8, step_rows), jnp.float32)
        for d in range(dps):
            item_base = ((item * dps + (dp ^ d)) * tensors + tensor) * items
            ids = wanted[0:1, row : row + step_rows] - item_base
            for first in range(0, items, step_items):
                logits = lax.dot_general(
                    catalogue[d][first : first + step_items, :],
                    hidden[row : row + step_rows, :],
                    NT,
                    preferred_element_type=jnp.float32,
                )
                item_ids = first + lax.broadcasted_iota(jnp.int32, logits.shape, 0)
                found = jnp.where(item_ids == ids, logits, 0.0)
                total += jnp.sum(jnp.exp(logits).reshape(-1, 8, step_rows), axis=0)
                target += jnp.sum(found.reshape(-1, 8, step_rows), axis=0)
        total = jnp.sum(total, axis=0, keepdims=True)
        target = jnp.sum(target, axis=0, keepdims=True)
        for part in range(step_rows // imps):
            owner = row // imps + part
            both = jnp.concatenate(
                [v[:, part * imps : (part + 1) * imps] for v in (total, target)], axis=1
            )
            for t in range(tensors):
                sums[owner * tensors + t] = both


def in_hbm(x):
    return pltpu.with_memory_space_constraint(x, pltpu.HBM)


def from_others(x, axes, count):
    return [x] + [
        lax.ppermute(x, axes, [(i, i ^ r) for i in range(count)]) for r in range(1, count)
    ]


def local(events, lengths, packing, positions, logged, w_uvqk, w_out, catalogue):
    rows, width = events.shape
    imps = positions.shape[1]
    hists = packing.shape[0]
    items = catalogue.shape[0]
    local_width = w_out.shape[0]
    items_axis, dps, tensors = (lax.axis_size(a) for a in ("item", "dp", "tensor"))
    receivers = items_axis * tensors
    params = pltpu.CompilerParams(vmem_limit_bytes=VMEM_LIMIT)
    place = jnp.stack([lax.axis_index(a) for a in ("item", "dp", "tensor")]).astype(jnp.int32)
    smem, vmem, hbm = spec(pltpu.SMEM), spec(pltpu.VMEM), spec(pltpu.HBM)

    all_w_out = from_others(w_out, "tensor", tensors)
    all_catalogue = from_others(catalogue, "dp", dps)
    chosen, limits, wanted = pl.pallas_call(
        functools.partial(pick_kernel, (items_axis, dps)),
        out_shape=(
            jax.ShapeDtypeStruct((items_axis, imps, width), jnp.bfloat16),
            jax.ShapeDtypeStruct((imps, 128), jnp.int32),
            jax.ShapeDtypeStruct((1, items_axis * imps), jnp.int32),
        ),
        in_specs=[smem] + [hbm] * 5,
        out_specs=(vmem, vmem, vmem),
        scratch_shapes=[
            pltpu.SMEM((hists,), jnp.int32),
            pltpu.SMEM((hists,), jnp.int32),
            pltpu.VMEM((hists, imps), jnp.int32),
            pltpu.VMEM((hists, imps), jnp.int32),
            pltpu.VMEM((rows, width), jnp.bfloat16),
            pltpu.SemaphoreType.DMA((4 + EVENT_PARTS,)),
        ],
        compiler_params=params,
        cost_estimate=pl.CostEstimate(
            flops=2 * imps * rows * width, bytes_accessed=2 * rows * width, transcendentals=0
        ),
        name="pick",
    )(place, *(in_hbm(x) for x in (packing, lengths, positions, logged, events)))
    all_chosen = lax.all_to_all(chosen, "item", split_axis=0, concat_axis=0, tiled=True)

    gated = pl.pallas_call(
        attend_kernel,
        out_shape=jax.ShapeDtypeStruct((receivers, imps, local_width), jnp.bfloat16),
        in_specs=[smem, vmem, vmem, vmem, vmem],
        out_specs=vmem,
        compiler_params=params,
        cost_estimate=pl.CostEstimate(
            flops=4 * rows * width * local_width,
            bytes_accessed=2 * rows * width + 8 * width * local_width,
            transcendentals=2 * rows * local_width,
        ),
        name="attend",
    )(place, limits, events, chosen, w_uvqk)
    all_gated = lax.all_to_all(gated, COLUMN, split_axis=0, concat_axis=0, tiled=True)

    state, sums = pl.pallas_call(
        functools.partial(score_kernel, (items_axis, dps, tensors)),
        out_shape=(
            jax.ShapeDtypeStruct((imps, width // tensors), jnp.bfloat16),
            jax.ShapeDtypeStruct((receivers, 1, 2 * imps), jnp.float32),
        ),
        in_specs=[smem] + [vmem] * (3 + tensors + dps),
        out_specs=(vmem, vmem),
        scratch_shapes=[pltpu.VMEM((items_axis * imps, width), jnp.bfloat16)],
        compiler_params=params,
        cost_estimate=pl.CostEstimate(
            flops=2 * items_axis * imps * width * (dps * items + local_width * tensors),
            bytes_accessed=2 * dps * items * width,
            transcendentals=items_axis * imps * dps * items,
        ),
        name="score",
    )(place, wanted, all_chosen, all_gated, *all_w_out, *all_catalogue)
    sums = lax.all_to_all(sums, COLUMN, split_axis=0, concat_axis=0, tiled=True)
    sums = jnp.sum(sums, axis=(0, 1))
    return (state, sums[imps:] - jnp.log(sums[:imps]))


def solution(mesh):
    placed = (
        P(("groups", "item", "dp"), None),
        P("groups"),
        P("groups"),
        P("groups", None),
        P("groups", None),
        P(None, "tensor"),
        P("tensor", None),
        P(("item", "dp", "tensor"), None),
    )
    return jax.shard_map(
        local,
        mesh=mesh,
        in_specs=placed,
        out_specs=(P(("groups", "item", "dp"), "tensor"), P(("groups", "item", "dp"))),
        check_vma=False,
    )
```

time: 63 us -> 54.3 us (0.86)
  starting transfers between devices: 24.3 us -> 4.3 us
  blocking collectives: 10.5 us -> 23.2 us
  waiting for transfers between devices: 17.1 us -> 13.5 us
  Pallas kernels: 5.77 us -> 8.73 us
  local copies, waits for them, and re-layouts: 3.64 us -> 2.82 us
    ppermute x16 -> x2, starting transfers between devices: 24.3 us -> 0.83 us  [from_others(): lax.ppermute(x, axes, [(i, i ^ r) for i in range(count)])]
    all_to_all x1 -> x2, blocking collectives: 10.5 us -> 23.2 us  [the longest x1 14.3 us: local(): lax.all_to_all(gated, COLUMN, split_axis=0, concat_axis=0, tiled=True)]
    ppermute x16 -> x2, waiting for transfers between devices: 17.1 us -> 6.87 us  [from_others(): lax.ppermute(x, axes, [(i, i ^ r) for i in range(count)])]
    all_to_all x0 -> x1, waiting for transfers between devices: none -> 6.61 us  [local(): lax.all_to_all(chosen, 'item', split_axis=0, concat_axis=0, tiled=True)]
    all_to_all x0 -> x1, starting transfers between devices: none -> 3.47 us  [local(): lax.all_to_all(chosen, 'item', split_axis=0, concat_axis=0, tiled=True)]
    pallas_call x3, Pallas kernels: 5.77 us -> 8.73 us  [the longest x1 3.54 us: local(): pl.pallas_call(functools.partial(score_kernel, (items_axis, dps, tensors)...]
    unnamed x16 -> x8, local copies, waits for them, and re-layouts: 3.64 us -> 2.82 us
  transfers between devices with their start and end apart: 16 -> 3, of which waited for: 6 -> 2; matrix products, arithmetic and copies ran while one was open for 0% -> 0% of each run, Pallas kernels for 0% -> 10%
where the time goes in v2:
time: 54.3 us; the launch traced here: 54 us
  blocking collectives  23.2 us (43%)
  waiting for transfers between devices  13.5 us (25%)
  Pallas kernels  8.73 us (16%)
  starting transfers between devices  4.3 us (8%)
  local copies, waits for them, and re-layouts  2.82 us (5%)
  other arithmetic  0.69 us (1%)
  between operations  0.69 us (1%)
    all_to_all x1, blocking collectives, local(): lax.all_to_all(gated, COLUMN, split_axis=0, concat_axis=0, tiled=True)  14.3 us
    all_to_all x1, blocking collectives, local(): sums = lax.all_to_all(sums, COLUMN, split_axis=0, concat_axis=0, tiled=True)  8.99 us
    ppermute x2, waiting for transfers between devices, from_others(): lax.ppermute(x, axes, [(i, i ^ r) for i in range(count)])  6.87 us
    all_to_all x1, waiting for transfers between devices, local(): lax.all_to_all(chosen, 'item', split_axis=0, concat_axis=0, tiled=True)  6.61 us
    pallas_call x1, Pallas kernels, local(): pl.pallas_call(functools.partial(score_kernel, (items_axis, dps, tensors)...  3.54 us
    all_to_all x1, starting transfers between devices, local(): lax.all_to_all(chosen, 'item', split_axis=0, concat_axis=0, tiled=True)  3.47 us
    pallas_call x1, Pallas kernels, local(): pl.pallas_call(functools.partial(pick_kernel, (items_axis, dps)), out_sha...  3 us
    unnamed x8, local copies, waits for them, and re-layouts  2.82 us
  transfers between devices with their start and end apart: 3, of which 2 were waited for; matrix products, arithmetic and copies ran while one was open for 0% of the time, Pallas kernels for 10%

profile of v2, /device:TPU:0, one launch (start us, length us, event | category | flops | bytes accessed | tf_op | source)
XLA Modules:
  0.0 54.0 jit_solution(11977254712308944639)
XLA Ops:
  0.6 0.0 copy-start
  0.6 0.5 collective-permute-start.1
  1.2 0.1 pad_add_fusion.place
  1.2 3.0 %pick.1 = (bf16[4,64,1024]{2,1,0:T(8,128)(2,1)}, s32[64,128]{1,0:T(8,128)S(1)}, s32[1,256]{1,0:T(1,128)S(1)}) custom-call(s32[3]{0:T(128)S(1)} %pad_add_fusion.place, s32[8]{0:T(128)} %packing.1, s32[8]{0:T(128)} %lengths.1, s32[8,64]{1,0:T(8,128)} %positions.1, s32[8,64]{1,0:T(8,128)} %logged.1, bf16[768,1024]{1,0:T(8,128)(2,1)} %events.3), custom_call_target="tpu_custom_call" | custom-call | flops 100663296 | bytes 1572864 | tf_op jit(solution)/shard_map/pick/pallas_call | solution.py:190
  4.2 0.0 copy-done
  4.3 0.0 copy-start.2
  4.3 1.2 %copy-done.2 = bf16[1024,512]{1,0:T(8,128)(2,1)S(1)} copy-done((bf16[1024,512]{1,0:T(8,128)(2,1)S(1)}, bf16[1024,512]{1,0:T(8,128)(2,1)}, u32[]{:S(2)}) %copy-start.2) | copy-done | bytes 1048600
  5.5 0.0 copy-start.3
  5.5 2.2 %attend.1 = bf16[8,64,128]{2,1,0:T(8,128)(2,1)S(1)} custom-call(s32[3]{0:T(128)S(1)} %pad_add_fusion.place, s32[64,128]{1,0:T(8,128)S(1)} %get-tuple-element.9.limits, bf16[768,1024]{1,0:T(8,128)(2,1)S(1)} %copy-done, bf16[4,64,1024]{2,1,0:T(8,128)(2,1)} %get-tuple-element.8.chosen, bf16[1024,512]{1,0:T(8,128)(2,1)S(1)} %copy-done.2), custom_call_target="tpu_custom_call" | custom-call | flops 402653184 | bytes 2621440 | tf_op jit(solution)/shard_map/attend/pallas_call | solution.py:215
  7.7 14.3 %all_to_all.15.gated = bf16[8,64,128]{2,1,0:T(8,128)(2,1)S(1)} all-to-all(bf16[8,64,128]{2,1,0:T(8,128)(2,1)S(1)} %attend.1), channel_id=1, replica_groups=mesh['groups'=2,'item'=4,'dp'=2,'tensor'=2] {'item','tensor'}, dimensions={0} | all-to-all | bytes 262144 | tf_op jit(solution)/shard_map/all_to_all | solution.py:228
  21.9 3.5 %all-to-all-start = ((bf16[4,64,1024]{2,1,0:T(8,128)(2,1)}), bf16[4,64,1024]{2,1,0:T(8,128)(2,1)S(1)}, u32[]{:S(2)}, u32[]{:S(2)}) async-start(bf16[4,64,1024]{2,1,0:T(8,128)(2,1)} %get-tuple-element.8.chosen), calls=%async_computation | async-start | bytes 1048576 | tf_op jit(solution)/shard_map/all_to_all | solution.py:213
  25.4 0.0 copy-done.3
  25.4 0.3 collective-permute-start
  25.7 6.9 %collective-permute-done.refs_1_ = bf16[128,1024]{1,0:T(8,128)(2,1)S(1)} collective-permute-done((bf16[128,1024]{1,0:T(8,128)(2,1)S(1)}, bf16[128,1024]{1,0:T(8,128)(2,1)S(1)}, u32[]{:S(2)}, u32[]{:S(2)}) %collective-permute-start) | collective-permute-done | bytes 262176 | tf_op jit(solution)/shard_map/ppermute | solution.py:172
  32.6 6.6 %all-to-all-done.chosen = bf16[4,64,1024]{2,1,0:T(8,128)(2,1)S(1)} async-done(((bf16[4,64,1024]{2,1,0:T(8,128)(2,1)}), bf16[4,64,1024]{2,1,0:T(8,128)(2,1)S(1)}, u32[]{:S(2)}, u32[]{:S(2)}) %all-to-all-start) | async-done | bytes 524320 | tf_op jit(solution)/shard_map/all_to_all | solution.py:213
  39.2 0.0 collective-permute-done.1.refs_3_
  39.2 0.0 copy-start.1
  39.2 1.6 %copy-done.1 = bf16[1024,1024]{1,0:T(8,128)(2,1)S(1)} copy-done((bf16[1024,1024]{1,0:T(8,128)(2,1)S(1)}, bf16[1024,1024]{1,0:T(8,128)(2,1)}, u32[]{:S(2)}) %copy-start.1) | copy-done | bytes 2097176
  40.8 3.5 %score.1 = (bf16[64,512]{1,0:T(8,128)(2,1)}, f32[8,1,128]{2,1,0:T(1,128)S(1)}) custom-call(s32[3]{0:T(128)S(1)} %pad_add_fusion.place, s32[1,256]{1,0:T(1,128)S(1)} %get-tuple-element.7.wanted, bf16[4,64,1024]{2,1,0:T(8,128)(2,1)S(1)} %all-to-all-done.chosen, bf16[8,64,128]{2,1,0:T(8,128)(2,1)S(1)} %all_to_all.15.gated, bf16[128,1024]{1,0:T(8,128)(2,1)S(1)} %copy-done.3, ...), custom_call_target="tpu_custom_call" | custom-call | flops 1207959552 | bytes 4194304 | tf_op jit(solution)/shard_map/score/pallas_call | solution.py:230
  44.4 9.0 %all_to_all.16 = f32[8,1,128]{2,1,0:T(1,128)S(1)} all-to-all(f32[8,1,128]{2,1,0:T(1,128)S(1)} %get-tuple-element.11), channel_id=1, replica_groups=mesh['groups'=2,'item'=4,'dp'=2,'tensor'=2] {'item','tensor'}, dimensions={0} | all-to-all | bytes 8192 | tf_op jit(solution)/shard_map/all_to_all | solution.py:247
  53.4 0.6 %log_subtract_fusion = f32[64]{0:T(128)} fusion(f32[128]{0:T(128)S(1)} %reduce_sum.9), kind=kLoop, calls=%fused_computation.1 | loop fusion | flops 64 | bytes 768 | tf_op jit(solution)/shard_map/sub | solution.py:249
  (1 shorter events, 0.0 us)
Async XLA Ops:
  0.6 3.6 %copy-start = (bf16[768,1024]{1,0:T(8,128)(2,1)S(1)}, bf16[768,1024]{1,0:T(8,128)(2,1)}, u32[]{:S(2)}) copy-start(bf16[768,1024]{1,0:T(8,128)(2,1)} %events.3) | copy-start | bytes 4718596
  0.6 38.6 %collective-permute-start.1 = (bf16[1024,1024]{1,0:T(8,128)(2,1)}, bf16[1024,1024]{1,0:T(8,128)(2,1)}, u32[]{:S(2)}, u32[]{:S(2)}) collective-permute-start(bf16[1024,1024]{1,0:T(8,128)(2,1)} %refs_2_.1), channel_id=1, source_target_pairs={{0,2},{2,0},{1,3},{3,1},{4,6},{6,4},{5,7},{7,5},{8,10},{10,8},{9,1... | collective-permute-start | bytes 6291464 | tf_op jit(solution)/shard_map/ppermute | solution.py:172
  4.3 1.2 %copy-start.2 = (bf16[1024,512]{1,0:T(8,128)(2,1)S(1)}, bf16[1024,512]{1,0:T(8,128)(2,1)}, u32[]{:S(2)}) copy-start(bf16[1024,512]{1,0:T(8,128)(2,1)} %w_uvqk.1) | copy-start | bytes 3145732
  5.5 19.9 %copy-start.3 = (bf16[128,1024]{1,0:T(8,128)(2,1)S(1)}, bf16[128,1024]{1,0:T(8,128)(2,1)}, u32[]{:S(2)}) copy-start(bf16[128,1024]{1,0:T(8,128)(2,1)} %refs_0_.1) | copy-start | bytes 786436
  21.9 17.3 %all-to-all-start = ((bf16[4,64,1024]{2,1,0:T(8,128)(2,1)}), bf16[4,64,1024]{2,1,0:T(8,128)(2,1)S(1)}, u32[]{:S(2)}, u32[]{:S(2)}) async-start(bf16[4,64,1024]{2,1,0:T(8,128)(2,1)} %get-tuple-element.8.chosen), calls=%async_computation | async-start | bytes 1048576 | tf_op jit(solution)/shard_map/all_to_all | solution.py:213
  25.4 7.2 %collective-permute-start = (bf16[128,1024]{1,0:T(8,128)(2,1)S(1)}, bf16[128,1024]{1,0:T(8,128)(2,1)S(1)}, u32[]{:S(2)}, u32[]{:S(2)}) collective-permute-start(bf16[128,1024]{1,0:T(8,128)(2,1)S(1)} %copy-done.3), channel_id=1, source_target_pairs={{0,1},{1,0},{2,3},{3,2},{4,5},{5,4},{6,7},{7,6},{8,9},{9,8},{10,11... | collective-permute-start | bytes 786440 | tf_op jit(solution)/shard_map/ppermute | solution.py:172
  39.2 1.6 %copy-start.1 = (bf16[1024,1024]{1,0:T(8,128)(2,1)S(1)}, bf16[1024,1024]{1,0:T(8,128)(2,1)}, u32[]{:S(2)}) copy-start(bf16[1024,1024]{1,0:T(8,128)(2,1)} %refs_2_.1) | copy-start | bytes 6291460

commit v3 on v2

--- a/solution.py
+++ b/solution.py
@@ -28,33 +28,34 @@
     positions,
     logged,
     events,
+    w_uvqk,
     chosen,
     limits,
     wanted,
+    events_v,
+    w_uvqk_v,
     packing_s,
     lengths_s,
     positions_v,
     logged_v,
-    events_v,
     sems,
 ):
     rows = events.shape[0]
     items_axis, dps = shards
     imps = positions.shape[1]
     part_rows = rows // EVENT_PARTS
+    parts = [pl.ds(k * part_rows, part_rows) for k in range(EVENT_PARTS)]
     copies = [
         pltpu.make_async_copy(source, target, sems.at[k])
         for k, (source, target) in enumerate(
             [
                 (packing, packing_s),
+                (positions, positions_v),
                 (lengths, lengths_s),
-                (positions, positions_v),
                 (logged, logged_v),
             ]
-            + [
-                (events.at[pl.ds(k * part_rows, part_rows)], events_v.at[pl.ds(k * part_rows, part_rows)])
-                for k in range(EVENT_PARTS)
-            ]
+            + [(events.at[part], events_v.at[part]) for part in parts]
+            + [(w_uvqk, w_uvqk_v)]
         )
     ]
     for copy in copies:
@@ -70,7 +71,8 @@
     spots = jnp.sum(jnp.where(diagonal, row, 0.0), axis=1, keepdims=True).astype(jnp.int32)
     limits[...] = jnp.broadcast_to(jnp.minimum(spots, lengths_s[history] - 1), limits.shape)
     for k in range(items_axis):
-        wanted[0:1, k * imps : (k + 1) * imps] = logged_v[pl.ds(packing_s[k * dps + dp], 1), :]
+        other = packing_s[(item ^ k) * dps + dp]
+        wanted[0:1, k * imps : (k + 1) * imps] = logged_v[pl.ds(other, 1), :]
     total = jnp.zeros((imps, events.shape[1]), jnp.float32)
     for k in range(EVENT_PARTS):
         copies[4 + k].wait()
@@ -81,14 +83,13 @@
             events_v[k * part_rows : (k + 1) * part_rows, :],
             preferred_element_type=jnp.float32,
         )
-    total = total.astype(jnp.bfloat16)
-    for k in range(items_axis):
-        chosen[k] = total
-
-
-def attend_kernel(place, limits, events, chosen, w_uvqk, gated):
+    chosen[...] = total.astype(jnp.bfloat16)
+    copies[-1].wait()
+
+
+def attend_kernel(limits, events, chosen, w_uvqk, gated):
     rows = events.shape[0]
-    own = chosen[place[0]]
+    own = chosen[...]
     lanes = lax.broadcasted_iota(jnp.int32, (own.shape[0], rows), 1)
     valid = lanes <= limits[:, 0:1]
     for head in range(gated.shape[2] // DH):
@@ -113,33 +114,39 @@
             gated[k, :, head * DH : (head + 1) * DH] = gated_rows
 
 
-def score_kernel(sizes, place, wanted, chosen, gated, *refs):
+def score_kernel(sizes, place, wanted, gated, *refs):
     items_axis, dps, tensors = sizes
+    chosen, refs = refs[:items_axis], refs[items_axis:]
     w_out, refs = refs[:tensors], refs[tensors:]
-    catalogue, refs = refs[:dps], refs[dps:]
-    state, sums, hidden = refs
+    catalogue, refs = list(refs[:dps]), refs[dps:]
+    state, sums, hidden, own_catalogue, sem = refs
+    fetch = pltpu.make_async_copy(catalogue[0], own_catalogue, sem)
+    fetch.start()
+    catalogue[0] = own_catalogue
     item, dp, tensor = place[0], place[1], place[2]
-    imps = chosen.shape[1]
-    items = catalogue[0].shape[0]
+    imps = chosen[0].shape[0]
+    items = own_catalogue.shape[0]
     for k in range(items_axis):
-        total = chosen[k].astype(jnp.float32)
+        total = chosen[k][...].astype(jnp.float32)
         for t in range(tensors):
             total += jnp.dot(
-                gated[k * tensors + (tensor ^ t)], w_out[t][...], preferred_element_type=jnp.float32
+                gated[(item ^ k) * tensors + (tensor ^ t)],
+                w_out[t][...],
+                preferred_element_type=jnp.float32,
             )
         hidden[k * imps : (k + 1) * imps, :] = total.astype(jnp.bfloat16)
     share = state.shape[1]
-    state[...] = hidden[
-        pl.ds(pl.multiple_of(item * imps, imps), imps),
-        pl.ds(pl.multiple_of(tensor * share, share), share),
-    ]
+    state[...] = hidden[0:imps, pl.ds(pl.multiple_of(tensor * share, share), share)]
     step_rows = min(256, items_axis * imps)
     step_items = min(256, items)
-    for row in range(0, items_axis * imps, step_rows):
-        total = jnp.zeros((8, step_rows), jnp.float32)
-        target = jnp.zeros((8, step_rows), jnp.float32)
-        for d in range(dps):
-            item_base = ((item * dps + (dp ^ d)) * tensors + tensor) * items
+    blocks = range(0, items_axis * imps, step_rows)
+    totals = {row: jnp.zeros((8, step_rows), jnp.float32) for row in blocks}
+    targets = dict(totals)
+    for d in reversed(range(dps)):
+        if d == 0:
+            fetch.wait()
+        item_base = ((item * dps + (dp ^ d)) * tensors + tensor) * items
+        for row in blocks:
             ids = wanted[0:1, row : row + step_rows] - item_base
             for first in range(0, items, step_items):
                 logits = lax.dot_general(
@@ -150,12 +157,13 @@
                 )
                 item_ids = first + lax.broadcasted_iota(jnp.int32, logits.shape, 0)
                 found = jnp.where(item_ids == ids, logits, 0.0)
-                total += jnp.sum(jnp.exp(logits).reshape(-1, 8, step_rows), axis=0)
-                target += jnp.sum(found.reshape(-1, 8, step_rows), axis=0)
-        total = jnp.sum(total, axis=0, keepdims=True)
-        target = jnp.sum(target, axis=0, keepdims=True)
+                totals[row] += jnp.sum(jnp.exp(logits).reshape(-1, 8, step_rows), axis=0)
+                targets[row] += jnp.sum(found.reshape(-1, 8, step_rows), axis=0)
+    for row in blocks:
+        total = jnp.sum(totals[row], axis=0, keepdims=True)
+        target = jnp.sum(targets[row], axis=0, keepdims=True)
         for part in range(step_rows // imps):
-            owner = row // imps + part
+            owner = item ^ (row // imps + part)
             both = jnp.concatenate(
                 [v[:, part * imps : (part + 1) * imps] for v in (total, target)], axis=1
             )
@@ -187,55 +195,57 @@
 
     all_w_out = from_others(w_out, "tensor", tensors)
     all_catalogue = from_others(catalogue, "dp", dps)
-    chosen, limits, wanted = pl.pallas_call(
+    chosen, limits, wanted, events, w_uvqk = pl.pallas_call(
         functools.partial(pick_kernel, (items_axis, dps)),
         out_shape=(
-            jax.ShapeDtypeStruct((items_axis, imps, width), jnp.bfloat16),
+            jax.ShapeDtypeStruct((imps, width), jnp.bfloat16),
             jax.ShapeDtypeStruct((imps, 128), jnp.int32),
             jax.ShapeDtypeStruct((1, items_axis * imps), jnp.int32),
-        ),
-        in_specs=[smem] + [hbm] * 5,
-        out_specs=(vmem, vmem, vmem),
+            jax.ShapeDtypeStruct(events.shape, events.dtype),
+            jax.ShapeDtypeStruct(w_uvqk.shape, w_uvqk.dtype),
+        ),
+        in_specs=[smem] + [hbm] * 6,
+        out_specs=(vmem,) * 5,
         scratch_shapes=[
             pltpu.SMEM((hists,), jnp.int32),
             pltpu.SMEM((hists,), jnp.int32),
             pltpu.VMEM((hists, imps), jnp.int32),
             pltpu.VMEM((hists, imps), jnp.int32),
-            pltpu.VMEM((rows, width), jnp.bfloat16),
-            pltpu.SemaphoreType.DMA((4 + EVENT_PARTS,)),
+            pltpu.SemaphoreType.DMA((5 + EVENT_PARTS,)),
         ],
         compiler_params=params,
         cost_estimate=pl.CostEstimate(
             flops=2 * imps * rows * width, bytes_accessed=2 * rows * width, transcendentals=0
         ),
         name="pick",
-    )(place, *(in_hbm(x) for x in (packing, lengths, positions, logged, events)))
-    all_chosen = lax.all_to_all(chosen, "item", split_axis=0, concat_axis=0, tiled=True)
+    )(place, *(in_hbm(x) for x in (packing, lengths, positions, logged, events, w_uvqk)))
+    all_chosen = from_others(chosen, "item", items_axis)
 
     gated = pl.pallas_call(
         attend_kernel,
         out_shape=jax.ShapeDtypeStruct((receivers, imps, local_width), jnp.bfloat16),
-        in_specs=[smem, vmem, vmem, vmem, vmem],
+        in_specs=[vmem] * 4,
         out_specs=vmem,
         compiler_params=params,
-        cost_estimate=pl.CostEstimate(
-            flops=4 * rows * width * local_width,
-            bytes_accessed=2 * rows * width + 8 * width * local_width,
-            transcendentals=2 * rows * local_width,
-        ),
+        cost_estimate=pl.CostEstimate(flops=0, bytes_accessed=0, transcendentals=0),
         name="attend",
-    )(place, limits, events, chosen, w_uvqk)
+    )(limits, events, chosen, w_uvqk)
     all_gated = lax.all_to_all(gated, COLUMN, split_axis=0, concat_axis=0, tiled=True)
 
+    own_catalogue, *other_catalogues = all_catalogue
     state, sums = pl.pallas_call(
         functools.partial(score_kernel, (items_axis, dps, tensors)),
         out_shape=(
             jax.ShapeDtypeStruct((imps, width // tensors), jnp.bfloat16),
             jax.ShapeDtypeStruct((receivers, 1, 2 * imps), jnp.float32),
         ),
-        in_specs=[smem] + [vmem] * (3 + tensors + dps),
+        in_specs=[smem] + [vmem] * (2 + items_axis + tensors) + [hbm] + [vmem] * (dps - 1),
         out_specs=(vmem, vmem),
-        scratch_shapes=[pltpu.VMEM((items_axis * imps, width), jnp.bfloat16)],
+        scratch_shapes=[
+            pltpu.VMEM((items_axis * imps, width), jnp.bfloat16),
+            pltpu.VMEM((items, width), jnp.bfloat16),
+            pltpu.SemaphoreType.DMA,
+        ],
         compiler_params=params,
         cost_estimate=pl.CostEstimate(
             flops=2 * items_axis * imps * width * (dps * items + local_width * tensors),
@@ -243,7 +253,15 @@
             transcendentals=items_axis * imps * dps * items,
         ),
         name="score",
-    )(place, wanted, all_chosen, all_gated, *all_w_out, *all_catalogue)
+    )(
+        place,
+        wanted,
+        all_gated,
+        *all_chosen,
+        *all_w_out,
+        in_hbm(own_catalogue),
+        *other_catalogues,
+    )
     sums = lax.all_to_all(sums, COLUMN, split_axis=0, concat_axis=0, tiled=True)
     sums = jnp.sum(sums, axis=(0, 1))
     return (state, sums[imps:] - jnp.log(sums[:imps]))

time: 54.3 us -> 44.6 us (0.82)
  blocking collectives: 23.2 us -> 11 us
  starting transfers between devices: 4.3 us -> 12.4 us
  local copies, waits for them, and re-layouts: 2.82 us -> 0.01 us
  waiting for transfers between devices: 13.5 us -> 11.5 us
  Pallas kernels: 8.73 us -> 8.15 us
    all_to_all x1 -> x0, blocking collectives: 14.3 us -> none  [local(): lax.all_to_all(gated, COLUMN, split_axis=0, concat_axis=0, tiled=True)]
    ppermute x2 -> x5, starting transfers between devices: 0.83 us -> 7.5 us  [from_others(): lax.ppermute(x, axes, [(i, i ^ r) for i in range(count)])]
    all_to_all x1, waiting for transfers between devices: 6.61 us -> 0.01 us  [local(): lax.all_to_all(gated, COLUMN, split_axis=0, concat_axis=0, tiled=True)]
    ppermute x2 -> x5, waiting for transfers between devices: 6.87 us -> 11.5 us  [from_others(): lax.ppermute(x, axes, [(i, i ^ r) for i in range(count)])]
    unnamed x8 -> x2, local copies, waits for them, and re-layouts: 2.82 us -> 0.01 us
    all_to_all x1, blocking collectives: 8.99 us -> 11 us  [local(): sums = lax.all_to_all(sums, COLUMN, split_axis=0, concat_axis=0, tiled=True)]
    all_to_all x1, starting transfers between devices: 3.47 us -> 4.88 us  [local(): lax.all_to_all(gated, COLUMN, split_axis=0, concat_axis=0, tiled=True)]
    pallas_call x1, Pallas kernels: 3 us -> 2.35 us  [local(): pl.pallas_call(functools.partial(pick_kernel, (items_axis, dps)), out_sha...]
  transfers between devices with their start and end apart: 3 -> 6, of which waited for: 2 -> 2; matrix products, arithmetic and copies ran while one was open for 0% -> 0% of each run, Pallas kernels for 10% -> 9%
where the time goes in v3:
time: 44.6 us; the launch traced here: 44.3 us
  starting transfers between devices  12.4 us (28%)
  waiting for transfers between devices  11.5 us (26%)
  blocking collectives  11 us (25%)
  Pallas kernels  8.15 us (18%)
  other arithmetic  0.69 us (2%)
  between operations  0.68 us (2%)
    ppermute x5, waiting for transfers between devices, from_others(): lax.ppermute(x, axes, [(i, i ^ r) for i in range(count)])  11.5 us
    all_to_all x1, blocking collectives, local(): sums = lax.all_to_all(sums, COLUMN, split_axis=0, concat_axis=0, tiled=True)  11 us
    ppermute x5, starting transfers between devices, from_others(): lax.ppermute(x, axes, [(i, i ^ r) for i in range(count)])  7.5 us
    all_to_all x1, starting transfers between devices, local(): lax.all_to_all(gated, COLUMN, split_axis=0, concat_axis=0, tiled=True)  4.88 us
    pallas_call x1, Pallas kernels, local(): pl.pallas_call(functools.partial(score_kernel, (items_axis, dps, tensors)...  4.06 us
    pallas_call x1, Pallas kernels, local(): pl.pallas_call(functools.partial(pick_kernel, (items_axis, dps)), out_sha...  2.35 us
    pallas_call x1, Pallas kernels, local(): pl.pallas_call(attend_kernel, out_shape=jax.ShapeDtypeStruct((receivers,...  1.74 us
  transfers between devices with their start and end apart: 6, of which 2 were waited for; matrix products, arithmetic and copies ran while one was open for 0% of the time, Pallas kernels for 9%

profile of v3, /device:TPU:0, one launch (start us, length us, event | category | flops | bytes accessed | tf_op | source)
XLA Modules:
  0.0 44.3 jit_solution(9406474211680645182)
XLA Ops:
  0.6 0.5 %collective-permute-start.4 = (bf16[1024,1024]{1,0:T(8,128)(2,1)}, bf16[1024,1024]{1,0:T(8,128)(2,1)S(1)}, u32[]{:S(2)}, u32[]{:S(2)}) collective-permute-start(bf16[1024,1024]{1,0:T(8,128)(2,1)} %refs_6_.1), channel_id=1, source_target_pairs={{0,2},{2,0},{1,3},{3,1},{4,6},{6,4},{5,7},{7,5},{8,10},{10,8},{9,1... | collective-permute-start | bytes 6291464 | tf_op jit(solution)/shard_map/ppermute | solution.py:180
  1.1 2.6 %collective-permute-start.3 = (bf16[128,1024]{1,0:T(8,128)(2,1)}, bf16[128,1024]{1,0:T(8,128)(2,1)S(1)}, u32[]{:S(2)}, u32[]{:S(2)}) collective-permute-start(bf16[128,1024]{1,0:T(8,128)(2,1)} %refs_4_.1), channel_id=1, source_target_pairs={{0,1},{1,0},{2,3},{3,2},{4,5},{5,4},{6,7},{7,6},{8,9},{9,8},{10,11... | collective-permute-start | bytes 786440 | tf_op jit(solution)/shard_map/ppermute | solution.py:180
  3.7 0.1 pad_add_fusion.place
  3.8 2.4 %pick.1 = (bf16[64,1024]{1,0:T(8,128)(2,1)S(1)}, s32[64,128]{1,0:T(8,128)S(1)}, s32[1,256]{1,0:T(1,128)S(1)}, bf16[768,1024]{1,0:T(8,128)(2,1)S(1)}, bf16[1024,512]{1,0:T(8,128)(2,1)S(1)}) custom-call(s32[3]{0:T(128)S(1)} %pad_add_fusion.place, s32[8]{0:T(128)} %packing.1, s32[8]{0:T(128)} %lengths.1, s32[8,64]{1,0:T(8,128)} %positions.1, s32[8,64]{1,0:T(8,128)} %logged.1, ...), custom_call_target="tpu_custom_call" | custom-call | flops 100663296 | bytes 1572864 | tf_op jit(solution)/shard_map/pick/pallas_call | solution.py:198
  6.1 0.0 copy-start
  6.2 1.7 %attend.1 = bf16[8,64,128]{2,1,0:T(8,128)(2,1)} custom-call(s32[64,128]{1,0:T(8,128)S(1)} %get-tuple-element.10.limits, bf16[768,1024]{1,0:T(8,128)(2,1)S(1)} %get-tuple-element.11.events, bf16[64,1024]{1,0:T(8,128)(2,1)S(1)} %get-tuple-element.12.chosen.refs_0_, bf16[1024,512]{1,0:T(8,128)(2,1)S(1)} %get-tuple-element.13.w_uvqk), custom_call_target="tpu_custom_call" | custom-call | tf_op jit(solution)/shard_map/attend/pallas_call | solution.py:224
  7.9 4.9 %all-to-all-start = ((bf16[8,64,128]{2,1,0:T(8,128)(2,1)}), bf16[8,64,128]{2,1,0:T(8,128)(2,1)S(1)}, u32[]{:S(2)}, u32[]{:S(2)}) async-start(bf16[8,64,128]{2,1,0:T(8,128)(2,1)} %attend.1), calls=%async_computation | async-start | bytes 262144 | tf_op jit(solution)/shard_map/all_to_all | solution.py:233
  12.8 2.0 %collective-permute-start = (bf16[64,1024]{1,0:T(8,128)(2,1)S(1)}, bf16[64,1024]{1,0:T(8,128)(2,1)S(1)}, u32[]{:S(2)}, u32[]{:S(2)}) collective-permute-start(bf16[64,1024]{1,0:T(8,128)(2,1)S(1)} %get-tuple-element.12.chosen.refs_0_), channel_id=1, source_target_pairs={{0,4},{4,0},{8,12},{12,8},{1,5},{5,1},{9,13},{13,9},{2,6},{6,2},{1... | collective-permute-start | bytes 393224 | tf_op jit(solution)/shard_map/ppermute | solution.py:180
  14.8 2.4 %collective-permute-start.1 = (bf16[64,1024]{1,0:T(8,128)(2,1)S(1)}, bf16[64,1024]{1,0:T(8,128)(2,1)S(1)}, u32[]{:S(2)}, u32[]{:S(2)}) collective-permute-start(bf16[64,1024]{1,0:T(8,128)(2,1)S(1)} %get-tuple-element.12.chosen.refs_0_), channel_id=1, source_target_pairs={{0,8},{4,12},{8,0},{12,4},{1,9},{5,13},{9,1},{13,5},{2,10},{6,14},... | collective-permute-start | bytes 393224 | tf_op jit(solution)/shard_map/ppermute | solution.py:180
  17.2 0.0 collective-permute-start.2
  17.2 5.4 %collective-permute-done.refs_1_ = bf16[64,1024]{1,0:T(8,128)(2,1)S(1)} collective-permute-done((bf16[64,1024]{1,0:T(8,128)(2,1)S(1)}, bf16[64,1024]{1,0:T(8,128)(2,1)S(1)}, u32[]{:S(2)}, u32[]{:S(2)}) %collective-permute-start) | collective-permute-done | bytes 131104 | tf_op jit(solution)/shard_map/ppermute | solution.py:180
  22.6 6.1 %collective-permute-done.1.refs_2_ = bf16[64,1024]{1,0:T(8,128)(2,1)S(1)} collective-permute-done((bf16[64,1024]{1,0:T(8,128)(2,1)S(1)}, bf16[64,1024]{1,0:T(8,128)(2,1)S(1)}, u32[]{:S(2)}, u32[]{:S(2)}) %collective-permute-start.1) | collective-permute-done | bytes 131104 | tf_op jit(solution)/shard_map/ppermute | solution.py:180
  28.7 0.0 collective-permute-done.2.refs_3_
  28.7 0.0 all-to-all-done.gated
  28.7 0.0 collective-permute-done.3.refs_5_
  28.7 0.0 collective-permute-done.4.refs_7_
  28.7 0.0 copy-done
  28.7 4.1 %score.1 = (bf16[64,512]{1,0:T(8,128)(2,1)}, f32[8,1,128]{2,1,0:T(1,128)S(1)}) custom-call(s32[3]{0:T(128)S(1)} %pad_add_fusion.place, s32[1,256]{1,0:T(1,128)S(1)} %get-tuple-element.9.wanted, bf16[8,64,128]{2,1,0:T(8,128)(2,1)S(1)} %all-to-all-done.gated, bf16[64,1024]{1,0:T(8,128)(2,1)S(1)} %get-tuple-element.12.chosen.refs_0_, ...), custom_call_target="tpu_custom_call" | custom-call | flops 1207959552 | bytes 4194304 | tf_op jit(solution)/shard_map/score/pallas_call | solution.py:236
  32.8 11.0 %all_to_all.10 = f32[8,1,128]{2,1,0:T(1,128)S(1)} all-to-all(f32[8,1,128]{2,1,0:T(1,128)S(1)} %get-tuple-element.15), channel_id=1, replica_groups=mesh['groups'=2,'item'=4,'dp'=2,'tensor'=2] {'item','tensor'}, dimensions={0} | all-to-all | bytes 8192 | tf_op jit(solution)/shard_map/all_to_all | solution.py:265
  43.7 0.6 %log_subtract_fusion = f32[64]{0:T(128)} fusion(f32[128]{0:T(128)S(1)} %reduce_sum.9), kind=kLoop, calls=%fused_computation.1 | loop fusion | flops 64 | bytes 768 | tf_op jit(solution)/shard_map/sub | solution.py:267
  (1 shorter events, 0.0 us)
Async XLA Ops:
  0.6 28.0 %collective-permute-start.4 = (bf16[1024,1024]{1,0:T(8,128)(2,1)}, bf16[1024,1024]{1,0:T(8,128)(2,1)S(1)}, u32[]{:S(2)}, u32[]{:S(2)}) collective-permute-start(bf16[1024,1024]{1,0:T(8,128)(2,1)} %refs_6_.1), channel_id=1, source_target_pairs={{0,2},{2,0},{1,3},{3,1},{4,6},{6,4},{5,7},{7,5},{8,10},{10,8},{9,1... | collective-permute-start | bytes 6291464 | tf_op jit(solution)/shard_map/ppermute | solution.py:180
  1.1 27.5 %collective-permute-start.3 = (bf16[128,1024]{1,0:T(8,128)(2,1)}, bf16[128,1024]{1,0:T(8,128)(2,1)S(1)}, u32[]{:S(2)}, u32[]{:S(2)}) collective-permute-start(bf16[128,1024]{1,0:T(8,128)(2,1)} %refs_4_.1), channel_id=1, source_target_pairs={{0,1},{1,0},{2,3},{3,2},{4,5},{5,4},{6,7},{7,6},{8,9},{9,8},{10,11... | collective-permute-start | bytes 786440 | tf_op jit(solution)/shard_map/ppermute | solution.py:180
  6.1 22.5 %copy-start = (bf16[128,1024]{1,0:T(8,128)(2,1)S(1)}, bf16[128,1024]{1,0:T(8,128)(2,1)}, u32[]{:S(2)}) copy-start(bf16[128,1024]{1,0:T(8,128)(2,1)} %refs_4_.1) | copy-start | bytes 786436
  7.9 20.8 %all-to-all-start = ((bf16[8,64,128]{2,1,0:T(8,128)(2,1)}), bf16[8,64,128]{2,1,0:T(8,128)(2,1)S(1)}, u32[]{:S(2)}, u32[]{:S(2)}) async-start(bf16[8,64,128]{2,1,0:T(8,128)(2,1)} %attend.1), calls=%async_computation | async-start | bytes 262144 | tf_op jit(solution)/shard_map/all_to_all | solution.py:233
  12.8 9.8 %collective-permute-start = (bf16[64,1024]{1,0:T(8,128)(2,1)S(1)}, bf16[64,1024]{1,0:T(8,128)(2,1)S(1)}, u32[]{:S(2)}, u32[]{:S(2)}) collective-permute-start(bf16[64,1024]{1,0:T(8,128)(2,1)S(1)} %get-tuple-element.12.chosen.refs_0_), channel_id=1, source_target_pairs={{0,4},{4,0},{8,12},{12,8},{1,5},{5,1},{9,13},{13,9},{2,6},{6,2},{1... | collective-permute-start | bytes 393224 | tf_op jit(solution)/shard_map/ppermute | solution.py:180
  14.8 13.9 %collective-permute-start.1 = (bf16[64,1024]{1,0:T(8,128)(2,1)S(1)}, bf16[64,1024]{1,0:T(8,128)(2,1)S(1)}, u32[]{:S(2)}, u32[]{:S(2)}) collective-permute-start(bf16[64,1024]{1,0:T(8,128)(2,1)S(1)} %get-tuple-element.12.chosen.refs_0_), channel_id=1, source_target_pairs={{0,8},{4,12},{8,0},{12,4},{1,9},{5,13},{9,1},{13,5},{2,10},{6,14},... | collective-permute-start | bytes 393224 | tf_op jit(solution)/shard_map/ppermute | solution.py:180
  17.2 11.5 %collective-permute-start.2 = (bf16[64,1024]{1,0:T(8,128)(2,1)S(1)}, bf16[64,1024]{1,0:T(8,128)(2,1)S(1)}, u32[]{:S(2)}, u32[]{:S(2)}) collective-permute-start(bf16[64,1024]{1,0:T(8,128)(2,1)S(1)} %get-tuple-element.12.chosen.refs_0_), channel_id=1, source_target_pairs={{0,12},{4,8},{8,4},{12,0},{1,13},{5,9},{9,5},{13,1},{2,14},{6,10},... | collective-permute-start | bytes 393224 | tf_op jit(solution)/shard_map/ppermute | solution.py:180

commit v4 on v3

--- a/solution.py
+++ b/solution.py
@@ -12,7 +12,7 @@
 SLOTS = ("item", "dp")
 COLUMN = ("item", "tensor")
 NT = (((1,), (1,)), ((), ()))
-VMEM_LIMIT = 32 * 1024 * 1024
+VMEM_LIMIT = 16 * 1024 * 1024
 EVENT_PARTS = 4
 
 
@@ -138,7 +138,7 @@
     share = state.shape[1]
     state[...] = hidden[0:imps, pl.ds(pl.multiple_of(tensor * share, share), share)]
     step_rows = min(256, items_axis * imps)
-    step_items = min(256, items)
+    step_items = min(1024, items)
     blocks = range(0, items_axis * imps, step_rows)
     totals = {row: jnp.zeros((8, step_rows), jnp.float32) for row in blocks}
     targets = dict(totals)
@@ -230,7 +230,12 @@
         cost_estimate=pl.CostEstimate(flops=0, bytes_accessed=0, transcendentals=0),
         name="attend",
     )(limits, events, chosen, w_uvqk)
-    all_gated = lax.all_to_all(gated, COLUMN, split_axis=0, concat_axis=0, tiled=True)
+    all_gated = lax.cond(
+        lengths[0] > 0,
+        lambda x: lax.all_to_all(x, COLUMN, split_axis=0, concat_axis=0, tiled=True),
+        lambda x: x,
+        gated,
+    )
 
     own_catalogue, *other_catalogues = all_catalogue
     state, sums = pl.pallas_call(

time: 44.6 us -> 41.9 us (0.939)
  blocking collectives: 11 us -> 24.2 us
  waiting for transfers between devices: 11.5 us -> 0.01 us
  starting transfers between devices: 12.4 us -> 7.54 us
    all_to_all x0 -> x1, blocking collectives: none -> 13.5 us  [local(): lax.all_to_all(x, COLUMN, split_axis=0, concat_axis=0, tiled=True)]
    ppermute x5, waiting for transfers between devices: 11.5 us -> 0.01 us  [from_others(): lax.ppermute(x, axes, [(i, i ^ r) for i in range(count)])]
    all_to_all x1 -> x0, starting transfers between devices: 4.88 us -> none  [local(): lax.all_to_all(gated, COLUMN, split_axis=0, concat_axis=0, tiled=True)]
    pallas_call x1, Pallas kernels: 4.06 us -> 4.99 us  [local(): pl.pallas_call(functools.partial(score_kernel, (items_axis, dps, tensors)...]
    pallas_call x1, Pallas kernels: 1.74 us -> 1.09 us  [local(): pl.pallas_call(attend_kernel, out_shape=jax.ShapeDtypeStruct((receivers,...]
  transfers between devices with their start and end apart: 6 -> 5, of which waited for: 2 -> 0; matrix products, arithmetic and copies ran while one was open for 0% -> 0% of each run, Pallas kernels for 9% -> 8%
where the time goes in v4:
time: 41.9 us; the launch traced here: 41.7 us
  blocking collectives  24.2 us (58%)
  Pallas kernels  8.44 us (20%)
  starting transfers between devices  7.54 us (18%)
  between operations  0.74 us (2%)
  other arithmetic  0.69 us (2%)
    all_to_all x1, blocking collectives, local(): lax.all_to_all(x, COLUMN, split_axis=0, concat_axis=0, tiled=True)  13.5 us
    all_to_all x1, blocking collectives, local(): sums = lax.all_to_all(sums, COLUMN, split_axis=0, concat_axis=0, tiled=True)  10.7 us
    ppermute x5, starting transfers between devices, from_others(): lax.ppermute(x, axes, [(i, i ^ r) for i in range(count)])  7.54 us
    pallas_call x1, Pallas kernels, local(): pl.pallas_call(functools.partial(score_kernel, (items_axis, dps, tensors)...  4.99 us
    pallas_call x1, Pallas kernels, local(): pl.pallas_call(functools.partial(pick_kernel, (items_axis, dps)), out_sha...  2.35 us
    pallas_call x1, Pallas kernels, local(): pl.pallas_call(attend_kernel, out_shape=jax.ShapeDtypeStruct((receivers,...  1.09 us
  transfers between devices with their start and end apart: 5, of which 0 were waited for; matrix products, arithmetic and copies ran while one was open for 0% of the time, Pallas kernels for 8%

profile of v4, /device:TPU:0, one launch (start us, length us, event | category | flops | bytes accessed | tf_op | source)
XLA Modules:
  0.0 41.7 jit_solution(9239839357713061090)
XLA Ops:
  0.6 0.0 copy-start.1
  0.6 0.5 %collective-permute-start.4 = (bf16[1024,1024]{1,0:T(8,128)(2,1)}, bf16[1024,1024]{1,0:T(8,128)(2,1)S(1)}, u32[]{:S(2)}, u32[]{:S(2)}) collective-permute-start(bf16[1024,1024]{1,0:T(8,128)(2,1)} %refs_6_.1), channel_id=1, source_target_pairs={{0,2},{2,0},{1,3},{3,1},{4,6},{6,4},{5,7},{7,5},{8,10},{10,8},{9,1... | collective-permute-start | bytes 6291464 | tf_op jit(solution)/shard_map/ppermute | solution.py:180
  1.2 2.6 %collective-permute-start.3 = (bf16[128,1024]{1,0:T(8,128)(2,1)}, bf16[128,1024]{1,0:T(8,128)(2,1)S(1)}, u32[]{:S(2)}, u32[]{:S(2)}) collective-permute-start(bf16[128,1024]{1,0:T(8,128)(2,1)} %refs_4_.1), channel_id=1, source_target_pairs={{0,1},{1,0},{2,3},{3,2},{4,5},{5,4},{6,7},{7,6},{8,9},{9,8},{10,11... | collective-permute-start | bytes 786440 | tf_op jit(solution)/shard_map/ppermute | solution.py:180
  3.7 0.1 pad_add_fusion.place
  3.8 2.4 %pick.1 = (bf16[64,1024]{1,0:T(8,128)(2,1)S(1)}, s32[64,128]{1,0:T(8,128)S(1)}, s32[1,256]{1,0:T(1,128)S(1)}, bf16[768,1024]{1,0:T(8,128)(2,1)S(1)}, bf16[1024,512]{1,0:T(8,128)(2,1)S(1)}) custom-call(s32[3]{0:T(128)S(1)} %pad_add_fusion.place, s32[8]{0:T(128)} %packing.1, s32[8]{0:T(128)} %lengths.1, s32[8,64]{1,0:T(8,128)} %positions.1, s32[8,64]{1,0:T(8,128)} %logged.1, ...), custom_call_target="tpu_custom_call" | custom-call | flops 100663296 | bytes 1572864 | tf_op jit(solution)/shard_map/pick/pallas_call | solution.py:198
  6.2 0.0 copy-start
  6.2 1.6 %collective-permute-start = (bf16[64,1024]{1,0:T(8,128)(2,1)S(1)}, bf16[64,1024]{1,0:T(8,128)(2,1)S(1)}, u32[]{:S(2)}, u32[]{:S(2)}) collective-permute-start(bf16[64,1024]{1,0:T(8,128)(2,1)S(1)} %get-tuple-element.17.chosen.refs_0_), channel_id=1, source_target_pairs={{0,4},{4,0},{8,12},{12,8},{1,5},{5,1},{9,13},{13,9},{2,6},{6,2},{1... | collective-permute-start | bytes 393224 | tf_op jit(solution)/shard_map/ppermute | solution.py:180
  7.8 2.6 %collective-permute-start.1 = (bf16[64,1024]{1,0:T(8,128)(2,1)S(1)}, bf16[64,1024]{1,0:T(8,128)(2,1)S(1)}, u32[]{:S(2)}, u32[]{:S(2)}) collective-permute-start(bf16[64,1024]{1,0:T(8,128)(2,1)S(1)} %get-tuple-element.17.chosen.refs_0_), channel_id=1, source_target_pairs={{0,8},{4,12},{8,0},{12,4},{1,9},{5,13},{9,1},{13,5},{2,10},{6,14},... | collective-permute-start | bytes 393224 | tf_op jit(solution)/shard_map/ppermute | solution.py:180
  10.4 0.2 collective-permute-start.2
  10.6 0.0 copy-done.1
  10.7 1.1 %attend.1 = bf16[8,64,128]{2,1,0:T(8,128)(2,1)S(1)} custom-call(s32[64,128]{1,0:T(8,128)S(1)} %get-tuple-element.15.limits, bf16[768,1024]{1,0:T(8,128)(2,1)S(1)} %get-tuple-element.16.events, bf16[64,1024]{1,0:T(8,128)(2,1)S(1)} %get-tuple-element.17.chosen.refs_0_, bf16[1024,512]{1,0:T(8,128)(2,1)S(1)} %get-tuple-element.18.w_uvqk), custom_call_target="tpu_custom_call" | custom-call | tf_op jit(solution)/shard_map/attend/pallas_call | solution.py:224
  11.8 13.5 %conditional.1 = (bf16[8,64,128]{2,1,0:T(8,128)(2,1)S(1)}) conditional(s32[]{:T(128)} %bitcast.3, bf16[8,64,128]{2,1,0:T(8,128)(2,1)S(1)} %attend.1, bf16[8,64,128]{2,1,0:T(8,128)(2,1)S(1)} %attend.1), branch_computations={%region_0.0_spmd, %region_1.0_spmd} | conditional | bytes 524296 | solution.py:233
  11.8 13.5 %all_to_all.9 = bf16[8,64,128]{2,1,0:T(8,128)(2,1)S(1)} all-to-all(bf16[8,64,128]{2,1,0:T(8,128)(2,1)S(1)} %copy.12), channel_id=1, replica_groups=mesh['groups'=2,'item'=4,'dp'=2,'tensor'=2] {'item','tensor'}, dimensions={0} | all-to-all | bytes 262144 | tf_op jit(solution)/shard_map/cond/branch_1_fun/all_to_all | solution.py:235
  25.3 0.0 collective-permute-done.refs_1_
  25.3 0.0 collective-permute-done.1.refs_2_
  25.3 0.0 collective-permute-done.2.refs_3_
  25.3 0.0 collective-permute-done.3.refs_5_
  25.3 0.0 collective-permute-done.4.refs_7_
  25.3 0.0 copy-done
  25.3 5.0 %score.1 = (bf16[64,512]{1,0:T(8,128)(2,1)}, f32[8,1,128]{2,1,0:T(1,128)S(1)}) custom-call(s32[3]{0:T(128)S(1)} %pad_add_fusion.place, s32[1,256]{1,0:T(1,128)S(1)} %get-tuple-element.14.wanted, bf16[8,64,128]{2,1,0:T(8,128)(2,1)S(1)} %get-tuple-element.21.gated, bf16[64,1024]{1,0:T(8,128)(2,1)S(1)} %get-tuple-element.17.chosen.refs_0_, ...), custom_call_target="tpu_custom_call" | custom-call | flops 1207959552 | bytes 4194304 | tf_op jit(solution)/shard_map/score/pallas_call | solution.py:241
  30.3 10.7 %all_to_all.10 = f32[8,1,128]{2,1,0:T(1,128)S(1)} all-to-all(f32[8,1,128]{2,1,0:T(1,128)S(1)} %get-tuple-element.20), channel_id=1, replica_groups=mesh['groups'=2,'item'=4,'dp'=2,'tensor'=2] {'item','tensor'}, dimensions={0} | all-to-all | bytes 8192 | tf_op jit(solution)/shard_map/all_to_all | solution.py:270
  41.1 0.6 %log_subtract_fusion = f32[64]{0:T(128)} fusion(f32[128]{0:T(128)S(1)} %reduce_sum.9), kind=kLoop, calls=%fused_computation.1 | loop fusion | flops 64 | bytes 768 | tf_op jit(solution)/shard_map/sub | solution.py:272
  (2 shorter events, 0.0 us)
Async XLA Ops:
  0.6 10.0 %copy-start.1 = (s32[8]{0:T(128)S(1)}, s32[8]{0:T(128)}, u32[]{:S(2)}) copy-start(s32[8]{0:T(128)} %lengths.1) | copy-start | bytes 100
  0.6 24.7 %collective-permute-start.4 = (bf16[1024,1024]{1,0:T(8,128)(2,1)}, bf16[1024,1024]{1,0:T(8,128)(2,1)S(1)}, u32[]{:S(2)}, u32[]{:S(2)}) collective-permute-start(bf16[1024,1024]{1,0:T(8,128)(2,1)} %refs_6_.1), channel_id=1, source_target_pairs={{0,2},{2,0},{1,3},{3,1},{4,6},{6,4},{5,7},{7,5},{8,10},{10,8},{9,1... | collective-permute-start | bytes 6291464 | tf_op jit(solution)/shard_map/ppermute | solution.py:180
  1.2 24.1 %collective-permute-start.3 = (bf16[128,1024]{1,0:T(8,128)(2,1)}, bf16[128,1024]{1,0:T(8,128)(2,1)S(1)}, u32[]{:S(2)}, u32[]{:S(2)}) collective-permute-start(bf16[128,1024]{1,0:T(8,128)(2,1)} %refs_4_.1), channel_id=1, source_target_pairs={{0,1},{1,0},{2,3},{3,2},{4,5},{5,4},{6,7},{7,6},{8,9},{9,8},{10,11... | collective-permute-start | bytes 786440 | tf_op jit(solution)/shard_map/ppermute | solution.py:180
  6.2 19.2 %copy-start = (bf16[128,1024]{1,0:T(8,128)(2,1)S(1)}, bf16[128,1024]{1,0:T(8,128)(2,1)}, u32[]{:S(2)}) copy-start(bf16[128,1024]{1,0:T(8,128)(2,1)} %refs_4_.1) | copy-start | bytes 786436
  6.2 19.1 %collective-permute-start = (bf16[64,1024]{1,0:T(8,128)(2,1)S(1)}, bf16[64,1024]{1,0:T(8,128)(2,1)S(1)}, u32[]{:S(2)}, u32[]{:S(2)}) collective-permute-start(bf16[64,1024]{1,0:T(8,128)(2,1)S(1)} %get-tuple-element.17.chosen.refs_0_), channel_id=1, source_target_pairs={{0,4},{4,0},{8,12},{12,8},{1,5},{5,1},{9,13},{13,9},{2,6},{6,2},{1... | collective-permute-start | bytes 393224 | tf_op jit(solution)/shard_map/ppermute | solution.py:180
  7.8 17.5 %collective-permute-start.1 = (bf16[64,1024]{1,0:T(8,128)(2,1)S(1)}, bf16[64,1024]{1,0:T(8,128)(2,1)S(1)}, u32[]{:S(2)}, u32[]{:S(2)}) collective-permute-start(bf16[64,1024]{1,0:T(8,128)(2,1)S(1)} %get-tuple-element.17.chosen.refs_0_), channel_id=1, source_target_pairs={{0,8},{4,12},{8,0},{12,4},{1,9},{5,13},{9,1},{13,5},{2,10},{6,14},... | collective-permute-start | bytes 393224 | tf_op jit(solution)/shard_map/ppermute | solution.py:180
  10.4 14.9 %collective-permute-start.2 = (bf16[64,1024]{1,0:T(8,128)(2,1)S(1)}, bf16[64,1024]{1,0:T(8,128)(2,1)S(1)}, u32[]{:S(2)}, u32[]{:S(2)}) collective-permute-start(bf16[64,1024]{1,0:T(8,128)(2,1)S(1)} %get-tuple-element.17.chosen.refs_0_), channel_id=1, source_target_pairs={{0,12},{4,8},{8,4},{12,0},{1,13},{5,9},{9,5},{13,1},{2,14},{6,10},... | collective-permute-start | bytes 393224 | tf_op jit(solution)/shard_map/ppermute | solution.py:180

commit v5 on v3

--- a/solution.py
+++ b/solution.py
@@ -12,8 +12,12 @@
 SLOTS = ("item", "dp")
 COLUMN = ("item", "tensor")
 NT = (((1,), (1,)), ((), ()))
-VMEM_LIMIT = 32 * 1024 * 1024
-EVENT_PARTS = 4
+VMEM_LIMIT = 16 * 1024 * 1024
+EVENT_PARTS = 3
+
+
+def rounds(count):
+    return [0] + sorted(range(1, count), key=lambda r: -(r & -2))
 
 
 def spec(space):
@@ -70,8 +74,8 @@
     )
     spots = jnp.sum(jnp.where(diagonal, row, 0.0), axis=1, keepdims=True).astype(jnp.int32)
     limits[...] = jnp.broadcast_to(jnp.minimum(spots, lengths_s[history] - 1), limits.shape)
-    for k in range(items_axis):
-        other = packing_s[(item ^ k) * dps + dp]
+    for k, r in enumerate(rounds(items_axis)):
+        other = packing_s[(item ^ r) * dps + dp]
         wanted[0:1, k * imps : (k + 1) * imps] = logged_v[pl.ds(other, 1), :]
     total = jnp.zeros((imps, events.shape[1]), jnp.float32)
     for k in range(EVENT_PARTS):
@@ -87,7 +91,15 @@
     copies[-1].wait()
 
 
-def attend_kernel(limits, events, chosen, w_uvqk, gated):
+def attend_kernel(
+    limits, events, chosen, w_uvqk, w_out, catalogue, gated, w_out_v, catalogue_v, sems
+):
+    fetches = [
+        pltpu.make_async_copy(w_out, w_out_v, sems.at[0]),
+        pltpu.make_async_copy(catalogue, catalogue_v, sems.at[1]),
+    ]
+    for fetch in fetches:
+        fetch.start()
     rows = events.shape[0]
     own = chosen[...]
     lanes = lax.broadcasted_iota(jnp.int32, (own.shape[0], rows), 1)
@@ -112,25 +124,31 @@
         )
         for k in range(gated.shape[0]):
             gated[k, :, head * DH : (head + 1) * DH] = gated_rows
+    for fetch in fetches:
+        fetch.wait()
 
 
 def score_kernel(sizes, place, wanted, gated, *refs):
     items_axis, dps, tensors = sizes
     chosen, refs = refs[:items_axis], refs[items_axis:]
     w_out, refs = refs[:tensors], refs[tensors:]
-    catalogue, refs = list(refs[:dps]), refs[dps:]
-    state, sums, hidden, own_catalogue, sem = refs
-    fetch = pltpu.make_async_copy(catalogue[0], own_catalogue, sem)
-    fetch.start()
-    catalogue[0] = own_catalogue
+    catalogue, refs = refs[:dps], refs[dps:]
+    state, sums, hidden, others, sems = refs
+    fetches = [
+        pltpu.make_async_copy(catalogue[d], others.at[d - 1], sems.at[d - 1]) for d in range(1, dps)
+    ]
+    for fetch in fetches:
+        fetch.start()
+    catalogue = [catalogue[0]] + [others.at[d - 1] for d in range(1, dps)]
     item, dp, tensor = place[0], place[1], place[2]
     imps = chosen[0].shape[0]
-    items = own_catalogue.shape[0]
+    items = catalogue[0].shape[0]
+    slot_rounds, tensor_rounds = rounds(items_axis), rounds(tensors)
     for k in range(items_axis):
         total = chosen[k][...].astype(jnp.float32)
         for t in range(tensors):
             total += jnp.dot(
-                gated[(item ^ k) * tensors + (tensor ^ t)],
+                gated[(item ^ slot_rounds[k]) * tensors + (tensor ^ tensor_rounds[t])],
                 w_out[t][...],
                 preferred_element_type=jnp.float32,
             )
@@ -138,14 +156,14 @@
     share = state.shape[1]
     state[...] = hidden[0:imps, pl.ds(pl.multiple_of(tensor * share, share), share)]
     step_rows = min(256, items_axis * imps)
-    step_items = min(256, items)
+    step_items = min(512, items)
     blocks = range(0, items_axis * imps, step_rows)
     totals = {row: jnp.zeros((8, step_rows), jnp.float32) for row in blocks}
     targets = dict(totals)
-    for d in reversed(range(dps)):
-        if d == 0:
-            fetch.wait()
-        item_base = ((item * dps + (dp ^ d)) * tensors + tensor) * items
+    for d in range(dps):
+        if d > 0:
+            fetches[d - 1].wait()
+        item_base = ((item * dps + (dp ^ rounds(dps)[d])) * tensors + tensor) * items
         for row in blocks:
             ids = wanted[0:1, row : row + step_rows] - item_base
             for first in range(0, items, step_items):
@@ -163,7 +181,7 @@
         total = jnp.sum(totals[row], axis=0, keepdims=True)
         target = jnp.sum(targets[row], axis=0, keepdims=True)
         for part in range(step_rows // imps):
-            owner = item ^ (row // imps + part)
+            owner = item ^ slot_rounds[row // imps + part]
             both = jnp.concatenate(
                 [v[:, part * imps : (part + 1) * imps] for v in (total, target)], axis=1
             )
@@ -177,7 +195,7 @@
 
 def from_others(x, axes, count):
     return [x] + [
-        lax.ppermute(x, axes, [(i, i ^ r) for i in range(count)]) for r in range(1, count)
+        lax.ppermute(x, axes, [(i, i ^ r) for i in range(count)]) for r in rounds(count)[1:]
     ]
 
 
@@ -193,8 +211,6 @@
     place = jnp.stack([lax.axis_index(a) for a in ("item", "dp", "tensor")]).astype(jnp.int32)
     smem, vmem, hbm = spec(pltpu.SMEM), spec(pltpu.VMEM), spec(pltpu.HBM)
 
-    all_w_out = from_others(w_out, "tensor", tensors)
-    all_catalogue = from_others(catalogue, "dp", dps)
     chosen, limits, wanted, events, w_uvqk = pl.pallas_call(
         functools.partial(pick_kernel, (items_axis, dps)),
         out_shape=(
@@ -221,30 +237,47 @@
     )(place, *(in_hbm(x) for x in (packing, lengths, positions, logged, events, w_uvqk)))
     all_chosen = from_others(chosen, "item", items_axis)
 
-    gated = pl.pallas_call(
+    gated, w_out, catalogue = pl.pallas_call(
         attend_kernel,
-        out_shape=jax.ShapeDtypeStruct((receivers, imps, local_width), jnp.bfloat16),
-        in_specs=[vmem] * 4,
-        out_specs=vmem,
+        out_shape=(
+            jax.ShapeDtypeStruct((receivers, imps, local_width), jnp.bfloat16),
+            jax.ShapeDtypeStruct(w_out.shape, w_out.dtype),
+            jax.ShapeDtypeStruct(catalogue.shape, catalogue.dtype),
+        ),
+        in_specs=[vmem] * 4 + [hbm] * 2,
+        out_specs=(vmem,) * 3,
+        scratch_shapes=[pltpu.SemaphoreType.DMA((2,))],
         compiler_params=params,
         cost_estimate=pl.CostEstimate(flops=0, bytes_accessed=0, transcendentals=0),
         name="attend",
-    )(limits, events, chosen, w_uvqk)
-    all_gated = lax.all_to_all(gated, COLUMN, split_axis=0, concat_axis=0, tiled=True)
-
-    own_catalogue, *other_catalogues = all_catalogue
+    )(limits, events, chosen, w_uvqk, in_hbm(w_out), in_hbm(catalogue))
+
+    def exchange(gated, w_out, catalogue):
+        return (
+            lax.all_to_all(gated, COLUMN, split_axis=0, concat_axis=0, tiled=True),
+            from_others(w_out, "tensor", tensors)[1:],
+            from_others(catalogue, "dp", dps)[1:],
+        )
+
+    def keep(gated, w_out, catalogue):
+        return gated, [w_out] * (tensors - 1), [catalogue] * (dps - 1)
+
+    all_gated, other_w_out, other_catalogues = lax.cond(
+        lengths[0] > 0, exchange, keep, gated, w_out, catalogue
+    )
+
     state, sums = pl.pallas_call(
         functools.partial(score_kernel, (items_axis, dps, tensors)),
         out_shape=(
             jax.ShapeDtypeStruct((imps, width // tensors), jnp.bfloat16),
             jax.ShapeDtypeStruct((receivers, 1, 2 * imps), jnp.float32),
         ),
-        in_specs=[smem] + [vmem] * (2 + items_axis + tensors) + [hbm] + [vmem] * (dps - 1),
+        in_specs=[smem] + [vmem] * (3 + items_axis + tensors) + [hbm] * (dps - 1),
         out_specs=(vmem, vmem),
         scratch_shapes=[
             pltpu.VMEM((items_axis * imps, width), jnp.bfloat16),
-            pltpu.VMEM((items, width), jnp.bfloat16),
-            pltpu.SemaphoreType.DMA,
+            pltpu.VMEM((dps - 1, items, width), jnp.bfloat16),
+            pltpu.SemaphoreType.DMA((dps - 1,)),
         ],
         compiler_params=params,
         cost_estimate=pl.CostEstimate(
@@ -258,9 +291,10 @@
         wanted,
         all_gated,
         *all_chosen,
-        *all_w_out,
-        in_hbm(own_catalogue),
-        *other_catalogues,
+        w_out,
+        *other_w_out,
+        catalogue,
+        *(in_hbm(x) for x in other_catalogues),
     )
     sums = lax.all_to_all(sums, COLUMN, split_axis=0, concat_axis=0, tiled=True)
     sums = jnp.sum(sums, axis=(0, 1))

time: 44.6 us -> 39.4 us (0.88)
  waiting for transfers between devices: 11.5 us -> 0.01 us
  blocking collectives: 11 us -> 21.8 us
  starting transfers between devices: 12.4 us -> 7.31 us
    ppermute x5, waiting for transfers between devices: 11.5 us -> 0.01 us  [from_others(): lax.ppermute(x, axes, [(i, i ^ r) for i in range(count)])]
    all_to_all x0 -> x1, blocking collectives: none -> 11.3 us  [exchange(): lax.all_to_all(gated, COLUMN, split_axis=0, concat_axis=0, tiled=True)]
    all_to_all x1 -> x0, starting transfers between devices: 4.88 us -> none  [local(): lax.all_to_all(gated, COLUMN, split_axis=0, concat_axis=0, tiled=True)]
    all_to_all x1, blocking collectives: 11 us -> 10.4 us  [local(): sums = lax.all_to_all(sums, COLUMN, split_axis=0, concat_axis=0, tiled=True)]
  transfers between devices with their start and end apart: 6 -> 5, of which waited for: 2 -> 0; matrix products, arithmetic and copies ran while one was open for 0% -> 0% of each run, Pallas kernels for 9% -> 4%
where the time goes in v5:
time: 39.4 us; the launch traced here: 39.1 us
  blocking collectives  21.8 us (55%)
  Pallas kernels  8.5 us (22%)
  starting transfers between devices  7.31 us (19%)
  between operations  0.73 us (2%)
  other arithmetic  0.69 us (2%)
    all_to_all x1, blocking collectives, exchange(): lax.all_to_all(gated, COLUMN, split_axis=0, concat_axis=0, tiled=True)  11.3 us
    all_to_all x1, blocking collectives, local(): sums = lax.all_to_all(sums, COLUMN, split_axis=0, concat_axis=0, tiled=True)  10.4 us
    ppermute x5, starting transfers between devices, from_others(): lax.ppermute(x, axes, [(i, i ^ r) for i in range(count)])  7.31 us
    pallas_call x1, Pallas kernels, local(): pl.pallas_call(functools.partial(score_kernel, (items_axis, dps, tensors)...  4.44 us
    pallas_call x1, Pallas kernels, local(): pl.pallas_call(functools.partial(pick_kernel, (items_axis, dps)), out_sha...  2.34 us
    pallas_call x1, Pallas kernels, local(): pl.pallas_call(attend_kernel, out_shape=(jax.ShapeDtypeStruct((receivers,...  1.72 us
  transfers between devices with their start and end apart: 5, of which 0 were waited for; matrix products, arithmetic and copies ran while one was open for 0% of the time, Pallas kernels for 4%

profile of v5, /device:TPU:0, one launch (start us, length us, event | category | flops | bytes accessed | tf_op | source)
XLA Modules:
  0.0 39.1 jit_solution(4582214491647438818)
XLA Ops:
  0.6 0.0 copy-start
  0.6 0.1 pad_add_fusion.place
  0.7 2.3 %pick.1 = (bf16[64,1024]{1,0:T(8,128)(2,1)S(1)}, s32[64,128]{1,0:T(8,128)S(1)}, s32[1,256]{1,0:T(1,128)S(1)}, bf16[768,1024]{1,0:T(8,128)(2,1)S(1)}, bf16[1024,512]{1,0:T(8,128)(2,1)S(1)}) custom-call(s32[3]{0:T(128)S(1)} %pad_add_fusion.place, s32[8]{0:T(128)} %packing.1, s32[8]{0:T(128)} %lengths.1, s32[8,64]{1,0:T(8,128)} %positions.1, s32[8,64]{1,0:T(8,128)} %logged.1, ...), custom_call_target="tpu_custom_call" | custom-call | flops 100663296 | bytes 1572864 | tf_op jit(solution)/shard_map/pick/pallas_call | solution.py:214
  3.1 4.1 %collective-permute-start.2 = (bf16[64,1024]{1,0:T(8,128)(2,1)S(1)}, bf16[64,1024]{1,0:T(8,128)(2,1)S(1)}, u32[]{:S(2)}, u32[]{:S(2)}) collective-permute-start(bf16[64,1024]{1,0:T(8,128)(2,1)S(1)} %get-tuple-element.32.chosen.refs_0_), channel_id=1, source_target_pairs={{0,8},{4,12},{8,0},{12,4},{1,9},{5,13},{9,1},{13,5},{2,10},{6,14},... | collective-permute-start | bytes 393224 | tf_op jit(solution)/shard_map/ppermute | solution.py:198
  7.2 1.3 %collective-permute-start.3 = (bf16[64,1024]{1,0:T(8,128)(2,1)S(1)}, bf16[64,1024]{1,0:T(8,128)(2,1)S(1)}, u32[]{:S(2)}, u32[]{:S(2)}) collective-permute-start(bf16[64,1024]{1,0:T(8,128)(2,1)S(1)} %get-tuple-element.32.chosen.refs_0_), channel_id=1, source_target_pairs={{0,12},{4,8},{8,4},{12,0},{1,13},{5,9},{9,5},{13,1},{2,14},{6,10},... | collective-permute-start | bytes 393224 | tf_op jit(solution)/shard_map/ppermute | solution.py:198
  8.5 0.2 collective-permute-start.4
  8.8 0.0 copy-done
  8.8 1.7 %attend.1 = (bf16[8,64,128]{2,1,0:T(8,128)(2,1)S(1)}, bf16[128,1024]{1,0:T(8,128)(2,1)S(1)}, bf16[1024,1024]{1,0:T(8,128)(2,1)S(1)}) custom-call(s32[64,128]{1,0:T(8,128)S(1)} %get-tuple-element.30.limits, bf16[768,1024]{1,0:T(8,128)(2,1)S(1)} %get-tuple-element.31.events, bf16[64,1024]{1,0:T(8,128)(2,1)S(1)} %get-tuple-element.32.chosen.refs_0_, ...), custom_call_target="tpu_custom_call" | custom-call | tf_op jit(solution)/shard_map/attend/pallas_call | solution.py:240
  10.5 13.0 %conditional.1 = (bf16[8,64,128]{2,1,0:T(8,128)(2,1)S(1)}, bf16[128,1024]{1,0:T(8,128)(2,1)}, bf16[1024,1024]{1,0:T(8,128)(2,1)}) conditional(s32[]{:T(128)} %bitcast.3, (bf16[8,64,128]{2,1,0:T(8,128)(2,1)S(1)}, bf16[128,1024]{1,0:T(8,128)(2,1)S(1)}, bf16[1024,1024]{1,0:T(8,128)(2,1)S(1)}) %attend.1, (bf16[8,64,128]{2,1,0:T(8,128)(2,1)S(1)}, ...), branch_computations={%region_0.0_spmd, %region_1.0_spmd} | conditional | bytes 9961576 | solution.py:265
  10.6 0.1 collective-permute-start.1
  10.6 1.6 %collective-permute-start = (bf16[128,1024]{1,0:T(8,128)(2,1)S(1)}, bf16[128,1024]{1,0:T(8,128)(2,1)}, u32[]{:S(2)}, u32[]{:S(2)}) collective-permute-start(bf16[128,1024]{1,0:T(8,128)(2,1)S(1)} %get-tuple-element.13), channel_id=1, source_target_pairs={{0,1},{1,0},{2,3},{3,2},{4,5},{5,4},{6,7},{7,6},{8,9},{9,8},{10,11... | collective-permute-start | bytes 786440 | tf_op jit(solution)/shard_map/cond/branch_1_fun/ppermute | solution.py:198
  12.2 11.3 %all_to_all.9 = bf16[8,64,128]{2,1,0:T(8,128)(2,1)S(1)} all-to-all(bf16[8,64,128]{2,1,0:T(8,128)(2,1)S(1)} %copy.16), channel_id=1, replica_groups=mesh['groups'=2,'item'=4,'dp'=2,'tensor'=2] {'item','tensor'}, dimensions={0} | all-to-all | bytes 262144 | tf_op jit(solution)/shard_map/cond/branch_1_fun/all_to_all | solution.py:257
  23.5 0.0 collective-permute-done
  23.5 0.0 collective-permute-done.1
  23.5 0.0 collective-permute-done.2.refs_1_
  23.6 0.0 collective-permute-done.3.refs_2_
  23.6 0.0 collective-permute-done.4.refs_3_
  23.6 4.4 %score.1 = (bf16[64,512]{1,0:T(8,128)(2,1)}, f32[8,1,128]{2,1,0:T(1,128)S(1)}) custom-call(s32[3]{0:T(128)S(1)} %pad_add_fusion.place, s32[1,256]{1,0:T(1,128)S(1)} %get-tuple-element.29.wanted, bf16[8,64,128]{2,1,0:T(8,128)(2,1)S(1)} %get-tuple-element.34.gated, bf16[64,1024]{1,0:T(8,128)(2,1)S(1)} %get-tuple-element.32.chosen.refs_0_, ...), custom_call_target="tpu_custom_call" | custom-call | flops 1207959552 | bytes 4194304 | tf_op jit(solution)/shard_map/score/pallas_call | solution.py:269
  28.0 10.4 %all_to_all.10 = f32[8,1,128]{2,1,0:T(1,128)S(1)} all-to-all(f32[8,1,128]{2,1,0:T(1,128)S(1)} %get-tuple-element.40), channel_id=1, replica_groups=mesh['groups'=2,'item'=4,'dp'=2,'tensor'=2] {'item','tensor'}, dimensions={0} | all-to-all | bytes 8192 | tf_op jit(solution)/shard_map/all_to_all | solution.py:299
  38.5 0.6 %log_subtract_fusion = f32[64]{0:T(128)} fusion(f32[128]{0:T(128)S(1)} %reduce_sum.9), kind=kLoop, calls=%fused_computation.1 | loop fusion | flops 64 | bytes 768 | tf_op jit(solution)/shard_map/sub | solution.py:301
  (2 shorter events, 0.0 us)
Async XLA Ops:
  0.6 8.1 %copy-start = (s32[8]{0:T(128)S(1)}, s32[8]{0:T(128)}, u32[]{:S(2)}) copy-start(s32[8]{0:T(128)} %lengths.1) | copy-start | bytes 100
  3.1 20.5 %collective-permute-start.2 = (bf16[64,1024]{1,0:T(8,128)(2,1)S(1)}, bf16[64,1024]{1,0:T(8,128)(2,1)S(1)}, u32[]{:S(2)}, u32[]{:S(2)}) collective-permute-start(bf16[64,1024]{1,0:T(8,128)(2,1)S(1)} %get-tuple-element.32.chosen.refs_0_), channel_id=1, source_target_pairs={{0,8},{4,12},{8,0},{12,4},{1,9},{5,13},{9,1},{13,5},{2,10},{6,14},... | collective-permute-start | bytes 393224 | tf_op jit(solution)/shard_map/ppermute | solution.py:198
  7.2 16.4 %collective-permute-start.3 = (bf16[64,1024]{1,0:T(8,128)(2,1)S(1)}, bf16[64,1024]{1,0:T(8,128)(2,1)S(1)}, u32[]{:S(2)}, u32[]{:S(2)}) collective-permute-start(bf16[64,1024]{1,0:T(8,128)(2,1)S(1)} %get-tuple-element.32.chosen.refs_0_), channel_id=1, source_target_pairs={{0,12},{4,8},{8,4},{12,0},{1,13},{5,9},{9,5},{13,1},{2,14},{6,10},... | collective-permute-start | bytes 393224 | tf_op jit(solution)/shard_map/ppermute | solution.py:198
  8.5 15.0 %collective-permute-start.4 = (bf16[64,1024]{1,0:T(8,128)(2,1)S(1)}, bf16[64,1024]{1,0:T(8,128)(2,1)S(1)}, u32[]{:S(2)}, u32[]{:S(2)}) collective-permute-start(bf16[64,1024]{1,0:T(8,128)(2,1)S(1)} %get-tuple-element.32.chosen.refs_0_), channel_id=1, source_target_pairs={{0,4},{4,0},{8,12},{12,8},{1,5},{5,1},{9,13},{13,9},{2,6},{6,2},{1... | collective-permute-start | bytes 393224 | tf_op jit(solution)/shard_map/ppermute | solution.py:198
  10.6 13.0 %collective-permute-start.1 = (bf16[1024,1024]{1,0:T(8,128)(2,1)S(1)}, bf16[1024,1024]{1,0:T(8,128)(2,1)}, u32[]{:S(2)}, u32[]{:S(2)}) collective-permute-start(bf16[1024,1024]{1,0:T(8,128)(2,1)S(1)} %get-tuple-element.14), channel_id=1, source_target_pairs={{0,2},{2,0},{1,3},{3,1},{4,6},{6,4},{5,7},{7,5},{8,10},{10,8},{9,1... | collective-permute-start | bytes 6291464 | tf_op jit(solution)/shard_map/cond/branch_1_fun/ppermute | solution.py:198
  10.6 12.9 %collective-permute-start = (bf16[128,1024]{1,0:T(8,128)(2,1)S(1)}, bf16[128,1024]{1,0:T(8,128)(2,1)}, u32[]{:S(2)}, u32[]{:S(2)}) collective-permute-start(bf16[128,1024]{1,0:T(8,128)(2,1)S(1)} %get-tuple-element.13), channel_id=1, source_target_pairs={{0,1},{1,0},{2,3},{3,2},{4,5},{5,4},{6,7},{7,6},{8,9},{9,8},{10,11... | collective-permute-start | bytes 786440 | tf_op jit(solution)/shard_map/cond/branch_1_fun/ppermute | solution.py:198

commit v6 on v5

--- a/solution.py
+++ b/solution.py
@@ -12,7 +12,7 @@
 SLOTS = ("item", "dp")
 COLUMN = ("item", "tensor")
 NT = (((1,), (1,)), ((), ()))
-VMEM_LIMIT = 16 * 1024 * 1024
+VMEM_LIMIT = 32 * 1024 * 1024
 EVENT_PARTS = 3
 
 
@@ -62,7 +62,7 @@
             + [(w_uvqk, w_uvqk_v)]
         )
     ]
-    for copy in copies:
+    for copy in copies[4:-1] + copies[:4]:
         copy.start()
     for copy in copies[:4]:
         copy.wait()
@@ -80,6 +80,8 @@
     total = jnp.zeros((imps, events.shape[1]), jnp.float32)
     for k in range(EVENT_PARTS):
         copies[4 + k].wait()
+        if k == 0:
+            copies[-1].start()
         lanes = k * part_rows + lax.broadcasted_iota(jnp.int32, (imps, part_rows), 1)
         one_hot = jnp.where(lanes == spots, 1.0, 0.0).astype(jnp.bfloat16)
         total += jnp.dot(
@@ -92,14 +94,10 @@
 
 
 def attend_kernel(
-    limits, events, chosen, w_uvqk, w_out, catalogue, gated, w_out_v, catalogue_v, sems
+    limits, events, chosen, w_uvqk, w_out, gated, w_out_v, sem
 ):
-    fetches = [
-        pltpu.make_async_copy(w_out, w_out_v, sems.at[0]),
-        pltpu.make_async_copy(catalogue, catalogue_v, sems.at[1]),
-    ]
-    for fetch in fetches:
-        fetch.start()
+    fetch = pltpu.make_async_copy(w_out, w_out_v, sem)
+    fetch.start()
     rows = events.shape[0]
     own = chosen[...]
     lanes = lax.broadcasted_iota(jnp.int32, (own.shape[0], rows), 1)
@@ -124,57 +122,71 @@
         )
         for k in range(gated.shape[0]):
             gated[k, :, head * DH : (head + 1) * DH] = gated_rows
-    for fetch in fetches:
-        fetch.wait()
+    fetch.wait()
 
 
 def score_kernel(sizes, place, wanted, gated, *refs):
     items_axis, dps, tensors = sizes
     chosen, refs = refs[:items_axis], refs[items_axis:]
     w_out, refs = refs[:tensors], refs[tensors:]
-    catalogue, refs = refs[:dps], refs[dps:]
-    state, sums, hidden, others, sems = refs
-    fetches = [
-        pltpu.make_async_copy(catalogue[d], others.at[d - 1], sems.at[d - 1]) for d in range(1, dps)
-    ]
-    for fetch in fetches:
-        fetch.start()
-    catalogue = [catalogue[0]] + [others.at[d - 1] for d in range(1, dps)]
+    catalogue, refs = list(refs[:dps]), refs[dps:]
+    state_hbm, sums, hidden, w_out_v, catalogue_v, w_sems, sems, state_sem = refs
     item, dp, tensor = place[0], place[1], place[2]
     imps = chosen[0].shape[0]
-    items = catalogue[0].shape[0]
+    items = catalogue_v.shape[0]
+    step_rows = min(256, items_axis * imps)
+    step_items = min(256, items)
+    steps = range(0, items, step_items)
+    w_fetches = [
+        pltpu.make_async_copy(w_out[t], w_out_v.at[t - 1], w_sems.at[t - 1])
+        for t in range(1, tensors)
+    ]
+    parts = [pl.ds(first, step_items) for first in steps]
+    fetches = [
+        pltpu.make_async_copy(catalogue[0].at[part], catalogue_v.at[part], sems.at[n])
+        for n, part in enumerate(parts)
+    ]
+    for fetch in w_fetches + fetches:
+        fetch.start()
+    catalogue[0] = catalogue_v
+
     slot_rounds, tensor_rounds = rounds(items_axis), rounds(tensors)
+    totals = [c[...].astype(jnp.float32) for c in chosen]
+    for t in range(tensors):
+        if t > 0:
+            w_fetches[t - 1].wait()
+        w_part = w_out[0][...] if t == 0 else w_out_v[t - 1]
+        for k in range(items_axis):
+            sender = (item ^ slot_rounds[k]) * tensors + (tensor ^ tensor_rounds[t])
+            totals[k] += jnp.dot(gated[sender], w_part, preferred_element_type=jnp.float32)
     for k in range(items_axis):
-        total = chosen[k][...].astype(jnp.float32)
-        for t in range(tensors):
-            total += jnp.dot(
-                gated[(item ^ slot_rounds[k]) * tensors + (tensor ^ tensor_rounds[t])],
-                w_out[t][...],
-                preferred_element_type=jnp.float32,
-            )
-        hidden[k * imps : (k + 1) * imps, :] = total.astype(jnp.bfloat16)
-    share = state.shape[1]
-    state[...] = hidden[0:imps, pl.ds(pl.multiple_of(tensor * share, share), share)]
-    step_rows = min(256, items_axis * imps)
-    step_items = min(512, items)
+        hidden[k * imps : (k + 1) * imps, :] = totals[k].astype(jnp.bfloat16)
+    share = state_hbm.shape[1]
+    state_copy = pltpu.make_async_copy(
+        hidden.at[pl.ds(0, imps), pl.ds(pl.multiple_of(tensor * share, share), share)],
+        state_hbm,
+        state_sem,
+    )
+    state_copy.start()
+
     blocks = range(0, items_axis * imps, step_rows)
     totals = {row: jnp.zeros((8, step_rows), jnp.float32) for row in blocks}
     targets = dict(totals)
     for d in range(dps):
-        if d > 0:
-            fetches[d - 1].wait()
         item_base = ((item * dps + (dp ^ rounds(dps)[d])) * tensors + tensor) * items
-        for row in blocks:
-            ids = wanted[0:1, row : row + step_rows] - item_base
-            for first in range(0, items, step_items):
+        ids = {row: wanted[0:1, row : row + step_rows] - item_base for row in blocks}
+        for first in steps:
+            if d == 0:
+                fetches[first // step_items].wait()
+            for row in blocks:
                 logits = lax.dot_general(
                     catalogue[d][first : first + step_items, :],
                     hidden[row : row + step_rows, :],
                     NT,
                     preferred_element_type=jnp.float32,
                 )
-                item_ids = first + lax.broadcasted_iota(jnp.int32, logits.shape, 0)
-                found = jnp.where(item_ids == ids, logits, 0.0)
+                item_ids = lax.broadcasted_iota(jnp.int32, logits.shape, 0)
+                found = jnp.where(item_ids == ids[row] - first, logits, 0.0)
                 totals[row] += jnp.sum(jnp.exp(logits).reshape(-1, 8, step_rows), axis=0)
                 targets[row] += jnp.sum(found.reshape(-1, 8, step_rows), axis=0)
     for row in blocks:
@@ -187,6 +199,7 @@
             )
             for t in range(tensors):
                 sums[owner * tensors + t] = both
+    state_copy.wait()
 
 
 def in_hbm(x):
@@ -211,6 +224,7 @@
     place = jnp.stack([lax.axis_index(a) for a in ("item", "dp", "tensor")]).astype(jnp.int32)
     smem, vmem, hbm = spec(pltpu.SMEM), spec(pltpu.VMEM), spec(pltpu.HBM)
 
+    other_catalogues = from_others(catalogue, "dp", dps)[1:]
     chosen, limits, wanted, events, w_uvqk = pl.pallas_call(
         functools.partial(pick_kernel, (items_axis, dps)),
         out_shape=(
@@ -237,34 +251,30 @@
     )(place, *(in_hbm(x) for x in (packing, lengths, positions, logged, events, w_uvqk)))
     all_chosen = from_others(chosen, "item", items_axis)
 
-    gated, w_out, catalogue = pl.pallas_call(
+    gated, w_out = pl.pallas_call(
         attend_kernel,
         out_shape=(
             jax.ShapeDtypeStruct((receivers, imps, local_width), jnp.bfloat16),
             jax.ShapeDtypeStruct(w_out.shape, w_out.dtype),
-            jax.ShapeDtypeStruct(catalogue.shape, catalogue.dtype),
-        ),
-        in_specs=[vmem] * 4 + [hbm] * 2,
-        out_specs=(vmem,) * 3,
-        scratch_shapes=[pltpu.SemaphoreType.DMA((2,))],
+        ),
+        in_specs=[vmem] * 4 + [hbm],
+        out_specs=(vmem,) * 2,
+        scratch_shapes=[pltpu.SemaphoreType.DMA],
         compiler_params=params,
         cost_estimate=pl.CostEstimate(flops=0, bytes_accessed=0, transcendentals=0),
         name="attend",
-    )(limits, events, chosen, w_uvqk, in_hbm(w_out), in_hbm(catalogue))
-
-    def exchange(gated, w_out, catalogue):
+    )(limits, events, chosen, w_uvqk, in_hbm(w_out))
+
+    def exchange(gated, w_out):
         return (
             lax.all_to_all(gated, COLUMN, split_axis=0, concat_axis=0, tiled=True),
             from_others(w_out, "tensor", tensors)[1:],
-            from_others(catalogue, "dp", dps)[1:],
         )
 
-    def keep(gated, w_out, catalogue):
-        return gated, [w_out] * (tensors - 1), [catalogue] * (dps - 1)
-
-    all_gated, other_w_out, other_catalogues = lax.cond(
-        lengths[0] > 0, exchange, keep, gated, w_out, catalogue
-    )
+    def keep(gated, w_out):
+        return gated, [w_out] * (tensors - 1)
+
+    all_gated, other_w_out = lax.cond(lengths[0] > 0, exchange, keep, gated, w_out)
 
     state, sums = pl.pallas_call(
         functools.partial(score_kernel, (items_axis, dps, tensors)),
@@ -272,12 +282,15 @@
             jax.ShapeDtypeStruct((imps, width // tensors), jnp.bfloat16),
             jax.ShapeDtypeStruct((receivers, 1, 2 * imps), jnp.float32),
         ),
-        in_specs=[smem] + [vmem] * (3 + items_axis + tensors) + [hbm] * (dps - 1),
-        out_specs=(vmem, vmem),
+        in_specs=[smem] + [vmem] * (3 + items_axis) + [hbm] * tensors + [vmem] * (dps - 1),
+        out_specs=(hbm, vmem),
         scratch_shapes=[
             pltpu.VMEM((items_axis * imps, width), jnp.bfloat16),
-            pltpu.VMEM((dps - 1, items, width), jnp.bfloat16),
-            pltpu.SemaphoreType.DMA((dps - 1,)),
+            pltpu.VMEM((max(tensors - 1, 1), local_width, width), jnp.bfloat16),
+            pltpu.VMEM((items, width), jnp.bfloat16),
+            pltpu.SemaphoreType.DMA((max(tensors - 1, 1),)),
+            pltpu.SemaphoreType.DMA((items // min(256, items),)),
+            pltpu.SemaphoreType.DMA,
         ],
         compiler_params=params,
         cost_estimate=pl.CostEstimate(
@@ -292,9 +305,8 @@
         all_gated,
         *all_chosen,
         w_out,
-        *other_w_out,
-        catalogue,
-        *(in_hbm(x) for x in other_catalogues),
+        *(in_hbm(x) for x in (*other_w_out, catalogue)),
+        *other_catalogues,
     )
     sums = lax.all_to_all(sums, COLUMN, split_axis=0, concat_axis=0, tiled=True)
     sums = jnp.sum(sums, axis=(0, 1))

time: 39.4 us -> 41.4 us (1.051)
  blocking collectives: 21.8 us -> 23.1 us
  Pallas kernels: 8.5 us -> 9.22 us
    all_to_all x1, blocking collectives: 10.4 us -> 11.8 us  [local(): sums = lax.all_to_all(sums, COLUMN, split_axis=0, concat_axis=0, tiled=True)]
    pallas_call x1, Pallas kernels: 2.34 us -> 3.18 us  [local(): pl.pallas_call(functools.partial(pick_kernel, (items_axis, dps)), out_sha...]
    pallas_call x1, Pallas kernels: 1.72 us -> 1.11 us  [local(): pl.pallas_call(attend_kernel, out_shape=(jax.ShapeDtypeStruct((receivers,...]
    pallas_call x1, Pallas kernels: 4.44 us -> 4.94 us  [local(): pl.pallas_call(functools.partial(score_kernel, (items_axis, dps, tensors)...]
  transfers between devices with their start and end apart: 5 -> 5, of which waited for: 0 -> 0; matrix products, arithmetic and copies ran while one was open for 0% -> 0% of each run, Pallas kernels for 4% -> 10%
where the time goes in v6:
time: 41.4 us; the launch traced here: 41.1 us
  blocking collectives  23.1 us (56%)
  Pallas kernels  9.22 us (22%)
  starting transfers between devices  7.32 us (18%)
  between operations  0.73 us (2%)
  other arithmetic  0.69 us (2%)
    all_to_all x1, blocking collectives, local(): sums = lax.all_to_all(sums, COLUMN, split_axis=0, concat_axis=0, tiled=True)  11.8 us
    all_to_all x1, blocking collectives, exchange(): lax.all_to_all(gated, COLUMN, split_axis=0, concat_axis=0, tiled=True)  11.3 us
    ppermute x5, starting transfers between devices, from_others(): lax.ppermute(x, axes, [(i, i ^ r) for i in range(count)])  7.32 us
    pallas_call x1, Pallas kernels, local(): pl.pallas_call(functools.partial(score_kernel, (items_axis, dps, tensors)...  4.94 us
    pallas_call x1, Pallas kernels, local(): pl.pallas_call(functools.partial(pick_kernel, (items_axis, dps)), out_sha...  3.18 us
    pallas_call x1, Pallas kernels, local(): pl.pallas_call(attend_kernel, out_shape=(jax.ShapeDtypeStruct((receivers,...  1.11 us
  transfers between devices with their start and end apart: 5, of which 0 were waited for; matrix products, arithmetic and copies ran while one was open for 0% of the time, Pallas kernels for 10%

profile of v6, /device:TPU:0, one launch (start us, length us, event | category | flops | bytes accessed | tf_op | source)
XLA Modules:
  0.0 41.1 jit_solution(12126677693821980047)
XLA Ops:
  0.6 0.0 copy-start
  0.6 0.5 %collective-permute-start.4 = (bf16[1024,1024]{1,0:T(8,128)(2,1)}, bf16[1024,1024]{1,0:T(8,128)(2,1)S(1)}, u32[]{:S(2)}, u32[]{:S(2)}) collective-permute-start(bf16[1024,1024]{1,0:T(8,128)(2,1)} %refs_6_.1), channel_id=1, source_target_pairs={{0,2},{2,0},{1,3},{3,1},{4,6},{6,4},{5,7},{7,5},{8,10},{10,8},{9,1... | collective-permute-start | bytes 6291464 | tf_op jit(solution)/shard_map/ppermute | solution.py:211
  1.2 0.1 pad_add_fusion.place
  1.2 3.2 %pick.1 = (bf16[64,1024]{1,0:T(8,128)(2,1)S(1)}, s32[64,128]{1,0:T(8,128)S(1)}, s32[1,256]{1,0:T(1,128)S(1)}, bf16[768,1024]{1,0:T(8,128)(2,1)S(1)}, bf16[1024,512]{1,0:T(8,128)(2,1)S(1)}) custom-call(s32[3]{0:T(128)S(1)} %pad_add_fusion.place, s32[8]{0:T(128)} %packing.1, s32[8]{0:T(128)} %lengths.1, s32[8,64]{1,0:T(8,128)} %positions.1, s32[8,64]{1,0:T(8,128)} %logged.1, ...), custom_call_target="tpu_custom_call" | custom-call | flops 100663296 | bytes 1572864 | tf_op jit(solution)/shard_map/pick/pallas_call | solution.py:228
  4.4 3.7 %collective-permute-start.1 = (bf16[64,1024]{1,0:T(8,128)(2,1)S(1)}, bf16[64,1024]{1,0:T(8,128)(2,1)S(1)}, u32[]{:S(2)}, u32[]{:S(2)}) collective-permute-start(bf16[64,1024]{1,0:T(8,128)(2,1)S(1)} %get-tuple-element.25.chosen.refs_0_), channel_id=1, source_target_pairs={{0,8},{4,12},{8,0},{12,4},{1,9},{5,13},{9,1},{13,5},{2,10},{6,14},... | collective-permute-start | bytes 393224 | tf_op jit(solution)/shard_map/ppermute | solution.py:211
  8.1 1.3 %collective-permute-start.2 = (bf16[64,1024]{1,0:T(8,128)(2,1)S(1)}, bf16[64,1024]{1,0:T(8,128)(2,1)S(1)}, u32[]{:S(2)}, u32[]{:S(2)}) collective-permute-start(bf16[64,1024]{1,0:T(8,128)(2,1)S(1)} %get-tuple-element.25.chosen.refs_0_), channel_id=1, source_target_pairs={{0,12},{4,8},{8,4},{12,0},{1,13},{5,9},{9,5},{13,1},{2,14},{6,10},... | collective-permute-start | bytes 393224 | tf_op jit(solution)/shard_map/ppermute | solution.py:211
  9.4 0.2 collective-permute-start.3
  9.7 0.0 copy-done
  9.7 1.1 %attend.1 = (bf16[8,64,128]{2,1,0:T(8,128)(2,1)S(1)}, bf16[128,1024]{1,0:T(8,128)(2,1)S(1)}) custom-call(s32[64,128]{1,0:T(8,128)S(1)} %get-tuple-element.23.limits, bf16[768,1024]{1,0:T(8,128)(2,1)S(1)} %get-tuple-element.24.events, bf16[64,1024]{1,0:T(8,128)(2,1)S(1)} %get-tuple-element.25.chosen.refs_0_, bf16[1024,512]{1,0:T(8,128)(2,1)S(1)} %get-tuple-element.26.w_uvqk, ...), custom_call_target="tpu_custom_call" | custom-call | tf_op jit(solution)/shard_map/attend/pallas_call | solution.py:254
  10.8 12.9 %conditional.1 = (bf16[8,64,128]{2,1,0:T(8,128)(2,1)S(1)}, bf16[128,1024]{1,0:T(8,128)(2,1)}) conditional(s32[]{:T(128)} %bitcast.3, (bf16[8,64,128]{2,1,0:T(8,128)(2,1)S(1)}, bf16[128,1024]{1,0:T(8,128)(2,1)S(1)}) %attend.1, (bf16[8,64,128]{2,1,0:T(8,128)(2,1)S(1)}, bf16[128,1024]{1,0:T(8,128)(2,1)S(1)}) %attend.1), branch_computations={%region_0.0_spmd, %region_1.0_spmd} | conditional | bytes 1572920 | solution.py:277
  10.9 1.5 %collective-permute-start = (bf16[128,1024]{1,0:T(8,128)(2,1)S(1)}, bf16[128,1024]{1,0:T(8,128)(2,1)}, u32[]{:S(2)}, u32[]{:S(2)}) collective-permute-start(bf16[128,1024]{1,0:T(8,128)(2,1)S(1)} %get-tuple-element.9), channel_id=1, source_target_pairs={{0,1},{1,0},{2,3},{3,2},{4,5},{5,4},{6,7},{7,6},{8,9},{9,8},{10,11... | collective-permute-start | bytes 786440 | tf_op jit(solution)/shard_map/cond/branch_1_fun/ppermute | solution.py:211
  12.4 11.3 %all_to_all.9 = bf16[8,64,128]{2,1,0:T(8,128)(2,1)S(1)} all-to-all(bf16[8,64,128]{2,1,0:T(8,128)(2,1)S(1)} %copy.14), channel_id=1, replica_groups=mesh['groups'=2,'item'=4,'dp'=2,'tensor'=2] {'item','tensor'}, dimensions={0} | all-to-all | bytes 262144 | tf_op jit(solution)/shard_map/cond/branch_1_fun/all_to_all | solution.py:270
  23.8 0.0 collective-permute-done
  23.8 0.0 collective-permute-done.1.refs_1_
  23.8 0.0 collective-permute-done.2.refs_2_
  23.8 0.0 collective-permute-done.3.refs_3_
  23.8 0.0 collective-permute-done.4.refs_7_
  23.8 4.9 %score.1 = (bf16[64,512]{1,0:T(8,128)(2,1)}, f32[8,1,128]{2,1,0:T(1,128)S(1)}) custom-call(s32[3]{0:T(128)S(1)} %pad_add_fusion.place, s32[1,256]{1,0:T(1,128)S(1)} %get-tuple-element.22.wanted, bf16[8,64,128]{2,1,0:T(8,128)(2,1)S(1)} %get-tuple-element.27.gated, bf16[64,1024]{1,0:T(8,128)(2,1)S(1)} %get-tuple-element.25.chosen.refs_0_, ...), custom_call_target="tpu_custom_call" | custom-call | flops 1207959552 | bytes 4194304 | tf_op jit(solution)/shard_map/score/pallas_call | solution.py:279
  28.7 11.8 %all_to_all.10 = f32[8,1,128]{2,1,0:T(1,128)S(1)} all-to-all(f32[8,1,128]{2,1,0:T(1,128)S(1)} %get-tuple-element.31), channel_id=1, replica_groups=mesh['groups'=2,'item'=4,'dp'=2,'tensor'=2] {'item','tensor'}, dimensions={0} | all-to-all | bytes 8192 | tf_op jit(solution)/shard_map/all_to_all | solution.py:311
  40.5 0.6 %log_subtract_fusion = f32[64]{0:T(128)} fusion(f32[128]{0:T(128)S(1)} %reduce_sum.9), kind=kLoop, calls=%fused_computation.1 | loop fusion | flops 64 | bytes 768 | tf_op jit(solution)/shard_map/sub | solution.py:313
  (2 shorter events, 0.0 us)
Async XLA Ops:
  0.6 9.0 %copy-start = (s32[8]{0:T(128)S(1)}, s32[8]{0:T(128)}, u32[]{:S(2)}) copy-start(s32[8]{0:T(128)} %lengths.1) | copy-start | bytes 100
  0.6 23.2 %collective-permute-start.4 = (bf16[1024,1024]{1,0:T(8,128)(2,1)}, bf16[1024,1024]{1,0:T(8,128)(2,1)S(1)}, u32[]{:S(2)}, u32[]{:S(2)}) collective-permute-start(bf16[1024,1024]{1,0:T(8,128)(2,1)} %refs_6_.1), channel_id=1, source_target_pairs={{0,2},{2,0},{1,3},{3,1},{4,6},{6,4},{5,7},{7,5},{8,10},{10,8},{9,1... | collective-permute-start | bytes 6291464 | tf_op jit(solution)/shard_map/ppermute | solution.py:211
  4.4 19.4 %collective-permute-start.1 = (bf16[64,1024]{1,0:T(8,128)(2,1)S(1)}, bf16[64,1024]{1,0:T(8,128)(2,1)S(1)}, u32[]{:S(2)}, u32[]{:S(2)}) collective-permute-start(bf16[64,1024]{1,0:T(8,128)(2,1)S(1)} %get-tuple-element.25.chosen.refs_0_), channel_id=1, source_target_pairs={{0,8},{4,12},{8,0},{12,4},{1,9},{5,13},{9,1},{13,5},{2,10},{6,14},... | collective-permute-start | bytes 393224 | tf_op jit(solution)/shard_map/ppermute | solution.py:211
  8.1 15.7 %collective-permute-start.2 = (bf16[64,1024]{1,0:T(8,128)(2,1)S(1)}, bf16[64,1024]{1,0:T(8,128)(2,1)S(1)}, u32[]{:S(2)}, u32[]{:S(2)}) collective-permute-start(bf16[64,1024]{1,0:T(8,128)(2,1)S(1)} %get-tuple-element.25.chosen.refs_0_), channel_id=1, source_target_pairs={{0,12},{4,8},{8,4},{12,0},{1,13},{5,9},{9,5},{13,1},{2,14},{6,10},... | collective-permute-start | bytes 393224 | tf_op jit(solution)/shard_map/ppermute | solution.py:211
  9.4 14.3 %collective-permute-start.3 = (bf16[64,1024]{1,0:T(8,128)(2,1)S(1)}, bf16[64,1024]{1,0:T(8,128)(2,1)S(1)}, u32[]{:S(2)}, u32[]{:S(2)}) collective-permute-start(bf16[64,1024]{1,0:T(8,128)(2,1)S(1)} %get-tuple-element.25.chosen.refs_0_), channel_id=1, source_target_pairs={{0,4},{4,0},{8,12},{12,8},{1,5},{5,1},{9,13},{13,9},{2,6},{6,2},{1... | collective-permute-start | bytes 393224 | tf_op jit(solution)/shard_map/ppermute | solution.py:211
  10.9 12.9 %collective-permute-start = (bf16[128,1024]{1,0:T(8,128)(2,1)S(1)}, bf16[128,1024]{1,0:T(8,128)(2,1)}, u32[]{:S(2)}, u32[]{:S(2)}) collective-permute-start(bf16[128,1024]{1,0:T(8,128)(2,1)S(1)} %get-tuple-element.9), channel_id=1, source_target_pairs={{0,1},{1,0},{2,3},{3,2},{4,5},{5,4},{6,7},{7,6},{8,9},{9,8},{10,11... | collective-permute-start | bytes 786440 | tf_op jit(solution)/shard_map/cond/branch_1_fun/ppermute | solution.py:211

commit v7 on v6

--- a/solution.py
+++ b/solution.py
@@ -12,12 +12,12 @@
 SLOTS = ("item", "dp")
 COLUMN = ("item", "tensor")
 NT = (((1,), (1,)), ((), ()))
-VMEM_LIMIT = 32 * 1024 * 1024
+MIB = 1024 * 1024
 EVENT_PARTS = 3
 
 
 def rounds(count):
-    return [0] + sorted(range(1, count), key=lambda r: -(r & -2))
+    return [0] + sorted(range(1, count), key=lambda r: (r & 3 == 3, -(r & -2)))
 
 
 def spec(space):
@@ -62,7 +62,7 @@
             + [(w_uvqk, w_uvqk_v)]
         )
     ]
-    for copy in copies[4:-1] + copies[:4]:
+    for copy in copies:
         copy.start()
     for copy in copies[:4]:
         copy.wait()
@@ -80,8 +80,6 @@
     total = jnp.zeros((imps, events.shape[1]), jnp.float32)
     for k in range(EVENT_PARTS):
         copies[4 + k].wait()
-        if k == 0:
-            copies[-1].start()
         lanes = k * part_rows + lax.broadcasted_iota(jnp.int32, (imps, part_rows), 1)
         one_hot = jnp.where(lanes == spots, 1.0, 0.0).astype(jnp.bfloat16)
         total += jnp.dot(
@@ -130,35 +128,27 @@
     chosen, refs = refs[:items_axis], refs[items_axis:]
     w_out, refs = refs[:tensors], refs[tensors:]
     catalogue, refs = list(refs[:dps]), refs[dps:]
-    state_hbm, sums, hidden, w_out_v, catalogue_v, w_sems, sems, state_sem = refs
+    state_hbm, sums, hidden, others, sems, state_sem = refs
+    fetches = [
+        pltpu.make_async_copy(catalogue[d], others.at[d - 1], sems.at[d - 1]) for d in range(1, dps)
+    ]
+    for fetch in fetches:
+        fetch.start()
+    catalogue[1:] = [others.at[d - 1] for d in range(1, dps)]
     item, dp, tensor = place[0], place[1], place[2]
     imps = chosen[0].shape[0]
-    items = catalogue_v.shape[0]
+    items = catalogue[0].shape[0]
     step_rows = min(256, items_axis * imps)
     step_items = min(256, items)
     steps = range(0, items, step_items)
-    w_fetches = [
-        pltpu.make_async_copy(w_out[t], w_out_v.at[t - 1], w_sems.at[t - 1])
-        for t in range(1, tensors)
-    ]
-    parts = [pl.ds(first, step_items) for first in steps]
-    fetches = [
-        pltpu.make_async_copy(catalogue[0].at[part], catalogue_v.at[part], sems.at[n])
-        for n, part in enumerate(parts)
-    ]
-    for fetch in w_fetches + fetches:
-        fetch.start()
-    catalogue[0] = catalogue_v
-
     slot_rounds, tensor_rounds = rounds(items_axis), rounds(tensors)
     totals = [c[...].astype(jnp.float32) for c in chosen]
     for t in range(tensors):
-        if t > 0:
-            w_fetches[t - 1].wait()
-        w_part = w_out[0][...] if t == 0 else w_out_v[t - 1]
         for k in range(items_axis):
             sender = (item ^ slot_rounds[k]) * tensors + (tensor ^ tensor_rounds[t])
-            totals[k] += jnp.dot(gated[sender], w_part, preferred_element_type=jnp.float32)
+            totals[k] += jnp.dot(
+                gated[sender], w_out[t][...], preferred_element_type=jnp.float32
+            )
     for k in range(items_axis):
         hidden[k * imps : (k + 1) * imps, :] = totals[k].astype(jnp.bfloat16)
     share = state_hbm.shape[1]
@@ -173,11 +163,11 @@
     totals = {row: jnp.zeros((8, step_rows), jnp.float32) for row in blocks}
     targets = dict(totals)
     for d in range(dps):
+        if d > 0:
+            fetches[d - 1].wait()
         item_base = ((item * dps + (dp ^ rounds(dps)[d])) * tensors + tensor) * items
         ids = {row: wanted[0:1, row : row + step_rows] - item_base for row in blocks}
         for first in steps:
-            if d == 0:
-                fetches[first // step_items].wait()
             for row in blocks:
                 logits = lax.dot_general(
                     catalogue[d][first : first + step_items, :],
@@ -206,10 +196,19 @@
     return pltpu.with_memory_space_constraint(x, pltpu.HBM)
 
 
+def send(x, axes, count, r):
+    return lax.ppermute(x, axes, [(i, i ^ r) for i in range(count)])
+
+
 def from_others(x, axes, count):
-    return [x] + [
-        lax.ppermute(x, axes, [(i, i ^ r) for i in range(count)]) for r in rounds(count)[1:]
-    ]
+    pieces = {}
+    for r in rounds(count)[1:]:
+        if r & 3 == 3:
+            held, pieces[r - 2] = lax.optimization_barrier((pieces[r - 1], pieces[r - 2]))
+            pieces[r] = send(held, axes, count, 1)
+        else:
+            pieces[r] = send(x, axes, count, r)
+    return list(pieces.values())
 
 
 def local(events, lengths, packing, positions, logged, w_uvqk, w_out, catalogue):
@@ -220,11 +219,12 @@
     local_width = w_out.shape[0]
     items_axis, dps, tensors = (lax.axis_size(a) for a in ("item", "dp", "tensor"))
     receivers = items_axis * tensors
-    params = pltpu.CompilerParams(vmem_limit_bytes=VMEM_LIMIT)
+    params = pltpu.CompilerParams(vmem_limit_bytes=(12 + 2 * items_axis) * MIB)
     place = jnp.stack([lax.axis_index(a) for a in ("item", "dp", "tensor")]).astype(jnp.int32)
     smem, vmem, hbm = spec(pltpu.SMEM), spec(pltpu.VMEM), spec(pltpu.HBM)
 
-    other_catalogues = from_others(catalogue, "dp", dps)[1:]
+    other_catalogues = from_others(catalogue, "dp", dps)
+    other_w_out = from_others(w_out, "tensor", tensors)
     chosen, limits, wanted, events, w_uvqk = pl.pallas_call(
         functools.partial(pick_kernel, (items_axis, dps)),
         out_shape=(
@@ -249,9 +249,9 @@
         ),
         name="pick",
     )(place, *(in_hbm(x) for x in (packing, lengths, positions, logged, events, w_uvqk)))
-    all_chosen = from_others(chosen, "item", items_axis)
-
-    gated, w_out = pl.pallas_call(
+    other_chosen = from_others(chosen, "item", items_axis)
+
+    gated, own_w_out = pl.pallas_call(
         attend_kernel,
         out_shape=(
             jax.ShapeDtypeStruct((receivers, imps, local_width), jnp.bfloat16),
@@ -265,16 +265,7 @@
         name="attend",
     )(limits, events, chosen, w_uvqk, in_hbm(w_out))
 
-    def exchange(gated, w_out):
-        return (
-            lax.all_to_all(gated, COLUMN, split_axis=0, concat_axis=0, tiled=True),
-            from_others(w_out, "tensor", tensors)[1:],
-        )
-
-    def keep(gated, w_out):
-        return gated, [w_out] * (tensors - 1)
-
-    all_gated, other_w_out = lax.cond(lengths[0] > 0, exchange, keep, gated, w_out)
+    all_gated = lax.all_to_all(gated, COLUMN, split_axis=0, concat_axis=0, tiled=True)
 
     state, sums = pl.pallas_call(
         functools.partial(score_kernel, (items_axis, dps, tensors)),
@@ -282,14 +273,12 @@
             jax.ShapeDtypeStruct((imps, width // tensors), jnp.bfloat16),
             jax.ShapeDtypeStruct((receivers, 1, 2 * imps), jnp.float32),
         ),
-        in_specs=[smem] + [vmem] * (3 + items_axis) + [hbm] * tensors + [vmem] * (dps - 1),
+        in_specs=[smem] + [vmem] * (3 + items_axis + tensors) + [hbm] * (dps - 1),
         out_specs=(hbm, vmem),
         scratch_shapes=[
             pltpu.VMEM((items_axis * imps, width), jnp.bfloat16),
-            pltpu.VMEM((max(tensors - 1, 1), local_width, width), jnp.bfloat16),
-            pltpu.VMEM((items, width), jnp.bfloat16),
-            pltpu.SemaphoreType.DMA((max(tensors - 1, 1),)),
-            pltpu.SemaphoreType.DMA((items // min(256, items),)),
+            pltpu.VMEM((dps - 1, items, width), jnp.bfloat16),
+            pltpu.SemaphoreType.DMA((dps - 1,)),
             pltpu.SemaphoreType.DMA,
         ],
         compiler_params=params,
@@ -303,10 +292,12 @@
         place,
         wanted,
         all_gated,
-        *all_chosen,
-        w_out,
-        *(in_hbm(x) for x in (*other_w_out, catalogue)),
-        *other_catalogues,
+        chosen,
+        *other_chosen,
+        own_w_out,
+        *other_w_out,
+        catalogue,
+        *(in_hbm(x) for x in other_catalogues),
     )
     sums = lax.all_to_all(sums, COLUMN, split_axis=0, concat_axis=0, tiled=True)
     sums = jnp.sum(sums, axis=(0, 1))

time: 41.4 us -> 38.3 us (0.925)
  blocking collectives: 23.1 us -> 10.1 us
  waiting for transfers between devices: 0.01 us -> 6.21 us
  starting transfers between devices: 7.32 us -> 12.6 us
  Pallas kernels: 9.22 us -> 7.68 us
    all_to_all x1 -> x0, blocking collectives: 11.3 us -> none  [exchange(): lax.all_to_all(gated, COLUMN, split_axis=0, concat_axis=0, tiled=True)]
    all_to_all x0 -> x1, waiting for transfers between devices: none -> 6.2 us  [local(): lax.all_to_all(gated, COLUMN, split_axis=0, concat_axis=0, tiled=True)]
    all_to_all x0 -> x1, starting transfers between devices: none -> 3.38 us  [local(): lax.all_to_all(gated, COLUMN, split_axis=0, concat_axis=0, tiled=True)]
    ppermute x5, starting transfers between devices: 7.32 us -> 9.24 us  [send(): return lax.ppermute(x, axes, [(i, i ^ r) for i in range(count)])]
    all_to_all x1, blocking collectives: 11.8 us -> 10.1 us  [local(): sums = lax.all_to_all(sums, COLUMN, split_axis=0, concat_axis=0, tiled=True)]
    pallas_call x1, Pallas kernels: 4.94 us -> 3.54 us  [local(): pl.pallas_call(functools.partial(score_kernel, (items_axis, dps, tensors)...]
    pallas_call x1, Pallas kernels: 3.18 us -> 2.34 us  [local(): pl.pallas_call(functools.partial(pick_kernel, (items_axis, dps)), out_sha...]
    pallas_call x1, Pallas kernels: 1.11 us -> 1.8 us  [local(): pl.pallas_call(attend_kernel, out_shape=(jax.ShapeDtypeStruct((receivers,...]
  transfers between devices with their start and end apart: 5 -> 6, of which waited for: 0 -> 1; matrix products, arithmetic and copies ran while one was open for 0% -> 0% of each run, Pallas kernels for 10% -> 11%
where the time goes in v7:
time: 38.3 us; the launch traced here: 38 us
  starting transfers between devices  12.6 us (33%)
  blocking collectives  10.1 us (26%)
  Pallas kernels  7.68 us (20%)
  waiting for transfers between devices  6.21 us (16%)
  between operations  0.71 us (2%)
  other arithmetic  0.69 us (2%)
    all_to_all x1, blocking collectives, local(): sums = lax.all_to_all(sums, COLUMN, split_axis=0, concat_axis=0, tiled=True)  10.1 us
    ppermute x5, starting transfers between devices, send(): return lax.ppermute(x, axes, [(i, i ^ r) for i in range(count)])  9.24 us
    all_to_all x1, waiting for transfers between devices, local(): lax.all_to_all(gated, COLUMN, split_axis=0, concat_axis=0, tiled=True)  6.2 us
    pallas_call x1, Pallas kernels, local(): pl.pallas_call(functools.partial(score_kernel, (items_axis, dps, tensors)...  3.54 us
    all_to_all x1, starting transfers between devices, local(): lax.all_to_all(gated, COLUMN, split_axis=0, concat_axis=0, tiled=True)  3.38 us
    pallas_call x1, Pallas kernels, local(): pl.pallas_call(functools.partial(pick_kernel, (items_axis, dps)), out_sha...  2.34 us
    pallas_call x1, Pallas kernels, local(): pl.pallas_call(attend_kernel, out_shape=(jax.ShapeDtypeStruct((receivers,...  1.8 us
  transfers between devices with their start and end apart: 6, of which 1 were waited for; matrix products, arithmetic and copies ran while one was open for 0% of the time, Pallas kernels for 11%

profile of v7, /device:TPU:0, one launch (start us, length us, event | category | flops | bytes accessed | tf_op | source)
XLA Modules:
  0.0 38.0 jit_solution(1638908404612157853)
XLA Ops:
  0.6 0.0 copy-start.1
  0.6 0.5 %collective-permute-start.4 = (bf16[1024,1024]{1,0:T(8,128)(2,1)}, bf16[1024,1024]{1,0:T(8,128)(2,1)}, u32[]{:S(2)}, u32[]{:S(2)}) collective-permute-start(bf16[1024,1024]{1,0:T(8,128)(2,1)} %refs_6_.1), channel_id=1, source_target_pairs={{0,2},{2,0},{1,3},{3,1},{4,6},{6,4},{5,7},{7,5},{8,10},{10,8},{9,1... | collective-permute-start | bytes 6291464 | tf_op jit(solution)/shard_map/ppermute | solution.py:200
  1.2 0.1 pad_add_fusion.place
  1.2 2.3 %pick.1 = (bf16[64,1024]{1,0:T(8,128)(2,1)S(1)}, s32[64,128]{1,0:T(8,128)S(1)}, s32[1,256]{1,0:T(1,128)S(1)}, bf16[768,1024]{1,0:T(8,128)(2,1)S(1)}, bf16[1024,512]{1,0:T(8,128)(2,1)S(1)}) custom-call(s32[3]{0:T(128)S(1)} %pad_add_fusion.place, s32[8]{0:T(128)} %packing.1, s32[8]{0:T(128)} %lengths.1, s32[8,64]{1,0:T(8,128)} %positions.1, s32[8,64]{1,0:T(8,128)} %logged.1, ...), custom_call_target="tpu_custom_call" | custom-call | flops 100663296 | bytes 1572864 | tf_op jit(solution)/shard_map/pick/pallas_call | solution.py:228
  3.6 0.0 copy-start
  3.6 3.7 %collective-permute-start = (bf16[64,1024]{1,0:T(8,128)(2,1)S(1)}, bf16[64,1024]{1,0:T(8,128)(2,1)S(1)}, u32[]{:S(2)}, u32[]{:S(2)}) collective-permute-start(bf16[64,1024]{1,0:T(8,128)(2,1)S(1)} %get-tuple-element.16.chosen.refs_0_), channel_id=1, source_target_pairs={{0,8},{4,12},{8,0},{12,4},{1,9},{5,13},{9,1},{13,5},{2,10},{6,14},... | collective-permute-start | bytes 393224 | tf_op jit(solution)/shard_map/ppermute | solution.py:200
  7.3 1.6 %collective-permute-start.1 = (bf16[64,1024]{1,0:T(8,128)(2,1)S(1)}, bf16[64,1024]{1,0:T(8,128)(2,1)S(1)}, u32[]{:S(2)}, u32[]{:S(2)}) collective-permute-start(bf16[64,1024]{1,0:T(8,128)(2,1)S(1)} %get-tuple-element.16.chosen.refs_0_), channel_id=1, source_target_pairs={{0,4},{4,0},{8,12},{12,8},{1,5},{5,1},{9,13},{13,9},{2,6},{6,2},{1... | collective-permute-start | bytes 393224 | tf_op jit(solution)/shard_map/ppermute | solution.py:200
  8.8 0.0 copy-done.1
  8.8 1.5 %collective-permute-start.3 = (bf16[128,1024]{1,0:T(8,128)(2,1)S(1)}, bf16[128,1024]{1,0:T(8,128)(2,1)S(1)}, u32[]{:S(2)}, u32[]{:S(2)}) collective-permute-start(bf16[128,1024]{1,0:T(8,128)(2,1)S(1)} %copy-done.1), channel_id=1, source_target_pairs={{0,1},{1,0},{2,3},{3,2},{4,5},{5,4},{6,7},{7,6},{8,9},{9,8},{10,11... | collective-permute-start | bytes 786440 | tf_op jit(solution)/shard_map/ppermute | solution.py:200
  10.3 1.8 %attend.1 = (bf16[8,64,128]{2,1,0:T(8,128)(2,1)}, bf16[128,1024]{1,0:T(8,128)(2,1)S(1)}) custom-call(s32[64,128]{1,0:T(8,128)S(1)} %get-tuple-element.14.limits, bf16[768,1024]{1,0:T(8,128)(2,1)S(1)} %get-tuple-element.15.events, bf16[64,1024]{1,0:T(8,128)(2,1)S(1)} %get-tuple-element.16.chosen.refs_0_, bf16[1024,512]{1,0:T(8,128)(2,1)S(1)} %get-tuple-element.17.w_uvqk, ...), custom_call_target="tpu_custom_call" | custom-call | tf_op jit(solution)/shard_map/attend/pallas_call | solution.py:254
  12.1 3.4 %all-to-all-start = ((bf16[8,64,128]{2,1,0:T(8,128)(2,1)}), bf16[8,64,128]{2,1,0:T(8,128)(2,1)S(1)}, u32[]{:S(2)}, u32[]{:S(2)}) async-start(bf16[8,64,128]{2,1,0:T(8,128)(2,1)} %get-tuple-element.18), calls=%async_computation | async-start | bytes 262144 | tf_op jit(solution)/shard_map/all_to_all | solution.py:268
  15.5 0.0 collective-permute-done.refs_1_
  15.5 0.0 collective-permute-done.1.refs_2_
  15.6 2.0 %collective-permute-start.2 = (bf16[64,1024]{1,0:T(8,128)(2,1)S(1)}, bf16[64,1024]{1,0:T(8,128)(2,1)S(1)}, u32[]{:S(2)}, u32[]{:S(2)}) collective-permute-start(bf16[64,1024]{1,0:T(8,128)(2,1)S(1)} %collective-permute-done.refs_1_), channel_id=1, source_target_pairs={{0,4},{4,0},{8,12},{12,8},{1,5},{5,1},{9,13},{13,9},{2,6},{6,2},{1... | collective-permute-start | bytes 393224 | tf_op jit(solution)/shard_map/ppermute | solution.py:200
  17.5 6.2 %all-to-all-done.gated = bf16[8,64,128]{2,1,0:T(8,128)(2,1)S(1)} async-done(((bf16[8,64,128]{2,1,0:T(8,128)(2,1)}), bf16[8,64,128]{2,1,0:T(8,128)(2,1)S(1)}, u32[]{:S(2)}, u32[]{:S(2)}) %all-to-all-start) | async-done | bytes 131104 | tf_op jit(solution)/shard_map/all_to_all | solution.py:268
  23.7 0.0 collective-permute-done.2.refs_3_
  23.7 0.0 collective-permute-done.3.refs_5_
  23.7 0.0 collective-permute-done.4.refs_7_
  23.7 0.0 copy-done
  23.8 3.5 %score.1 = (bf16[64,512]{1,0:T(8,128)(2,1)}, f32[8,1,128]{2,1,0:T(1,128)S(1)}) custom-call(s32[3]{0:T(128)S(1)} %pad_add_fusion.place, s32[1,256]{1,0:T(1,128)S(1)} %get-tuple-element.13.wanted, bf16[8,64,128]{2,1,0:T(8,128)(2,1)S(1)} %all-to-all-done.gated, bf16[64,1024]{1,0:T(8,128)(2,1)S(1)} %get-tuple-element.16.chosen.refs_0_, ...), custom_call_target="tpu_custom_call" | custom-call | flops 1207959552 | bytes 4194304 | tf_op jit(solution)/shard_map/score/pallas_call | solution.py:270
  27.3 10.1 %all_to_all.10 = f32[8,1,128]{2,1,0:T(1,128)S(1)} all-to-all(f32[8,1,128]{2,1,0:T(1,128)S(1)} %get-tuple-element.23), channel_id=1, replica_groups=mesh['groups'=2,'item'=4,'dp'=2,'tensor'=2] {'item','tensor'}, dimensions={0} | all-to-all | bytes 8192 | tf_op jit(solution)/shard_map/all_to_all | solution.py:302
  37.4 0.6 %log_subtract_fusion = f32[64]{0:T(128)} fusion(f32[128]{0:T(128)S(1)} %reduce_sum.9), kind=kLoop, calls=%fused_computation.1 | loop fusion | flops 64 | bytes 768 | tf_op jit(solution)/shard_map/sub | solution.py:304
  (1 shorter events, 0.0 us)
Async XLA Ops:
  0.6 8.2 %copy-start.1 = (bf16[128,1024]{1,0:T(8,128)(2,1)S(1)}, bf16[128,1024]{1,0:T(8,128)(2,1)}, u32[]{:S(2)}) copy-start(bf16[128,1024]{1,0:T(8,128)(2,1)} %w_out.1) | copy-start | bytes 786436
  0.6 23.1 %collective-permute-start.4 = (bf16[1024,1024]{1,0:T(8,128)(2,1)}, bf16[1024,1024]{1,0:T(8,128)(2,1)}, u32[]{:S(2)}, u32[]{:S(2)}) collective-permute-start(bf16[1024,1024]{1,0:T(8,128)(2,1)} %refs_6_.1), channel_id=1, source_target_pairs={{0,2},{2,0},{1,3},{3,1},{4,6},{6,4},{5,7},{7,5},{8,10},{10,8},{9,1... | collective-permute-start | bytes 6291464 | tf_op jit(solution)/shard_map/ppermute | solution.py:200
  3.6 20.2 %copy-start = (bf16[1024,1024]{1,0:T(8,128)(2,1)S(1)}, bf16[1024,1024]{1,0:T(8,128)(2,1)}, u32[]{:S(2)}) copy-start(bf16[1024,1024]{1,0:T(8,128)(2,1)} %refs_6_.1) | copy-start | bytes 6291460
  3.6 11.9 %collective-permute-start = (bf16[64,1024]{1,0:T(8,128)(2,1)S(1)}, bf16[64,1024]{1,0:T(8,128)(2,1)S(1)}, u32[]{:S(2)}, u32[]{:S(2)}) collective-permute-start(bf16[64,1024]{1,0:T(8,128)(2,1)S(1)} %get-tuple-element.16.chosen.refs_0_), channel_id=1, source_target_pairs={{0,8},{4,12},{8,0},{12,4},{1,9},{5,13},{9,1},{13,5},{2,10},{6,14},... | collective-permute-start | bytes 393224 | tf_op jit(solution)/shard_map/ppermute | solution.py:200
  7.3 8.3 %collective-permute-start.1 = (bf16[64,1024]{1,0:T(8,128)(2,1)S(1)}, bf16[64,1024]{1,0:T(8,128)(2,1)S(1)}, u32[]{:S(2)}, u32[]{:S(2)}) collective-permute-start(bf16[64,1024]{1,0:T(8,128)(2,1)S(1)} %get-tuple-element.16.chosen.refs_0_), channel_id=1, source_target_pairs={{0,4},{4,0},{8,12},{12,8},{1,5},{5,1},{9,13},{13,9},{2,6},{6,2},{1... | collective-permute-start | bytes 393224 | tf_op jit(solution)/shard_map/ppermute | solution.py:200
  8.8 14.9 %collective-permute-start.3 = (bf16[128,1024]{1,0:T(8,128)(2,1)S(1)}, bf16[128,1024]{1,0:T(8,128)(2,1)S(1)}, u32[]{:S(2)}, u32[]{:S(2)}) collective-permute-start(bf16[128,1024]{1,0:T(8,128)(2,1)S(1)} %copy-done.1), channel_id=1, source_target_pairs={{0,1},{1,0},{2,3},{3,2},{4,5},{5,4},{6,7},{7,6},{8,9},{9,8},{10,11... | collective-permute-start | bytes 786440 | tf_op jit(solution)/shard_map/ppermute | solution.py:200
  12.1 11.6 %all-to-all-start = ((bf16[8,64,128]{2,1,0:T(8,128)(2,1)}), bf16[8,64,128]{2,1,0:T(8,128)(2,1)S(1)}, u32[]{:S(2)}, u32[]{:S(2)}) async-start(bf16[8,64,128]{2,1,0:T(8,128)(2,1)} %get-tuple-element.18), calls=%async_computation | async-start | bytes 262144 | tf_op jit(solution)/shard_map/all_to_all | solution.py:268
  15.6 8.2 %collective-permute-start.2 = (bf16[64,1024]{1,0:T(8,128)(2,1)S(1)}, bf16[64,1024]{1,0:T(8,128)(2,1)S(1)}, u32[]{:S(2)}, u32[]{:S(2)}) collective-permute-start(bf16[64,1024]{1,0:T(8,128)(2,1)S(1)} %collective-permute-done.refs_1_), channel_id=1, source_target_pairs={{0,4},{4,0},{8,12},{12,8},{1,5},{5,1},{9,13},{13,9},{2,6},{6,2},{1... | collective-permute-start | bytes 393224 | tf_op jit(solution)/shard_map/ppermute | solution.py:200

commit v8 on v7

--- a/solution.py
+++ b/solution.py
@@ -38,6 +38,7 @@
     wanted,
     events_v,
     w_uvqk_v,
+    done,
     packing_s,
     lengths_s,
     positions_v,
@@ -90,22 +91,20 @@
     chosen[...] = total.astype(jnp.bfloat16)
     copies[-1].wait()
 
-
-def attend_kernel(
-    limits, events, chosen, w_uvqk, w_out, gated, w_out_v, sem
-):
-    fetch = pltpu.make_async_copy(w_out, w_out_v, sem)
-    fetch.start()
-    rows = events.shape[0]
-    own = chosen[...]
-    lanes = lax.broadcasted_iota(jnp.int32, (own.shape[0], rows), 1)
+    @pl.when(item * 2 < items_axis)
+    def _():
+        attention(limits, events_v, chosen, w_uvqk_v, done)
+
+
+def attention(limits, events, own, w_uvqk, store):
+    lanes = lax.broadcasted_iota(jnp.int32, (own.shape[0], events.shape[0]), 1)
     valid = lanes <= limits[:, 0:1]
-    for head in range(gated.shape[2] // DH):
+    for head in range(w_uvqk.shape[1] // (4 * DH)):
         first = head * 4 * DH
         w_part = [w_uvqk[:, first + k * DH : first + (k + 1) * DH] for k in range(4)]
         w_gate_query = jnp.concatenate([w_part[0], w_part[2]], axis=1)
         w_value_key = jnp.concatenate([w_part[1], w_part[3]], axis=1)
-        gate_query = jnp.dot(own, w_gate_query, preferred_element_type=jnp.float32)
+        gate_query = jnp.dot(own[...], w_gate_query, preferred_element_type=jnp.float32)
         gate_query = jax.nn.silu(gate_query).astype(jnp.bfloat16)
         value_key = jnp.dot(events[...], w_value_key, preferred_element_type=jnp.float32)
         value_key = jax.nn.silu(value_key).astype(jnp.bfloat16)
@@ -115,11 +114,28 @@
         weights = jnp.where(valid, jax.nn.silu(scores), 0.0).astype(jnp.bfloat16)
         attended = jnp.dot(weights, value_key[:, :DH], preferred_element_type=jnp.float32)
         inverse = lax.rsqrt(jnp.mean(attended * attended, axis=-1, keepdims=True) + 1e-06)
-        gated_rows = (attended * inverse * gate_query[:, :DH].astype(jnp.float32)).astype(
-            jnp.bfloat16
-        )
-        for k in range(gated.shape[0]):
-            gated[k, :, head * DH : (head + 1) * DH] = gated_rows
+        store[:, head * DH : (head + 1) * DH] = (
+            attended * inverse * gate_query[:, :DH].astype(jnp.float32)
+        ).astype(jnp.bfloat16)
+
+
+def attend_kernel(
+    items_axis, place, limits, events, chosen, w_uvqk, done, w_out, gated, w_out_v, rows, sem
+):
+    fetch = pltpu.make_async_copy(w_out, w_out_v, sem)
+    fetch.start()
+    early = place[0] * 2 < items_axis
+
+    @pl.when(early)
+    def _():
+        rows[...] = done[...]
+
+    @pl.when(jnp.logical_not(early))
+    def _():
+        attention(limits, events, chosen, w_uvqk, rows)
+
+    for k in range(gated.shape[0]):
+        gated[k] = rows[...]
     fetch.wait()
 
 
@@ -128,7 +144,7 @@
     chosen, refs = refs[:items_axis], refs[items_axis:]
     w_out, refs = refs[:tensors], refs[tensors:]
     catalogue, refs = list(refs[:dps]), refs[dps:]
-    state_hbm, sums, hidden, others, sems, state_sem = refs
+    state_hbm, sums, hidden, gates, others, sems, state_sem = refs
     fetches = [
         pltpu.make_async_copy(catalogue[d], others.at[d - 1], sems.at[d - 1]) for d in range(1, dps)
     ]
@@ -142,15 +158,16 @@
     step_items = min(256, items)
     steps = range(0, items, step_items)
     slot_rounds, tensor_rounds = rounds(items_axis), rounds(tensors)
-    totals = [c[...].astype(jnp.float32) for c in chosen]
-    for t in range(tensors):
-        for k in range(items_axis):
+    local_width = w_out[0].shape[0]
+    for k in range(items_axis):
+        for t in range(tensors):
             sender = (item ^ slot_rounds[k]) * tensors + (tensor ^ tensor_rounds[t])
-            totals[k] += jnp.dot(
-                gated[sender], w_out[t][...], preferred_element_type=jnp.float32
-            )
+            gates[k * imps : (k + 1) * imps, t * local_width : (t + 1) * local_width] = gated[sender]
+    w_whole = jnp.concatenate([w[...] for w in w_out], axis=0)
+    mixed = jnp.dot(gates[...], w_whole, preferred_element_type=jnp.float32)
     for k in range(items_axis):
-        hidden[k * imps : (k + 1) * imps, :] = totals[k].astype(jnp.bfloat16)
+        rows = slice(k * imps, (k + 1) * imps)
+        hidden[rows, :] = (mixed[rows] + chosen[k][...].astype(jnp.float32)).astype(jnp.bfloat16)
     share = state_hbm.shape[1]
     state_copy = pltpu.make_async_copy(
         hidden.at[pl.ds(0, imps), pl.ds(pl.multiple_of(tensor * share, share), share)],
@@ -225,7 +242,7 @@
 
     other_catalogues = from_others(catalogue, "dp", dps)
     other_w_out = from_others(w_out, "tensor", tensors)
-    chosen, limits, wanted, events, w_uvqk = pl.pallas_call(
+    chosen, limits, wanted, events, w_uvqk, done = pl.pallas_call(
         functools.partial(pick_kernel, (items_axis, dps)),
         out_shape=(
             jax.ShapeDtypeStruct((imps, width), jnp.bfloat16),
@@ -233,9 +250,10 @@
             jax.ShapeDtypeStruct((1, items_axis * imps), jnp.int32),
             jax.ShapeDtypeStruct(events.shape, events.dtype),
             jax.ShapeDtypeStruct(w_uvqk.shape, w_uvqk.dtype),
+            jax.ShapeDtypeStruct((imps, local_width), jnp.bfloat16),
         ),
         in_specs=[smem] + [hbm] * 6,
-        out_specs=(vmem,) * 5,
+        out_specs=(vmem,) * 6,
         scratch_shapes=[
             pltpu.SMEM((hists,), jnp.int32),
             pltpu.SMEM((hists,), jnp.int32),
@@ -252,18 +270,21 @@
     other_chosen = from_others(chosen, "item", items_axis)
 
     gated, own_w_out = pl.pallas_call(
-        attend_kernel,
+        functools.partial(attend_kernel, items_axis),
         out_shape=(
             jax.ShapeDtypeStruct((receivers, imps, local_width), jnp.bfloat16),
             jax.ShapeDtypeStruct(w_out.shape, w_out.dtype),
         ),
-        in_specs=[vmem] * 4 + [hbm],
+        in_specs=[smem] + [vmem] * 5 + [hbm],
         out_specs=(vmem,) * 2,
-        scratch_shapes=[pltpu.SemaphoreType.DMA],
+        scratch_shapes=[
+            pltpu.VMEM((imps, local_width), jnp.bfloat16),
+            pltpu.SemaphoreType.DMA,
+        ],
         compiler_params=params,
         cost_estimate=pl.CostEstimate(flops=0, bytes_accessed=0, transcendentals=0),
         name="attend",
-    )(limits, events, chosen, w_uvqk, in_hbm(w_out))
+    )(place, limits, events, chosen, w_uvqk, done, in_hbm(w_out))
 
     all_gated = lax.all_to_all(gated, COLUMN, split_axis=0, concat_axis=0, tiled=True)
 
@@ -277,6 +298,7 @@
         out_specs=(hbm, vmem),
         scratch_shapes=[
             pltpu.VMEM((items_axis * imps, width), jnp.bfloat16),
+            pltpu.VMEM((items_axis * imps, local_width * tensors), jnp.bfloat16),
             pltpu.VMEM((dps - 1, items, width), jnp.bfloat16),
             pltpu.SemaphoreType.DMA((dps - 1,)),
             pltpu.SemaphoreType.DMA,

time: 38.3 us -> 38.3 us (level)
  starting transfers between devices: 12.6 us -> 11.5 us
  Pallas kernels: 7.68 us -> 8.72 us
    pallas_call x1, Pallas kernels: 2.34 us -> 3.44 us  [local(): pl.pallas_call(functools.partial(pick_kernel, (items_axis, dps)), out_sha...]
    ppermute x5, starting transfers between devices: 9.24 us -> 8.14 us  [send(): return lax.ppermute(x, axes, [(i, i ^ r) for i in range(count)])]
    pallas_call x1, Pallas kernels: 3.54 us -> 3.13 us  [local(): pl.pallas_call(functools.partial(score_kernel, (items_axis, dps, tensors)...]
  transfers between devices with their start and end apart: 6 -> 6, of which waited for: 1 -> 1; matrix products, arithmetic and copies ran while one was open for 0% -> 0% of each run, Pallas kernels for 11% -> 15%
where the time goes in v8:
time: 38.3 us; the launch traced here: 37.9 us
  starting transfers between devices  11.5 us (30%)
  blocking collectives  10.1 us (26%)
  Pallas kernels  8.72 us (23%)
  waiting for transfers between devices  6.21 us (16%)
  between operations  0.71 us (2%)
  other arithmetic  0.69 us (2%)
    all_to_all x1, blocking collectives, local(): sums = lax.all_to_all(sums, COLUMN, split_axis=0, concat_axis=0, tiled=True)  10.1 us
    ppermute x5, starting transfers between devices, send(): return lax.ppermute(x, axes, [(i, i ^ r) for i in range(count)])  8.14 us
    all_to_all x1, waiting for transfers between devices, local(): lax.all_to_all(gated, COLUMN, split_axis=0, concat_axis=0, tiled=True)  6.2 us
    pallas_call x1, Pallas kernels, local(): pl.pallas_call(functools.partial(pick_kernel, (items_axis, dps)), out_sha...  3.44 us
    all_to_all x1, starting transfers between devices, local(): lax.all_to_all(gated, COLUMN, split_axis=0, concat_axis=0, tiled=True)  3.38 us
    pallas_call x1, Pallas kernels, local(): pl.pallas_call(functools.partial(score_kernel, (items_axis, dps, tensors)...  3.13 us
    pallas_call x1, Pallas kernels, local(): pl.pallas_call(functools.partial(attend_kernel, items_axis), out_shape=(j...  2.15 us
  transfers between devices with their start and end apart: 6, of which 1 were waited for; matrix products, arithmetic and copies ran while one was open for 0% of the time, Pallas kernels for 15%

profile of v8, /device:TPU:0, one launch (start us, length us, event | category | flops | bytes accessed | tf_op | source)
XLA Modules:
  0.0 37.9 jit_solution(1966032969106778185)
XLA Ops:
  0.6 0.0 copy-start.1
  0.6 0.5 %collective-permute-start.4 = (bf16[1024,1024]{1,0:T(8,128)(2,1)}, bf16[1024,1024]{1,0:T(8,128)(2,1)}, u32[]{:S(2)}, u32[]{:S(2)}) collective-permute-start(bf16[1024,1024]{1,0:T(8,128)(2,1)} %refs_6_.1), channel_id=1, source_target_pairs={{0,2},{2,0},{1,3},{3,1},{4,6},{6,4},{5,7},{7,5},{8,10},{10,8},{9,1... | collective-permute-start | bytes 6291464 | tf_op jit(solution)/shard_map/ppermute | solution.py:217
  1.2 0.1 pad_add_fusion.place
  1.2 3.4 %pick.1 = (bf16[64,1024]{1,0:T(8,128)(2,1)S(1)}, s32[64,128]{1,0:T(8,128)S(1)}, s32[1,256]{1,0:T(1,128)S(1)}, bf16[768,1024]{1,0:T(8,128)(2,1)S(1)}, bf16[1024,5...) custom-call(s32[3]{0:T(128)S(1)} %pad_add_fusion.place, s32[8]{0:T(128)} %packing.1, s32[8]{0:T(128)} %lengths.1, ...), custom_call_target="tpu_custom_call" | custom-call | flops 100663296 | bytes 1572864 | tf_op jit(solution)/shard_map/pick/pallas_call | solution.py:245
  4.7 0.0 copy-start
  4.7 2.6 %collective-permute-start = (bf16[64,1024]{1,0:T(8,128)(2,1)S(1)}, bf16[64,1024]{1,0:T(8,128)(2,1)S(1)}, u32[]{:S(2)}, u32[]{:S(2)}) collective-permute-start(bf16[64,1024]{1,0:T(8,128)(2,1)S(1)} %get-tuple-element.17.chosen.refs_0_), channel_id=1, source_target_pairs={{0,8},{4,12},{8,0},{12,4},{1,9},{5,13},{9,1},{13,5},{2,10},{6,14},... | collective-permute-start | bytes 393224 | tf_op jit(solution)/shard_map/ppermute | solution.py:217
  7.3 1.6 %collective-permute-start.1 = (bf16[64,1024]{1,0:T(8,128)(2,1)S(1)}, bf16[64,1024]{1,0:T(8,128)(2,1)S(1)}, u32[]{:S(2)}, u32[]{:S(2)}) collective-permute-start(bf16[64,1024]{1,0:T(8,128)(2,1)S(1)} %get-tuple-element.17.chosen.refs_0_), channel_id=1, source_target_pairs={{0,4},{4,0},{8,12},{12,8},{1,5},{5,1},{9,13},{13,9},{2,6},{6,2},{1... | collective-permute-start | bytes 393224 | tf_op jit(solution)/shard_map/ppermute | solution.py:217
  8.8 0.0 copy-done.1
  8.8 1.5 %collective-permute-start.3 = (bf16[128,1024]{1,0:T(8,128)(2,1)S(1)}, bf16[128,1024]{1,0:T(8,128)(2,1)S(1)}, u32[]{:S(2)}, u32[]{:S(2)}) collective-permute-start(bf16[128,1024]{1,0:T(8,128)(2,1)S(1)} %copy-done.1), channel_id=1, source_target_pairs={{0,1},{1,0},{2,3},{3,2},{4,5},{5,4},{6,7},{7,6},{8,9},{9,8},{10,11... | collective-permute-start | bytes 786440 | tf_op jit(solution)/shard_map/ppermute | solution.py:217
  10.3 2.1 %attend.1 = (bf16[8,64,128]{2,1,0:T(8,128)(2,1)}, bf16[128,1024]{1,0:T(8,128)(2,1)S(1)}) custom-call(s32[3]{0:T(128)S(1)} %pad_add_fusion.place, s32[64,128]{1,0:T(8,128)S(1)} %get-tuple-element.15.limits, bf16[768,1024]{1,0:T(8,128)(2,1)S(1)} %get-tuple-element.16.events, bf16[64,1024]{1,0:T(8,128)(2,1)S(1)} %get-tuple-element.17.chosen.refs_0_, ...), custom_call_target="tpu_custom_call" | custom-call | tf_op jit(solution)/shard_map/attend/pallas_call | solution.py:272
  12.5 3.4 %all-to-all-start = ((bf16[8,64,128]{2,1,0:T(8,128)(2,1)}), bf16[8,64,128]{2,1,0:T(8,128)(2,1)S(1)}, u32[]{:S(2)}, u32[]{:S(2)}) async-start(bf16[8,64,128]{2,1,0:T(8,128)(2,1)} %get-tuple-element.20), calls=%async_computation | async-start | bytes 262144 | tf_op jit(solution)/shard_map/all_to_all | solution.py:289
  15.9 0.0 collective-permute-done.refs_1_
  15.9 0.0 collective-permute-done.1.refs_2_
  15.9 2.0 %collective-permute-start.2 = (bf16[64,1024]{1,0:T(8,128)(2,1)S(1)}, bf16[64,1024]{1,0:T(8,128)(2,1)S(1)}, u32[]{:S(2)}, u32[]{:S(2)}) collective-permute-start(bf16[64,1024]{1,0:T(8,128)(2,1)S(1)} %collective-permute-done.refs_1_), channel_id=1, source_target_pairs={{0,4},{4,0},{8,12},{12,8},{1,5},{5,1},{9,13},{13,9},{2,6},{6,2},{1... | collective-permute-start | bytes 393224 | tf_op jit(solution)/shard_map/ppermute | solution.py:217
  17.9 6.2 %all-to-all-done.gated = bf16[8,64,128]{2,1,0:T(8,128)(2,1)S(1)} async-done(((bf16[8,64,128]{2,1,0:T(8,128)(2,1)}), bf16[8,64,128]{2,1,0:T(8,128)(2,1)S(1)}, u32[]{:S(2)}, u32[]{:S(2)}) %all-to-all-start) | async-done | bytes 131104 | tf_op jit(solution)/shard_map/all_to_all | solution.py:289
  24.1 0.0 collective-permute-done.2.refs_3_
  24.1 0.0 collective-permute-done.3.refs_5_
  24.1 0.0 collective-permute-done.4.refs_7_
  24.1 0.0 copy-done
  24.1 3.1 %score.1 = (bf16[64,512]{1,0:T(8,128)(2,1)}, f32[8,1,128]{2,1,0:T(1,128)S(1)}) custom-call(s32[3]{0:T(128)S(1)} %pad_add_fusion.place, s32[1,256]{1,0:T(1,128)S(1)} %get-tuple-element.14.wanted, bf16[8,64,128]{2,1,0:T(8,128)(2,1)S(1)} %all-to-all-done.gated, bf16[64,1024]{1,0:T(8,128)(2,1)S(1)} %get-tuple-element.17.chosen.refs_0_, ...), custom_call_target="tpu_custom_call" | custom-call | flops 1207959552 | bytes 4194304 | tf_op jit(solution)/shard_map/score/pallas_call | solution.py:291
  27.3 10.1 %all_to_all.10 = f32[8,1,128]{2,1,0:T(1,128)S(1)} all-to-all(f32[8,1,128]{2,1,0:T(1,128)S(1)} %get-tuple-element.25), channel_id=1, replica_groups=mesh['groups'=2,'item'=4,'dp'=2,'tensor'=2] {'item','tensor'}, dimensions={0} | all-to-all | bytes 8192 | tf_op jit(solution)/shard_map/all_to_all | solution.py:324
  37.3 0.6 %log_subtract_fusion = f32[64]{0:T(128)} fusion(f32[128]{0:T(128)S(1)} %reduce_sum.9), kind=kLoop, calls=%fused_computation.1 | loop fusion | flops 64 | bytes 768 | tf_op jit(solution)/shard_map/sub | solution.py:326
  (1 shorter events, 0.0 us)
Async XLA Ops:
  0.6 8.2 %copy-start.1 = (bf16[128,1024]{1,0:T(8,128)(2,1)S(1)}, bf16[128,1024]{1,0:T(8,128)(2,1)}, u32[]{:S(2)}) copy-start(bf16[128,1024]{1,0:T(8,128)(2,1)} %w_out.1) | copy-start | bytes 786436
  0.6 23.5 %collective-permute-start.4 = (bf16[1024,1024]{1,0:T(8,128)(2,1)}, bf16[1024,1024]{1,0:T(8,128)(2,1)}, u32[]{:S(2)}, u32[]{:S(2)}) collective-permute-start(bf16[1024,1024]{1,0:T(8,128)(2,1)} %refs_6_.1), channel_id=1, source_target_pairs={{0,2},{2,0},{1,3},{3,1},{4,6},{6,4},{5,7},{7,5},{8,10},{10,8},{9,1... | collective-permute-start | bytes 6291464 | tf_op jit(solution)/shard_map/ppermute | solution.py:217
  4.7 19.4 %copy-start = (bf16[1024,1024]{1,0:T(8,128)(2,1)S(1)}, bf16[1024,1024]{1,0:T(8,128)(2,1)}, u32[]{:S(2)}) copy-start(bf16[1024,1024]{1,0:T(8,128)(2,1)} %refs_6_.1) | copy-start | bytes 6291460
  4.7 11.2 %collective-permute-start = (bf16[64,1024]{1,0:T(8,128)(2,1)S(1)}, bf16[64,1024]{1,0:T(8,128)(2,1)S(1)}, u32[]{:S(2)}, u32[]{:S(2)}) collective-permute-start(bf16[64,1024]{1,0:T(8,128)(2,1)S(1)} %get-tuple-element.17.chosen.refs_0_), channel_id=1, source_target_pairs={{0,8},{4,12},{8,0},{12,4},{1,9},{5,13},{9,1},{13,5},{2,10},{6,14},... | collective-permute-start | bytes 393224 | tf_op jit(solution)/shard_map/ppermute | solution.py:217
  7.3 8.6 %collective-permute-start.1 = (bf16[64,1024]{1,0:T(8,128)(2,1)S(1)}, bf16[64,1024]{1,0:T(8,128)(2,1)S(1)}, u32[]{:S(2)}, u32[]{:S(2)}) collective-permute-start(bf16[64,1024]{1,0:T(8,128)(2,1)S(1)} %get-tuple-element.17.chosen.refs_0_), channel_id=1, source_target_pairs={{0,4},{4,0},{8,12},{12,8},{1,5},{5,1},{9,13},{13,9},{2,6},{6,2},{1... | collective-permute-start | bytes 393224 | tf_op jit(solution)/shard_map/ppermute | solution.py:217
  8.8 15.2 %collective-permute-start.3 = (bf16[128,1024]{1,0:T(8,128)(2,1)S(1)}, bf16[128,1024]{1,0:T(8,128)(2,1)S(1)}, u32[]{:S(2)}, u32[]{:S(2)}) collective-permute-start(bf16[128,1024]{1,0:T(8,128)(2,1)S(1)} %copy-done.1), channel_id=1, source_target_pairs={{0,1},{1,0},{2,3},{3,2},{4,5},{5,4},{6,7},{7,6},{8,9},{9,8},{10,11... | collective-permute-start | bytes 786440 | tf_op jit(solution)/shard_map/ppermute | solution.py:217
  12.5 11.6 %all-to-all-start = ((bf16[8,64,128]{2,1,0:T(8,128)(2,1)}), bf16[8,64,128]{2,1,0:T(8,128)(2,1)S(1)}, u32[]{:S(2)}, u32[]{:S(2)}) async-start(bf16[8,64,128]{2,1,0:T(8,128)(2,1)} %get-tuple-element.20), calls=%async_computation | async-start | bytes 262144 | tf_op jit(solution)/shard_map/all_to_all | solution.py:289
  15.9 8.2 %collective-permute-start.2 = (bf16[64,1024]{1,0:T(8,128)(2,1)S(1)}, bf16[64,1024]{1,0:T(8,128)(2,1)S(1)}, u32[]{:S(2)}, u32[]{:S(2)}) collective-permute-start(bf16[64,1024]{1,0:T(8,128)(2,1)S(1)} %collective-permute-done.refs_1_), channel_id=1, source_target_pairs={{0,4},{4,0},{8,12},{12,8},{1,5},{5,1},{9,13},{13,9},{2,6},{6,2},{1... | collective-permute-start | bytes 393224 | tf_op jit(solution)/shard_map/ppermute | solution.py:217

commit v9 on v8

--- a/solution.py
+++ b/solution.py
@@ -38,12 +38,14 @@
     wanted,
     events_v,
     w_uvqk_v,
-    done,
+    gated,
+    gated_rows,
     packing_s,
     lengths_s,
     positions_v,
     logged_v,
     sems,
+    gated_sems,
 ):
     rows = events.shape[0]
     items_axis, dps = shards
@@ -91,9 +93,10 @@
     chosen[...] = total.astype(jnp.bfloat16)
     copies[-1].wait()
 
-    @pl.when(item * 2 < items_axis)
+    @pl.when(is_early(item, items_axis))
     def _():
-        attention(limits, events_v, chosen, w_uvqk_v, done)
+        attention(limits, events_v, chosen, w_uvqk_v, gated_rows)
+        hand_out(gated_rows, gated, gated_sems)
 
 
 def attention(limits, events, own, w_uvqk, store):
@@ -119,24 +122,27 @@
         ).astype(jnp.bfloat16)
 
 
+def is_early(item, items_axis):
+    return item * 4 < items_axis
+
+
+def hand_out(rows, gated, sems):
+    copies = [pltpu.make_async_copy(rows, gated.at[k], sems.at[k]) for k in range(gated.shape[0])]
+    for copy in copies:
+        copy.start()
+    for copy in copies:
+        copy.wait()
+
+
 def attend_kernel(
-    items_axis, place, limits, events, chosen, w_uvqk, done, w_out, gated, w_out_v, rows, sem
+    items_axis, place, limits, events, chosen, w_uvqk, gated_in, gated, rows, sems
 ):
-    fetch = pltpu.make_async_copy(w_out, w_out_v, sem)
-    fetch.start()
-    early = place[0] * 2 < items_axis
-
-    @pl.when(early)
-    def _():
-        rows[...] = done[...]
-
-    @pl.when(jnp.logical_not(early))
+    del gated_in
+
+    @pl.when(jnp.logical_not(is_early(place[0], items_axis)))
     def _():
         attention(limits, events, chosen, w_uvqk, rows)
-
-    for k in range(gated.shape[0]):
-        gated[k] = rows[...]
-    fetch.wait()
+        hand_out(rows, gated, sems)
 
 
 def score_kernel(sizes, place, wanted, gated, *refs):
@@ -242,7 +248,7 @@
 
     other_catalogues = from_others(catalogue, "dp", dps)
     other_w_out = from_others(w_out, "tensor", tensors)
-    chosen, limits, wanted, events, w_uvqk, done = pl.pallas_call(
+    chosen, limits, wanted, events, w_uvqk, gated = pl.pallas_call(
         functools.partial(pick_kernel, (items_axis, dps)),
         out_shape=(
             jax.ShapeDtypeStruct((imps, width), jnp.bfloat16),
@@ -250,16 +256,18 @@
             jax.ShapeDtypeStruct((1, items_axis * imps), jnp.int32),
             jax.ShapeDtypeStruct(events.shape, events.dtype),
             jax.ShapeDtypeStruct(w_uvqk.shape, w_uvqk.dtype),
-            jax.ShapeDtypeStruct((imps, local_width), jnp.bfloat16),
+            pltpu.HBM((receivers, imps, local_width), jnp.bfloat16),
         ),
         in_specs=[smem] + [hbm] * 6,
-        out_specs=(vmem,) * 6,
+        out_specs=(vmem,) * 5 + (hbm,),
         scratch_shapes=[
+            pltpu.VMEM((imps, local_width), jnp.bfloat16),
             pltpu.SMEM((hists,), jnp.int32),
             pltpu.SMEM((hists,), jnp.int32),
             pltpu.VMEM((hists, imps), jnp.int32),
             pltpu.VMEM((hists, imps), jnp.int32),
             pltpu.SemaphoreType.DMA((5 + EVENT_PARTS,)),
+            pltpu.SemaphoreType.DMA((receivers,)),
         ],
         compiler_params=params,
         cost_estimate=pl.CostEstimate(
@@ -269,23 +277,20 @@
     )(place, *(in_hbm(x) for x in (packing, lengths, positions, logged, events, w_uvqk)))
     other_chosen = from_others(chosen, "item", items_axis)
 
-    gated, own_w_out = pl.pallas_call(
+    gated = pl.pallas_call(
         functools.partial(attend_kernel, items_axis),
-        out_shape=(
-            jax.ShapeDtypeStruct((receivers, imps, local_width), jnp.bfloat16),
-            jax.ShapeDtypeStruct(w_out.shape, w_out.dtype),
-        ),
-        in_specs=[smem] + [vmem] * 5 + [hbm],
-        out_specs=(vmem,) * 2,
+        out_shape=jax.ShapeDtypeStruct(gated.shape, gated.dtype),
+        in_specs=[smem] + [vmem] * 4 + [hbm],
+        out_specs=hbm,
         scratch_shapes=[
             pltpu.VMEM((imps, local_width), jnp.bfloat16),
-            pltpu.SemaphoreType.DMA,
+            pltpu.SemaphoreType.DMA((receivers,)),
         ],
+        input_output_aliases={5: 0},
         compiler_params=params,
         cost_estimate=pl.CostEstimate(flops=0, bytes_accessed=0, transcendentals=0),
         name="attend",
-    )(place, limits, events, chosen, w_uvqk, done, in_hbm(w_out))
-
+    )(place, limits, events, chosen, w_uvqk, in_hbm(gated))
     all_gated = lax.all_to_all(gated, COLUMN, split_axis=0, concat_axis=0, tiled=True)
 
     state, sums = pl.pallas_call(
@@ -316,7 +321,7 @@
         all_gated,
         chosen,
         *other_chosen,
-        own_w_out,
+        w_out,
         *other_w_out,
         catalogue,
         *(in_hbm(x) for x in other_catalogues),

time: 38.3 us -> 38.2 us (level)
  starting transfers between devices: 11.5 us -> 12.6 us
  Pallas kernels: 8.72 us -> 7.92 us
    all_to_all x1, starting transfers between devices: 3.38 us -> 5 us  [local(): lax.all_to_all(gated, COLUMN, split_axis=0, concat_axis=0, tiled=True)]
    pallas_call x1, Pallas kernels: 2.15 us -> 0.62 us  [local(): pl.pallas_call(functools.partial(attend_kernel, items_axis), out_shape=ja...]
    pallas_call x1, Pallas kernels: 3.44 us -> 4.15 us  [local(): pl.pallas_call(functools.partial(pick_kernel, (items_axis, dps)), out_sha...]
    ppermute x5, starting transfers between devices: 8.14 us -> 7.6 us  [send(): return lax.ppermute(x, axes, [(i, i ^ r) for i in range(count)])]
  transfers between devices with their start and end apart: 6 -> 6, of which waited for: 1 -> 1; matrix products, arithmetic and copies ran while one was open for 0% -> 0% of each run, Pallas kernels for 15% -> 13%
where the time goes in v9:
time: 38.2 us; the launch traced here: 37.9 us
  starting transfers between devices  12.6 us (33%)
  blocking collectives  9.84 us (26%)
  Pallas kernels  7.92 us (21%)
  waiting for transfers between devices  6.12 us (16%)
  between operations  0.7 us (2%)
  other arithmetic  0.69 us (2%)
    all_to_all x1, blocking collectives, local(): sums = lax.all_to_all(sums, COLUMN, split_axis=0, concat_axis=0, tiled=True)  9.84 us
    ppermute x5, starting transfers between devices, send(): return lax.ppermute(x, axes, [(i, i ^ r) for i in range(count)])  7.6 us
    all_to_all x1, waiting for transfers between devices, local(): lax.all_to_all(gated, COLUMN, split_axis=0, concat_axis=0, tiled=True)  6.1 us
    all_to_all x1, starting transfers between devices, local(): lax.all_to_all(gated, COLUMN, split_axis=0, concat_axis=0, tiled=True)  5 us
    pallas_call x1, Pallas kernels, local(): pl.pallas_call(functools.partial(pick_kernel, (items_axis, dps)), out_sha...  4.15 us
    pallas_call x1, Pallas kernels, local(): pl.pallas_call(functools.partial(score_kernel, (items_axis, dps, tensors)...  3.15 us
  transfers between devices with their start and end apart: 6, of which 1 were waited for; matrix products, arithmetic and copies ran while one was open for 0% of the time, Pallas kernels for 13%

profile of v9, /device:TPU:0, one launch (start us, length us, event | category | flops | bytes accessed | tf_op | source)
XLA Modules:
  0.0 37.9 jit_solution(4748722506675497133)
XLA Ops:
  0.6 0.0 copy-start.1
  0.6 0.5 %collective-permute-start.4 = (bf16[1024,1024]{1,0:T(8,128)(2,1)}, bf16[1024,1024]{1,0:T(8,128)(2,1)}, u32[]{:S(2)}, u32[]{:S(2)}) collective-permute-start(bf16[1024,1024]{1,0:T(8,128)(2,1)} %refs_6_.1), channel_id=1, source_target_pairs={{0,2},{2,0},{1,3},{3,1},{4,6},{6,4},{5,7},{7,5},{8,10},{10,8},{9,1... | collective-permute-start | bytes 6291464 | tf_op jit(solution)/shard_map/ppermute | solution.py:223
  1.2 0.1 pad_add_fusion.place
  1.2 4.2 %pick.1 = (bf16[64,1024]{1,0:T(8,128)(2,1)S(1)}, s32[64,128]{1,0:T(8,128)S(1)}, s32[1,256]{1,0:T(1,128)S(1)}, bf16[768,1024]{1,0:T(8,128)(2,1)S(1)}, bf16[1024,5...) custom-call(s32[3]{0:T(128)S(1)} %pad_add_fusion.place, s32[8]{0:T(128)} %packing.1, s32[8]{0:T(128)} %lengths.1, ...), custom_call_target="tpu_custom_call" | custom-call | flops 100663296 | bytes 1572864 | tf_op jit(solution)/shard_map/pick/pallas_call | solution.py:251
  5.4 0.0 copy-start
  5.4 1.9 %collective-permute-start = (bf16[64,1024]{1,0:T(8,128)(2,1)S(1)}, bf16[64,1024]{1,0:T(8,128)(2,1)S(1)}, u32[]{:S(2)}, u32[]{:S(2)}) collective-permute-start(bf16[64,1024]{1,0:T(8,128)(2,1)S(1)} %get-tuple-element.15.chosen.refs_0_), channel_id=1, source_target_pairs={{0,8},{4,12},{8,0},{12,4},{1,9},{5,13},{9,1},{13,5},{2,10},{6,14},... | collective-permute-start | bytes 393224 | tf_op jit(solution)/shard_map/ppermute | solution.py:223
  7.3 1.6 %collective-permute-start.1 = (bf16[64,1024]{1,0:T(8,128)(2,1)S(1)}, bf16[64,1024]{1,0:T(8,128)(2,1)S(1)}, u32[]{:S(2)}, u32[]{:S(2)}) collective-permute-start(bf16[64,1024]{1,0:T(8,128)(2,1)S(1)} %get-tuple-element.15.chosen.refs_0_), channel_id=1, source_target_pairs={{0,4},{4,0},{8,12},{12,8},{1,5},{5,1},{9,13},{13,9},{2,6},{6,2},{1... | collective-permute-start | bytes 393224 | tf_op jit(solution)/shard_map/ppermute | solution.py:223
  8.9 0.0 copy-done.1
  8.9 1.5 %collective-permute-start.3 = (bf16[128,1024]{1,0:T(8,128)(2,1)S(1)}, bf16[128,1024]{1,0:T(8,128)(2,1)S(1)}, u32[]{:S(2)}, u32[]{:S(2)}) collective-permute-start(bf16[128,1024]{1,0:T(8,128)(2,1)S(1)} %copy-done.1), channel_id=1, source_target_pairs={{0,1},{1,0},{2,3},{3,2},{4,5},{5,4},{6,7},{7,6},{8,9},{9,8},{10,11... | collective-permute-start | bytes 786440 | tf_op jit(solution)/shard_map/ppermute | solution.py:223
  10.4 0.6 %attend.1 = bf16[8,64,128]{2,1,0:T(8,128)(2,1)} custom-call(s32[3]{0:T(128)S(1)} %pad_add_fusion.place, s32[64,128]{1,0:T(8,128)S(1)} %get-tuple-element.13.limits, bf16[768,1024]{1,0:T(8,128)(2,1)S(1)} %get-tuple-element.14.events, bf16[64,1024]{1,0:T(8,128)(2,1)S(1)} %get-tuple-element.15.chosen.refs_0_, ...), custom_call_target="tpu_custom_call", output_to_operand_aliasing={{}: (5, {})} | custom-call | tf_op jit(solution)/shard_map/attend/pallas_call | solution.py:280
  11.0 5.0 %all-to-all-start = ((bf16[8,64,128]{2,1,0:T(8,128)(2,1)}), bf16[8,64,128]{2,1,0:T(8,128)(2,1)S(1)}, u32[]{:S(2)}, u32[]{:S(2)}) async-start(bf16[8,64,128]{2,1,0:T(8,128)(2,1)} %attend.1), calls=%async_computation | async-start | bytes 262144 | tf_op jit(solution)/shard_map/all_to_all | solution.py:294
  16.0 0.0 collective-permute-done.refs_1_
  16.0 0.0 collective-permute-done.1.refs_2_
  16.1 2.1 %collective-permute-start.2 = (bf16[64,1024]{1,0:T(8,128)(2,1)S(1)}, bf16[64,1024]{1,0:T(8,128)(2,1)S(1)}, u32[]{:S(2)}, u32[]{:S(2)}) collective-permute-start(bf16[64,1024]{1,0:T(8,128)(2,1)S(1)} %collective-permute-done.refs_1_), channel_id=1, source_target_pairs={{0,4},{4,0},{8,12},{12,8},{1,5},{5,1},{9,13},{13,9},{2,6},{6,2},{1... | collective-permute-start | bytes 393224 | tf_op jit(solution)/shard_map/ppermute | solution.py:223
  18.1 6.1 %all-to-all-done.gated = bf16[8,64,128]{2,1,0:T(8,128)(2,1)S(1)} async-done(((bf16[8,64,128]{2,1,0:T(8,128)(2,1)}), bf16[8,64,128]{2,1,0:T(8,128)(2,1)S(1)}, u32[]{:S(2)}, u32[]{:S(2)}) %all-to-all-start) | async-done | bytes 131104 | tf_op jit(solution)/shard_map/all_to_all | solution.py:294
  24.2 0.0 collective-permute-done.2.refs_3_
  24.2 0.0 collective-permute-done.3.refs_5_
  24.2 0.0 collective-permute-done.4.refs_7_
  24.2 0.0 copy-done
  24.3 3.2 %score.1 = (bf16[64,512]{1,0:T(8,128)(2,1)}, f32[8,1,128]{2,1,0:T(1,128)S(1)}) custom-call(s32[3]{0:T(128)S(1)} %pad_add_fusion.place, s32[1,256]{1,0:T(1,128)S(1)} %get-tuple-element.12.wanted, bf16[8,64,128]{2,1,0:T(8,128)(2,1)S(1)} %all-to-all-done.gated, bf16[64,1024]{1,0:T(8,128)(2,1)S(1)} %get-tuple-element.15.chosen.refs_0_, ...), custom_call_target="tpu_custom_call" | custom-call | flops 1207959552 | bytes 4194304 | tf_op jit(solution)/shard_map/score/pallas_call | solution.py:296
  27.4 9.8 %all_to_all.10 = f32[8,1,128]{2,1,0:T(1,128)S(1)} all-to-all(f32[8,1,128]{2,1,0:T(1,128)S(1)} %get-tuple-element.21), channel_id=1, replica_groups=mesh['groups'=2,'item'=4,'dp'=2,'tensor'=2] {'item','tensor'}, dimensions={0} | all-to-all | bytes 8192 | tf_op jit(solution)/shard_map/all_to_all | solution.py:329
  37.3 0.6 %log_subtract_fusion = f32[64]{0:T(128)} fusion(f32[128]{0:T(128)S(1)} %reduce_sum.9), kind=kLoop, calls=%fused_computation.1 | loop fusion | flops 64 | bytes 768 | tf_op jit(solution)/shard_map/sub | solution.py:331
  (1 shorter events, 0.0 us)
Async XLA Ops:
  0.6 8.3 %copy-start.1 = (bf16[128,1024]{1,0:T(8,128)(2,1)S(1)}, bf16[128,1024]{1,0:T(8,128)(2,1)}, u32[]{:S(2)}) copy-start(bf16[128,1024]{1,0:T(8,128)(2,1)} %refs_4_.1) | copy-start | bytes 786436
  0.6 23.6 %collective-permute-start.4 = (bf16[1024,1024]{1,0:T(8,128)(2,1)}, bf16[1024,1024]{1,0:T(8,128)(2,1)}, u32[]{:S(2)}, u32[]{:S(2)}) collective-permute-start(bf16[1024,1024]{1,0:T(8,128)(2,1)} %refs_6_.1), channel_id=1, source_target_pairs={{0,2},{2,0},{1,3},{3,1},{4,6},{6,4},{5,7},{7,5},{8,10},{10,8},{9,1... | collective-permute-start | bytes 6291464 | tf_op jit(solution)/shard_map/ppermute | solution.py:223
  5.4 18.9 %copy-start = (bf16[1024,1024]{1,0:T(8,128)(2,1)S(1)}, bf16[1024,1024]{1,0:T(8,128)(2,1)}, u32[]{:S(2)}) copy-start(bf16[1024,1024]{1,0:T(8,128)(2,1)} %refs_6_.1) | copy-start | bytes 6291460
  5.4 10.6 %collective-permute-start = (bf16[64,1024]{1,0:T(8,128)(2,1)S(1)}, bf16[64,1024]{1,0:T(8,128)(2,1)S(1)}, u32[]{:S(2)}, u32[]{:S(2)}) collective-permute-start(bf16[64,1024]{1,0:T(8,128)(2,1)S(1)} %get-tuple-element.15.chosen.refs_0_), channel_id=1, source_target_pairs={{0,8},{4,12},{8,0},{12,4},{1,9},{5,13},{9,1},{13,5},{2,10},{6,14},... | collective-permute-start | bytes 393224 | tf_op jit(solution)/shard_map/ppermute | solution.py:223
  7.3 8.7 %collective-permute-start.1 = (bf16[64,1024]{1,0:T(8,128)(2,1)S(1)}, bf16[64,1024]{1,0:T(8,128)(2,1)S(1)}, u32[]{:S(2)}, u32[]{:S(2)}) collective-permute-start(bf16[64,1024]{1,0:T(8,128)(2,1)S(1)} %get-tuple-element.15.chosen.refs_0_), channel_id=1, source_target_pairs={{0,4},{4,0},{8,12},{12,8},{1,5},{5,1},{9,13},{13,9},{2,6},{6,2},{1... | collective-permute-start | bytes 393224 | tf_op jit(solution)/shard_map/ppermute | solution.py:223
  8.9 15.3 %collective-permute-start.3 = (bf16[128,1024]{1,0:T(8,128)(2,1)S(1)}, bf16[128,1024]{1,0:T(8,128)(2,1)S(1)}, u32[]{:S(2)}, u32[]{:S(2)}) collective-permute-start(bf16[128,1024]{1,0:T(8,128)(2,1)S(1)} %copy-done.1), channel_id=1, source_target_pairs={{0,1},{1,0},{2,3},{3,2},{4,5},{5,4},{6,7},{7,6},{8,9},{9,8},{10,11... | collective-permute-start | bytes 786440 | tf_op jit(solution)/shard_map/ppermute | solution.py:223
  11.0 13.2 %all-to-all-start = ((bf16[8,64,128]{2,1,0:T(8,128)(2,1)}), bf16[8,64,128]{2,1,0:T(8,128)(2,1)S(1)}, u32[]{:S(2)}, u32[]{:S(2)}) async-start(bf16[8,64,128]{2,1,0:T(8,128)(2,1)} %attend.1), calls=%async_computation | async-start | bytes 262144 | tf_op jit(solution)/shard_map/all_to_all | solution.py:294
  16.1 8.2 %collective-permute-start.2 = (bf16[64,1024]{1,0:T(8,128)(2,1)S(1)}, bf16[64,1024]{1,0:T(8,128)(2,1)S(1)}, u32[]{:S(2)}, u32[]{:S(2)}) collective-permute-start(bf16[64,1024]{1,0:T(8,128)(2,1)S(1)} %collective-permute-done.refs_1_), channel_id=1, source_target_pairs={{0,4},{4,0},{8,12},{12,8},{1,5},{5,1},{9,13},{13,9},{2,6},{6,2},{1... | collective-permute-start | bytes 393224 | tf_op jit(solution)/shard_map/ppermute | solution.py:223

commit v10 on v9

--- a/solution.py
+++ b/solution.py
@@ -26,7 +26,6 @@
 
 def pick_kernel(
     shards,
-    place,
     packing,
     lengths,
     positions,
@@ -69,7 +68,7 @@
         copy.start()
     for copy in copies[:4]:
         copy.wait()
-    item, dp = place[0], place[1]
+    item, dp = lax.axis_index("item"), lax.axis_index("dp")
     history = packing_s[item * dps + dp]
     row = positions_v[pl.ds(history, 1), :].astype(jnp.float32)
     diagonal = lax.broadcasted_iota(jnp.int32, (imps, imps), 0) == lax.broadcasted_iota(
@@ -135,17 +134,17 @@
 
 
 def attend_kernel(
-    items_axis, place, limits, events, chosen, w_uvqk, gated_in, gated, rows, sems
+    items_axis, limits, events, chosen, w_uvqk, gated_in, gated, rows, sems
 ):
     del gated_in
 
-    @pl.when(jnp.logical_not(is_early(place[0], items_axis)))
+    @pl.when(jnp.logical_not(is_early(lax.axis_index("item"), items_axis)))
     def _():
         attention(limits, events, chosen, w_uvqk, rows)
         hand_out(rows, gated, sems)
 
 
-def score_kernel(sizes, place, wanted, gated, *refs):
+def score_kernel(sizes, wanted, gated, *refs):
     items_axis, dps, tensors = sizes
     chosen, refs = refs[:items_axis], refs[items_axis:]
     w_out, refs = refs[:tensors], refs[tensors:]
@@ -157,7 +156,7 @@
     for fetch in fetches:
         fetch.start()
     catalogue[1:] = [others.at[d - 1] for d in range(1, dps)]
-    item, dp, tensor = place[0], place[1], place[2]
+    item, dp, tensor = (lax.axis_index(a) for a in ("item", "dp", "tensor"))
     imps = chosen[0].shape[0]
     items = catalogue[0].shape[0]
     step_rows = min(256, items_axis * imps)
@@ -223,15 +222,17 @@
     return lax.ppermute(x, axes, [(i, i ^ r) for i in range(count)])
 
 
-def from_others(x, axes, count):
+def from_others(x, axes, count, beside=()):
     pieces = {}
     for r in rounds(count)[1:]:
         if r & 3 == 3:
-            held, pieces[r - 2] = lax.optimization_barrier((pieces[r - 1], pieces[r - 2]))
+            held, pieces[r - 2], beside = lax.optimization_barrier(
+                (pieces[r - 1], pieces[r - 2], beside)
+            )
             pieces[r] = send(held, axes, count, 1)
         else:
             pieces[r] = send(x, axes, count, r)
-    return list(pieces.values())
+    return list(pieces.values()), beside
 
 
 def local(events, lengths, packing, positions, logged, w_uvqk, w_out, catalogue):
@@ -243,11 +244,10 @@
     items_axis, dps, tensors = (lax.axis_size(a) for a in ("item", "dp", "tensor"))
     receivers = items_axis * tensors
     params = pltpu.CompilerParams(vmem_limit_bytes=(12 + 2 * items_axis) * MIB)
-    place = jnp.stack([lax.axis_index(a) for a in ("item", "dp", "tensor")]).astype(jnp.int32)
-    smem, vmem, hbm = spec(pltpu.SMEM), spec(pltpu.VMEM), spec(pltpu.HBM)
-
-    other_catalogues = from_others(catalogue, "dp", dps)
-    other_w_out = from_others(w_out, "tensor", tensors)
+    vmem, hbm = spec(pltpu.VMEM), spec(pltpu.HBM)
+
+    other_catalogues, _ = from_others(catalogue, "dp", dps)
+    other_w_out, _ = from_others(w_out, "tensor", tensors)
     chosen, limits, wanted, events, w_uvqk, gated = pl.pallas_call(
         functools.partial(pick_kernel, (items_axis, dps)),
         out_shape=(
@@ -258,7 +258,7 @@
             jax.ShapeDtypeStruct(w_uvqk.shape, w_uvqk.dtype),
             pltpu.HBM((receivers, imps, local_width), jnp.bfloat16),
         ),
-        in_specs=[smem] + [hbm] * 6,
+        in_specs=[hbm] * 6,
         out_specs=(vmem,) * 5 + (hbm,),
         scratch_shapes=[
             pltpu.VMEM((imps, local_width), jnp.bfloat16),
@@ -274,23 +274,23 @@
             flops=2 * imps * rows * width, bytes_accessed=2 * rows * width, transcendentals=0
         ),
         name="pick",
-    )(place, *(in_hbm(x) for x in (packing, lengths, positions, logged, events, w_uvqk)))
-    other_chosen = from_others(chosen, "item", items_axis)
+    )(*(in_hbm(x) for x in (packing, lengths, positions, logged, events, w_uvqk)))
+    other_chosen, other_w_out = from_others(chosen, "item", items_axis, other_w_out)
 
     gated = pl.pallas_call(
         functools.partial(attend_kernel, items_axis),
         out_shape=jax.ShapeDtypeStruct(gated.shape, gated.dtype),
-        in_specs=[smem] + [vmem] * 4 + [hbm],
+        in_specs=[vmem] * 4 + [hbm],
         out_specs=hbm,
         scratch_shapes=[
             pltpu.VMEM((imps, local_width), jnp.bfloat16),
             pltpu.SemaphoreType.DMA((receivers,)),
         ],
-        input_output_aliases={5: 0},
+        input_output_aliases={4: 0},
         compiler_params=params,
         cost_estimate=pl.CostEstimate(flops=0, bytes_accessed=0, transcendentals=0),
         name="attend",
-    )(place, limits, events, chosen, w_uvqk, in_hbm(gated))
+    )(limits, events, chosen, w_uvqk, in_hbm(gated))
     all_gated = lax.all_to_all(gated, COLUMN, split_axis=0, concat_axis=0, tiled=True)
 
     state, sums = pl.pallas_call(
@@ -299,7 +299,7 @@
             jax.ShapeDtypeStruct((imps, width // tensors), jnp.bfloat16),
             jax.ShapeDtypeStruct((receivers, 1, 2 * imps), jnp.float32),
         ),
-        in_specs=[smem] + [vmem] * (3 + items_axis + tensors) + [hbm] * (dps - 1),
+        in_specs=[vmem] * (3 + items_axis + tensors) + [hbm] * (dps - 1),
         out_specs=(hbm, vmem),
         scratch_shapes=[
             pltpu.VMEM((items_axis * imps, width), jnp.bfloat16),
@@ -316,7 +316,6 @@
         ),
         name="score",
     )(
-        place,
         wanted,
         all_gated,
         chosen,

time: 38.2 us -> 36.5 us (0.955)
  Pallas kernels: 7.92 us -> 6.34 us
  waiting for transfers between devices: 6.12 us -> 7.59 us
  starting transfers between devices: 12.6 us -> 11.2 us
    ppermute x5, waiting for transfers between devices: 0.01 us -> 1.44 us  [send(): return lax.ppermute(x, axes, [(i, i ^ r) for i in range(count)])]
    ppermute x5, starting transfers between devices: 7.6 us -> 6.24 us  [send(): return lax.ppermute(x, axes, [(i, i ^ r) for i in range(count)])]
    pallas_call x1, Pallas kernels: 0.62 us -> 0.07 us  [local(): pl.pallas_call(functools.partial(attend_kernel, items_axis), out_shape=ja...]
    pallas_call x1, Pallas kernels: 4.15 us -> 3.62 us  [local(): pl.pallas_call(functools.partial(pick_kernel, (items_axis, dps)), out_sha...]
    pallas_call x1, Pallas kernels: 3.15 us -> 2.65 us  [local(): pl.pallas_call(functools.partial(score_kernel, (items_axis, dps, tensors)...]
  transfers between devices with their start and end apart: 6 -> 6, of which waited for: 1 -> 3; matrix products, arithmetic and copies ran while one was open for 0% -> 0% of each run, Pallas kernels for 13% -> 10%
where the time goes in v10:
time: 36.5 us; the launch traced here: 36.2 us
  starting transfers between devices  11.2 us (31%)
  blocking collectives  9.74 us (27%)
  waiting for transfers between devices  7.59 us (21%)
  Pallas kernels  6.34 us (17%)
  between operations  0.69 us (2%)
  other arithmetic  0.61 us (2%)
    all_to_all x1, blocking collectives, local(): sums = lax.all_to_all(sums, COLUMN, split_axis=0, concat_axis=0, tiled=True)  9.74 us
    ppermute x5, starting transfers between devices, send(): return lax.ppermute(x, axes, [(i, i ^ r) for i in range(count)])  6.24 us
    all_to_all x1, waiting for transfers between devices, local(): lax.all_to_all(gated, COLUMN, split_axis=0, concat_axis=0, tiled=True)  6.15 us
    all_to_all x1, starting transfers between devices, local(): lax.all_to_all(gated, COLUMN, split_axis=0, concat_axis=0, tiled=True)  5 us
    pallas_call x1, Pallas kernels, local(): pl.pallas_call(functools.partial(pick_kernel, (items_axis, dps)), out_sha...  3.62 us
    pallas_call x1, Pallas kernels, local(): pl.pallas_call(functools.partial(score_kernel, (items_axis, dps, tensors)...  2.65 us
    ppermute x5, waiting for transfers between devices, send(): return lax.ppermute(x, axes, [(i, i ^ r) for i in range(count)])  1.44 us
  transfers between devices with their start and end apart: 6, of which 3 were waited for; matrix products, arithmetic and copies ran while one was open for 0% of the time, Pallas kernels for 10%

profile of v10, /device:TPU:0, one launch (start us, length us, event | category | flops | bytes accessed | tf_op | source)
XLA Modules:
  0.0 36.2 jit_solution(16073025486968483658)
XLA Ops:
  0.6 0.5 %collective-permute-start.4 = (bf16[1024,1024]{1,0:T(8,128)(2,1)}, bf16[1024,1024]{1,0:T(8,128)(2,1)}, u32[]{:S(2)}, u32[]{:S(2)}) collective-permute-start(bf16[1024,1024]{1,0:T(8,128)(2,1)} %refs_6_.1), channel_id=1, source_target_pairs={{0,2},{2,0},{1,3},{3,1},{4,6},{6,4},{5,7},{7,5},{8,10},{10,8},{9,1... | collective-permute-start | bytes 6291464 | tf_op jit(solution)/shard_map/ppermute | solution.py:222
  1.1 2.6 %collective-permute-start.2 = (bf16[128,1024]{1,0:T(8,128)(2,1)}, bf16[128,1024]{1,0:T(8,128)(2,1)S(1)}, u32[]{:S(2)}, u32[]{:S(2)}) collective-permute-start(bf16[128,1024]{1,0:T(8,128)(2,1)} %refs_4_.1), channel_id=1, source_target_pairs={{0,1},{1,0},{2,3},{3,2},{4,5},{5,4},{6,7},{7,6},{8,9},{9,8},{10,11... | collective-permute-start | bytes 786440 | tf_op jit(solution)/shard_map/ppermute | solution.py:222
  3.7 3.6 %pick.1 = (bf16[64,1024]{1,0:T(8,128)(2,1)S(1)}, s32[64,128]{1,0:T(8,128)S(1)}, s32[1,256]{1,0:T(1,128)S(1)}, bf16[768,1024]{1,0:T(8,128)(2,1)S(1)}, bf16[1024,5...) custom-call(s32[8]{0:T(128)} %packing.1, s32[8]{0:T(128)} %lengths.1, s32[8,64]{1,0:T(8,128)} %positions.1, ...), custom_call_target="tpu_custom_call" | custom-call | flops 100663296 | bytes 1572864 | tf_op jit(solution)/shard_map/pick/pallas_call | solution.py:251
  7.3 0.0 copy-start
  7.4 0.0 copy-start.1
  7.4 0.9 %collective-permute-start = (bf16[64,1024]{1,0:T(8,128)(2,1)S(1)}, bf16[64,1024]{1,0:T(8,128)(2,1)S(1)}, u32[]{:S(2)}, u32[]{:S(2)}) collective-permute-start(bf16[64,1024]{1,0:T(8,128)(2,1)S(1)} %get-tuple-element.16.chosen.refs_0_), channel_id=1, source_target_pairs={{0,8},{4,12},{8,0},{12,4},{1,9},{5,13},{9,1},{13,5},{2,10},{6,14},... | collective-permute-start | bytes 393224 | tf_op jit(solution)/shard_map/ppermute | solution.py:222
  8.3 1.6 %collective-permute-start.1 = (bf16[64,1024]{1,0:T(8,128)(2,1)S(1)}, bf16[64,1024]{1,0:T(8,128)(2,1)S(1)}, u32[]{:S(2)}, u32[]{:S(2)}) collective-permute-start(bf16[64,1024]{1,0:T(8,128)(2,1)S(1)} %get-tuple-element.16.chosen.refs_0_), channel_id=1, source_target_pairs={{0,4},{4,0},{8,12},{12,8},{1,5},{5,1},{9,13},{13,9},{2,6},{6,2},{1... | collective-permute-start | bytes 393224 | tf_op jit(solution)/shard_map/ppermute | solution.py:222
  9.9 0.1 attend.1
  9.9 5.0 %all-to-all-start = ((bf16[8,64,128]{2,1,0:T(8,128)(2,1)}), bf16[8,64,128]{2,1,0:T(8,128)(2,1)S(1)}, u32[]{:S(2)}, u32[]{:S(2)}) async-start(bf16[8,64,128]{2,1,0:T(8,128)(2,1)} %attend.1), calls=%async_computation | async-start | bytes 262144 | tf_op jit(solution)/shard_map/all_to_all | solution.py:294
  14.9 1.1 %collective-permute-done.refs_1_ = bf16[64,1024]{1,0:T(8,128)(2,1)S(1)} collective-permute-done((bf16[64,1024]{1,0:T(8,128)(2,1)S(1)}, bf16[64,1024]{1,0:T(8,128)(2,1)S(1)}, u32[]{:S(2)}, u32[]{:S(2)}) %collective-permute-start) | collective-permute-done | bytes 131104 | tf_op jit(solution)/shard_map/ppermute | solution.py:222
  16.1 0.3 collective-permute-done.1.refs_2_
  16.4 0.0 collective-permute-done.2.refs_5_
  16.4 0.7 %collective-permute-start.3 = (bf16[64,1024]{1,0:T(8,128)(2,1)S(1)}, bf16[64,1024]{1,0:T(8,128)(2,1)S(1)}, u32[]{:S(2)}, u32[]{:S(2)}) collective-permute-start(bf16[64,1024]{1,0:T(8,128)(2,1)S(1)} %collective-permute-done.refs_1_), channel_id=1, source_target_pairs={{0,4},{4,0},{8,12},{12,8},{1,5},{5,1},{9,13},{13,9},{2,6},{6,2},{1... | collective-permute-start | bytes 393224 | tf_op jit(solution)/shard_map/ppermute | solution.py:222
  17.0 6.1 %all-to-all-done.gated = bf16[8,64,128]{2,1,0:T(8,128)(2,1)S(1)} async-done(((bf16[8,64,128]{2,1,0:T(8,128)(2,1)}), bf16[8,64,128]{2,1,0:T(8,128)(2,1)S(1)}, u32[]{:S(2)}, u32[]{:S(2)}) %all-to-all-start) | async-done | bytes 131104 | tf_op jit(solution)/shard_map/all_to_all | solution.py:294
  23.2 0.0 collective-permute-done.3.refs_3_
  23.2 0.0 collective-permute-done.4.refs_7_
  23.2 0.0 copy-done
  23.2 0.0 copy-done.1
  23.2 2.6 %score.1 = (bf16[64,512]{1,0:T(8,128)(2,1)}, f32[8,1,128]{2,1,0:T(1,128)S(1)}) custom-call(s32[1,256]{1,0:T(1,128)S(1)} %get-tuple-element.13.wanted, bf16[8,64,128]{2,1,0:T(8,128)(2,1)S(1)} %all-to-all-done.gated, bf16[64,1024]{1,0:T(8,128)(2,1)S(1)} %get-tuple-element.16.chosen.refs_0_, bf16[64,1024]{1,0:T(8,128)(2,1)S(1)} %collective-permute-done.refs_1_, ...), custom_call_target="tpu_custom_call" | custom-call | flops 1207959552 | bytes 4194304 | tf_op jit(solution)/shard_map/score/pallas_call | solution.py:296
  25.9 9.7 %all_to_all.10 = f32[8,1,128]{2,1,0:T(1,128)S(1)} all-to-all(f32[8,1,128]{2,1,0:T(1,128)S(1)} %get-tuple-element.23), channel_id=1, replica_groups=mesh['groups'=2,'item'=4,'dp'=2,'tensor'=2] {'item','tensor'}, dimensions={0} | all-to-all | bytes 8192 | tf_op jit(solution)/shard_map/all_to_all | solution.py:328
  35.6 0.6 %log_subtract_fusion = f32[64]{0:T(128)} fusion(f32[128]{0:T(128)S(1)} %reduce_sum.9), kind=kLoop, calls=%fused_computation | loop fusion | flops 64 | bytes 768 | tf_op jit(solution)/shard_map/sub | solution.py:330
  (1 shorter events, 0.0 us)
Async XLA Ops:
  0.6 22.6 %collective-permute-start.4 = (bf16[1024,1024]{1,0:T(8,128)(2,1)}, bf16[1024,1024]{1,0:T(8,128)(2,1)}, u32[]{:S(2)}, u32[]{:S(2)}) collective-permute-start(bf16[1024,1024]{1,0:T(8,128)(2,1)} %refs_6_.1), channel_id=1, source_target_pairs={{0,2},{2,0},{1,3},{3,1},{4,6},{6,4},{5,7},{7,5},{8,10},{10,8},{9,1... | collective-permute-start | bytes 6291464 | tf_op jit(solution)/shard_map/ppermute | solution.py:222
  1.1 15.2 %collective-permute-start.2 = (bf16[128,1024]{1,0:T(8,128)(2,1)}, bf16[128,1024]{1,0:T(8,128)(2,1)S(1)}, u32[]{:S(2)}, u32[]{:S(2)}) collective-permute-start(bf16[128,1024]{1,0:T(8,128)(2,1)} %refs_4_.1), channel_id=1, source_target_pairs={{0,1},{1,0},{2,3},{3,2},{4,5},{5,4},{6,7},{7,6},{8,9},{9,8},{10,11... | collective-permute-start | bytes 786440 | tf_op jit(solution)/shard_map/ppermute | solution.py:222
  7.3 15.9 %copy-start = (bf16[1024,1024]{1,0:T(8,128)(2,1)S(1)}, bf16[1024,1024]{1,0:T(8,128)(2,1)}, u32[]{:S(2)}) copy-start(bf16[1024,1024]{1,0:T(8,128)(2,1)} %refs_6_.1) | copy-start | bytes 6291460
  7.4 15.8 %copy-start.1 = (bf16[128,1024]{1,0:T(8,128)(2,1)S(1)}, bf16[128,1024]{1,0:T(8,128)(2,1)}, u32[]{:S(2)}) copy-start(bf16[128,1024]{1,0:T(8,128)(2,1)} %refs_4_.1) | copy-start | bytes 786436
  7.4 8.7 %collective-permute-start = (bf16[64,1024]{1,0:T(8,128)(2,1)S(1)}, bf16[64,1024]{1,0:T(8,128)(2,1)S(1)}, u32[]{:S(2)}, u32[]{:S(2)}) collective-permute-start(bf16[64,1024]{1,0:T(8,128)(2,1)S(1)} %get-tuple-element.16.chosen.refs_0_), channel_id=1, source_target_pairs={{0,8},{4,12},{8,0},{12,4},{1,9},{5,13},{9,1},{13,5},{2,10},{6,14},... | collective-permute-start | bytes 393224 | tf_op jit(solution)/shard_map/ppermute | solution.py:222
  8.3 8.1 %collective-permute-start.1 = (bf16[64,1024]{1,0:T(8,128)(2,1)S(1)}, bf16[64,1024]{1,0:T(8,128)(2,1)S(1)}, u32[]{:S(2)}, u32[]{:S(2)}) collective-permute-start(bf16[64,1024]{1,0:T(8,128)(2,1)S(1)} %get-tuple-element.16.chosen.refs_0_), channel_id=1, source_target_pairs={{0,4},{4,0},{8,12},{12,8},{1,5},{5,1},{9,13},{13,9},{2,6},{6,2},{1... | collective-permute-start | bytes 393224 | tf_op jit(solution)/shard_map/ppermute | solution.py:222
  9.9 13.3 %all-to-all-start = ((bf16[8,64,128]{2,1,0:T(8,128)(2,1)}), bf16[8,64,128]{2,1,0:T(8,128)(2,1)S(1)}, u32[]{:S(2)}, u32[]{:S(2)}) async-start(bf16[8,64,128]{2,1,0:T(8,128)(2,1)} %attend.1), calls=%async_computation | async-start | bytes 262144 | tf_op jit(solution)/shard_map/all_to_all | solution.py:294
  16.4 6.8 %collective-permute-start.3 = (bf16[64,1024]{1,0:T(8,128)(2,1)S(1)}, bf16[64,1024]{1,0:T(8,128)(2,1)S(1)}, u32[]{:S(2)}, u32[]{:S(2)}) collective-permute-start(bf16[64,1024]{1,0:T(8,128)(2,1)S(1)} %collective-permute-done.refs_1_), channel_id=1, source_target_pairs={{0,4},{4,0},{8,12},{12,8},{1,5},{5,1},{9,13},{13,9},{2,6},{6,2},{1... | collective-permute-start | bytes 393224 | tf_op jit(solution)/shard_map/ppermute | solution.py:222

commit v11 on v10

--- a/solution.py
+++ b/solution.py
@@ -10,7 +10,7 @@
 
 DH = 128
 SLOTS = ("item", "dp")
-COLUMN = ("item", "tensor")
+COLUMN = ("tensor", "item")
 NT = (((1,), (1,)), ((), ()))
 MIB = 1024 * 1024
 EVENT_PARTS = 3
@@ -37,14 +37,12 @@
     wanted,
     events_v,
     w_uvqk_v,
-    gated,
-    gated_rows,
+    done,
     packing_s,
     lengths_s,
     positions_v,
     logged_v,
     sems,
-    gated_sems,
 ):
     rows = events.shape[0]
     items_axis, dps = shards
@@ -94,8 +92,7 @@
 
     @pl.when(is_early(item, items_axis))
     def _():
-        attention(limits, events_v, chosen, w_uvqk_v, gated_rows)
-        hand_out(gated_rows, gated, gated_sems)
+        attention(limits, events_v, chosen, w_uvqk_v, done)
 
 
 def attention(limits, events, own, w_uvqk, store):
@@ -125,23 +122,22 @@
     return item * 4 < items_axis
 
 
-def hand_out(rows, gated, sems):
+def attend_kernel(items_axis, limits, events, chosen, w_uvqk, done, gated, rows, sems):
+    early = is_early(lax.axis_index("item"), items_axis)
+
+    @pl.when(early)
+    def _():
+        rows[...] = done[...]
+
+    @pl.when(jnp.logical_not(early))
+    def _():
+        attention(limits, events, chosen, w_uvqk, rows)
+
     copies = [pltpu.make_async_copy(rows, gated.at[k], sems.at[k]) for k in range(gated.shape[0])]
     for copy in copies:
         copy.start()
     for copy in copies:
         copy.wait()
-
-
-def attend_kernel(
-    items_axis, limits, events, chosen, w_uvqk, gated_in, gated, rows, sems
-):
-    del gated_in
-
-    @pl.when(jnp.logical_not(is_early(lax.axis_index("item"), items_axis)))
-    def _():
-        attention(limits, events, chosen, w_uvqk, rows)
-        hand_out(rows, gated, sems)
 
 
 def score_kernel(sizes, wanted, gated, *refs):
@@ -160,13 +156,13 @@
     imps = chosen[0].shape[0]
     items = catalogue[0].shape[0]
     step_rows = min(256, items_axis * imps)
-    step_items = min(256, items)
+    step_items = min(512, items)
     steps = range(0, items, step_items)
     slot_rounds, tensor_rounds = rounds(items_axis), rounds(tensors)
     local_width = w_out[0].shape[0]
     for k in range(items_axis):
         for t in range(tensors):
-            sender = (item ^ slot_rounds[k]) * tensors + (tensor ^ tensor_rounds[t])
+            sender = (tensor ^ tensor_rounds[t]) * items_axis + (item ^ slot_rounds[k])
             gates[k * imps : (k + 1) * imps, t * local_width : (t + 1) * local_width] = gated[sender]
     w_whole = jnp.concatenate([w[...] for w in w_out], axis=0)
     mixed = jnp.dot(gates[...], w_whole, preferred_element_type=jnp.float32)
@@ -210,7 +206,7 @@
                 [v[:, part * imps : (part + 1) * imps] for v in (total, target)], axis=1
             )
             for t in range(tensors):
-                sums[owner * tensors + t] = both
+                sums[t * items_axis + owner] = both
     state_copy.wait()
 
 
@@ -248,7 +244,7 @@
 
     other_catalogues, _ = from_others(catalogue, "dp", dps)
     other_w_out, _ = from_others(w_out, "tensor", tensors)
-    chosen, limits, wanted, events, w_uvqk, gated = pl.pallas_call(
+    chosen, limits, wanted, events, w_uvqk, done = pl.pallas_call(
         functools.partial(pick_kernel, (items_axis, dps)),
         out_shape=(
             jax.ShapeDtypeStruct((imps, width), jnp.bfloat16),
@@ -256,18 +252,16 @@
             jax.ShapeDtypeStruct((1, items_axis * imps), jnp.int32),
             jax.ShapeDtypeStruct(events.shape, events.dtype),
             jax.ShapeDtypeStruct(w_uvqk.shape, w_uvqk.dtype),
-            pltpu.HBM((receivers, imps, local_width), jnp.bfloat16),
+            jax.ShapeDtypeStruct((imps, local_width), jnp.bfloat16),
         ),
         in_specs=[hbm] * 6,
-        out_specs=(vmem,) * 5 + (hbm,),
+        out_specs=(vmem,) * 6,
         scratch_shapes=[
-            pltpu.VMEM((imps, local_width), jnp.bfloat16),
             pltpu.SMEM((hists,), jnp.int32),
             pltpu.SMEM((hists,), jnp.int32),
             pltpu.VMEM((hists, imps), jnp.int32),
             pltpu.VMEM((hists, imps), jnp.int32),
             pltpu.SemaphoreType.DMA((5 + EVENT_PARTS,)),
-            pltpu.SemaphoreType.DMA((receivers,)),
         ],
         compiler_params=params,
         cost_estimate=pl.CostEstimate(
@@ -279,18 +273,17 @@
 
     gated = pl.pallas_call(
         functools.partial(attend_kernel, items_axis),
-        out_shape=jax.ShapeDtypeStruct(gated.shape, gated.dtype),
-        in_specs=[vmem] * 4 + [hbm],
+        out_shape=pltpu.HBM((receivers, imps, local_width), jnp.bfloat16),
+        in_specs=[vmem] * 5,
         out_specs=hbm,
         scratch_shapes=[
             pltpu.VMEM((imps, local_width), jnp.bfloat16),
             pltpu.SemaphoreType.DMA((receivers,)),
         ],
-        input_output_aliases={4: 0},
         compiler_params=params,
         cost_estimate=pl.CostEstimate(flops=0, bytes_accessed=0, transcendentals=0),
         name="attend",
-    )(limits, events, chosen, w_uvqk, in_hbm(gated))
+    )(limits, events, chosen, w_uvqk, done)
     all_gated = lax.all_to_all(gated, COLUMN, split_axis=0, concat_axis=0, tiled=True)
 
     state, sums = pl.pallas_call(

time: 36.5 us -> 36.2 us (level)
  starting transfers between devices: 11.2 us -> 10.3 us
  waiting for transfers between devices: 7.59 us -> 8.08 us
    all_to_all x1, starting transfers between devices: 5 us -> 3.7 us  [local(): lax.all_to_all(gated, COLUMN, split_axis=0, concat_axis=0, tiled=True)]
    pallas_call x1, Pallas kernels: 3.62 us -> 2.89 us  [local(): pl.pallas_call(functools.partial(pick_kernel, (items_axis, dps)), out_sha...]
    pallas_call x1, Pallas kernels: 0.07 us -> 0.72 us  [local(): pl.pallas_call(functools.partial(attend_kernel, items_axis), out_shape=pl...]
    ppermute x5, waiting for transfers between devices: 1.44 us -> 2.06 us  [send(): return lax.ppermute(x, axes, [(i, i ^ r) for i in range(count)])]
where the time goes in v11:
time: 36.2 us; the launch traced here: 35.9 us
  starting transfers between devices  10.3 us (28%)
  blocking collectives  9.72 us (27%)
  waiting for transfers between devices  8.08 us (22%)
  Pallas kernels  6.52 us (18%)
  between operations  0.69 us (2%)
  other arithmetic  0.61 us (2%)
    all_to_all x1, blocking collectives, local(): sums = lax.all_to_all(sums, COLUMN, split_axis=0, concat_axis=0, tiled=True)  9.72 us
    ppermute x5, starting transfers between devices, send(): return lax.ppermute(x, axes, [(i, i ^ r) for i in range(count)])  6.57 us
    all_to_all x1, waiting for transfers between devices, local(): lax.all_to_all(gated, COLUMN, split_axis=0, concat_axis=0, tiled=True)  6.02 us
    all_to_all x1, starting transfers between devices, local(): lax.all_to_all(gated, COLUMN, split_axis=0, concat_axis=0, tiled=True)  3.7 us
    pallas_call x1, Pallas kernels, local(): pl.pallas_call(functools.partial(score_kernel, (items_axis, dps, tensors)...  2.9 us
    pallas_call x1, Pallas kernels, local(): pl.pallas_call(functools.partial(pick_kernel, (items_axis, dps)), out_sha...  2.89 us
    ppermute x5, waiting for transfers between devices, send(): return lax.ppermute(x, axes, [(i, i ^ r) for i in range(count)])  2.06 us
    pallas_call x1, Pallas kernels, local(): pl.pallas_call(functools.partial(attend_kernel, items_axis), out_shape=pl...  0.72 us
  transfers between devices with their start and end apart: 6, of which 3 were waited for; matrix products, arithmetic and copies ran while one was open for 0% of the time, Pallas kernels for 10%

profile of v11, /device:TPU:0, one launch (start us, length us, event | category | flops | bytes accessed | tf_op | source)
XLA Modules:
  0.0 35.9 jit_solution(11348709727240255982)
XLA Ops:
  0.6 0.5 %collective-permute-start.4 = (bf16[1024,1024]{1,0:T(8,128)(2,1)}, bf16[1024,1024]{1,0:T(8,128)(2,1)}, u32[]{:S(2)}, u32[]{:S(2)}) collective-permute-start(bf16[1024,1024]{1,0:T(8,128)(2,1)} %refs_6_.1), channel_id=1, source_target_pairs={{0,2},{2,0},{1,3},{3,1},{4,6},{6,4},{5,7},{7,5},{8,10},{10,8},{9,1... | collective-permute-start | bytes 6291464 | tf_op jit(solution)/shard_map/ppermute | solution.py:218
  1.1 2.6 %collective-permute-start.2 = (bf16[128,1024]{1,0:T(8,128)(2,1)}, bf16[128,1024]{1,0:T(8,128)(2,1)S(1)}, u32[]{:S(2)}, u32[]{:S(2)}) collective-permute-start(bf16[128,1024]{1,0:T(8,128)(2,1)} %refs_4_.1), channel_id=1, source_target_pairs={{0,1},{1,0},{2,3},{3,2},{4,5},{5,4},{6,7},{7,6},{8,9},{9,8},{10,11... | collective-permute-start | bytes 786440 | tf_op jit(solution)/shard_map/ppermute | solution.py:218
  3.7 2.9 %pick.1 = (bf16[64,1024]{1,0:T(8,128)(2,1)S(1)}, s32[64,128]{1,0:T(8,128)S(1)}, s32[1,256]{1,0:T(1,128)S(1)}, bf16[768,1024]{1,0:T(8,128)(2,1)S(1)}, bf16[1024,5...) custom-call(s32[8]{0:T(128)} %packing.1, s32[8]{0:T(128)} %lengths.1, s32[8,64]{1,0:T(8,128)} %positions.1, ...), custom_call_target="tpu_custom_call" | custom-call | flops 100663296 | bytes 1572864 | tf_op jit(solution)/shard_map/pick/pallas_call | solution.py:247
  6.6 0.0 copy-start
  6.6 0.0 copy-start.1
  6.6 1.6 %collective-permute-start = (bf16[64,1024]{1,0:T(8,128)(2,1)S(1)}, bf16[64,1024]{1,0:T(8,128)(2,1)S(1)}, u32[]{:S(2)}, u32[]{:S(2)}) collective-permute-start(bf16[64,1024]{1,0:T(8,128)(2,1)S(1)} %get-tuple-element.16.chosen.refs_0_), channel_id=1, source_target_pairs={{0,8},{4,12},{8,0},{12,4},{1,9},{5,13},{9,1},{13,5},{2,10},{6,14},... | collective-permute-start | bytes 393224 | tf_op jit(solution)/shard_map/ppermute | solution.py:218
  8.2 1.6 %collective-permute-start.1 = (bf16[64,1024]{1,0:T(8,128)(2,1)S(1)}, bf16[64,1024]{1,0:T(8,128)(2,1)S(1)}, u32[]{:S(2)}, u32[]{:S(2)}) collective-permute-start(bf16[64,1024]{1,0:T(8,128)(2,1)S(1)} %get-tuple-element.16.chosen.refs_0_), channel_id=1, source_target_pairs={{0,4},{4,0},{8,12},{12,8},{1,5},{5,1},{9,13},{13,9},{2,6},{6,2},{1... | collective-permute-start | bytes 393224 | tf_op jit(solution)/shard_map/ppermute | solution.py:218
  9.8 0.7 %attend.1 = bf16[8,64,128]{2,1,0:T(8,128)(2,1)} custom-call(s32[64,128]{1,0:T(8,128)S(1)} %get-tuple-element.14.limits, bf16[768,1024]{1,0:T(8,128)(2,1)S(1)} %get-tuple-element.15.events, bf16[64,1024]{1,0:T(8,128)(2,1)S(1)} %get-tuple-element.16.chosen.refs_0_, bf16[1024,512]{1,0:T(8,128)(2,1)S(1)} %get-tuple-element.17.w_uvqk, ...), custom_call_target="tpu_custom_call" | custom-call | tf_op jit(solution)/shard_map/attend/pallas_call | solution.py:274
  10.5 3.7 %all-to-all-start = ((bf16[8,64,128]{2,1,0:T(8,128)(2,1)}), bf16[8,64,128]{2,1,0:T(8,128)(2,1)S(1)}, u32[]{:S(2)}, u32[]{:S(2)}) async-start(bf16[8,64,128]{2,1,0:T(8,128)(2,1)} %attend.1), calls=%async_computation | async-start | bytes 262144 | tf_op jit(solution)/shard_map/all_to_all | solution.py:287
  14.2 1.8 %collective-permute-done.refs_1_ = bf16[64,1024]{1,0:T(8,128)(2,1)S(1)} collective-permute-done((bf16[64,1024]{1,0:T(8,128)(2,1)S(1)}, bf16[64,1024]{1,0:T(8,128)(2,1)S(1)}, u32[]{:S(2)}, u32[]{:S(2)}) %collective-permute-start) | collective-permute-done | bytes 131104 | tf_op jit(solution)/shard_map/ppermute | solution.py:218
  16.0 0.3 collective-permute-done.1.refs_2_
  16.3 0.0 collective-permute-done.2.refs_5_
  16.3 0.4 collective-permute-start.3
  16.6 6.0 %all-to-all-done.gated = bf16[8,64,128]{2,1,0:T(8,128)(2,1)S(1)} async-done(((bf16[8,64,128]{2,1,0:T(8,128)(2,1)}), bf16[8,64,128]{2,1,0:T(8,128)(2,1)S(1)}, u32[]{:S(2)}, u32[]{:S(2)}) %all-to-all-start) | async-done | bytes 131104 | tf_op jit(solution)/shard_map/all_to_all | solution.py:287
  22.7 0.0 collective-permute-done.3.refs_3_
  22.7 0.0 collective-permute-done.4.refs_7_
  22.7 0.0 copy-done
  22.7 0.0 copy-done.1
  22.7 2.9 %score.1 = (bf16[64,512]{1,0:T(8,128)(2,1)}, f32[8,1,128]{2,1,0:T(1,128)S(1)}) custom-call(s32[1,256]{1,0:T(1,128)S(1)} %get-tuple-element.13.wanted, bf16[8,64,128]{2,1,0:T(8,128)(2,1)S(1)} %all-to-all-done.gated, bf16[64,1024]{1,0:T(8,128)(2,1)S(1)} %get-tuple-element.16.chosen.refs_0_, bf16[64,1024]{1,0:T(8,128)(2,1)S(1)} %collective-permute-done.refs_1_, ...), custom_call_target="tpu_custom_call" | custom-call | flops 1207959552 | bytes 4194304 | tf_op jit(solution)/shard_map/score/pallas_call | solution.py:289
  25.6 9.7 %all_to_all.10 = f32[8,1,128]{2,1,0:T(1,128)S(1)} all-to-all(f32[8,1,128]{2,1,0:T(1,128)S(1)} %get-tuple-element.23), channel_id=1, replica_groups=mesh['groups'=2,'item'=4,'dp'=2,'tensor'=2] {'tensor','item'}, dimensions={0} | all-to-all | bytes 8192 | tf_op jit(solution)/shard_map/all_to_all | solution.py:321
  35.3 0.6 %log_subtract_fusion = f32[64]{0:T(128)} fusion(f32[128]{0:T(128)S(1)} %reduce_sum.9), kind=kLoop, calls=%fused_computation | loop fusion | flops 64 | bytes 768 | tf_op jit(solution)/shard_map/sub | solution.py:323
  (1 shorter events, 0.0 us)
Async XLA Ops:
  0.6 22.0 %collective-permute-start.4 = (bf16[1024,1024]{1,0:T(8,128)(2,1)}, bf16[1024,1024]{1,0:T(8,128)(2,1)}, u32[]{:S(2)}, u32[]{:S(2)}) collective-permute-start(bf16[1024,1024]{1,0:T(8,128)(2,1)} %refs_6_.1), channel_id=1, source_target_pairs={{0,2},{2,0},{1,3},{3,1},{4,6},{6,4},{5,7},{7,5},{8,10},{10,8},{9,1... | collective-permute-start | bytes 6291464 | tf_op jit(solution)/shard_map/ppermute | solution.py:218
  1.1 15.1 %collective-permute-start.2 = (bf16[128,1024]{1,0:T(8,128)(2,1)}, bf16[128,1024]{1,0:T(8,128)(2,1)S(1)}, u32[]{:S(2)}, u32[]{:S(2)}) collective-permute-start(bf16[128,1024]{1,0:T(8,128)(2,1)} %refs_4_.1), channel_id=1, source_target_pairs={{0,1},{1,0},{2,3},{3,2},{4,5},{5,4},{6,7},{7,6},{8,9},{9,8},{10,11... | collective-permute-start | bytes 786440 | tf_op jit(solution)/shard_map/ppermute | solution.py:218
  6.6 16.0 %copy-start = (bf16[1024,1024]{1,0:T(8,128)(2,1)S(1)}, bf16[1024,1024]{1,0:T(8,128)(2,1)}, u32[]{:S(2)}) copy-start(bf16[1024,1024]{1,0:T(8,128)(2,1)} %refs_6_.1) | copy-start | bytes 6291460
  6.6 16.0 %copy-start.1 = (bf16[128,1024]{1,0:T(8,128)(2,1)S(1)}, bf16[128,1024]{1,0:T(8,128)(2,1)}, u32[]{:S(2)}) copy-start(bf16[128,1024]{1,0:T(8,128)(2,1)} %refs_4_.1) | copy-start | bytes 786436
  6.6 9.4 %collective-permute-start = (bf16[64,1024]{1,0:T(8,128)(2,1)S(1)}, bf16[64,1024]{1,0:T(8,128)(2,1)S(1)}, u32[]{:S(2)}, u32[]{:S(2)}) collective-permute-start(bf16[64,1024]{1,0:T(8,128)(2,1)S(1)} %get-tuple-element.16.chosen.refs_0_), channel_id=1, source_target_pairs={{0,8},{4,12},{8,0},{12,4},{1,9},{5,13},{9,1},{13,5},{2,10},{6,14},... | collective-permute-start | bytes 393224 | tf_op jit(solution)/shard_map/ppermute | solution.py:218
  8.2 8.1 %collective-permute-start.1 = (bf16[64,1024]{1,0:T(8,128)(2,1)S(1)}, bf16[64,1024]{1,0:T(8,128)(2,1)S(1)}, u32[]{:S(2)}, u32[]{:S(2)}) collective-permute-start(bf16[64,1024]{1,0:T(8,128)(2,1)S(1)} %get-tuple-element.16.chosen.refs_0_), channel_id=1, source_target_pairs={{0,4},{4,0},{8,12},{12,8},{1,5},{5,1},{9,13},{13,9},{2,6},{6,2},{1... | collective-permute-start | bytes 393224 | tf_op jit(solution)/shard_map/ppermute | solution.py:218
  10.5 12.1 %all-to-all-start = ((bf16[8,64,128]{2,1,0:T(8,128)(2,1)}), bf16[8,64,128]{2,1,0:T(8,128)(2,1)S(1)}, u32[]{:S(2)}, u32[]{:S(2)}) async-start(bf16[8,64,128]{2,1,0:T(8,128)(2,1)} %attend.1), calls=%async_computation | async-start | bytes 262144 | tf_op jit(solution)/shard_map/all_to_all | solution.py:287
  16.3 6.4 %collective-permute-start.3 = (bf16[64,1024]{1,0:T(8,128)(2,1)S(1)}, bf16[64,1024]{1,0:T(8,128)(2,1)S(1)}, u32[]{:S(2)}, u32[]{:S(2)}) collective-permute-start(bf16[64,1024]{1,0:T(8,128)(2,1)S(1)} %collective-permute-done.refs_1_), channel_id=1, source_target_pairs={{0,4},{4,0},{8,12},{12,8},{1,5},{5,1},{9,13},{13,9},{2,6},{6,2},{1... | collective-permute-start | bytes 393224 | tf_op jit(solution)/shard_map/ppermute | solution.py:218

commit v12 on v11

--- a/solution.py
+++ b/solution.py
@@ -156,7 +156,7 @@
     imps = chosen[0].shape[0]
     items = catalogue[0].shape[0]
     step_rows = min(256, items_axis * imps)
-    step_items = min(512, items)
+    step_items = min(128, items)
     steps = range(0, items, step_items)
     slot_rounds, tensor_rounds = rounds(items_axis), rounds(tensors)
     local_width = w_out[0].shape[0]
@@ -218,17 +218,15 @@
     return lax.ppermute(x, axes, [(i, i ^ r) for i in range(count)])
 
 
-def from_others(x, axes, count, beside=()):
+def from_others(x, axes, count):
     pieces = {}
     for r in rounds(count)[1:]:
         if r & 3 == 3:
-            held, pieces[r - 2], beside = lax.optimization_barrier(
-                (pieces[r - 1], pieces[r - 2], beside)
-            )
+            held, pieces[r - 2] = lax.optimization_barrier((pieces[r - 1], pieces[r - 2]))
             pieces[r] = send(held, axes, count, 1)
         else:
             pieces[r] = send(x, axes, count, r)
-    return list(pieces.values()), beside
+    return list(pieces.values())
 
 
 def local(events, lengths, packing, positions, logged, w_uvqk, w_out, catalogue):
@@ -242,8 +240,8 @@
     params = pltpu.CompilerParams(vmem_limit_bytes=(12 + 2 * items_axis) * MIB)
     vmem, hbm = spec(pltpu.VMEM), spec(pltpu.HBM)
 
-    other_catalogues, _ = from_others(catalogue, "dp", dps)
-    other_w_out, _ = from_others(w_out, "tensor", tensors)
+    other_catalogues = from_others(catalogue, "dp", dps)
+    other_w_out = from_others(w_out, "tensor", tensors)
     chosen, limits, wanted, events, w_uvqk, done = pl.pallas_call(
         functools.partial(pick_kernel, (items_axis, dps)),
         out_shape=(
@@ -269,7 +267,7 @@
         ),
         name="pick",
     )(*(in_hbm(x) for x in (packing, lengths, positions, logged, events, w_uvqk)))
-    other_chosen, other_w_out = from_others(chosen, "item", items_axis, other_w_out)
+    other_chosen = from_others(chosen, "item", items_axis)
 
     gated = pl.pallas_call(
         functools.partial(attend_kernel, items_axis),

time: 36.2 us -> 36.5 us (level)
  waiting for transfers between devices: 8.08 us -> 6.4 us
  starting transfers between devices: 10.3 us -> 11.9 us
  Pallas kernels: 6.52 us -> 6.99 us
    ppermute x5, waiting for transfers between devices: 2.06 us -> 0.01 us  [send(): return lax.ppermute(x, axes, [(i, i ^ r) for i in range(count)])]
    ppermute x5, starting transfers between devices: 6.57 us -> 8.24 us  [send(): return lax.ppermute(x, axes, [(i, i ^ r) for i in range(count)])]
    pallas_call x1, Pallas kernels: 2.9 us -> 3.37 us  [local(): pl.pallas_call(functools.partial(score_kernel, (items_axis, dps, tensors)...]
    all_to_all x1, waiting for transfers between devices: 6.02 us -> 6.39 us  [local(): lax.all_to_all(gated, COLUMN, split_axis=0, concat_axis=0, tiled=True)]
  transfers between devices with their start and end apart: 6 -> 6, of which waited for: 3 -> 1; matrix products, arithmetic and copies ran while one was open for 0% -> 0% of each run, Pallas kernels for 10% -> 10%
where the time goes in v12:
time: 36.5 us; the launch traced here: 36.2 us
  starting transfers between devices  11.9 us (33%)
  blocking collectives  9.51 us (26%)
  Pallas kernels  6.99 us (19%)
  waiting for transfers between devices  6.4 us (18%)
  between operations  0.7 us (2%)
  other arithmetic  0.61 us (2%)
    all_to_all x1, blocking collectives, local(): sums = lax.all_to_all(sums, COLUMN, split_axis=0, concat_axis=0, tiled=True)  9.51 us
    ppermute x5, starting transfers between devices, send(): return lax.ppermute(x, axes, [(i, i ^ r) for i in range(count)])  8.24 us
    all_to_all x1, waiting for transfers between devices, local(): lax.all_to_all(gated, COLUMN, split_axis=0, concat_axis=0, tiled=True)  6.39 us
    all_to_all x1, starting transfers between devices, local(): lax.all_to_all(gated, COLUMN, split_axis=0, concat_axis=0, tiled=True)  3.69 us
    pallas_call x1, Pallas kernels, local(): pl.pallas_call(functools.partial(score_kernel, (items_axis, dps, tensors)...  3.37 us
    pallas_call x1, Pallas kernels, local(): pl.pallas_call(functools.partial(pick_kernel, (items_axis, dps)), out_sha...  2.89 us
  transfers between devices with their start and end apart: 6, of which 1 were waited for; matrix products, arithmetic and copies ran while one was open for 0% of the time, Pallas kernels for 10%

profile of v12, /device:TPU:0, one launch (start us, length us, event | category | flops | bytes accessed | tf_op | source)
XLA Modules:
  0.0 36.2 jit_solution(3099379764260338488)
XLA Ops:
  0.6 0.0 copy-start.1
  0.6 0.5 %collective-permute-start.4 = (bf16[1024,1024]{1,0:T(8,128)(2,1)}, bf16[1024,1024]{1,0:T(8,128)(2,1)}, u32[]{:S(2)}, u32[]{:S(2)}) collective-permute-start(bf16[1024,1024]{1,0:T(8,128)(2,1)} %refs_6_.1), channel_id=1, source_target_pairs={{0,2},{2,0},{1,3},{3,1},{4,6},{6,4},{5,7},{7,5},{8,10},{10,8},{9,1... | collective-permute-start | bytes 6291464 | tf_op jit(solution)/shard_map/ppermute | solution.py:218
  1.2 2.9 %pick.1 = (bf16[64,1024]{1,0:T(8,128)(2,1)S(1)}, s32[64,128]{1,0:T(8,128)S(1)}, s32[1,256]{1,0:T(1,128)S(1)}, bf16[768,1024]{1,0:T(8,128)(2,1)S(1)}, bf16[1024,5...) custom-call(s32[8]{0:T(128)} %packing.1, s32[8]{0:T(128)} %lengths.1, s32[8,64]{1,0:T(8,128)} %positions.1, ...), custom_call_target="tpu_custom_call" | custom-call | flops 100663296 | bytes 1572864 | tf_op jit(solution)/shard_map/pick/pallas_call | solution.py:245
  4.1 0.0 copy-start
  4.1 2.6 %collective-permute-start = (bf16[64,1024]{1,0:T(8,128)(2,1)S(1)}, bf16[64,1024]{1,0:T(8,128)(2,1)S(1)}, u32[]{:S(2)}, u32[]{:S(2)}) collective-permute-start(bf16[64,1024]{1,0:T(8,128)(2,1)S(1)} %get-tuple-element.15.chosen.refs_0_), channel_id=1, source_target_pairs={{0,8},{4,12},{8,0},{12,4},{1,9},{5,13},{9,1},{13,5},{2,10},{6,14},... | collective-permute-start | bytes 393224 | tf_op jit(solution)/shard_map/ppermute | solution.py:218
  6.6 1.6 %collective-permute-start.1 = (bf16[64,1024]{1,0:T(8,128)(2,1)S(1)}, bf16[64,1024]{1,0:T(8,128)(2,1)S(1)}, u32[]{:S(2)}, u32[]{:S(2)}) collective-permute-start(bf16[64,1024]{1,0:T(8,128)(2,1)S(1)} %get-tuple-element.15.chosen.refs_0_), channel_id=1, source_target_pairs={{0,4},{4,0},{8,12},{12,8},{1,5},{5,1},{9,13},{13,9},{2,6},{6,2},{1... | collective-permute-start | bytes 393224 | tf_op jit(solution)/shard_map/ppermute | solution.py:218
  8.2 0.0 copy-done.1
  8.2 1.5 %collective-permute-start.3 = (bf16[128,1024]{1,0:T(8,128)(2,1)S(1)}, bf16[128,1024]{1,0:T(8,128)(2,1)S(1)}, u32[]{:S(2)}, u32[]{:S(2)}) collective-permute-start(bf16[128,1024]{1,0:T(8,128)(2,1)S(1)} %copy-done.1), channel_id=1, source_target_pairs={{0,1},{1,0},{2,3},{3,2},{4,5},{5,4},{6,7},{7,6},{8,9},{9,8},{10,11... | collective-permute-start | bytes 786440 | tf_op jit(solution)/shard_map/ppermute | solution.py:218
  9.7 0.7 %attend.1 = bf16[8,64,128]{2,1,0:T(8,128)(2,1)} custom-call(s32[64,128]{1,0:T(8,128)S(1)} %get-tuple-element.13.limits, bf16[768,1024]{1,0:T(8,128)(2,1)S(1)} %get-tuple-element.14.events, bf16[64,1024]{1,0:T(8,128)(2,1)S(1)} %get-tuple-element.15.chosen.refs_0_, bf16[1024,512]{1,0:T(8,128)(2,1)S(1)} %get-tuple-element.16.w_uvqk, ...), custom_call_target="tpu_custom_call" | custom-call | tf_op jit(solution)/shard_map/attend/pallas_call | solution.py:272
  10.5 3.7 %all-to-all-start = ((bf16[8,64,128]{2,1,0:T(8,128)(2,1)}), bf16[8,64,128]{2,1,0:T(8,128)(2,1)S(1)}, u32[]{:S(2)}, u32[]{:S(2)}) async-start(bf16[8,64,128]{2,1,0:T(8,128)(2,1)} %attend.1), calls=%async_computation | async-start | bytes 262144 | tf_op jit(solution)/shard_map/all_to_all | solution.py:285
  14.1 0.0 collective-permute-done.refs_1_
  14.2 0.0 collective-permute-done.1.refs_2_
  14.2 2.1 %collective-permute-start.2 = (bf16[64,1024]{1,0:T(8,128)(2,1)S(1)}, bf16[64,1024]{1,0:T(8,128)(2,1)S(1)}, u32[]{:S(2)}, u32[]{:S(2)}) collective-permute-start(bf16[64,1024]{1,0:T(8,128)(2,1)S(1)} %collective-permute-done.refs_1_), channel_id=1, source_target_pairs={{0,4},{4,0},{8,12},{12,8},{1,5},{5,1},{9,13},{13,9},{2,6},{6,2},{1... | collective-permute-start | bytes 393224 | tf_op jit(solution)/shard_map/ppermute | solution.py:218
  16.2 6.4 %all-to-all-done.gated = bf16[8,64,128]{2,1,0:T(8,128)(2,1)S(1)} async-done(((bf16[8,64,128]{2,1,0:T(8,128)(2,1)}), bf16[8,64,128]{2,1,0:T(8,128)(2,1)S(1)}, u32[]{:S(2)}, u32[]{:S(2)}) %all-to-all-start) | async-done | bytes 131104 | tf_op jit(solution)/shard_map/all_to_all | solution.py:285
  22.6 0.0 collective-permute-done.2.refs_3_
  22.6 0.0 collective-permute-done.3.refs_5_
  22.6 0.0 collective-permute-done.4.refs_7_
  22.6 0.0 copy-done
  22.7 3.4 %score.1 = (bf16[64,512]{1,0:T(8,128)(2,1)}, f32[8,1,128]{2,1,0:T(1,128)S(1)}) custom-call(s32[1,256]{1,0:T(1,128)S(1)} %get-tuple-element.12.wanted, bf16[8,64,128]{2,1,0:T(8,128)(2,1)S(1)} %all-to-all-done.gated, bf16[64,1024]{1,0:T(8,128)(2,1)S(1)} %get-tuple-element.15.chosen.refs_0_, bf16[64,1024]{1,0:T(8,128)(2,1)S(1)} %collective-permute-done.refs_1_, ...), custom_call_target="tpu_custom_call" | custom-call | flops 1207959552 | bytes 4194304 | tf_op jit(solution)/shard_map/score/pallas_call | solution.py:287
  26.0 9.5 %all_to_all.10 = f32[8,1,128]{2,1,0:T(1,128)S(1)} all-to-all(f32[8,1,128]{2,1,0:T(1,128)S(1)} %get-tuple-element.21), channel_id=1, replica_groups=mesh['groups'=2,'item'=4,'dp'=2,'tensor'=2] {'tensor','item'}, dimensions={0} | all-to-all | bytes 8192 | tf_op jit(solution)/shard_map/all_to_all | solution.py:319
  35.6 0.6 %log_subtract_fusion = f32[64]{0:T(128)} fusion(f32[128]{0:T(128)S(1)} %reduce_sum.9), kind=kLoop, calls=%fused_computation | loop fusion | flops 64 | bytes 768 | tf_op jit(solution)/shard_map/sub | solution.py:321
  (1 shorter events, 0.0 us)
Async XLA Ops:
  0.6 7.6 %copy-start.1 = (bf16[128,1024]{1,0:T(8,128)(2,1)S(1)}, bf16[128,1024]{1,0:T(8,128)(2,1)}, u32[]{:S(2)}) copy-start(bf16[128,1024]{1,0:T(8,128)(2,1)} %refs_4_.1) | copy-start | bytes 786436
  0.6 22.0 %collective-permute-start.4 = (bf16[1024,1024]{1,0:T(8,128)(2,1)}, bf16[1024,1024]{1,0:T(8,128)(2,1)}, u32[]{:S(2)}, u32[]{:S(2)}) collective-permute-start(bf16[1024,1024]{1,0:T(8,128)(2,1)} %refs_6_.1), channel_id=1, source_target_pairs={{0,2},{2,0},{1,3},{3,1},{4,6},{6,4},{5,7},{7,5},{8,10},{10,8},{9,1... | collective-permute-start | bytes 6291464 | tf_op jit(solution)/shard_map/ppermute | solution.py:218
  4.1 18.6 %copy-start = (bf16[1024,1024]{1,0:T(8,128)(2,1)S(1)}, bf16[1024,1024]{1,0:T(8,128)(2,1)}, u32[]{:S(2)}) copy-start(bf16[1024,1024]{1,0:T(8,128)(2,1)} %refs_6_.1) | copy-start | bytes 6291460
  4.1 10.1 %collective-permute-start = (bf16[64,1024]{1,0:T(8,128)(2,1)S(1)}, bf16[64,1024]{1,0:T(8,128)(2,1)S(1)}, u32[]{:S(2)}, u32[]{:S(2)}) collective-permute-start(bf16[64,1024]{1,0:T(8,128)(2,1)S(1)} %get-tuple-element.15.chosen.refs_0_), channel_id=1, source_target_pairs={{0,8},{4,12},{8,0},{12,4},{1,9},{5,13},{9,1},{13,5},{2,10},{6,14},... | collective-permute-start | bytes 393224 | tf_op jit(solution)/shard_map/ppermute | solution.py:218
  6.6 7.5 %collective-permute-start.1 = (bf16[64,1024]{1,0:T(8,128)(2,1)S(1)}, bf16[64,1024]{1,0:T(8,128)(2,1)S(1)}, u32[]{:S(2)}, u32[]{:S(2)}) collective-permute-start(bf16[64,1024]{1,0:T(8,128)(2,1)S(1)} %get-tuple-element.15.chosen.refs_0_), channel_id=1, source_target_pairs={{0,4},{4,0},{8,12},{12,8},{1,5},{5,1},{9,13},{13,9},{2,6},{6,2},{1... | collective-permute-start | bytes 393224 | tf_op jit(solution)/shard_map/ppermute | solution.py:218
  8.2 14.4 %collective-permute-start.3 = (bf16[128,1024]{1,0:T(8,128)(2,1)S(1)}, bf16[128,1024]{1,0:T(8,128)(2,1)S(1)}, u32[]{:S(2)}, u32[]{:S(2)}) collective-permute-start(bf16[128,1024]{1,0:T(8,128)(2,1)S(1)} %copy-done.1), channel_id=1, source_target_pairs={{0,1},{1,0},{2,3},{3,2},{4,5},{5,4},{6,7},{7,6},{8,9},{9,8},{10,11... | collective-permute-start | bytes 786440 | tf_op jit(solution)/shard_map/ppermute | solution.py:218
  10.5 12.2 %all-to-all-start = ((bf16[8,64,128]{2,1,0:T(8,128)(2,1)}), bf16[8,64,128]{2,1,0:T(8,128)(2,1)S(1)}, u32[]{:S(2)}, u32[]{:S(2)}) async-start(bf16[8,64,128]{2,1,0:T(8,128)(2,1)} %attend.1), calls=%async_computation | async-start | bytes 262144 | tf_op jit(solution)/shard_map/all_to_all | solution.py:285
  14.2 8.5 %collective-permute-start.2 = (bf16[64,1024]{1,0:T(8,128)(2,1)S(1)}, bf16[64,1024]{1,0:T(8,128)(2,1)S(1)}, u32[]{:S(2)}, u32[]{:S(2)}) collective-permute-start(bf16[64,1024]{1,0:T(8,128)(2,1)S(1)} %collective-permute-done.refs_1_), channel_id=1, source_target_pairs={{0,4},{4,0},{8,12},{12,8},{1,5},{5,1},{9,13},{13,9},{2,6},{6,2},{1... | collective-permute-start | bytes 393224 | tf_op jit(solution)/shard_map/ppermute | solution.py:218

commit v13 on v12

--- a/solution.py
+++ b/solution.py
@@ -36,8 +36,8 @@
     limits,
     wanted,
     events_v,
+    done,
     w_uvqk_v,
-    done,
     packing_s,
     lengths_s,
     positions_v,
@@ -62,11 +62,13 @@
             + [(w_uvqk, w_uvqk_v)]
         )
     ]
-    for copy in copies:
+    for copy in copies[:-1]:
         copy.start()
+    item, dp = lax.axis_index("item"), lax.axis_index("dp")
+    early = is_early(item, items_axis)
+    pl.when(early)(copies[-1].start)
     for copy in copies[:4]:
         copy.wait()
-    item, dp = lax.axis_index("item"), lax.axis_index("dp")
     history = packing_s[item * dps + dp]
     row = positions_v[pl.ds(history, 1), :].astype(jnp.float32)
     diagonal = lax.broadcasted_iota(jnp.int32, (imps, imps), 0) == lax.broadcasted_iota(
@@ -88,10 +90,10 @@
             preferred_element_type=jnp.float32,
         )
     chosen[...] = total.astype(jnp.bfloat16)
-    copies[-1].wait()
-
-    @pl.when(is_early(item, items_axis))
+
+    @pl.when(early)
     def _():
+        copies[-1].wait()
         attention(limits, events_v, chosen, w_uvqk_v, done)
 
 
@@ -156,7 +158,7 @@
     imps = chosen[0].shape[0]
     items = catalogue[0].shape[0]
     step_rows = min(256, items_axis * imps)
-    step_items = min(128, items)
+    step_items = min(256, items)
     steps = range(0, items, step_items)
     slot_rounds, tensor_rounds = rounds(items_axis), rounds(tensors)
     local_width = w_out[0].shape[0]
@@ -242,19 +244,19 @@
 
     other_catalogues = from_others(catalogue, "dp", dps)
     other_w_out = from_others(w_out, "tensor", tensors)
-    chosen, limits, wanted, events, w_uvqk, done = pl.pallas_call(
+    chosen, limits, wanted, events, done = pl.pallas_call(
         functools.partial(pick_kernel, (items_axis, dps)),
         out_shape=(
             jax.ShapeDtypeStruct((imps, width), jnp.bfloat16),
             jax.ShapeDtypeStruct((imps, 128), jnp.int32),
             jax.ShapeDtypeStruct((1, items_axis * imps), jnp.int32),
             jax.ShapeDtypeStruct(events.shape, events.dtype),
-            jax.ShapeDtypeStruct(w_uvqk.shape, w_uvqk.dtype),
             jax.ShapeDtypeStruct((imps, local_width), jnp.bfloat16),
         ),
         in_specs=[hbm] * 6,
-        out_specs=(vmem,) * 6,
+        out_specs=(vmem,) * 5,
         scratch_shapes=[
+            pltpu.VMEM(w_uvqk.shape, w_uvqk.dtype),
             pltpu.SMEM((hists,), jnp.int32),
             pltpu.SMEM((hists,), jnp.int32),
             pltpu.VMEM((hists, imps), jnp.int32),

time: 36.5 us -> 35.9 us (0.984)
  starting transfers between devices: 11.9 us -> 11.3 us
  waiting for transfers between devices: 6.4 us -> 6.94 us
  Pallas kernels: 6.99 us -> 6.54 us
    ppermute x5, starting transfers between devices: 8.24 us -> 7.54 us  [send(): return lax.ppermute(x, axes, [(i, i ^ r) for i in range(count)])]
    ppermute x5, waiting for transfers between devices: 0.01 us -> 0.71 us  [send(): return lax.ppermute(x, axes, [(i, i ^ r) for i in range(count)])]
    pallas_call x1, Pallas kernels: 3.37 us -> 2.91 us  [local(): pl.pallas_call(functools.partial(score_kernel, (items_axis, dps, tensors)...]
  transfers between devices with their start and end apart: 6 -> 6, of which waited for: 1 -> 2; matrix products, arithmetic and copies ran while one was open for 0% -> 0% of each run, Pallas kernels for 10% -> 10%
where the time goes in v13:
time: 35.9 us; the launch traced here: 35.6 us
  starting transfers between devices  11.3 us (31%)
  blocking collectives  9.5 us (26%)
  waiting for transfers between devices  6.94 us (19%)
  Pallas kernels  6.54 us (18%)
  between operations  0.7 us (2%)
  other arithmetic  0.61 us (2%)
    all_to_all x1, blocking collectives, local(): sums = lax.all_to_all(sums, COLUMN, split_axis=0, concat_axis=0, tiled=True)  9.5 us
    ppermute x5, starting transfers between devices, send(): return lax.ppermute(x, axes, [(i, i ^ r) for i in range(count)])  7.54 us
    all_to_all x1, waiting for transfers between devices, local(): lax.all_to_all(gated, COLUMN, split_axis=0, concat_axis=0, tiled=True)  6.23 us
    all_to_all x1, starting transfers between devices, local(): lax.all_to_all(gated, COLUMN, split_axis=0, concat_axis=0, tiled=True)  3.78 us
    pallas_call x1, Pallas kernels, local(): pl.pallas_call(functools.partial(score_kernel, (items_axis, dps, tensors)...  2.91 us
    pallas_call x1, Pallas kernels, local(): pl.pallas_call(functools.partial(pick_kernel, (items_axis, dps)), out_sha...  2.89 us
    pallas_call x1, Pallas kernels, local(): pl.pallas_call(functools.partial(attend_kernel, items_axis), out_shape=pl...  0.73 us
  transfers between devices with their start and end apart: 6, of which 2 were waited for; matrix products, arithmetic and copies ran while one was open for 0% of the time, Pallas kernels for 10%

profile of v13, /device:TPU:0, one launch (start us, length us, event | category | flops | bytes accessed | tf_op | source)
XLA Modules:
  0.0 35.6 jit_solution(683458582804329401)
XLA Ops:
  0.6 0.0 copy-start
  0.6 0.0 copy-start.2
  0.7 0.5 %collective-permute-start.4 = (bf16[1024,1024]{1,0:T(8,128)(2,1)}, bf16[1024,1024]{1,0:T(8,128)(2,1)}, u32[]{:S(2)}, u32[]{:S(2)}) collective-permute-start(bf16[1024,1024]{1,0:T(8,128)(2,1)} %refs_6_.1), channel_id=1, source_target_pairs={{0,2},{2,0},{1,3},{3,1},{4,6},{6,4},{5,7},{7,5},{8,10},{10,8},{9,1... | collective-permute-start | bytes 6291464 | tf_op jit(solution)/shard_map/ppermute | solution.py:220
  1.2 2.9 %pick.1 = (bf16[64,1024]{1,0:T(8,128)(2,1)S(1)}, s32[64,128]{1,0:T(8,128)S(1)}, s32[1,256]{1,0:T(1,128)S(1)}, bf16[768,1024]{1,0:T(8,128)(2,1)S(1)}, bf16[64,128]{1,0:T(8,128)(2,1)S(1)}) custom-call(s32[8]{0:T(128)} %packing.1, s32[8]{0:T(128)} %lengths.1, s32[8,64]{1,0:T(8,128)} %positions.1, s32[8,64]{1,0:T(8,128)} %logged.1, bf16[768,1024]{1,0:T(8,128)(2,1)} %events.1, ...), custom_call_target="tpu_custom_call" | custom-call | flops 100663296 | bytes 1572864 | tf_op jit(solution)/shard_map/pick/pallas_call | solution.py:247
  4.1 0.0 copy-start.1
  4.1 1.6 %collective-permute-start.1 = (bf16[64,1024]{1,0:T(8,128)(2,1)S(1)}, bf16[64,1024]{1,0:T(8,128)(2,1)S(1)}, u32[]{:S(2)}, u32[]{:S(2)}) collective-permute-start(bf16[64,1024]{1,0:T(8,128)(2,1)S(1)} %get-tuple-element.14.chosen.refs_0_), channel_id=1, source_target_pairs={{0,4},{4,0},{8,12},{12,8},{1,5},{5,1},{9,13},{13,9},{2,6},{6,2},{1... | collective-permute-start | bytes 393224 | tf_op jit(solution)/shard_map/ppermute | solution.py:220
  5.6 2.6 %collective-permute-start = (bf16[64,1024]{1,0:T(8,128)(2,1)S(1)}, bf16[64,1024]{1,0:T(8,128)(2,1)S(1)}, u32[]{:S(2)}, u32[]{:S(2)}) collective-permute-start(bf16[64,1024]{1,0:T(8,128)(2,1)S(1)} %get-tuple-element.14.chosen.refs_0_), channel_id=1, source_target_pairs={{0,8},{4,12},{8,0},{12,4},{1,9},{5,13},{9,1},{13,5},{2,10},{6,14},... | collective-permute-start | bytes 393224 | tf_op jit(solution)/shard_map/ppermute | solution.py:220
  8.2 0.0 copy-done.2
  8.2 1.5 %collective-permute-start.3 = (bf16[128,1024]{1,0:T(8,128)(2,1)S(1)}, bf16[128,1024]{1,0:T(8,128)(2,1)S(1)}, u32[]{:S(2)}, u32[]{:S(2)}) collective-permute-start(bf16[128,1024]{1,0:T(8,128)(2,1)S(1)} %copy-done.2), channel_id=1, source_target_pairs={{0,1},{1,0},{2,3},{3,2},{4,5},{5,4},{6,7},{7,6},{8,9},{9,8},{10,11... | collective-permute-start | bytes 786440 | tf_op jit(solution)/shard_map/ppermute | solution.py:220
  9.7 0.0 copy-done
  9.7 0.7 %attend.1 = bf16[8,64,128]{2,1,0:T(8,128)(2,1)} custom-call(s32[64,128]{1,0:T(8,128)S(1)} %get-tuple-element.12.limits, bf16[768,1024]{1,0:T(8,128)(2,1)S(1)} %get-tuple-element.13.events, bf16[64,1024]{1,0:T(8,128)(2,1)S(1)} %get-tuple-element.14.chosen.refs_0_, bf16[1024,512]{1,0:T(8,128)(2,1)S(1)} %copy-done, bf16[64,128]{1,0:T(8,128)(2,1)S(1)} %get-tuple-element.15.done), custom_call_target="tpu_custom_call" | custom-call | tf_op jit(solution)/shard_map/attend/pallas_call | solution.py:274
  10.5 3.8 %all-to-all-start = ((bf16[8,64,128]{2,1,0:T(8,128)(2,1)}), bf16[8,64,128]{2,1,0:T(8,128)(2,1)S(1)}, u32[]{:S(2)}, u32[]{:S(2)}) async-start(bf16[8,64,128]{2,1,0:T(8,128)(2,1)} %attend.1), calls=%async_computation | async-start | bytes 262144 | tf_op jit(solution)/shard_map/all_to_all | solution.py:287
  14.2 0.0 collective-permute-done.1.refs_2_
  14.2 0.7 %collective-permute-done.refs_1_ = bf16[64,1024]{1,0:T(8,128)(2,1)S(1)} collective-permute-done((bf16[64,1024]{1,0:T(8,128)(2,1)S(1)}, bf16[64,1024]{1,0:T(8,128)(2,1)S(1)}, u32[]{:S(2)}, u32[]{:S(2)}) %collective-permute-start) | collective-permute-done | bytes 131104 | tf_op jit(solution)/shard_map/ppermute | solution.py:220
  14.9 1.4 %collective-permute-start.2 = (bf16[64,1024]{1,0:T(8,128)(2,1)S(1)}, bf16[64,1024]{1,0:T(8,128)(2,1)S(1)}, u32[]{:S(2)}, u32[]{:S(2)}) collective-permute-start(bf16[64,1024]{1,0:T(8,128)(2,1)S(1)} %collective-permute-done.refs_1_), channel_id=1, source_target_pairs={{0,4},{4,0},{8,12},{12,8},{1,5},{5,1},{9,13},{13,9},{2,6},{6,2},{1... | collective-permute-start | bytes 393224 | tf_op jit(solution)/shard_map/ppermute | solution.py:220
  16.3 6.2 %all-to-all-done.gated = bf16[8,64,128]{2,1,0:T(8,128)(2,1)S(1)} async-done(((bf16[8,64,128]{2,1,0:T(8,128)(2,1)}), bf16[8,64,128]{2,1,0:T(8,128)(2,1)S(1)}, u32[]{:S(2)}, u32[]{:S(2)}) %all-to-all-start) | async-done | bytes 131104 | tf_op jit(solution)/shard_map/all_to_all | solution.py:287
  22.6 0.0 collective-permute-done.3.refs_5_
  22.6 0.0 collective-permute-done.2.refs_3_
  22.6 0.0 collective-permute-done.4.refs_7_
  22.6 0.0 copy-done.1
  22.6 2.9 %score.1 = (bf16[64,512]{1,0:T(8,128)(2,1)}, f32[8,1,128]{2,1,0:T(1,128)S(1)}) custom-call(s32[1,256]{1,0:T(1,128)S(1)} %get-tuple-element.11.wanted, bf16[8,64,128]{2,1,0:T(8,128)(2,1)S(1)} %all-to-all-done.gated, bf16[64,1024]{1,0:T(8,128)(2,1)S(1)} %get-tuple-element.14.chosen.refs_0_, bf16[64,1024]{1,0:T(8,128)(2,1)S(1)} %collective-permute-done.refs_1_, ...), custom_call_target="tpu_custom_call" | custom-call | flops 1207959552 | bytes 4194304 | tf_op jit(solution)/shard_map/score/pallas_call | solution.py:289
  25.5 9.5 %all_to_all.10 = f32[8,1,128]{2,1,0:T(1,128)S(1)} all-to-all(f32[8,1,128]{2,1,0:T(1,128)S(1)} %get-tuple-element.19), channel_id=1, replica_groups=mesh['groups'=2,'item'=4,'dp'=2,'tensor'=2] {'tensor','item'}, dimensions={0} | all-to-all | bytes 8192 | tf_op jit(solution)/shard_map/all_to_all | solution.py:321
  35.0 0.6 %log_subtract_fusion = f32[64]{0:T(128)} fusion(f32[128]{0:T(128)S(1)} %reduce_sum.9), kind=kLoop, calls=%fused_computation | loop fusion | flops 64 | bytes 768 | tf_op jit(solution)/shard_map/sub | solution.py:323
  (1 shorter events, 0.0 us)
Async XLA Ops:
  0.6 9.1 %copy-start = (bf16[1024,512]{1,0:T(8,128)(2,1)S(1)}, bf16[1024,512]{1,0:T(8,128)(2,1)}, u32[]{:S(2)}) copy-start(bf16[1024,512]{1,0:T(8,128)(2,1)} %w_uvqk.3) | copy-start | bytes 3145732
  0.6 7.6 %copy-start.2 = (bf16[128,1024]{1,0:T(8,128)(2,1)S(1)}, bf16[128,1024]{1,0:T(8,128)(2,1)}, u32[]{:S(2)}) copy-start(bf16[128,1024]{1,0:T(8,128)(2,1)} %refs_4_.1) | copy-start | bytes 786436
  0.7 21.9 %collective-permute-start.4 = (bf16[1024,1024]{1,0:T(8,128)(2,1)}, bf16[1024,1024]{1,0:T(8,128)(2,1)}, u32[]{:S(2)}, u32[]{:S(2)}) collective-permute-start(bf16[1024,1024]{1,0:T(8,128)(2,1)} %refs_6_.1), channel_id=1, source_target_pairs={{0,2},{2,0},{1,3},{3,1},{4,6},{6,4},{5,7},{7,5},{8,10},{10,8},{9,1... | collective-permute-start | bytes 6291464 | tf_op jit(solution)/shard_map/ppermute | solution.py:220
  4.1 18.5 %copy-start.1 = (bf16[1024,1024]{1,0:T(8,128)(2,1)S(1)}, bf16[1024,1024]{1,0:T(8,128)(2,1)}, u32[]{:S(2)}) copy-start(bf16[1024,1024]{1,0:T(8,128)(2,1)} %refs_6_.1) | copy-start | bytes 6291460
  4.1 10.2 %collective-permute-start.1 = (bf16[64,1024]{1,0:T(8,128)(2,1)S(1)}, bf16[64,1024]{1,0:T(8,128)(2,1)S(1)}, u32[]{:S(2)}, u32[]{:S(2)}) collective-permute-start(bf16[64,1024]{1,0:T(8,128)(2,1)S(1)} %get-tuple-element.14.chosen.refs_0_), channel_id=1, source_target_pairs={{0,4},{4,0},{8,12},{12,8},{1,5},{5,1},{9,13},{13,9},{2,6},{6,2},{1... | collective-permute-start | bytes 393224 | tf_op jit(solution)/shard_map/ppermute | solution.py:220
  5.6 9.3 %collective-permute-start = (bf16[64,1024]{1,0:T(8,128)(2,1)S(1)}, bf16[64,1024]{1,0:T(8,128)(2,1)S(1)}, u32[]{:S(2)}, u32[]{:S(2)}) collective-permute-start(bf16[64,1024]{1,0:T(8,128)(2,1)S(1)} %get-tuple-element.14.chosen.refs_0_), channel_id=1, source_target_pairs={{0,8},{4,12},{8,0},{12,4},{1,9},{5,13},{9,1},{13,5},{2,10},{6,14},... | collective-permute-start | bytes 393224 | tf_op jit(solution)/shard_map/ppermute | solution.py:220
  8.2 14.3 %collective-permute-start.3 = (bf16[128,1024]{1,0:T(8,128)(2,1)S(1)}, bf16[128,1024]{1,0:T(8,128)(2,1)S(1)}, u32[]{:S(2)}, u32[]{:S(2)}) collective-permute-start(bf16[128,1024]{1,0:T(8,128)(2,1)S(1)} %copy-done.2), channel_id=1, source_target_pairs={{0,1},{1,0},{2,3},{3,2},{4,5},{5,4},{6,7},{7,6},{8,9},{9,8},{10,11... | collective-permute-start | bytes 786440 | tf_op jit(solution)/shard_map/ppermute | solution.py:220
  10.5 12.1 %all-to-all-start = ((bf16[8,64,128]{2,1,0:T(8,128)(2,1)}), bf16[8,64,128]{2,1,0:T(8,128)(2,1)S(1)}, u32[]{:S(2)}, u32[]{:S(2)}) async-start(bf16[8,64,128]{2,1,0:T(8,128)(2,1)} %attend.1), calls=%async_computation | async-start | bytes 262144 | tf_op jit(solution)/shard_map/all_to_all | solution.py:287
  14.9 7.6 %collective-permute-start.2 = (bf16[64,1024]{1,0:T(8,128)(2,1)S(1)}, bf16[64,1024]{1,0:T(8,128)(2,1)S(1)}, u32[]{:S(2)}, u32[]{:S(2)}) collective-permute-start(bf16[64,1024]{1,0:T(8,128)(2,1)S(1)} %collective-permute-done.refs_1_), channel_id=1, source_target_pairs={{0,4},{4,0},{8,12},{12,8},{1,5},{5,1},{9,13},{13,9},{2,6},{6,2},{1... | collective-permute-start | bytes 393224 | tf_op jit(solution)/shard_map/ppermute | solution.py:220

commit v14 on v13

--- a/solution.py
+++ b/solution.py
@@ -164,7 +164,7 @@
     local_width = w_out[0].shape[0]
     for k in range(items_axis):
         for t in range(tensors):
-            sender = (tensor ^ tensor_rounds[t]) * items_axis + (item ^ slot_rounds[k])
+            sender = rank(item ^ slot_rounds[k], tensor ^ tensor_rounds[t], items_axis)
             gates[k * imps : (k + 1) * imps, t * local_width : (t + 1) * local_width] = gated[sender]
     w_whole = jnp.concatenate([w[...] for w in w_out], axis=0)
     mixed = jnp.dot(gates[...], w_whole, preferred_element_type=jnp.float32)
@@ -208,12 +208,26 @@
                 [v[:, part * imps : (part + 1) * imps] for v in (total, target)], axis=1
             )
             for t in range(tensors):
-                sums[t * items_axis + owner] = both
+                sums[rank(owner, t, items_axis)] = both
     state_copy.wait()
 
 
 def in_hbm(x):
     return pltpu.with_memory_space_constraint(x, pltpu.HBM)
+
+
+def rank(item, tensor, items_axis):
+    return tensor * items_axis + (item + items_axis - 1) % items_axis
+
+
+def exchange(x, items_axis, tensors):
+    group = [0] * (items_axis * tensors)
+    for tensor in range(tensors):
+        for item in range(items_axis):
+            group[rank(item, tensor, items_axis)] = tensor * items_axis + item
+    return lax.all_to_all(
+        x, COLUMN, split_axis=0, concat_axis=0, tiled=True, axis_index_groups=[group]
+    )
 
 
 def send(x, axes, count, r):
@@ -284,7 +298,7 @@
         cost_estimate=pl.CostEstimate(flops=0, bytes_accessed=0, transcendentals=0),
         name="attend",
     )(limits, events, chosen, w_uvqk, done)
-    all_gated = lax.all_to_all(gated, COLUMN, split_axis=0, concat_axis=0, tiled=True)
+    all_gated = exchange(gated, items_axis, tensors)
 
     state, sums = pl.pallas_call(
         functools.partial(score_kernel, (items_axis, dps, tensors)),
@@ -318,7 +332,7 @@
         catalogue,
         *(in_hbm(x) for x in other_catalogues),
     )
-    sums = lax.all_to_all(sums, COLUMN, split_axis=0, concat_axis=0, tiled=True)
+    sums = exchange(sums, items_axis, tensors)
     sums = jnp.sum(sums, axis=(0, 1))
     return (state, sums[imps:] - jnp.log(sums[:imps]))
 

time: 35.9 us -> 35.1 us (0.978)
  blocking collectives: 9.5 us -> 9.11 us
    ppermute x5, starting transfers between devices: 7.54 us -> 6.32 us  [send(): return lax.ppermute(x, axes, [(i, i ^ r) for i in range(count)])]
    all_to_all x1, starting transfers between devices: 3.78 us -> 4.84 us  [exchange(): lax.all_to_all(x, COLUMN, split_axis=0, concat_axis=0, tiled=True, axis_i...]
    ppermute x5, waiting for transfers between devices: 0.71 us -> 0.01 us  [send(): return lax.ppermute(x, axes, [(i, i ^ r) for i in range(count)])]
    all_to_all x1, waiting for transfers between devices: 6.23 us -> 6.65 us  [exchange(): lax.all_to_all(x, COLUMN, split_axis=0, concat_axis=0, tiled=True, axis_i...]
    all_to_all x1, blocking collectives: 9.5 us -> 9.11 us  [exchange(): lax.all_to_all(x, COLUMN, split_axis=0, concat_axis=0, tiled=True, axis_i...]
  transfers between devices with their start and end apart: 6 -> 6, of which waited for: 2 -> 1; matrix products, arithmetic and copies ran while one was open for 0% -> 0% of each run, Pallas kernels for 10% -> 10%
where the time goes in v14:
time: 35.1 us; the launch traced here: 34.8 us
  starting transfers between devices  11.2 us (32%)
  blocking collectives  9.11 us (26%)
  waiting for transfers between devices  6.66 us (19%)
  Pallas kernels  6.49 us (18%)
  between operations  0.7 us (2%)
  other arithmetic  0.61 us (2%)
    all_to_all x1, blocking collectives, exchange(): lax.all_to_all(x, COLUMN, split_axis=0, concat_axis=0, tiled=True, axis_i...  9.11 us
    all_to_all x1, waiting for transfers between devices, exchange(): lax.all_to_all(x, COLUMN, split_axis=0, concat_axis=0, tiled=True, axis_i...  6.65 us
    ppermute x5, starting transfers between devices, send(): return lax.ppermute(x, axes, [(i, i ^ r) for i in range(count)])  6.32 us
    all_to_all x1, starting transfers between devices, exchange(): lax.all_to_all(x, COLUMN, split_axis=0, concat_axis=0, tiled=True, axis_i...  4.84 us
    pallas_call x1, Pallas kernels, local(): pl.pallas_call(functools.partial(pick_kernel, (items_axis, dps)), out_sha...  2.89 us
    pallas_call x1, Pallas kernels, local(): pl.pallas_call(functools.partial(score_kernel, (items_axis, dps, tensors)...  2.87 us
    pallas_call x1, Pallas kernels, local(): pl.pallas_call(functools.partial(attend_kernel, items_axis), out_shape=pl...  0.73 us
  transfers between devices with their start and end apart: 6, of which 1 were waited for; matrix products, arithmetic and copies ran while one was open for 0% of the time, Pallas kernels for 10%

profile of v14, /device:TPU:0, one launch (start us, length us, event | category | flops | bytes accessed | tf_op | source)
XLA Modules:
  0.0 34.8 jit_solution(11390742719416512799)
XLA Ops:
  0.6 0.0 copy-start
  0.6 0.0 copy-start.2
  0.7 0.5 %collective-permute-start.4 = (bf16[1024,1024]{1,0:T(8,128)(2,1)}, bf16[1024,1024]{1,0:T(8,128)(2,1)}, u32[]{:S(2)}, u32[]{:S(2)}) collective-permute-start(bf16[1024,1024]{1,0:T(8,128)(2,1)} %refs_6_.1), channel_id=1, source_target_pairs={{0,2},{2,0},{1,3},{3,1},{4,6},{6,4},{5,7},{7,5},{8,10},{10,8},{9,1... | collective-permute-start | bytes 6291464 | tf_op jit(solution)/shard_map/ppermute | solution.py:234
  1.2 2.9 %pick.1 = (bf16[64,1024]{1,0:T(8,128)(2,1)S(1)}, s32[64,128]{1,0:T(8,128)S(1)}, s32[1,256]{1,0:T(1,128)S(1)}, bf16[768,1024]{1,0:T(8,128)(2,1)S(1)}, bf16[64,128]{1,0:T(8,128)(2,1)S(1)}) custom-call(s32[8]{0:T(128)} %packing.1, s32[8]{0:T(128)} %lengths.1, s32[8,64]{1,0:T(8,128)} %positions.1, s32[8,64]{1,0:T(8,128)} %logged.1, bf16[768,1024]{1,0:T(8,128)(2,1)} %events.1, ...), custom_call_target="tpu_custom_call" | custom-call | flops 100663296 | bytes 1572864 | tf_op jit(solution)/shard_map/pick/pallas_call | solution.py:261
  4.1 0.0 copy-start.1
  4.1 1.6 %collective-permute-start.1 = (bf16[64,1024]{1,0:T(8,128)(2,1)S(1)}, bf16[64,1024]{1,0:T(8,128)(2,1)S(1)}, u32[]{:S(2)}, u32[]{:S(2)}) collective-permute-start(bf16[64,1024]{1,0:T(8,128)(2,1)S(1)} %get-tuple-element.14.chosen.refs_0_), channel_id=1, source_target_pairs={{0,4},{4,0},{8,12},{12,8},{1,5},{5,1},{9,13},{13,9},{2,6},{6,2},{1... | collective-permute-start | bytes 393224 | tf_op jit(solution)/shard_map/ppermute | solution.py:234
  5.6 2.6 %collective-permute-start = (bf16[64,1024]{1,0:T(8,128)(2,1)S(1)}, bf16[64,1024]{1,0:T(8,128)(2,1)S(1)}, u32[]{:S(2)}, u32[]{:S(2)}) collective-permute-start(bf16[64,1024]{1,0:T(8,128)(2,1)S(1)} %get-tuple-element.14.chosen.refs_0_), channel_id=1, source_target_pairs={{0,8},{4,12},{8,0},{12,4},{1,9},{5,13},{9,1},{13,5},{2,10},{6,14},... | collective-permute-start | bytes 393224 | tf_op jit(solution)/shard_map/ppermute | solution.py:234
  8.2 0.0 copy-done.2
  8.2 1.5 %collective-permute-start.3 = (bf16[128,1024]{1,0:T(8,128)(2,1)S(1)}, bf16[128,1024]{1,0:T(8,128)(2,1)S(1)}, u32[]{:S(2)}, u32[]{:S(2)}) collective-permute-start(bf16[128,1024]{1,0:T(8,128)(2,1)S(1)} %copy-done.2), channel_id=1, source_target_pairs={{0,1},{1,0},{2,3},{3,2},{4,5},{5,4},{6,7},{7,6},{8,9},{9,8},{10,11... | collective-permute-start | bytes 786440 | tf_op jit(solution)/shard_map/ppermute | solution.py:234
  9.7 0.0 copy-done
  9.7 0.7 %attend.1 = bf16[8,64,128]{2,1,0:T(8,128)(2,1)} custom-call(s32[64,128]{1,0:T(8,128)S(1)} %get-tuple-element.12.limits, bf16[768,1024]{1,0:T(8,128)(2,1)S(1)} %get-tuple-element.13.events, bf16[64,1024]{1,0:T(8,128)(2,1)S(1)} %get-tuple-element.14.chosen.refs_0_, bf16[1024,512]{1,0:T(8,128)(2,1)S(1)} %copy-done, bf16[64,128]{1,0:T(8,128)(2,1)S(1)} %get-tuple-element.15.done), custom_call_target="tpu_custom_call" | custom-call | tf_op jit(solution)/shard_map/attend/pallas_call | solution.py:288
  10.5 4.8 %all-to-all-start = ((bf16[8,64,128]{2,1,0:T(8,128)(2,1)}), bf16[8,64,128]{2,1,0:T(8,128)(2,1)S(1)}, u32[]{:S(2)}, u32[]{:S(2)}) async-start(bf16[8,64,128]{2,1,0:T(8,128)(2,1)} %attend.1), calls=%async_computation | async-start | bytes 262144 | tf_op jit(solution)/shard_map/all_to_all | solution.py:228
  15.3 0.0 collective-permute-done.1.refs_2_
  15.3 0.0 collective-permute-done.refs_1_
  15.3 0.2 collective-permute-start.2
  15.5 6.7 %all-to-all-done.gated = bf16[8,64,128]{2,1,0:T(8,128)(2,1)S(1)} async-done(((bf16[8,64,128]{2,1,0:T(8,128)(2,1)}), bf16[8,64,128]{2,1,0:T(8,128)(2,1)S(1)}, u32[]{:S(2)}, u32[]{:S(2)}) %all-to-all-start) | async-done | bytes 131104 | tf_op jit(solution)/shard_map/all_to_all | solution.py:228
  22.1 0.0 collective-permute-done.3.refs_5_
  22.1 0.0 collective-permute-done.2.refs_3_
  22.1 0.0 collective-permute-done.4.refs_7_
  22.1 0.0 copy-done.1
  22.2 2.9 %score.1 = (bf16[64,512]{1,0:T(8,128)(2,1)}, f32[8,1,128]{2,1,0:T(1,128)S(1)}) custom-call(s32[1,256]{1,0:T(1,128)S(1)} %get-tuple-element.11.wanted, bf16[8,64,128]{2,1,0:T(8,128)(2,1)S(1)} %all-to-all-done.gated, bf16[64,1024]{1,0:T(8,128)(2,1)S(1)} %get-tuple-element.14.chosen.refs_0_, bf16[64,1024]{1,0:T(8,128)(2,1)S(1)} %collective-permute-done.refs_1_, ...), custom_call_target="tpu_custom_call" | custom-call | flops 1207959552 | bytes 4194304 | tf_op jit(solution)/shard_map/score/pallas_call | solution.py:303
  25.0 9.1 %all_to_all.10 = f32[8,1,128]{2,1,0:T(1,128)S(1)} all-to-all(f32[8,1,128]{2,1,0:T(1,128)S(1)} %get-tuple-element.19), channel_id=1, replica_groups={{4,8,12,0,5,9,13,1},{6,10,14,2,7,11,15,3},{20,24,28,16,21,25,29,17},{22..., dimensions={0} | all-to-all | bytes 8192 | tf_op jit(solution)/shard_map/all_to_all | solution.py:228
  34.2 0.6 %log_subtract_fusion = f32[64]{0:T(128)} fusion(f32[128]{0:T(128)S(1)} %reduce_sum.9), kind=kLoop, calls=%fused_computation | loop fusion | flops 64 | bytes 768 | tf_op jit(solution)/shard_map/sub | solution.py:337
  (1 shorter events, 0.0 us)
Async XLA Ops:
  0.6 9.1 %copy-start = (bf16[1024,512]{1,0:T(8,128)(2,1)S(1)}, bf16[1024,512]{1,0:T(8,128)(2,1)}, u32[]{:S(2)}) copy-start(bf16[1024,512]{1,0:T(8,128)(2,1)} %w_uvqk.3) | copy-start | bytes 3145732
  0.6 7.6 %copy-start.2 = (bf16[128,1024]{1,0:T(8,128)(2,1)S(1)}, bf16[128,1024]{1,0:T(8,128)(2,1)}, u32[]{:S(2)}) copy-start(bf16[128,1024]{1,0:T(8,128)(2,1)} %refs_4_.1) | copy-start | bytes 786436
  0.7 21.5 %collective-permute-start.4 = (bf16[1024,1024]{1,0:T(8,128)(2,1)}, bf16[1024,1024]{1,0:T(8,128)(2,1)}, u32[]{:S(2)}, u32[]{:S(2)}) collective-permute-start(bf16[1024,1024]{1,0:T(8,128)(2,1)} %refs_6_.1), channel_id=1, source_target_pairs={{0,2},{2,0},{1,3},{3,1},{4,6},{6,4},{5,7},{7,5},{8,10},{10,8},{9,1... | collective-permute-start | bytes 6291464 | tf_op jit(solution)/shard_map/ppermute | solution.py:234
  4.1 18.1 %copy-start.1 = (bf16[1024,1024]{1,0:T(8,128)(2,1)S(1)}, bf16[1024,1024]{1,0:T(8,128)(2,1)}, u32[]{:S(2)}) copy-start(bf16[1024,1024]{1,0:T(8,128)(2,1)} %refs_6_.1) | copy-start | bytes 6291460
  4.1 11.2 %collective-permute-start.1 = (bf16[64,1024]{1,0:T(8,128)(2,1)S(1)}, bf16[64,1024]{1,0:T(8,128)(2,1)S(1)}, u32[]{:S(2)}, u32[]{:S(2)}) collective-permute-start(bf16[64,1024]{1,0:T(8,128)(2,1)S(1)} %get-tuple-element.14.chosen.refs_0_), channel_id=1, source_target_pairs={{0,4},{4,0},{8,12},{12,8},{1,5},{5,1},{9,13},{13,9},{2,6},{6,2},{1... | collective-permute-start | bytes 393224 | tf_op jit(solution)/shard_map/ppermute | solution.py:234
  5.6 9.7 %collective-permute-start = (bf16[64,1024]{1,0:T(8,128)(2,1)S(1)}, bf16[64,1024]{1,0:T(8,128)(2,1)S(1)}, u32[]{:S(2)}, u32[]{:S(2)}) collective-permute-start(bf16[64,1024]{1,0:T(8,128)(2,1)S(1)} %get-tuple-element.14.chosen.refs_0_), channel_id=1, source_target_pairs={{0,8},{4,12},{8,0},{12,4},{1,9},{5,13},{9,1},{13,5},{2,10},{6,14},... | collective-permute-start | bytes 393224 | tf_op jit(solution)/shard_map/ppermute | solution.py:234
  8.2 13.9 %collective-permute-start.3 = (bf16[128,1024]{1,0:T(8,128)(2,1)S(1)}, bf16[128,1024]{1,0:T(8,128)(2,1)S(1)}, u32[]{:S(2)}, u32[]{:S(2)}) collective-permute-start(bf16[128,1024]{1,0:T(8,128)(2,1)S(1)} %copy-done.2), channel_id=1, source_target_pairs={{0,1},{1,0},{2,3},{3,2},{4,5},{5,4},{6,7},{7,6},{8,9},{9,8},{10,11... | collective-permute-start | bytes 786440 | tf_op jit(solution)/shard_map/ppermute | solution.py:234
  10.5 11.7 %all-to-all-start = ((bf16[8,64,128]{2,1,0:T(8,128)(2,1)}), bf16[8,64,128]{2,1,0:T(8,128)(2,1)S(1)}, u32[]{:S(2)}, u32[]{:S(2)}) async-start(bf16[8,64,128]{2,1,0:T(8,128)(2,1)} %attend.1), calls=%async_computation | async-start | bytes 262144 | tf_op jit(solution)/shard_map/all_to_all | solution.py:228
  15.3 6.8 %collective-permute-start.2 = (bf16[64,1024]{1,0:T(8,128)(2,1)S(1)}, bf16[64,1024]{1,0:T(8,128)(2,1)S(1)}, u32[]{:S(2)}, u32[]{:S(2)}) collective-permute-start(bf16[64,1024]{1,0:T(8,128)(2,1)S(1)} %collective-permute-done.refs_1_), channel_id=1, source_target_pairs={{0,4},{4,0},{8,12},{12,8},{1,5},{5,1},{9,13},{13,9},{2,6},{6,2},{1... | collective-permute-start | bytes 393224 | tf_op jit(solution)/shard_map/ppermute | solution.py:234

commit v15 on v14

--- a/solution.py
+++ b/solution.py
@@ -164,7 +164,8 @@
     local_width = w_out[0].shape[0]
     for k in range(items_axis):
         for t in range(tensors):
-            sender = rank(item ^ slot_rounds[k], tensor ^ tensor_rounds[t], items_axis)
+            other, head = item ^ slot_rounds[k], tensor ^ tensor_rounds[t]
+            sender = rank(other, head, items_axis, items_axis // 2)
             gates[k * imps : (k + 1) * imps, t * local_width : (t + 1) * local_width] = gated[sender]
     w_whole = jnp.concatenate([w[...] for w in w_out], axis=0)
     mixed = jnp.dot(gates[...], w_whole, preferred_element_type=jnp.float32)
@@ -208,7 +209,7 @@
                 [v[:, part * imps : (part + 1) * imps] for v in (total, target)], axis=1
             )
             for t in range(tensors):
-                sums[rank(owner, t, items_axis)] = both
+                sums[rank(owner, t, items_axis, items_axis - 1)] = both
     state_copy.wait()
 
 
@@ -216,15 +217,15 @@
     return pltpu.with_memory_space_constraint(x, pltpu.HBM)
 
 
-def rank(item, tensor, items_axis):
-    return tensor * items_axis + (item + items_axis - 1) % items_axis
-
-
-def exchange(x, items_axis, tensors):
+def rank(item, tensor, items_axis, first):
+    return tensor * items_axis + (item + items_axis - first) % items_axis
+
+
+def exchange(x, items_axis, tensors, first):
     group = [0] * (items_axis * tensors)
     for tensor in range(tensors):
         for item in range(items_axis):
-            group[rank(item, tensor, items_axis)] = tensor * items_axis + item
+            group[rank(item, tensor, items_axis, first)] = tensor * items_axis + item
     return lax.all_to_all(
         x, COLUMN, split_axis=0, concat_axis=0, tiled=True, axis_index_groups=[group]
     )
@@ -298,7 +299,7 @@
         cost_estimate=pl.CostEstimate(flops=0, bytes_accessed=0, transcendentals=0),
         name="attend",
     )(limits, events, chosen, w_uvqk, done)
-    all_gated = exchange(gated, items_axis, tensors)
+    all_gated = exchange(gated, items_axis, tensors, items_axis // 2)
 
     state, sums = pl.pallas_call(
         functools.partial(score_kernel, (items_axis, dps, tensors)),
@@ -332,7 +333,7 @@
         catalogue,
         *(in_hbm(x) for x in other_catalogues),
     )
-    sums = exchange(sums, items_axis, tensors)
+    sums = exchange(sums, items_axis, tensors, items_axis - 1)
     sums = jnp.sum(sums, axis=(0, 1))
     return (state, sums[imps:] - jnp.log(sums[:imps]))
 

time: 35.1 us -> 34 us (0.969)
  waiting for transfers between devices: 6.66 us -> 5.55 us
    all_to_all x1, waiting for transfers between devices: 6.65 us -> 5.29 us  [exchange(): lax.all_to_all(x, COLUMN, split_axis=0, concat_axis=0, tiled=True, axis_i...]
    ppermute x5, starting transfers between devices: 6.32 us -> 6.79 us  [send(): return lax.ppermute(x, axes, [(i, i ^ r) for i in range(count)])]
  transfers between devices with their start and end apart: 6 -> 6, of which waited for: 1 -> 2; matrix products, arithmetic and copies ran while one was open for 0% -> 0% of each run, Pallas kernels for 10% -> 11%
where the time goes in v15:
time: 34 us; the launch traced here: 33.7 us
  starting transfers between devices  11.5 us (34%)
  blocking collectives  9.05 us (27%)
  Pallas kernels  6.25 us (18%)
  waiting for transfers between devices  5.55 us (16%)
  between operations  0.69 us (2%)
  other arithmetic  0.61 us (2%)
    all_to_all x1, blocking collectives, exchange(): lax.all_to_all(x, COLUMN, split_axis=0, concat_axis=0, tiled=True, axis_i...  9.05 us
    ppermute x5, starting transfers between devices, send(): return lax.ppermute(x, axes, [(i, i ^ r) for i in range(count)])  6.79 us
    all_to_all x1, waiting for transfers between devices, exchange(): lax.all_to_all(x, COLUMN, split_axis=0, concat_axis=0, tiled=True, axis_i...  5.29 us
    all_to_all x1, starting transfers between devices, exchange(): lax.all_to_all(x, COLUMN, split_axis=0, concat_axis=0, tiled=True, axis_i...  4.72 us
    pallas_call x1, Pallas kernels, local(): pl.pallas_call(functools.partial(pick_kernel, (items_axis, dps)), out_sha...  2.89 us
    pallas_call x1, Pallas kernels, local(): pl.pallas_call(functools.partial(score_kernel, (items_axis, dps, tensors)...  2.62 us
    pallas_call x1, Pallas kernels, local(): pl.pallas_call(functools.partial(attend_kernel, items_axis), out_shape=pl...  0.73 us
  transfers between devices with their start and end apart: 6, of which 2 were waited for; matrix products, arithmetic and copies ran while one was open for 0% of the time, Pallas kernels for 11%

profile of v15, /device:TPU:0, one launch (start us, length us, event | category | flops | bytes accessed | tf_op | source)
XLA Modules:
  0.0 33.7 jit_solution(17169348706511989379)
XLA Ops:
  0.6 0.0 copy-start
  0.6 0.0 copy-start.2
  0.7 0.5 %collective-permute-start.4 = (bf16[1024,1024]{1,0:T(8,128)(2,1)}, bf16[1024,1024]{1,0:T(8,128)(2,1)}, u32[]{:S(2)}, u32[]{:S(2)}) collective-permute-start(bf16[1024,1024]{1,0:T(8,128)(2,1)} %refs_6_.1), channel_id=1, source_target_pairs={{0,2},{2,0},{1,3},{3,1},{4,6},{6,4},{5,7},{7,5},{8,10},{10,8},{9,1... | collective-permute-start | bytes 6291464 | tf_op jit(solution)/shard_map/ppermute | solution.py:235
  1.2 2.9 %pick.1 = (bf16[64,1024]{1,0:T(8,128)(2,1)S(1)}, s32[64,128]{1,0:T(8,128)S(1)}, s32[1,256]{1,0:T(1,128)S(1)}, bf16[768,1024]{1,0:T(8,128)(2,1)S(1)}, bf16[64,128]{1,0:T(8,128)(2,1)S(1)}) custom-call(s32[8]{0:T(128)} %packing.1, s32[8]{0:T(128)} %lengths.1, s32[8,64]{1,0:T(8,128)} %positions.1, s32[8,64]{1,0:T(8,128)} %logged.1, bf16[768,1024]{1,0:T(8,128)(2,1)} %events.1, ...), custom_call_target="tpu_custom_call" | custom-call | flops 100663296 | bytes 1572864 | tf_op jit(solution)/shard_map/pick/pallas_call | solution.py:262
  4.1 0.0 copy-start.1
  4.1 1.6 %collective-permute-start.1 = (bf16[64,1024]{1,0:T(8,128)(2,1)S(1)}, bf16[64,1024]{1,0:T(8,128)(2,1)S(1)}, u32[]{:S(2)}, u32[]{:S(2)}) collective-permute-start(bf16[64,1024]{1,0:T(8,128)(2,1)S(1)} %get-tuple-element.14.chosen.refs_0_), channel_id=1, source_target_pairs={{0,4},{4,0},{8,12},{12,8},{1,5},{5,1},{9,13},{13,9},{2,6},{6,2},{1... | collective-permute-start | bytes 393224 | tf_op jit(solution)/shard_map/ppermute | solution.py:235
  5.6 2.6 %collective-permute-start = (bf16[64,1024]{1,0:T(8,128)(2,1)S(1)}, bf16[64,1024]{1,0:T(8,128)(2,1)S(1)}, u32[]{:S(2)}, u32[]{:S(2)}) collective-permute-start(bf16[64,1024]{1,0:T(8,128)(2,1)S(1)} %get-tuple-element.14.chosen.refs_0_), channel_id=1, source_target_pairs={{0,8},{4,12},{8,0},{12,4},{1,9},{5,13},{9,1},{13,5},{2,10},{6,14},... | collective-permute-start | bytes 393224 | tf_op jit(solution)/shard_map/ppermute | solution.py:235
  8.2 0.0 copy-done.2
  8.2 1.5 %collective-permute-start.3 = (bf16[128,1024]{1,0:T(8,128)(2,1)S(1)}, bf16[128,1024]{1,0:T(8,128)(2,1)S(1)}, u32[]{:S(2)}, u32[]{:S(2)}) collective-permute-start(bf16[128,1024]{1,0:T(8,128)(2,1)S(1)} %copy-done.2), channel_id=1, source_target_pairs={{0,1},{1,0},{2,3},{3,2},{4,5},{5,4},{6,7},{7,6},{8,9},{9,8},{10,11... | collective-permute-start | bytes 786440 | tf_op jit(solution)/shard_map/ppermute | solution.py:235
  9.7 0.0 copy-done
  9.7 0.7 %attend.1 = bf16[8,64,128]{2,1,0:T(8,128)(2,1)} custom-call(s32[64,128]{1,0:T(8,128)S(1)} %get-tuple-element.12.limits, bf16[768,1024]{1,0:T(8,128)(2,1)S(1)} %get-tuple-element.13.events, bf16[64,1024]{1,0:T(8,128)(2,1)S(1)} %get-tuple-element.14.chosen.refs_0_, bf16[1024,512]{1,0:T(8,128)(2,1)S(1)} %copy-done, bf16[64,128]{1,0:T(8,128)(2,1)S(1)} %get-tuple-element.15.done), custom_call_target="tpu_custom_call" | custom-call | tf_op jit(solution)/shard_map/attend/pallas_call | solution.py:289
  10.5 4.7 %all-to-all-start = ((bf16[8,64,128]{2,1,0:T(8,128)(2,1)}), bf16[8,64,128]{2,1,0:T(8,128)(2,1)S(1)}, u32[]{:S(2)}, u32[]{:S(2)}) async-start(bf16[8,64,128]{2,1,0:T(8,128)(2,1)} %attend.1), calls=%async_computation | async-start | bytes 262144 | tf_op jit(solution)/shard_map/all_to_all | solution.py:229
  15.2 0.0 collective-permute-done.1.refs_2_
  15.2 0.0 collective-permute-done.refs_1_
  15.2 0.6 %collective-permute-start.2 = (bf16[64,1024]{1,0:T(8,128)(2,1)S(1)}, bf16[64,1024]{1,0:T(8,128)(2,1)S(1)}, u32[]{:S(2)}, u32[]{:S(2)}) collective-permute-start(bf16[64,1024]{1,0:T(8,128)(2,1)S(1)} %collective-permute-done.refs_1_), channel_id=1, source_target_pairs={{0,4},{4,0},{8,12},{12,8},{1,5},{5,1},{9,13},{13,9},{2,6},{6,2},{1... | collective-permute-start | bytes 393224 | tf_op jit(solution)/shard_map/ppermute | solution.py:235
  15.8 5.3 %all-to-all-done.gated = bf16[8,64,128]{2,1,0:T(8,128)(2,1)S(1)} async-done(((bf16[8,64,128]{2,1,0:T(8,128)(2,1)}), bf16[8,64,128]{2,1,0:T(8,128)(2,1)S(1)}, u32[]{:S(2)}, u32[]{:S(2)}) %all-to-all-start) | async-done | bytes 131104 | tf_op jit(solution)/shard_map/all_to_all | solution.py:229
  21.1 0.0 collective-permute-done.3.refs_5_
  21.1 0.3 collective-permute-done.2.refs_3_
  21.4 0.0 collective-permute-done.4.refs_7_
  21.4 0.0 copy-done.1
  21.4 2.6 %score.1 = (bf16[64,512]{1,0:T(8,128)(2,1)}, f32[8,1,128]{2,1,0:T(1,128)S(1)}) custom-call(s32[1,256]{1,0:T(1,128)S(1)} %get-tuple-element.11.wanted, bf16[8,64,128]{2,1,0:T(8,128)(2,1)S(1)} %all-to-all-done.gated, bf16[64,1024]{1,0:T(8,128)(2,1)S(1)} %get-tuple-element.14.chosen.refs_0_, bf16[64,1024]{1,0:T(8,128)(2,1)S(1)} %collective-permute-done.refs_1_, ...), custom_call_target="tpu_custom_call" | custom-call | flops 1207959552 | bytes 4194304 | tf_op jit(solution)/shard_map/score/pallas_call | solution.py:304
  24.0 9.0 %all_to_all.10 = f32[8,1,128]{2,1,0:T(1,128)S(1)} all-to-all(f32[8,1,128]{2,1,0:T(1,128)S(1)} %get-tuple-element.19), channel_id=1, replica_groups={{12,0,4,8,13,1,5,9},{14,2,6,10,15,3,7,11},{28,16,20,24,29,17,21,25},{30..., dimensions={0} | all-to-all | bytes 8192 | tf_op jit(solution)/shard_map/all_to_all | solution.py:229
  33.1 0.6 %log_subtract_fusion = f32[64]{0:T(128)} fusion(f32[128]{0:T(128)S(1)} %reduce_sum.9), kind=kLoop, calls=%fused_computation | loop fusion | flops 64 | bytes 768 | tf_op jit(solution)/shard_map/sub | solution.py:338
  (1 shorter events, 0.0 us)
Async XLA Ops:
  0.6 9.1 %copy-start = (bf16[1024,512]{1,0:T(8,128)(2,1)S(1)}, bf16[1024,512]{1,0:T(8,128)(2,1)}, u32[]{:S(2)}) copy-start(bf16[1024,512]{1,0:T(8,128)(2,1)} %w_uvqk.3) | copy-start | bytes 3145732
  0.6 7.6 %copy-start.2 = (bf16[128,1024]{1,0:T(8,128)(2,1)S(1)}, bf16[128,1024]{1,0:T(8,128)(2,1)}, u32[]{:S(2)}) copy-start(bf16[128,1024]{1,0:T(8,128)(2,1)} %refs_4_.1) | copy-start | bytes 786436
  0.7 20.7 %collective-permute-start.4 = (bf16[1024,1024]{1,0:T(8,128)(2,1)}, bf16[1024,1024]{1,0:T(8,128)(2,1)}, u32[]{:S(2)}, u32[]{:S(2)}) collective-permute-start(bf16[1024,1024]{1,0:T(8,128)(2,1)} %refs_6_.1), channel_id=1, source_target_pairs={{0,2},{2,0},{1,3},{3,1},{4,6},{6,4},{5,7},{7,5},{8,10},{10,8},{9,1... | collective-permute-start | bytes 6291464 | tf_op jit(solution)/shard_map/ppermute | solution.py:235
  4.1 17.3 %copy-start.1 = (bf16[1024,1024]{1,0:T(8,128)(2,1)S(1)}, bf16[1024,1024]{1,0:T(8,128)(2,1)}, u32[]{:S(2)}) copy-start(bf16[1024,1024]{1,0:T(8,128)(2,1)} %refs_6_.1) | copy-start | bytes 6291460
  4.1 11.1 %collective-permute-start.1 = (bf16[64,1024]{1,0:T(8,128)(2,1)S(1)}, bf16[64,1024]{1,0:T(8,128)(2,1)S(1)}, u32[]{:S(2)}, u32[]{:S(2)}) collective-permute-start(bf16[64,1024]{1,0:T(8,128)(2,1)S(1)} %get-tuple-element.14.chosen.refs_0_), channel_id=1, source_target_pairs={{0,4},{4,0},{8,12},{12,8},{1,5},{5,1},{9,13},{13,9},{2,6},{6,2},{1... | collective-permute-start | bytes 393224 | tf_op jit(solution)/shard_map/ppermute | solution.py:235
  5.6 9.5 %collective-permute-start = (bf16[64,1024]{1,0:T(8,128)(2,1)S(1)}, bf16[64,1024]{1,0:T(8,128)(2,1)S(1)}, u32[]{:S(2)}, u32[]{:S(2)}) collective-permute-start(bf16[64,1024]{1,0:T(8,128)(2,1)S(1)} %get-tuple-element.14.chosen.refs_0_), channel_id=1, source_target_pairs={{0,8},{4,12},{8,0},{12,4},{1,9},{5,13},{9,1},{13,5},{2,10},{6,14},... | collective-permute-start | bytes 393224 | tf_op jit(solution)/shard_map/ppermute | solution.py:235
  8.2 12.9 %collective-permute-start.3 = (bf16[128,1024]{1,0:T(8,128)(2,1)S(1)}, bf16[128,1024]{1,0:T(8,128)(2,1)S(1)}, u32[]{:S(2)}, u32[]{:S(2)}) collective-permute-start(bf16[128,1024]{1,0:T(8,128)(2,1)S(1)} %copy-done.2), channel_id=1, source_target_pairs={{0,1},{1,0},{2,3},{3,2},{4,5},{5,4},{6,7},{7,6},{8,9},{9,8},{10,11... | collective-permute-start | bytes 786440 | tf_op jit(solution)/shard_map/ppermute | solution.py:235
  10.5 10.7 %all-to-all-start = ((bf16[8,64,128]{2,1,0:T(8,128)(2,1)}), bf16[8,64,128]{2,1,0:T(8,128)(2,1)S(1)}, u32[]{:S(2)}, u32[]{:S(2)}) async-start(bf16[8,64,128]{2,1,0:T(8,128)(2,1)} %attend.1), calls=%async_computation | async-start | bytes 262144 | tf_op jit(solution)/shard_map/all_to_all | solution.py:229
  15.2 6.2 %collective-permute-start.2 = (bf16[64,1024]{1,0:T(8,128)(2,1)S(1)}, bf16[64,1024]{1,0:T(8,128)(2,1)S(1)}, u32[]{:S(2)}, u32[]{:S(2)}) collective-permute-start(bf16[64,1024]{1,0:T(8,128)(2,1)S(1)} %collective-permute-done.refs_1_), channel_id=1, source_target_pairs={{0,4},{4,0},{8,12},{12,8},{1,5},{5,1},{9,13},{13,9},{2,6},{6,2},{1... | collective-permute-start | bytes 393224 | tf_op jit(solution)/shard_map/ppermute | solution.py:235

commit v16 on v15

--- a/solution.py
+++ b/solution.py
@@ -36,8 +36,8 @@
     limits,
     wanted,
     events_v,
+    w_uvqk_v,
     done,
-    w_uvqk_v,
     packing_s,
     lengths_s,
     positions_v,
@@ -62,13 +62,11 @@
             + [(w_uvqk, w_uvqk_v)]
         )
     ]
-    for copy in copies[:-1]:
+    for copy in copies:
         copy.start()
-    item, dp = lax.axis_index("item"), lax.axis_index("dp")
-    early = is_early(item, items_axis)
-    pl.when(early)(copies[-1].start)
     for copy in copies[:4]:
         copy.wait()
+    item, dp = lax.axis_index("item"), lax.axis_index("dp")
     history = packing_s[item * dps + dp]
     row = positions_v[pl.ds(history, 1), :].astype(jnp.float32)
     diagonal = lax.broadcasted_iota(jnp.int32, (imps, imps), 0) == lax.broadcasted_iota(
@@ -90,10 +88,10 @@
             preferred_element_type=jnp.float32,
         )
     chosen[...] = total.astype(jnp.bfloat16)
-
-    @pl.when(early)
+    copies[-1].wait()
+
+    @pl.when(is_early(item, items_axis))
     def _():
-        copies[-1].wait()
         attention(limits, events_v, chosen, w_uvqk_v, done)
 
 
@@ -218,6 +216,7 @@
 
 
 def rank(item, tensor, items_axis, first):
+    tensor = lax.axis_size("tensor") - 1 - tensor
     return tensor * items_axis + (item + items_axis - first) % items_axis
 
 
@@ -259,19 +258,19 @@
 
     other_catalogues = from_others(catalogue, "dp", dps)
     other_w_out = from_others(w_out, "tensor", tensors)
-    chosen, limits, wanted, events, done = pl.pallas_call(
+    chosen, limits, wanted, events, w_uvqk, done = pl.pallas_call(
         functools.partial(pick_kernel, (items_axis, dps)),
         out_shape=(
             jax.ShapeDtypeStruct((imps, width), jnp.bfloat16),
             jax.ShapeDtypeStruct((imps, 128), jnp.int32),
             jax.ShapeDtypeStruct((1, items_axis * imps), jnp.int32),
             jax.ShapeDtypeStruct(events.shape, events.dtype),
+            jax.ShapeDtypeStruct(w_uvqk.shape, w_uvqk.dtype),
             jax.ShapeDtypeStruct((imps, local_width), jnp.bfloat16),
         ),
         in_specs=[hbm] * 6,
-        out_specs=(vmem,) * 5,
+        out_specs=(vmem,) * 6,
         scratch_shapes=[
-            pltpu.VMEM(w_uvqk.shape, w_uvqk.dtype),
             pltpu.SMEM((hists,), jnp.int32),
             pltpu.SMEM((hists,), jnp.int32),
             pltpu.VMEM((hists, imps), jnp.int32),

time: 34 us -> 33.3 us (0.979)
  blocking collectives: 9.05 us -> 8.12 us
  starting transfers between devices: 11.5 us -> 12 us
    all_to_all x1, blocking collectives: 9.05 us -> 8.12 us  [exchange(): lax.all_to_all(x, COLUMN, split_axis=0, concat_axis=0, tiled=True, axis_i...]
    all_to_all x1, waiting for transfers between devices: 5.29 us -> 4.59 us  [exchange(): lax.all_to_all(x, COLUMN, split_axis=0, concat_axis=0, tiled=True, axis_i...]
    ppermute x5, waiting for transfers between devices: 0.27 us -> 0.76 us  [send(): return lax.ppermute(x, axes, [(i, i ^ r) for i in range(count)])]
    all_to_all x1, starting transfers between devices: 4.72 us -> 5.19 us  [exchange(): lax.all_to_all(x, COLUMN, split_axis=0, concat_axis=0, tiled=True, axis_i...]
where the time goes in v16:
time: 33.3 us; the launch traced here: 33 us
  starting transfers between devices  12 us (36%)
  blocking collectives  8.12 us (24%)
  Pallas kernels  6.25 us (19%)
  waiting for transfers between devices  5.34 us (16%)
  between operations  0.69 us (2%)
  other arithmetic  0.61 us (2%)
    all_to_all x1, blocking collectives, exchange(): lax.all_to_all(x, COLUMN, split_axis=0, concat_axis=0, tiled=True, axis_i...  8.12 us
    ppermute x5, starting transfers between devices, send(): return lax.ppermute(x, axes, [(i, i ^ r) for i in range(count)])  6.79 us
    all_to_all x1, starting transfers between devices, exchange(): lax.all_to_all(x, COLUMN, split_axis=0, concat_axis=0, tiled=True, axis_i...  5.19 us
    all_to_all x1, waiting for transfers between devices, exchange(): lax.all_to_all(x, COLUMN, split_axis=0, concat_axis=0, tiled=True, axis_i...  4.59 us
    pallas_call x1, Pallas kernels, local(): pl.pallas_call(functools.partial(pick_kernel, (items_axis, dps)), out_sha...  2.89 us
    pallas_call x1, Pallas kernels, local(): pl.pallas_call(functools.partial(score_kernel, (items_axis, dps, tensors)...  2.64 us
    ppermute x5, waiting for transfers between devices, send(): return lax.ppermute(x, axes, [(i, i ^ r) for i in range(count)])  0.76 us
    pallas_call x1, Pallas kernels, local(): pl.pallas_call(functools.partial(attend_kernel, items_axis), out_shape=pl...  0.72 us
  transfers between devices with their start and end apart: 6, of which 2 were waited for; matrix products, arithmetic and copies ran while one was open for 0% of the time, Pallas kernels for 11%

profile of v16, /device:TPU:0, one launch (start us, length us, event | category | flops | bytes accessed | tf_op | source)
XLA Modules:
  0.0 33.0 jit_solution(2531786510880645674)
XLA Ops:
  0.6 0.0 copy-start.1
  0.6 0.5 %collective-permute-start.4 = (bf16[1024,1024]{1,0:T(8,128)(2,1)}, bf16[1024,1024]{1,0:T(8,128)(2,1)}, u32[]{:S(2)}, u32[]{:S(2)}) collective-permute-start(bf16[1024,1024]{1,0:T(8,128)(2,1)} %refs_6_.1), channel_id=1, source_target_pairs={{0,2},{2,0},{1,3},{3,1},{4,6},{6,4},{5,7},{7,5},{8,10},{10,8},{9,1... | collective-permute-start | bytes 6291464 | tf_op jit(solution)/shard_map/ppermute | solution.py:234
  1.2 2.9 %pick.1 = (bf16[64,1024]{1,0:T(8,128)(2,1)S(1)}, s32[64,128]{1,0:T(8,128)S(1)}, s32[1,256]{1,0:T(1,128)S(1)}, bf16[768,1024]{1,0:T(8,128)(2,1)S(1)}, bf16[1024,5...) custom-call(s32[8]{0:T(128)} %packing.1, s32[8]{0:T(128)} %lengths.1, s32[8,64]{1,0:T(8,128)} %positions.1, ...), custom_call_target="tpu_custom_call" | custom-call | flops 100663296 | bytes 1572864 | tf_op jit(solution)/shard_map/pick/pallas_call | solution.py:261
  4.1 0.0 copy-start
  4.1 2.6 %collective-permute-start = (bf16[64,1024]{1,0:T(8,128)(2,1)S(1)}, bf16[64,1024]{1,0:T(8,128)(2,1)S(1)}, u32[]{:S(2)}, u32[]{:S(2)}) collective-permute-start(bf16[64,1024]{1,0:T(8,128)(2,1)S(1)} %get-tuple-element.15.chosen.refs_0_), channel_id=1, source_target_pairs={{0,8},{4,12},{8,0},{12,4},{1,9},{5,13},{9,1},{13,5},{2,10},{6,14},... | collective-permute-start | bytes 393224 | tf_op jit(solution)/shard_map/ppermute | solution.py:234
  6.6 1.6 %collective-permute-start.1 = (bf16[64,1024]{1,0:T(8,128)(2,1)S(1)}, bf16[64,1024]{1,0:T(8,128)(2,1)S(1)}, u32[]{:S(2)}, u32[]{:S(2)}) collective-permute-start(bf16[64,1024]{1,0:T(8,128)(2,1)S(1)} %get-tuple-element.15.chosen.refs_0_), channel_id=1, source_target_pairs={{0,4},{4,0},{8,12},{12,8},{1,5},{5,1},{9,13},{13,9},{2,6},{6,2},{1... | collective-permute-start | bytes 393224 | tf_op jit(solution)/shard_map/ppermute | solution.py:234
  8.2 0.0 copy-done.1
  8.2 1.5 %collective-permute-start.3 = (bf16[128,1024]{1,0:T(8,128)(2,1)S(1)}, bf16[128,1024]{1,0:T(8,128)(2,1)S(1)}, u32[]{:S(2)}, u32[]{:S(2)}) collective-permute-start(bf16[128,1024]{1,0:T(8,128)(2,1)S(1)} %copy-done.1), channel_id=1, source_target_pairs={{0,1},{1,0},{2,3},{3,2},{4,5},{5,4},{6,7},{7,6},{8,9},{9,8},{10,11... | collective-permute-start | bytes 786440 | tf_op jit(solution)/shard_map/ppermute | solution.py:234
  9.7 0.7 %attend.1 = bf16[8,64,128]{2,1,0:T(8,128)(2,1)} custom-call(s32[64,128]{1,0:T(8,128)S(1)} %get-tuple-element.13.limits, bf16[768,1024]{1,0:T(8,128)(2,1)S(1)} %get-tuple-element.14.events, bf16[64,1024]{1,0:T(8,128)(2,1)S(1)} %get-tuple-element.15.chosen.refs_0_, bf16[1024,512]{1,0:T(8,128)(2,1)S(1)} %get-tuple-element.16.w_uvqk, ...), custom_call_target="tpu_custom_call" | custom-call | tf_op jit(solution)/shard_map/attend/pallas_call | solution.py:288
  10.5 5.2 %all-to-all-start = ((bf16[8,64,128]{2,1,0:T(8,128)(2,1)}), bf16[8,64,128]{2,1,0:T(8,128)(2,1)S(1)}, u32[]{:S(2)}, u32[]{:S(2)}) async-start(bf16[8,64,128]{2,1,0:T(8,128)(2,1)} %attend.1), calls=%async_computation | async-start | bytes 262144 | tf_op jit(solution)/shard_map/all_to_all | solution.py:228
  15.6 0.0 collective-permute-done.refs_1_
  15.6 0.0 collective-permute-done.1.refs_2_
  15.7 0.6 %collective-permute-start.2 = (bf16[64,1024]{1,0:T(8,128)(2,1)S(1)}, bf16[64,1024]{1,0:T(8,128)(2,1)S(1)}, u32[]{:S(2)}, u32[]{:S(2)}) collective-permute-start(bf16[64,1024]{1,0:T(8,128)(2,1)S(1)} %collective-permute-done.refs_1_), channel_id=1, source_target_pairs={{0,4},{4,0},{8,12},{12,8},{1,5},{5,1},{9,13},{13,9},{2,6},{6,2},{1... | collective-permute-start | bytes 393224 | tf_op jit(solution)/shard_map/ppermute | solution.py:234
  16.3 4.6 %all-to-all-done.gated = bf16[8,64,128]{2,1,0:T(8,128)(2,1)S(1)} async-done(((bf16[8,64,128]{2,1,0:T(8,128)(2,1)}), bf16[8,64,128]{2,1,0:T(8,128)(2,1)S(1)}, u32[]{:S(2)}, u32[]{:S(2)}) %all-to-all-start) | async-done | bytes 131104 | tf_op jit(solution)/shard_map/all_to_all | solution.py:228
  20.9 0.7 %collective-permute-done.2.refs_3_ = bf16[64,1024]{1,0:T(8,128)(2,1)S(1)} collective-permute-done((bf16[64,1024]{1,0:T(8,128)(2,1)S(1)}, bf16[64,1024]{1,0:T(8,128)(2,1)S(1)}, u32[]{:S(2)}, u32[]{:S(2)}) %collective-permute-start.2) | collective-permute-done | bytes 131104 | tf_op jit(solution)/shard_map/ppermute | solution.py:234
  21.6 0.0 collective-permute-done.3.refs_5_
  21.6 0.0 collective-permute-done.4.refs_7_
  21.6 0.0 copy-done
  21.6 2.6 %score.1 = (bf16[64,512]{1,0:T(8,128)(2,1)}, f32[8,1,128]{2,1,0:T(1,128)S(1)}) custom-call(s32[1,256]{1,0:T(1,128)S(1)} %get-tuple-element.12.wanted, bf16[8,64,128]{2,1,0:T(8,128)(2,1)S(1)} %all-to-all-done.gated, bf16[64,1024]{1,0:T(8,128)(2,1)S(1)} %get-tuple-element.15.chosen.refs_0_, bf16[64,1024]{1,0:T(8,128)(2,1)S(1)} %collective-permute-done.refs_1_, ...), custom_call_target="tpu_custom_call" | custom-call | flops 1207959552 | bytes 4194304 | tf_op jit(solution)/shard_map/score/pallas_call | solution.py:303
  24.3 8.1 %all_to_all.10 = f32[8,1,128]{2,1,0:T(1,128)S(1)} all-to-all(f32[8,1,128]{2,1,0:T(1,128)S(1)} %get-tuple-element.21), channel_id=1, replica_groups={{13,1,5,9,12,0,4,8},{15,3,7,11,14,2,6,10},{29,17,21,25,28,16,20,24},{31..., dimensions={0} | all-to-all | bytes 8192 | tf_op jit(solution)/shard_map/all_to_all | solution.py:228
  32.4 0.6 %log_subtract_fusion = f32[64]{0:T(128)} fusion(f32[128]{0:T(128)S(1)} %reduce_sum.9), kind=kLoop, calls=%fused_computation | loop fusion | flops 64 | bytes 768 | tf_op jit(solution)/shard_map/sub | solution.py:337
  (1 shorter events, 0.0 us)
Async XLA Ops:
  0.6 7.6 %copy-start.1 = (bf16[128,1024]{1,0:T(8,128)(2,1)S(1)}, bf16[128,1024]{1,0:T(8,128)(2,1)}, u32[]{:S(2)}) copy-start(bf16[128,1024]{1,0:T(8,128)(2,1)} %refs_4_.1) | copy-start | bytes 786436
  0.6 21.0 %collective-permute-start.4 = (bf16[1024,1024]{1,0:T(8,128)(2,1)}, bf16[1024,1024]{1,0:T(8,128)(2,1)}, u32[]{:S(2)}, u32[]{:S(2)}) collective-permute-start(bf16[1024,1024]{1,0:T(8,128)(2,1)} %refs_6_.1), channel_id=1, source_target_pairs={{0,2},{2,0},{1,3},{3,1},{4,6},{6,4},{5,7},{7,5},{8,10},{10,8},{9,1... | collective-permute-start | bytes 6291464 | tf_op jit(solution)/shard_map/ppermute | solution.py:234
  4.1 17.6 %copy-start = (bf16[1024,1024]{1,0:T(8,128)(2,1)S(1)}, bf16[1024,1024]{1,0:T(8,128)(2,1)}, u32[]{:S(2)}) copy-start(bf16[1024,1024]{1,0:T(8,128)(2,1)} %refs_6_.1) | copy-start | bytes 6291460
  4.1 11.6 %collective-permute-start = (bf16[64,1024]{1,0:T(8,128)(2,1)S(1)}, bf16[64,1024]{1,0:T(8,128)(2,1)S(1)}, u32[]{:S(2)}, u32[]{:S(2)}) collective-permute-start(bf16[64,1024]{1,0:T(8,128)(2,1)S(1)} %get-tuple-element.15.chosen.refs_0_), channel_id=1, source_target_pairs={{0,8},{4,12},{8,0},{12,4},{1,9},{5,13},{9,1},{13,5},{2,10},{6,14},... | collective-permute-start | bytes 393224 | tf_op jit(solution)/shard_map/ppermute | solution.py:234
  6.6 9.0 %collective-permute-start.1 = (bf16[64,1024]{1,0:T(8,128)(2,1)S(1)}, bf16[64,1024]{1,0:T(8,128)(2,1)S(1)}, u32[]{:S(2)}, u32[]{:S(2)}) collective-permute-start(bf16[64,1024]{1,0:T(8,128)(2,1)S(1)} %get-tuple-element.15.chosen.refs_0_), channel_id=1, source_target_pairs={{0,4},{4,0},{8,12},{12,8},{1,5},{5,1},{9,13},{13,9},{2,6},{6,2},{1... | collective-permute-start | bytes 393224 | tf_op jit(solution)/shard_map/ppermute | solution.py:234
  8.2 13.4 %collective-permute-start.3 = (bf16[128,1024]{1,0:T(8,128)(2,1)S(1)}, bf16[128,1024]{1,0:T(8,128)(2,1)S(1)}, u32[]{:S(2)}, u32[]{:S(2)}) collective-permute-start(bf16[128,1024]{1,0:T(8,128)(2,1)S(1)} %copy-done.1), channel_id=1, source_target_pairs={{0,1},{1,0},{2,3},{3,2},{4,5},{5,4},{6,7},{7,6},{8,9},{9,8},{10,11... | collective-permute-start | bytes 786440 | tf_op jit(solution)/shard_map/ppermute | solution.py:234
  10.5 10.4 %all-to-all-start = ((bf16[8,64,128]{2,1,0:T(8,128)(2,1)}), bf16[8,64,128]{2,1,0:T(8,128)(2,1)S(1)}, u32[]{:S(2)}, u32[]{:S(2)}) async-start(bf16[8,64,128]{2,1,0:T(8,128)(2,1)} %attend.1), calls=%async_computation | async-start | bytes 262144 | tf_op jit(solution)/shard_map/all_to_all | solution.py:228
  15.7 6.0 %collective-permute-start.2 = (bf16[64,1024]{1,0:T(8,128)(2,1)S(1)}, bf16[64,1024]{1,0:T(8,128)(2,1)S(1)}, u32[]{:S(2)}, u32[]{:S(2)}) collective-permute-start(bf16[64,1024]{1,0:T(8,128)(2,1)S(1)} %collective-permute-done.refs_1_), channel_id=1, source_target_pairs={{0,4},{4,0},{8,12},{12,8},{1,5},{5,1},{9,13},{13,9},{2,6},{6,2},{1... | collective-permute-start | bytes 393224 | tf_op jit(solution)/shard_map/ppermute | solution.py:234

commit v17 on v16

--- a/solution.py
+++ b/solution.py
@@ -163,7 +163,7 @@
     for k in range(items_axis):
         for t in range(tensors):
             other, head = item ^ slot_rounds[k], tensor ^ tensor_rounds[t]
-            sender = rank(other, head, items_axis, items_axis // 2)
+            sender = rank(other, head, items_axis, (items_axis - 1) // 2)
             gates[k * imps : (k + 1) * imps, t * local_width : (t + 1) * local_width] = gated[sender]
     w_whole = jnp.concatenate([w[...] for w in w_out], axis=0)
     mixed = jnp.dot(gates[...], w_whole, preferred_element_type=jnp.float32)
@@ -298,7 +298,7 @@
         cost_estimate=pl.CostEstimate(flops=0, bytes_accessed=0, transcendentals=0),
         name="attend",
     )(limits, events, chosen, w_uvqk, done)
-    all_gated = exchange(gated, items_axis, tensors, items_axis // 2)
+    all_gated = exchange(gated, items_axis, tensors, (items_axis - 1) // 2)
 
     state, sums = pl.pallas_call(
         functools.partial(score_kernel, (items_axis, dps, tensors)),

time: 33.3 us -> 33.9 us (1.018)
  waiting for transfers between devices: 5.34 us -> 5.7 us
    all_to_all x1, waiting for transfers between devices: 4.59 us -> 5.49 us  [exchange(): lax.all_to_all(x, COLUMN, split_axis=0, concat_axis=0, tiled=True, axis_i...]
    ppermute x5, waiting for transfers between devices: 0.76 us -> 0.21 us  [send(): return lax.ppermute(x, axes, [(i, i ^ r) for i in range(count)])]
where the time goes in v17:
time: 33.9 us; the launch traced here: 33.6 us
  starting transfers between devices  11.9 us (35%)
  blocking collectives  8.12 us (24%)
  Pallas kernels  6.48 us (19%)
  waiting for transfers between devices  5.7 us (17%)
  between operations  0.69 us (2%)
  other arithmetic  0.61 us (2%)
    all_to_all x1, blocking collectives, exchange(): lax.all_to_all(x, COLUMN, split_axis=0, concat_axis=0, tiled=True, axis_i...  8.12 us
    ppermute x5, starting transfers between devices, send(): return lax.ppermute(x, axes, [(i, i ^ r) for i in range(count)])  6.79 us
    all_to_all x1, waiting for transfers between devices, exchange(): lax.all_to_all(x, COLUMN, split_axis=0, concat_axis=0, tiled=True, axis_i...  5.49 us
    all_to_all x1, starting transfers between devices, exchange(): lax.all_to_all(x, COLUMN, split_axis=0, concat_axis=0, tiled=True, axis_i...  5.15 us
    pallas_call x1, Pallas kernels, local(): pl.pallas_call(functools.partial(pick_kernel, (items_axis, dps)), out_sha...  2.89 us
    pallas_call x1, Pallas kernels, local(): pl.pallas_call(functools.partial(score_kernel, (items_axis, dps, tensors)...  2.87 us
    pallas_call x1, Pallas kernels, local(): pl.pallas_call(functools.partial(attend_kernel, items_axis), out_shape=pl...  0.72 us
  transfers between devices with their start and end apart: 6, of which 2 were waited for; matrix products, arithmetic and copies ran while one was open for 0% of the time, Pallas kernels for 11%

profile of v17, /device:TPU:0, one launch (start us, length us, event | category | flops | bytes accessed | tf_op | source)
XLA Modules:
  0.0 33.6 jit_solution(13008275583922557019)
XLA Ops:
  0.6 0.0 copy-start.1
  0.6 0.5 %collective-permute-start.4 = (bf16[1024,1024]{1,0:T(8,128)(2,1)}, bf16[1024,1024]{1,0:T(8,128)(2,1)}, u32[]{:S(2)}, u32[]{:S(2)}) collective-permute-start(bf16[1024,1024]{1,0:T(8,128)(2,1)} %refs_6_.1), channel_id=1, source_target_pairs={{0,2},{2,0},{1,3},{3,1},{4,6},{6,4},{5,7},{7,5},{8,10},{10,8},{9,1... | collective-permute-start | bytes 6291464 | tf_op jit(solution)/shard_map/ppermute | solution.py:234
  1.2 2.9 %pick.1 = (bf16[64,1024]{1,0:T(8,128)(2,1)S(1)}, s32[64,128]{1,0:T(8,128)S(1)}, s32[1,256]{1,0:T(1,128)S(1)}, bf16[768,1024]{1,0:T(8,128)(2,1)S(1)}, bf16[1024,5...) custom-call(s32[8]{0:T(128)} %packing.1, s32[8]{0:T(128)} %lengths.1, s32[8,64]{1,0:T(8,128)} %positions.1, ...), custom_call_target="tpu_custom_call" | custom-call | flops 100663296 | bytes 1572864 | tf_op jit(solution)/shard_map/pick/pallas_call | solution.py:261
  4.1 0.0 copy-start
  4.1 2.6 %collective-permute-start = (bf16[64,1024]{1,0:T(8,128)(2,1)S(1)}, bf16[64,1024]{1,0:T(8,128)(2,1)S(1)}, u32[]{:S(2)}, u32[]{:S(2)}) collective-permute-start(bf16[64,1024]{1,0:T(8,128)(2,1)S(1)} %get-tuple-element.15.chosen.refs_0_), channel_id=1, source_target_pairs={{0,8},{4,12},{8,0},{12,4},{1,9},{5,13},{9,1},{13,5},{2,10},{6,14},... | collective-permute-start | bytes 393224 | tf_op jit(solution)/shard_map/ppermute | solution.py:234
  6.6 1.6 %collective-permute-start.1 = (bf16[64,1024]{1,0:T(8,128)(2,1)S(1)}, bf16[64,1024]{1,0:T(8,128)(2,1)S(1)}, u32[]{:S(2)}, u32[]{:S(2)}) collective-permute-start(bf16[64,1024]{1,0:T(8,128)(2,1)S(1)} %get-tuple-element.15.chosen.refs_0_), channel_id=1, source_target_pairs={{0,4},{4,0},{8,12},{12,8},{1,5},{5,1},{9,13},{13,9},{2,6},{6,2},{1... | collective-permute-start | bytes 393224 | tf_op jit(solution)/shard_map/ppermute | solution.py:234
  8.2 0.0 copy-done.1
  8.2 1.5 %collective-permute-start.3 = (bf16[128,1024]{1,0:T(8,128)(2,1)S(1)}, bf16[128,1024]{1,0:T(8,128)(2,1)S(1)}, u32[]{:S(2)}, u32[]{:S(2)}) collective-permute-start(bf16[128,1024]{1,0:T(8,128)(2,1)S(1)} %copy-done.1), channel_id=1, source_target_pairs={{0,1},{1,0},{2,3},{3,2},{4,5},{5,4},{6,7},{7,6},{8,9},{9,8},{10,11... | collective-permute-start | bytes 786440 | tf_op jit(solution)/shard_map/ppermute | solution.py:234
  9.7 0.7 %attend.1 = bf16[8,64,128]{2,1,0:T(8,128)(2,1)} custom-call(s32[64,128]{1,0:T(8,128)S(1)} %get-tuple-element.13.limits, bf16[768,1024]{1,0:T(8,128)(2,1)S(1)} %get-tuple-element.14.events, bf16[64,1024]{1,0:T(8,128)(2,1)S(1)} %get-tuple-element.15.chosen.refs_0_, bf16[1024,512]{1,0:T(8,128)(2,1)S(1)} %get-tuple-element.16.w_uvqk, ...), custom_call_target="tpu_custom_call" | custom-call | tf_op jit(solution)/shard_map/attend/pallas_call | solution.py:288
  10.5 5.2 %all-to-all-start = ((bf16[8,64,128]{2,1,0:T(8,128)(2,1)}), bf16[8,64,128]{2,1,0:T(8,128)(2,1)S(1)}, u32[]{:S(2)}, u32[]{:S(2)}) async-start(bf16[8,64,128]{2,1,0:T(8,128)(2,1)} %attend.1), calls=%async_computation | async-start | bytes 262144 | tf_op jit(solution)/shard_map/all_to_all | solution.py:228
  15.6 0.0 collective-permute-done.refs_1_
  15.6 0.0 collective-permute-done.1.refs_2_
  15.6 0.6 %collective-permute-start.2 = (bf16[64,1024]{1,0:T(8,128)(2,1)S(1)}, bf16[64,1024]{1,0:T(8,128)(2,1)S(1)}, u32[]{:S(2)}, u32[]{:S(2)}) collective-permute-start(bf16[64,1024]{1,0:T(8,128)(2,1)S(1)} %collective-permute-done.refs_1_), channel_id=1, source_target_pairs={{0,4},{4,0},{8,12},{12,8},{1,5},{5,1},{9,13},{13,9},{2,6},{6,2},{1... | collective-permute-start | bytes 393224 | tf_op jit(solution)/shard_map/ppermute | solution.py:234
  16.2 5.5 %all-to-all-done.gated = bf16[8,64,128]{2,1,0:T(8,128)(2,1)S(1)} async-done(((bf16[8,64,128]{2,1,0:T(8,128)(2,1)}), bf16[8,64,128]{2,1,0:T(8,128)(2,1)S(1)}, u32[]{:S(2)}, u32[]{:S(2)}) %all-to-all-start) | async-done | bytes 131104 | tf_op jit(solution)/shard_map/all_to_all | solution.py:228
  21.7 0.2 collective-permute-done.2.refs_3_
  21.9 0.0 collective-permute-done.3.refs_5_
  21.9 0.0 collective-permute-done.4.refs_7_
  21.9 0.0 copy-done
  21.9 2.9 %score.1 = (bf16[64,512]{1,0:T(8,128)(2,1)}, f32[8,1,128]{2,1,0:T(1,128)S(1)}) custom-call(s32[1,256]{1,0:T(1,128)S(1)} %get-tuple-element.12.wanted, bf16[8,64,128]{2,1,0:T(8,128)(2,1)S(1)} %all-to-all-done.gated, bf16[64,1024]{1,0:T(8,128)(2,1)S(1)} %get-tuple-element.15.chosen.refs_0_, bf16[64,1024]{1,0:T(8,128)(2,1)S(1)} %collective-permute-done.refs_1_, ...), custom_call_target="tpu_custom_call" | custom-call | flops 1207959552 | bytes 4194304 | tf_op jit(solution)/shard_map/score/pallas_call | solution.py:303
  24.8 8.1 %all_to_all.10 = f32[8,1,128]{2,1,0:T(1,128)S(1)} all-to-all(f32[8,1,128]{2,1,0:T(1,128)S(1)} %get-tuple-element.21), channel_id=1, replica_groups={{13,1,5,9,12,0,4,8},{15,3,7,11,14,2,6,10},{29,17,21,25,28,16,20,24},{31..., dimensions={0} | all-to-all | bytes 8192 | tf_op jit(solution)/shard_map/all_to_all | solution.py:228
  33.0 0.6 %log_subtract_fusion = f32[64]{0:T(128)} fusion(f32[128]{0:T(128)S(1)} %reduce_sum.9), kind=kLoop, calls=%fused_computation | loop fusion | flops 64 | bytes 768 | tf_op jit(solution)/shard_map/sub | solution.py:337
  (1 shorter events, 0.0 us)
Async XLA Ops:
  0.6 7.6 %copy-start.1 = (bf16[128,1024]{1,0:T(8,128)(2,1)S(1)}, bf16[128,1024]{1,0:T(8,128)(2,1)}, u32[]{:S(2)}) copy-start(bf16[128,1024]{1,0:T(8,128)(2,1)} %refs_4_.1) | copy-start | bytes 786436
  0.6 21.3 %collective-permute-start.4 = (bf16[1024,1024]{1,0:T(8,128)(2,1)}, bf16[1024,1024]{1,0:T(8,128)(2,1)}, u32[]{:S(2)}, u32[]{:S(2)}) collective-permute-start(bf16[1024,1024]{1,0:T(8,128)(2,1)} %refs_6_.1), channel_id=1, source_target_pairs={{0,2},{2,0},{1,3},{3,1},{4,6},{6,4},{5,7},{7,5},{8,10},{10,8},{9,1... | collective-permute-start | bytes 6291464 | tf_op jit(solution)/shard_map/ppermute | solution.py:234
  4.1 17.9 %copy-start = (bf16[1024,1024]{1,0:T(8,128)(2,1)S(1)}, bf16[1024,1024]{1,0:T(8,128)(2,1)}, u32[]{:S(2)}) copy-start(bf16[1024,1024]{1,0:T(8,128)(2,1)} %refs_6_.1) | copy-start | bytes 6291460
  4.1 11.5 %collective-permute-start = (bf16[64,1024]{1,0:T(8,128)(2,1)S(1)}, bf16[64,1024]{1,0:T(8,128)(2,1)S(1)}, u32[]{:S(2)}, u32[]{:S(2)}) collective-permute-start(bf16[64,1024]{1,0:T(8,128)(2,1)S(1)} %get-tuple-element.15.chosen.refs_0_), channel_id=1, source_target_pairs={{0,8},{4,12},{8,0},{12,4},{1,9},{5,13},{9,1},{13,5},{2,10},{6,14},... | collective-permute-start | bytes 393224 | tf_op jit(solution)/shard_map/ppermute | solution.py:234
  6.6 9.0 %collective-permute-start.1 = (bf16[64,1024]{1,0:T(8,128)(2,1)S(1)}, bf16[64,1024]{1,0:T(8,128)(2,1)S(1)}, u32[]{:S(2)}, u32[]{:S(2)}) collective-permute-start(bf16[64,1024]{1,0:T(8,128)(2,1)S(1)} %get-tuple-element.15.chosen.refs_0_), channel_id=1, source_target_pairs={{0,4},{4,0},{8,12},{12,8},{1,5},{5,1},{9,13},{13,9},{2,6},{6,2},{1... | collective-permute-start | bytes 393224 | tf_op jit(solution)/shard_map/ppermute | solution.py:234
  8.2 13.7 %collective-permute-start.3 = (bf16[128,1024]{1,0:T(8,128)(2,1)S(1)}, bf16[128,1024]{1,0:T(8,128)(2,1)S(1)}, u32[]{:S(2)}, u32[]{:S(2)}) collective-permute-start(bf16[128,1024]{1,0:T(8,128)(2,1)S(1)} %copy-done.1), channel_id=1, source_target_pairs={{0,1},{1,0},{2,3},{3,2},{4,5},{5,4},{6,7},{7,6},{8,9},{9,8},{10,11... | collective-permute-start | bytes 786440 | tf_op jit(solution)/shard_map/ppermute | solution.py:234
  10.5 11.3 %all-to-all-start = ((bf16[8,64,128]{2,1,0:T(8,128)(2,1)}), bf16[8,64,128]{2,1,0:T(8,128)(2,1)S(1)}, u32[]{:S(2)}, u32[]{:S(2)}) async-start(bf16[8,64,128]{2,1,0:T(8,128)(2,1)} %attend.1), calls=%async_computation | async-start | bytes 262144 | tf_op jit(solution)/shard_map/all_to_all | solution.py:228
  15.6 6.3 %collective-permute-start.2 = (bf16[64,1024]{1,0:T(8,128)(2,1)S(1)}, bf16[64,1024]{1,0:T(8,128)(2,1)S(1)}, u32[]{:S(2)}, u32[]{:S(2)}) collective-permute-start(bf16[64,1024]{1,0:T(8,128)(2,1)S(1)} %collective-permute-done.refs_1_), channel_id=1, source_target_pairs={{0,4},{4,0},{8,12},{12,8},{1,5},{5,1},{9,13},{13,9},{2,6},{6,2},{1... | collective-permute-start | bytes 393224 | tf_op jit(solution)/shard_map/ppermute | solution.py:234

commit v18 on v16

--- a/solution.py
+++ b/solution.py
@@ -13,7 +13,7 @@
 COLUMN = ("tensor", "item")
 NT = (((1,), (1,)), ((), ()))
 MIB = 1024 * 1024
-EVENT_PARTS = 3
+EVENT_PARTS = 6
 
 
 def rounds(count):
@@ -217,7 +217,7 @@
 
 def rank(item, tensor, items_axis, first):
     tensor = lax.axis_size("tensor") - 1 - tensor
-    return tensor * items_axis + (item + items_axis - first) % items_axis
+    return tensor * items_axis + ((item + items_axis - first) & (items_axis - 1))
 
 
 def exchange(x, items_axis, tensors, first):

time: 33.3 us -> 33.6 us (level)
  no operation moved by 1% of the time
where the time goes in v18:
time: 33.6 us; the launch traced here: 33.3 us
  starting transfers between devices  12 us (36%)
  blocking collectives  8.12 us (24%)
  Pallas kernels  6.51 us (19%)
  waiting for transfers between devices  5.34 us (16%)
  between operations  0.69 us (2%)
  other arithmetic  0.61 us (2%)
    all_to_all x1, blocking collectives, exchange(): lax.all_to_all(x, COLUMN, split_axis=0, concat_axis=0, tiled=True, axis_i...  8.12 us
    ppermute x5, starting transfers between devices, send(): return lax.ppermute(x, axes, [(i, i ^ r) for i in range(count)])  6.79 us
    all_to_all x1, starting transfers between devices, exchange(): lax.all_to_all(x, COLUMN, split_axis=0, concat_axis=0, tiled=True, axis_i...  5.2 us
    all_to_all x1, waiting for transfers between devices, exchange(): lax.all_to_all(x, COLUMN, split_axis=0, concat_axis=0, tiled=True, axis_i...  4.58 us
    pallas_call x1, Pallas kernels, local(): pl.pallas_call(functools.partial(pick_kernel, (items_axis, dps)), out_sha...  2.92 us
    pallas_call x1, Pallas kernels, local(): pl.pallas_call(functools.partial(score_kernel, (items_axis, dps, tensors)...  2.86 us
    ppermute x5, waiting for transfers between devices, send(): return lax.ppermute(x, axes, [(i, i ^ r) for i in range(count)])  0.76 us
    pallas_call x1, Pallas kernels, local(): pl.pallas_call(functools.partial(attend_kernel, items_axis), out_shape=pl...  0.72 us
  transfers between devices with their start and end apart: 6, of which 2 were waited for; matrix products, arithmetic and copies ran while one was open for 0% of the time, Pallas kernels for 11%

profile of v18, /device:TPU:0, one launch (start us, length us, event | category | flops | bytes accessed | tf_op | source)
XLA Modules:
  0.0 33.3 jit_solution(6781429148188813725)
XLA Ops:
  0.6 0.0 copy-start.1
  0.6 0.5 %collective-permute-start.4 = (bf16[1024,1024]{1,0:T(8,128)(2,1)}, bf16[1024,1024]{1,0:T(8,128)(2,1)}, u32[]{:S(2)}, u32[]{:S(2)}) collective-permute-start(bf16[1024,1024]{1,0:T(8,128)(2,1)} %refs_6_.1), channel_id=1, source_target_pairs={{0,2},{2,0},{1,3},{3,1},{4,6},{6,4},{5,7},{7,5},{8,10},{10,8},{9,1... | collective-permute-start | bytes 6291464 | tf_op jit(solution)/shard_map/ppermute | solution.py:234
  1.2 2.9 %pick.1 = (bf16[64,1024]{1,0:T(8,128)(2,1)S(1)}, s32[64,128]{1,0:T(8,128)S(1)}, s32[1,256]{1,0:T(1,128)S(1)}, bf16[768,1024]{1,0:T(8,128)(2,1)S(1)}, bf16[1024,5...) custom-call(s32[8]{0:T(128)} %packing.1, s32[8]{0:T(128)} %lengths.1, s32[8,64]{1,0:T(8,128)} %positions.1, ...), custom_call_target="tpu_custom_call" | custom-call | flops 100663296 | bytes 1572864 | tf_op jit(solution)/shard_map/pick/pallas_call | solution.py:261
  4.1 0.0 copy-start
  4.1 2.6 %collective-permute-start = (bf16[64,1024]{1,0:T(8,128)(2,1)S(1)}, bf16[64,1024]{1,0:T(8,128)(2,1)S(1)}, u32[]{:S(2)}, u32[]{:S(2)}) collective-permute-start(bf16[64,1024]{1,0:T(8,128)(2,1)S(1)} %get-tuple-element.15.chosen.refs_0_), channel_id=1, source_target_pairs={{0,8},{4,12},{8,0},{12,4},{1,9},{5,13},{9,1},{13,5},{2,10},{6,14},... | collective-permute-start | bytes 393224 | tf_op jit(solution)/shard_map/ppermute | solution.py:234
  6.7 1.6 %collective-permute-start.1 = (bf16[64,1024]{1,0:T(8,128)(2,1)S(1)}, bf16[64,1024]{1,0:T(8,128)(2,1)S(1)}, u32[]{:S(2)}, u32[]{:S(2)}) collective-permute-start(bf16[64,1024]{1,0:T(8,128)(2,1)S(1)} %get-tuple-element.15.chosen.refs_0_), channel_id=1, source_target_pairs={{0,4},{4,0},{8,12},{12,8},{1,5},{5,1},{9,13},{13,9},{2,6},{6,2},{1... | collective-permute-start | bytes 393224 | tf_op jit(solution)/shard_map/ppermute | solution.py:234
  8.3 0.0 copy-done.1
  8.3 1.5 %collective-permute-start.3 = (bf16[128,1024]{1,0:T(8,128)(2,1)S(1)}, bf16[128,1024]{1,0:T(8,128)(2,1)S(1)}, u32[]{:S(2)}, u32[]{:S(2)}) collective-permute-start(bf16[128,1024]{1,0:T(8,128)(2,1)S(1)} %copy-done.1), channel_id=1, source_target_pairs={{0,1},{1,0},{2,3},{3,2},{4,5},{5,4},{6,7},{7,6},{8,9},{9,8},{10,11... | collective-permute-start | bytes 786440 | tf_op jit(solution)/shard_map/ppermute | solution.py:234
  9.7 0.7 %attend.1 = bf16[8,64,128]{2,1,0:T(8,128)(2,1)} custom-call(s32[64,128]{1,0:T(8,128)S(1)} %get-tuple-element.13.limits, bf16[768,1024]{1,0:T(8,128)(2,1)S(1)} %get-tuple-element.14.events, bf16[64,1024]{1,0:T(8,128)(2,1)S(1)} %get-tuple-element.15.chosen.refs_0_, bf16[1024,512]{1,0:T(8,128)(2,1)S(1)} %get-tuple-element.16.w_uvqk, ...), custom_call_target="tpu_custom_call" | custom-call | tf_op jit(solution)/shard_map/attend/pallas_call | solution.py:288
  10.5 5.2 %all-to-all-start = ((bf16[8,64,128]{2,1,0:T(8,128)(2,1)}), bf16[8,64,128]{2,1,0:T(8,128)(2,1)S(1)}, u32[]{:S(2)}, u32[]{:S(2)}) async-start(bf16[8,64,128]{2,1,0:T(8,128)(2,1)} %attend.1), calls=%async_computation | async-start | bytes 262144 | tf_op jit(solution)/shard_map/all_to_all | solution.py:228
  15.7 0.0 collective-permute-done.refs_1_
  15.7 0.0 collective-permute-done.1.refs_2_
  15.7 0.6 %collective-permute-start.2 = (bf16[64,1024]{1,0:T(8,128)(2,1)S(1)}, bf16[64,1024]{1,0:T(8,128)(2,1)S(1)}, u32[]{:S(2)}, u32[]{:S(2)}) collective-permute-start(bf16[64,1024]{1,0:T(8,128)(2,1)S(1)} %collective-permute-done.refs_1_), channel_id=1, source_target_pairs={{0,4},{4,0},{8,12},{12,8},{1,5},{5,1},{9,13},{13,9},{2,6},{6,2},{1... | collective-permute-start | bytes 393224 | tf_op jit(solution)/shard_map/ppermute | solution.py:234
  16.3 4.6 %all-to-all-done.gated = bf16[8,64,128]{2,1,0:T(8,128)(2,1)S(1)} async-done(((bf16[8,64,128]{2,1,0:T(8,128)(2,1)}), bf16[8,64,128]{2,1,0:T(8,128)(2,1)S(1)}, u32[]{:S(2)}, u32[]{:S(2)}) %all-to-all-start) | async-done | bytes 131104 | tf_op jit(solution)/shard_map/all_to_all | solution.py:228
  20.9 0.7 %collective-permute-done.2.refs_3_ = bf16[64,1024]{1,0:T(8,128)(2,1)S(1)} collective-permute-done((bf16[64,1024]{1,0:T(8,128)(2,1)S(1)}, bf16[64,1024]{1,0:T(8,128)(2,1)S(1)}, u32[]{:S(2)}, u32[]{:S(2)}) %collective-permute-start.2) | collective-permute-done | bytes 131104 | tf_op jit(solution)/shard_map/ppermute | solution.py:234
  21.6 0.0 collective-permute-done.3.refs_5_
  21.6 0.0 collective-permute-done.4.refs_7_
  21.6 0.0 copy-done
  21.7 2.9 %score.1 = (bf16[64,512]{1,0:T(8,128)(2,1)}, f32[8,1,128]{2,1,0:T(1,128)S(1)}) custom-call(s32[1,256]{1,0:T(1,128)S(1)} %get-tuple-element.12.wanted, bf16[8,64,128]{2,1,0:T(8,128)(2,1)S(1)} %all-to-all-done.gated, bf16[64,1024]{1,0:T(8,128)(2,1)S(1)} %get-tuple-element.15.chosen.refs_0_, bf16[64,1024]{1,0:T(8,128)(2,1)S(1)} %collective-permute-done.refs_1_, ...), custom_call_target="tpu_custom_call" | custom-call | flops 1207959552 | bytes 4194304 | tf_op jit(solution)/shard_map/score/pallas_call | solution.py:303
  24.5 8.1 %all_to_all.10 = f32[8,1,128]{2,1,0:T(1,128)S(1)} all-to-all(f32[8,1,128]{2,1,0:T(1,128)S(1)} %get-tuple-element.21), channel_id=1, replica_groups={{13,1,5,9,12,0,4,8},{15,3,7,11,14,2,6,10},{29,17,21,25,28,16,20,24},{31..., dimensions={0} | all-to-all | bytes 8192 | tf_op jit(solution)/shard_map/all_to_all | solution.py:228
  32.7 0.6 %log_subtract_fusion = f32[64]{0:T(128)} fusion(f32[128]{0:T(128)S(1)} %reduce_sum.9), kind=kLoop, calls=%fused_computation | loop fusion | flops 64 | bytes 768 | tf_op jit(solution)/shard_map/sub | solution.py:337
  (1 shorter events, 0.0 us)
Async XLA Ops:
  0.6 7.6 %copy-start.1 = (bf16[128,1024]{1,0:T(8,128)(2,1)S(1)}, bf16[128,1024]{1,0:T(8,128)(2,1)}, u32[]{:S(2)}) copy-start(bf16[128,1024]{1,0:T(8,128)(2,1)} %refs_4_.1) | copy-start | bytes 786436
  0.6 21.0 %collective-permute-start.4 = (bf16[1024,1024]{1,0:T(8,128)(2,1)}, bf16[1024,1024]{1,0:T(8,128)(2,1)}, u32[]{:S(2)}, u32[]{:S(2)}) collective-permute-start(bf16[1024,1024]{1,0:T(8,128)(2,1)} %refs_6_.1), channel_id=1, source_target_pairs={{0,2},{2,0},{1,3},{3,1},{4,6},{6,4},{5,7},{7,5},{8,10},{10,8},{9,1... | collective-permute-start | bytes 6291464 | tf_op jit(solution)/shard_map/ppermute | solution.py:234
  4.1 17.6 %copy-start = (bf16[1024,1024]{1,0:T(8,128)(2,1)S(1)}, bf16[1024,1024]{1,0:T(8,128)(2,1)}, u32[]{:S(2)}) copy-start(bf16[1024,1024]{1,0:T(8,128)(2,1)} %refs_6_.1) | copy-start | bytes 6291460
  4.1 11.6 %collective-permute-start = (bf16[64,1024]{1,0:T(8,128)(2,1)S(1)}, bf16[64,1024]{1,0:T(8,128)(2,1)S(1)}, u32[]{:S(2)}, u32[]{:S(2)}) collective-permute-start(bf16[64,1024]{1,0:T(8,128)(2,1)S(1)} %get-tuple-element.15.chosen.refs_0_), channel_id=1, source_target_pairs={{0,8},{4,12},{8,0},{12,4},{1,9},{5,13},{9,1},{13,5},{2,10},{6,14},... | collective-permute-start | bytes 393224 | tf_op jit(solution)/shard_map/ppermute | solution.py:234
  6.7 9.0 %collective-permute-start.1 = (bf16[64,1024]{1,0:T(8,128)(2,1)S(1)}, bf16[64,1024]{1,0:T(8,128)(2,1)S(1)}, u32[]{:S(2)}, u32[]{:S(2)}) collective-permute-start(bf16[64,1024]{1,0:T(8,128)(2,1)S(1)} %get-tuple-element.15.chosen.refs_0_), channel_id=1, source_target_pairs={{0,4},{4,0},{8,12},{12,8},{1,5},{5,1},{9,13},{13,9},{2,6},{6,2},{1... | collective-permute-start | bytes 393224 | tf_op jit(solution)/shard_map/ppermute | solution.py:234
  8.3 13.4 %collective-permute-start.3 = (bf16[128,1024]{1,0:T(8,128)(2,1)S(1)}, bf16[128,1024]{1,0:T(8,128)(2,1)S(1)}, u32[]{:S(2)}, u32[]{:S(2)}) collective-permute-start(bf16[128,1024]{1,0:T(8,128)(2,1)S(1)} %copy-done.1), channel_id=1, source_target_pairs={{0,1},{1,0},{2,3},{3,2},{4,5},{5,4},{6,7},{7,6},{8,9},{9,8},{10,11... | collective-permute-start | bytes 786440 | tf_op jit(solution)/shard_map/ppermute | solution.py:234
  10.5 10.4 %all-to-all-start = ((bf16[8,64,128]{2,1,0:T(8,128)(2,1)}), bf16[8,64,128]{2,1,0:T(8,128)(2,1)S(1)}, u32[]{:S(2)}, u32[]{:S(2)}) async-start(bf16[8,64,128]{2,1,0:T(8,128)(2,1)} %attend.1), calls=%async_computation | async-start | bytes 262144 | tf_op jit(solution)/shard_map/all_to_all | solution.py:228
  15.7 6.0 %collective-permute-start.2 = (bf16[64,1024]{1,0:T(8,128)(2,1)S(1)}, bf16[64,1024]{1,0:T(8,128)(2,1)S(1)}, u32[]{:S(2)}, u32[]{:S(2)}) collective-permute-start(bf16[64,1024]{1,0:T(8,128)(2,1)S(1)} %collective-permute-done.refs_1_), channel_id=1, source_target_pairs={{0,4},{4,0},{8,12},{12,8},{1,5},{5,1},{9,13},{13,9},{2,6},{6,2},{1... | collective-permute-start | bytes 393224 | tf_op jit(solution)/shard_map/ppermute | solution.py:234

commit v19 on v16

--- a/solution.py
+++ b/solution.py
@@ -207,7 +207,7 @@
                 [v[:, part * imps : (part + 1) * imps] for v in (total, target)], axis=1
             )
             for t in range(tensors):
-                sums[rank(owner, t, items_axis, items_axis - 1)] = both
+                sums[rank(owner, tensors - 1 - t, items_axis, items_axis - 1)] = both
     state_copy.wait()
 
 
@@ -216,15 +216,15 @@
 
 
 def rank(item, tensor, items_axis, first):
-    tensor = lax.axis_size("tensor") - 1 - tensor
     return tensor * items_axis + (item + items_axis - first) % items_axis
 
 
-def exchange(x, items_axis, tensors, first):
+def exchange(x, items_axis, tensors, first, last_tensor_leads):
     group = [0] * (items_axis * tensors)
     for tensor in range(tensors):
         for item in range(items_axis):
-            group[rank(item, tensor, items_axis, first)] = tensor * items_axis + item
+            place = tensors - 1 - tensor if last_tensor_leads else tensor
+            group[rank(item, place, items_axis, first)] = tensor * items_axis + item
     return lax.all_to_all(
         x, COLUMN, split_axis=0, concat_axis=0, tiled=True, axis_index_groups=[group]
     )
@@ -298,7 +298,7 @@
         cost_estimate=pl.CostEstimate(flops=0, bytes_accessed=0, transcendentals=0),
         name="attend",
     )(limits, events, chosen, w_uvqk, done)
-    all_gated = exchange(gated, items_axis, tensors, items_axis // 2)
+    all_gated = exchange(gated, items_axis, tensors, items_axis // 2, False)
 
     state, sums = pl.pallas_call(
         functools.partial(score_kernel, (items_axis, dps, tensors)),
@@ -332,7 +332,7 @@
         catalogue,
         *(in_hbm(x) for x in other_catalogues),
     )
-    sums = exchange(sums, items_axis, tensors, items_axis - 1)
+    sums = exchange(sums, items_axis, tensors, items_axis - 1, True)
     sums = jnp.sum(sums, axis=(0, 1))
     return (state, sums[imps:] - jnp.log(sums[:imps]))
 

time: 33.3 us -> 33.3 us (level)
  starting transfers between devices: 12 us -> 11.5 us
    all_to_all x1, waiting for transfers between devices: 4.59 us -> 5.28 us  [exchange(): lax.all_to_all(x, COLUMN, split_axis=0, concat_axis=0, tiled=True, axis_i...]
    all_to_all x1, starting transfers between devices: 5.19 us -> 4.72 us  [exchange(): lax.all_to_all(x, COLUMN, split_axis=0, concat_axis=0, tiled=True, axis_i...]
    ppermute x5, waiting for transfers between devices: 0.76 us -> 0.37 us  [send(): return lax.ppermute(x, axes, [(i, i ^ r) for i in range(count)])]
where the time goes in v19:
time: 33.3 us; the launch traced here: 33 us
  starting transfers between devices  11.5 us (35%)
  blocking collectives  8.31 us (25%)
  Pallas kernels  6.24 us (19%)
  waiting for transfers between devices  5.64 us (17%)
  between operations  0.69 us (2%)
  other arithmetic  0.61 us (2%)
    all_to_all x1, blocking collectives, exchange(): lax.all_to_all(x, COLUMN, split_axis=0, concat_axis=0, tiled=True, axis_i...  8.31 us
    ppermute x5, starting transfers between devices, send(): return lax.ppermute(x, axes, [(i, i ^ r) for i in range(count)])  6.8 us
    all_to_all x1, waiting for transfers between devices, exchange(): lax.all_to_all(x, COLUMN, split_axis=0, concat_axis=0, tiled=True, axis_i...  5.28 us
    all_to_all x1, starting transfers between devices, exchange(): lax.all_to_all(x, COLUMN, split_axis=0, concat_axis=0, tiled=True, axis_i...  4.72 us
    pallas_call x1, Pallas kernels, local(): pl.pallas_call(functools.partial(pick_kernel, (items_axis, dps)), out_sha...  2.89 us
    pallas_call x1, Pallas kernels, local(): pl.pallas_call(functools.partial(score_kernel, (items_axis, dps, tensors)...  2.63 us
    pallas_call x1, Pallas kernels, local(): pl.pallas_call(functools.partial(attend_kernel, items_axis), out_shape=pl...  0.72 us
  transfers between devices with their start and end apart: 6, of which 2 were waited for; matrix products, arithmetic and copies ran while one was open for 0% of the time, Pallas kernels for 11%

profile of v19, /device:TPU:0, one launch (start us, length us, event | category | flops | bytes accessed | tf_op | source)
XLA Modules:
  0.0 33.0 jit_solution(11115246987638379054)
XLA Ops:
  0.6 0.0 copy-start.1
  0.6 0.5 %collective-permute-start.4 = (bf16[1024,1024]{1,0:T(8,128)(2,1)}, bf16[1024,1024]{1,0:T(8,128)(2,1)}, u32[]{:S(2)}, u32[]{:S(2)}) collective-permute-start(bf16[1024,1024]{1,0:T(8,128)(2,1)} %refs_6_.1), channel_id=1, source_target_pairs={{0,2},{2,0},{1,3},{3,1},{4,6},{6,4},{5,7},{7,5},{8,10},{10,8},{9,1... | collective-permute-start | bytes 6291464 | tf_op jit(solution)/shard_map/ppermute | solution.py:234
  1.2 2.9 %pick.1 = (bf16[64,1024]{1,0:T(8,128)(2,1)S(1)}, s32[64,128]{1,0:T(8,128)S(1)}, s32[1,256]{1,0:T(1,128)S(1)}, bf16[768,1024]{1,0:T(8,128)(2,1)S(1)}, bf16[1024,5...) custom-call(s32[8]{0:T(128)} %packing.1, s32[8]{0:T(128)} %lengths.1, s32[8,64]{1,0:T(8,128)} %positions.1, ...), custom_call_target="tpu_custom_call" | custom-call | flops 100663296 | bytes 1572864 | tf_op jit(solution)/shard_map/pick/pallas_call | solution.py:261
  4.1 0.0 copy-start
  4.1 2.6 %collective-permute-start = (bf16[64,1024]{1,0:T(8,128)(2,1)S(1)}, bf16[64,1024]{1,0:T(8,128)(2,1)S(1)}, u32[]{:S(2)}, u32[]{:S(2)}) collective-permute-start(bf16[64,1024]{1,0:T(8,128)(2,1)S(1)} %get-tuple-element.15.chosen.refs_0_), channel_id=1, source_target_pairs={{0,8},{4,12},{8,0},{12,4},{1,9},{5,13},{9,1},{13,5},{2,10},{6,14},... | collective-permute-start | bytes 393224 | tf_op jit(solution)/shard_map/ppermute | solution.py:234
  6.6 1.6 %collective-permute-start.1 = (bf16[64,1024]{1,0:T(8,128)(2,1)S(1)}, bf16[64,1024]{1,0:T(8,128)(2,1)S(1)}, u32[]{:S(2)}, u32[]{:S(2)}) collective-permute-start(bf16[64,1024]{1,0:T(8,128)(2,1)S(1)} %get-tuple-element.15.chosen.refs_0_), channel_id=1, source_target_pairs={{0,4},{4,0},{8,12},{12,8},{1,5},{5,1},{9,13},{13,9},{2,6},{6,2},{1... | collective-permute-start | bytes 393224 | tf_op jit(solution)/shard_map/ppermute | solution.py:234
  8.2 0.0 copy-done.1
  8.2 1.5 %collective-permute-start.3 = (bf16[128,1024]{1,0:T(8,128)(2,1)S(1)}, bf16[128,1024]{1,0:T(8,128)(2,1)S(1)}, u32[]{:S(2)}, u32[]{:S(2)}) collective-permute-start(bf16[128,1024]{1,0:T(8,128)(2,1)S(1)} %copy-done.1), channel_id=1, source_target_pairs={{0,1},{1,0},{2,3},{3,2},{4,5},{5,4},{6,7},{7,6},{8,9},{9,8},{10,11... | collective-permute-start | bytes 786440 | tf_op jit(solution)/shard_map/ppermute | solution.py:234
  9.7 0.7 %attend.1 = bf16[8,64,128]{2,1,0:T(8,128)(2,1)} custom-call(s32[64,128]{1,0:T(8,128)S(1)} %get-tuple-element.13.limits, bf16[768,1024]{1,0:T(8,128)(2,1)S(1)} %get-tuple-element.14.events, bf16[64,1024]{1,0:T(8,128)(2,1)S(1)} %get-tuple-element.15.chosen.refs_0_, bf16[1024,512]{1,0:T(8,128)(2,1)S(1)} %get-tuple-element.16.w_uvqk, ...), custom_call_target="tpu_custom_call" | custom-call | tf_op jit(solution)/shard_map/attend/pallas_call | solution.py:288
  10.5 4.7 %all-to-all-start = ((bf16[8,64,128]{2,1,0:T(8,128)(2,1)}), bf16[8,64,128]{2,1,0:T(8,128)(2,1)S(1)}, u32[]{:S(2)}, u32[]{:S(2)}) async-start(bf16[8,64,128]{2,1,0:T(8,128)(2,1)} %attend.1), calls=%async_computation | async-start | bytes 262144 | tf_op jit(solution)/shard_map/all_to_all | solution.py:228
  15.2 0.0 collective-permute-done.refs_1_
  15.2 0.0 collective-permute-done.1.refs_2_
  15.2 0.6 %collective-permute-start.2 = (bf16[64,1024]{1,0:T(8,128)(2,1)S(1)}, bf16[64,1024]{1,0:T(8,128)(2,1)S(1)}, u32[]{:S(2)}, u32[]{:S(2)}) collective-permute-start(bf16[64,1024]{1,0:T(8,128)(2,1)S(1)} %collective-permute-done.refs_1_), channel_id=1, source_target_pairs={{0,4},{4,0},{8,12},{12,8},{1,5},{5,1},{9,13},{13,9},{2,6},{6,2},{1... | collective-permute-start | bytes 393224 | tf_op jit(solution)/shard_map/ppermute | solution.py:234
  15.8 5.3 %all-to-all-done.gated = bf16[8,64,128]{2,1,0:T(8,128)(2,1)S(1)} async-done(((bf16[8,64,128]{2,1,0:T(8,128)(2,1)}), bf16[8,64,128]{2,1,0:T(8,128)(2,1)S(1)}, u32[]{:S(2)}, u32[]{:S(2)}) %all-to-all-start) | async-done | bytes 131104 | tf_op jit(solution)/shard_map/all_to_all | solution.py:228
  21.1 0.4 %collective-permute-done.2.refs_3_ = bf16[64,1024]{1,0:T(8,128)(2,1)S(1)} collective-permute-done((bf16[64,1024]{1,0:T(8,128)(2,1)S(1)}, bf16[64,1024]{1,0:T(8,128)(2,1)S(1)}, u32[]{:S(2)}, u32[]{:S(2)}) %collective-permute-start.2) | collective-permute-done | bytes 131104 | tf_op jit(solution)/shard_map/ppermute | solution.py:234
  21.4 0.0 collective-permute-done.3.refs_5_
  21.5 0.0 collective-permute-done.4.refs_7_
  21.5 0.0 copy-done
  21.5 2.6 %score.1 = (bf16[64,512]{1,0:T(8,128)(2,1)}, f32[8,1,128]{2,1,0:T(1,128)S(1)}) custom-call(s32[1,256]{1,0:T(1,128)S(1)} %get-tuple-element.12.wanted, bf16[8,64,128]{2,1,0:T(8,128)(2,1)S(1)} %all-to-all-done.gated, bf16[64,1024]{1,0:T(8,128)(2,1)S(1)} %get-tuple-element.15.chosen.refs_0_, bf16[64,1024]{1,0:T(8,128)(2,1)S(1)} %collective-permute-done.refs_1_, ...), custom_call_target="tpu_custom_call" | custom-call | flops 1207959552 | bytes 4194304 | tf_op jit(solution)/shard_map/score/pallas_call | solution.py:303
  24.1 8.3 %all_to_all.10 = f32[8,1,128]{2,1,0:T(1,128)S(1)} all-to-all(f32[8,1,128]{2,1,0:T(1,128)S(1)} %get-tuple-element.21), channel_id=1, replica_groups={{13,1,5,9,12,0,4,8},{15,3,7,11,14,2,6,10},{29,17,21,25,28,16,20,24},{31..., dimensions={0} | all-to-all | bytes 8192 | tf_op jit(solution)/shard_map/all_to_all | solution.py:228
  32.4 0.6 %log_subtract_fusion = f32[64]{0:T(128)} fusion(f32[128]{0:T(128)S(1)} %reduce_sum.9), kind=kLoop, calls=%fused_computation | loop fusion | flops 64 | bytes 768 | tf_op jit(solution)/shard_map/sub | solution.py:337
  (1 shorter events, 0.0 us)
Async XLA Ops:
  0.6 7.6 %copy-start.1 = (bf16[128,1024]{1,0:T(8,128)(2,1)S(1)}, bf16[128,1024]{1,0:T(8,128)(2,1)}, u32[]{:S(2)}) copy-start(bf16[128,1024]{1,0:T(8,128)(2,1)} %refs_4_.1) | copy-start | bytes 786436
  0.6 20.8 %collective-permute-start.4 = (bf16[1024,1024]{1,0:T(8,128)(2,1)}, bf16[1024,1024]{1,0:T(8,128)(2,1)}, u32[]{:S(2)}, u32[]{:S(2)}) collective-permute-start(bf16[1024,1024]{1,0:T(8,128)(2,1)} %refs_6_.1), channel_id=1, source_target_pairs={{0,2},{2,0},{1,3},{3,1},{4,6},{6,4},{5,7},{7,5},{8,10},{10,8},{9,1... | collective-permute-start | bytes 6291464 | tf_op jit(solution)/shard_map/ppermute | solution.py:234
  4.1 17.4 %copy-start = (bf16[1024,1024]{1,0:T(8,128)(2,1)S(1)}, bf16[1024,1024]{1,0:T(8,128)(2,1)}, u32[]{:S(2)}) copy-start(bf16[1024,1024]{1,0:T(8,128)(2,1)} %refs_6_.1) | copy-start | bytes 6291460
  4.1 11.1 %collective-permute-start = (bf16[64,1024]{1,0:T(8,128)(2,1)S(1)}, bf16[64,1024]{1,0:T(8,128)(2,1)S(1)}, u32[]{:S(2)}, u32[]{:S(2)}) collective-permute-start(bf16[64,1024]{1,0:T(8,128)(2,1)S(1)} %get-tuple-element.15.chosen.refs_0_), channel_id=1, source_target_pairs={{0,8},{4,12},{8,0},{12,4},{1,9},{5,13},{9,1},{13,5},{2,10},{6,14},... | collective-permute-start | bytes 393224 | tf_op jit(solution)/shard_map/ppermute | solution.py:234
  6.6 8.5 %collective-permute-start.1 = (bf16[64,1024]{1,0:T(8,128)(2,1)S(1)}, bf16[64,1024]{1,0:T(8,128)(2,1)S(1)}, u32[]{:S(2)}, u32[]{:S(2)}) collective-permute-start(bf16[64,1024]{1,0:T(8,128)(2,1)S(1)} %get-tuple-element.15.chosen.refs_0_), channel_id=1, source_target_pairs={{0,4},{4,0},{8,12},{12,8},{1,5},{5,1},{9,13},{13,9},{2,6},{6,2},{1... | collective-permute-start | bytes 393224 | tf_op jit(solution)/shard_map/ppermute | solution.py:234
  8.2 13.2 %collective-permute-start.3 = (bf16[128,1024]{1,0:T(8,128)(2,1)S(1)}, bf16[128,1024]{1,0:T(8,128)(2,1)S(1)}, u32[]{:S(2)}, u32[]{:S(2)}) collective-permute-start(bf16[128,1024]{1,0:T(8,128)(2,1)S(1)} %copy-done.1), channel_id=1, source_target_pairs={{0,1},{1,0},{2,3},{3,2},{4,5},{5,4},{6,7},{7,6},{8,9},{9,8},{10,11... | collective-permute-start | bytes 786440 | tf_op jit(solution)/shard_map/ppermute | solution.py:234
  10.5 10.6 %all-to-all-start = ((bf16[8,64,128]{2,1,0:T(8,128)(2,1)}), bf16[8,64,128]{2,1,0:T(8,128)(2,1)S(1)}, u32[]{:S(2)}, u32[]{:S(2)}) async-start(bf16[8,64,128]{2,1,0:T(8,128)(2,1)} %attend.1), calls=%async_computation | async-start | bytes 262144 | tf_op jit(solution)/shard_map/all_to_all | solution.py:228
  15.2 6.3 %collective-permute-start.2 = (bf16[64,1024]{1,0:T(8,128)(2,1)S(1)}, bf16[64,1024]{1,0:T(8,128)(2,1)S(1)}, u32[]{:S(2)}, u32[]{:S(2)}) collective-permute-start(bf16[64,1024]{1,0:T(8,128)(2,1)S(1)} %collective-permute-done.refs_1_), channel_id=1, source_target_pairs={{0,4},{4,0},{8,12},{12,8},{1,5},{5,1},{9,13},{13,9},{2,6},{6,2},{1... | collective-permute-start | bytes 393224 | tf_op jit(solution)/shard_map/ppermute | solution.py:234
